TPU v7x, 256 devices: a whole 4x4x8 slice. The times are simulated.
256 devices in a mesh: ctx: 32 (over z, y_lo, core), head: 8 (over x, y_hi).
Axes of the slice: x: 4, y: 4 (y_hi: 2, y_lo: 2; y = y_hi * 2 + y_lo), z: 8, core: 2. Of those that a mesh axis runs over, the one named last changes fastest.
Arguments:
- queries: bfloat16 [6144, 4096], P('ctx', 'head'), may hold values from -9 to 9
- keys: bfloat16 [6144, 1024], P('ctx', 'head'), may hold values from -9 to 9
- values: bfloat16 [6144, 1024], P('ctx', 'head'), may hold values from -6 to 6
- grad_out: bfloat16 [6144, 4096], P('ctx', 'head'), may hold values from -6 to 6
- out_weight: bfloat16 [4096, 4096], P('head'), may hold values from -0.09375 to 0.09375
- lengths: int32 [8], replicated, may hold values from 1 to 1536, 6144 in all
Outputs:
- grad_queries: bfloat16 [6144, 4096], P('ctx', 'head')
- grad_keys: bfloat16 [6144, 1024], P('ctx', 'head')
- grad_values: bfloat16 [6144, 1024], P('ctx', 'head')
Inputs may be any that keep to these rules, and one draw needn't show every extreme that they name: `lengths`: the 8 documents fill all 6144 positions in order; each has at most 1536 tokens and one has exactly 1536.
All inputs are finite; a program needn't handle non-finite values.
Results may differ from a plain program's by a relative error of at most 0.0064.
Values may be sent and summed in bfloat16 or wider, within the bound.
No kernel may reach another device: no remote copies, remote signals or barrier semaphores. Data moves between devices by JAX's collectives and lax.ppermute only.
A program may use at most 64 MiB of HBM per device.

v0:
```python
import jax
import jax.numpy as jnp
from jax import lax
from jax.sharding import PartitionSpec as P

HEAD_DIM = 128


NEG = -1e30


def from_behind(x, axis, by):
    peers = lax.axis_size(axis)
    pairs = [(i, i + by) for i in range(peers) if 0 <= i + by < peers]
    return lax.ppermute(x, axis, pairs)


def shifted(value, axis, steps):
    count = lax.axis_size(axis)
    pairs = [(source, (source + steps) % count) for source in range(count)]
    return lax.ppermute(value, axis, pairs)


def segment_of(doc_ends, positions):
    return jnp.sum((doc_ends[None, :] <= positions[:, None]).astype(jnp.int32), axis=1)


def local(queries, keys, values, grad_out, out_weight, lengths):
    scaling = HEAD_DIM ** (-0.5)
    row_count = queries.shape[0]
    kv_width = keys.shape[1]
    kv_local = kv_width // HEAD_DIM
    group_size = queries.shape[1] // kv_width
    loop_len = lax.axis_size("ctx")
    my_block = lax.axis_index("ctx")
    doc_ends = jnp.cumsum(lengths)
    offsets = jnp.arange(row_count, dtype=jnp.int32)
    query_pos = my_block * row_count + offsets
    query_doc = segment_of(doc_ends, query_pos)
    grad_attn = lax.dot_general(
        lax.all_gather(grad_out, "head", axis=1, tiled=True),
        out_weight,
        (((1,), (1,)), ((), ())),
        preferred_element_type=jnp.float32,
    ).astype(jnp.bfloat16)
    query_four = queries.reshape(row_count, kv_local, group_size, HEAD_DIM)
    grad_four = grad_attn.reshape(row_count, kv_local, group_size, HEAD_DIM)
    reach_len = loop_len - 1

    def block_visible(source):
        key_pos = source * row_count + offsets
        key_doc = segment_of(doc_ends, key_pos)
        return (
            (query_doc[:, None] == key_doc[None, :])
            & (key_pos[None, :] <= query_pos[:, None])
            & (source >= 0)
        )

    def masked_scores(key_rows, visible):
        scores = (
            jnp.einsum("qgsd,kgd->gsqk", query_four, key_rows, preferred_element_type=jnp.float32)
            * scaling
        )
        return jnp.where(visible[None, None], scores, NEG)

    def forward_update(soft_state, kv_pair, source):
        run_max, run_sum, run_dot = soft_state
        key_rows = kv_pair[0].reshape(row_count, kv_local, HEAD_DIM)
        value_rows = kv_pair[1].reshape(row_count, kv_local, HEAD_DIM)
        visible = block_visible(source)
        scores = masked_scores(key_rows, visible)
        new_max = jnp.maximum(run_max, jnp.max(scores, axis=-1))
        weights = jnp.where(visible[None, None], jnp.exp(scores - new_max[..., None]), 0.0)
        grad_prob = jnp.einsum(
            "qgsd,kgd->gsqk", grad_four, value_rows, preferred_element_type=jnp.float32
        )
        factor = jnp.exp(run_max - new_max)
        new_sum = run_sum * factor + jnp.sum(weights, axis=-1)
        new_dot = run_dot * factor + jnp.sum(weights * grad_prob, axis=-1)
        return (new_max, new_sum, new_dot)

    def forward_step(soft_state, kv_pair, source):
        return forward_update(soft_state, kv_pair, source)

    kv_start = jnp.stack([keys, values])
    stat_shape = (kv_local, group_size, row_count)
    soft_state = (
        jnp.full(stat_shape, NEG, jnp.float32),
        jnp.zeros(stat_shape, jnp.float32),
        jnp.zeros(stat_shape, jnp.float32),
    )
    soft_state = forward_step(soft_state, kv_start, my_block)
    kept_blocks = jnp.zeros((max(reach_len, 1), 2, row_count, kv_width), kv_start.dtype)

    def forward_turn(turn_index, carried):
        kv_pair, current, stored = carried
        kv_pair = from_behind(kv_pair, "ctx", 1)
        return (kv_pair, forward_step(current, kv_pair, my_block - turn_index), stored)

    moved_pair, soft_state, kept_blocks = lax.fori_loop(
        1, reach_len + 1, forward_turn, (kv_start, soft_state, kept_blocks)
    )
    run_max, run_sum, run_dot = soft_state
    log_total = run_max + jnp.log(run_sum)
    row_dot = run_dot / run_sum

    def backward_update(kv_pair, source):
        key_rows = kv_pair[0].reshape(row_count, kv_local, HEAD_DIM)
        value_rows = kv_pair[1].reshape(row_count, kv_local, HEAD_DIM)
        visible = block_visible(source)
        scores = masked_scores(key_rows, visible)
        probability = jnp.where(visible[None, None], jnp.exp(scores - log_total[..., None]), 0.0)
        grad_prob = jnp.einsum(
            "qgsd,kgd->gsqk", grad_four, value_rows, preferred_element_type=jnp.float32
        )
        dscore = probability * (grad_prob - row_dot[..., None])
        prob_round = probability.astype(jnp.bfloat16)
        dscore_round = dscore.astype(jnp.bfloat16)
        value_add = jnp.einsum(
            "gsqk,qgsd->kgd", prob_round, grad_four, preferred_element_type=jnp.float32
        )
        key_add = (
            jnp.einsum(
                "gsqk,qgsd->kgd", dscore_round, query_four, preferred_element_type=jnp.float32
            )
            * scaling
        )
        query_add = (
            jnp.einsum("gsqk,kgd->qgsd", dscore_round, key_rows, preferred_element_type=jnp.float32)
            * scaling
        )
        kv_add = jnp.stack(
            [key_add.reshape(row_count, kv_width), value_add.reshape(row_count, kv_width)]
        )
        return (query_add, kv_add)

    def backward_step(kv_pair, source):
        return backward_update(kv_pair, source)

    query_grad, kv_grad = backward_step(kv_start, my_block)

    def backward_turn(turn_index, carried):
        kv_pair, travel_grad, query_acc = carried
        kv_pair = from_behind(kv_pair, "ctx", 1)
        travel_grad = shifted(travel_grad, "ctx", 1)
        query_add, kv_add = backward_step(kv_pair, my_block - turn_index)
        return (kv_pair, travel_grad + kv_add, query_acc + query_add)

    moved_pair, kv_grad, query_grad = lax.fori_loop(
        1, reach_len + 1, backward_turn, (kv_start, kv_grad, query_grad)
    )
    kv_grad = shifted(kv_grad.astype(jnp.bfloat16), "ctx", -reach_len).astype(kv_grad.dtype)
    grad_queries = query_grad.reshape(row_count, queries.shape[1]).astype(jnp.bfloat16)
    return (grad_queries, kv_grad[0].astype(jnp.bfloat16), kv_grad[1].astype(jnp.bfloat16))


def solution(mesh):
    return jax.shard_map(
        local,
        mesh=mesh,
        in_specs=(
            P("ctx", "head"),
            P("ctx", "head"),
            P("ctx", "head"),
            P("ctx", "head"),
            P("head", None),
            P(),
        ),
        out_specs=(P("ctx", "head"), P("ctx", "head"), P("ctx", "head")),
        check_vma=False,
    )
```

profile of v0, /device:TPU:128, one launch (start us, length us, event | category | flops | bytes accessed | tf_op | source)
XLA Modules:
  0.0 683.2 jit_solution(6794058345203768758)
XLA Ops:
  12.1 57.6 %all-gather.2.cloned.1.call-done = bf16[192,4096]{1,0:T(8,128)(2,1)} async-done(((bf16[192,512]{1,0:T(8,128)(2,1)}), bf16[192,4096]{1,0:T(8,128)(2,1)}) %all-gather.2.cloned.1.call-update) | async-done | bytes 1572880 | tf_op jit(solution)/shard_map/all_gather | solution.py:41
  74.5 277.8 %while.38 = (s32[]{:T(128)}, bf16[2,192,128]{2,1,0:T(8,128)(2,1)S(1)}, f32[1,4,192]{2,1,0:T(4,128)S(1)}, f32[1,4,192]{2,1,0:T(4,128)S(1)}, f32[1,4,192]{2,1,0:T(...) while((s32[]{:T(128)}, ...), condition=%wide.region_10.11_spmd.clone, body=%wide.region_5.10_spmd.clone.sunk | while | flops 77126592 | bytes 3282167 | solution.py:100
  76.8 5.9 collective-permute-done
  85.8 5.9 collective-permute-done
  94.7 5.9 collective-permute-done
  103.7 5.9 collective-permute-done
  112.7 5.9 collective-permute-done
  121.6 5.9 collective-permute-done
  130.6 5.9 collective-permute-done
  139.5 5.9 collective-permute-done
  148.5 5.9 collective-permute-done
  157.4 5.9 collective-permute-done
  166.4 5.9 collective-permute-done
  175.4 5.9 collective-permute-done
  184.3 5.9 collective-permute-done
  193.3 5.9 collective-permute-done
  202.2 5.9 collective-permute-done
  211.2 5.9 collective-permute-done
  220.2 5.9 collective-permute-done
  229.1 5.9 collective-permute-done
  238.1 5.9 collective-permute-done
  247.0 5.9 collective-permute-done
  256.0 5.9 collective-permute-done
  264.9 5.9 collective-permute-done
  273.9 5.9 collective-permute-done
  282.9 5.9 collective-permute-done
  291.8 5.9 collective-permute-done
  300.8 5.9 collective-permute-done
  309.7 5.9 collective-permute-done
  318.7 5.9 collective-permute-done
  345.6 5.9 collective-permute-done
  353.5 315.9 %while.39 = (s32[]{:T(128)}, bf16[2,192,128]{2,1,0:T(8,128)(2,1)S(1)}, f32[2,192,128]{2,1,0:T(8,128)S(1)}, f32[192,1,4,128]{3,0,2,1:T(8,128)S(1)}, s32[192]{0:T(...) while((s32[]{:T(128)}, ...), condition=%wide.region_13.14_spmd.clone, body=%wide.region_11.13_spmd.clone.sunk | while | flops 190395072 | bytes 6932775 | solution.py:149
  (844 shorter events, 435.1 us)
Async XLA Ops:
  7.2 62.6 %all-gather.2.cloned.1.call-start = ((), (), s32[]{:S(2)}) async-start(), calls=%async_computation | async-start | bytes 1769472 | tf_op jit(solution)/shard_map/all_gather | solution.py:41
  355.5 8.2 %collective-permute-start.2 = (f32[2,192,128]{2,1,0:T(8,128)S(1)}, f32[2,192,128]{2,1,0:T(8,128)S(1)}, u32[]{:S(2)}, u32[]{:S(2)}) collective-permute-start(f32[2,192,128]{2,1,0:T(8,128)S(1)} %get-tuple-element.823), channel_id=1, source_target_pairs={{0,8},{8,16},{16,24},{24,32},{32,40},{40,48},{48,56},{56,64},{64,7... | collective-permute-start | bytes 589832 | tf_op jit(solution)/shard_map/while/body/eval_jaxpr/ppermute | solution.py:21
  365.7 8.2 %collective-permute-start.2 = (f32[2,192,128]{2,1,0:T(8,128)S(1)}, f32[2,192,128]{2,1,0:T(8,128)S(1)}, u32[]{:S(2)}, u32[]{:S(2)}) collective-permute-start(f32[2,192,128]{2,1,0:T(8,128)S(1)} %get-tuple-element.823), channel_id=1, source_target_pairs={{0,8},{8,16},{16,24},{24,32},{32,40},{40,48},{48,56},{56,64},{64,7... | collective-permute-start | bytes 589832 | tf_op jit(solution)/shard_map/while/body/eval_jaxpr/ppermute | solution.py:21
  375.9 8.2 %collective-permute-start.2 = (f32[2,192,128]{2,1,0:T(8,128)S(1)}, f32[2,192,128]{2,1,0:T(8,128)S(1)}, u32[]{:S(2)}, u32[]{:S(2)}) collective-permute-start(f32[2,192,128]{2,1,0:T(8,128)S(1)} %get-tuple-element.823), channel_id=1, source_target_pairs={{0,8},{8,16},{16,24},{24,32},{32,40},{40,48},{48,56},{56,64},{64,7... | collective-permute-start | bytes 589832 | tf_op jit(solution)/shard_map/while/body/eval_jaxpr/ppermute | solution.py:21
  386.1 8.2 %collective-permute-start.2 = (f32[2,192,128]{2,1,0:T(8,128)S(1)}, f32[2,192,128]{2,1,0:T(8,128)S(1)}, u32[]{:S(2)}, u32[]{:S(2)}) collective-permute-start(f32[2,192,128]{2,1,0:T(8,128)S(1)} %get-tuple-element.823), channel_id=1, source_target_pairs={{0,8},{8,16},{16,24},{24,32},{32,40},{40,48},{48,56},{56,64},{64,7... | collective-permute-start | bytes 589832 | tf_op jit(solution)/shard_map/while/body/eval_jaxpr/ppermute | solution.py:21
  396.2 8.2 %collective-permute-start.2 = (f32[2,192,128]{2,1,0:T(8,128)S(1)}, f32[2,192,128]{2,1,0:T(8,128)S(1)}, u32[]{:S(2)}, u32[]{:S(2)}) collective-permute-start(f32[2,192,128]{2,1,0:T(8,128)S(1)} %get-tuple-element.823), channel_id=1, source_target_pairs={{0,8},{8,16},{16,24},{24,32},{32,40},{40,48},{48,56},{56,64},{64,7... | collective-permute-start | bytes 589832 | tf_op jit(solution)/shard_map/while/body/eval_jaxpr/ppermute | solution.py:21
  406.4 8.2 %collective-permute-start.2 = (f32[2,192,128]{2,1,0:T(8,128)S(1)}, f32[2,192,128]{2,1,0:T(8,128)S(1)}, u32[]{:S(2)}, u32[]{:S(2)}) collective-permute-start(f32[2,192,128]{2,1,0:T(8,128)S(1)} %get-tuple-element.823), channel_id=1, source_target_pairs={{0,8},{8,16},{16,24},{24,32},{32,40},{40,48},{48,56},{56,64},{64,7... | collective-permute-start | bytes 589832 | tf_op jit(solution)/shard_map/while/body/eval_jaxpr/ppermute | solution.py:21
  416.6 8.2 %collective-permute-start.2 = (f32[2,192,128]{2,1,0:T(8,128)S(1)}, f32[2,192,128]{2,1,0:T(8,128)S(1)}, u32[]{:S(2)}, u32[]{:S(2)}) collective-permute-start(f32[2,192,128]{2,1,0:T(8,128)S(1)} %get-tuple-element.823), channel_id=1, source_target_pairs={{0,8},{8,16},{16,24},{24,32},{32,40},{40,48},{48,56},{56,64},{64,7... | collective-permute-start | bytes 589832 | tf_op jit(solution)/shard_map/while/body/eval_jaxpr/ppermute | solution.py:21
  426.8 8.2 %collective-permute-start.2 = (f32[2,192,128]{2,1,0:T(8,128)S(1)}, f32[2,192,128]{2,1,0:T(8,128)S(1)}, u32[]{:S(2)}, u32[]{:S(2)}) collective-permute-start(f32[2,192,128]{2,1,0:T(8,128)S(1)} %get-tuple-element.823), channel_id=1, source_target_pairs={{0,8},{8,16},{16,24},{24,32},{32,40},{40,48},{48,56},{56,64},{64,7... | collective-permute-start | bytes 589832 | tf_op jit(solution)/shard_map/while/body/eval_jaxpr/ppermute | solution.py:21
  437.0 8.2 %collective-permute-start.2 = (f32[2,192,128]{2,1,0:T(8,128)S(1)}, f32[2,192,128]{2,1,0:T(8,128)S(1)}, u32[]{:S(2)}, u32[]{:S(2)}) collective-permute-start(f32[2,192,128]{2,1,0:T(8,128)S(1)} %get-tuple-element.823), channel_id=1, source_target_pairs={{0,8},{8,16},{16,24},{24,32},{32,40},{40,48},{48,56},{56,64},{64,7... | collective-permute-start | bytes 589832 | tf_op jit(solution)/shard_map/while/body/eval_jaxpr/ppermute | solution.py:21
  447.2 8.2 %collective-permute-start.2 = (f32[2,192,128]{2,1,0:T(8,128)S(1)}, f32[2,192,128]{2,1,0:T(8,128)S(1)}, u32[]{:S(2)}, u32[]{:S(2)}) collective-permute-start(f32[2,192,128]{2,1,0:T(8,128)S(1)} %get-tuple-element.823), channel_id=1, source_target_pairs={{0,8},{8,16},{16,24},{24,32},{32,40},{40,48},{48,56},{56,64},{64,7... | collective-permute-start | bytes 589832 | tf_op jit(solution)/shard_map/while/body/eval_jaxpr/ppermute | solution.py:21
  457.4 8.2 %collective-permute-start.2 = (f32[2,192,128]{2,1,0:T(8,128)S(1)}, f32[2,192,128]{2,1,0:T(8,128)S(1)}, u32[]{:S(2)}, u32[]{:S(2)}) collective-permute-start(f32[2,192,128]{2,1,0:T(8,128)S(1)} %get-tuple-element.823), channel_id=1, source_target_pairs={{0,8},{8,16},{16,24},{24,32},{32,40},{40,48},{48,56},{56,64},{64,7... | collective-permute-start | bytes 589832 | tf_op jit(solution)/shard_map/while/body/eval_jaxpr/ppermute | solution.py:21
  467.6 8.2 %collective-permute-start.2 = (f32[2,192,128]{2,1,0:T(8,128)S(1)}, f32[2,192,128]{2,1,0:T(8,128)S(1)}, u32[]{:S(2)}, u32[]{:S(2)}) collective-permute-start(f32[2,192,128]{2,1,0:T(8,128)S(1)} %get-tuple-element.823), channel_id=1, source_target_pairs={{0,8},{8,16},{16,24},{24,32},{32,40},{40,48},{48,56},{56,64},{64,7... | collective-permute-start | bytes 589832 | tf_op jit(solution)/shard_map/while/body/eval_jaxpr/ppermute | solution.py:21
  477.8 8.2 %collective-permute-start.2 = (f32[2,192,128]{2,1,0:T(8,128)S(1)}, f32[2,192,128]{2,1,0:T(8,128)S(1)}, u32[]{:S(2)}, u32[]{:S(2)}) collective-permute-start(f32[2,192,128]{2,1,0:T(8,128)S(1)} %get-tuple-element.823), channel_id=1, source_target_pairs={{0,8},{8,16},{16,24},{24,32},{32,40},{40,48},{48,56},{56,64},{64,7... | collective-permute-start | bytes 589832 | tf_op jit(solution)/shard_map/while/body/eval_jaxpr/ppermute | solution.py:21
  487.9 8.2 %collective-permute-start.2 = (f32[2,192,128]{2,1,0:T(8,128)S(1)}, f32[2,192,128]{2,1,0:T(8,128)S(1)}, u32[]{:S(2)}, u32[]{:S(2)}) collective-permute-start(f32[2,192,128]{2,1,0:T(8,128)S(1)} %get-tuple-element.823), channel_id=1, source_target_pairs={{0,8},{8,16},{16,24},{24,32},{32,40},{40,48},{48,56},{56,64},{64,7... | collective-permute-start | bytes 589832 | tf_op jit(solution)/shard_map/while/body/eval_jaxpr/ppermute | solution.py:21
  498.1 8.2 %collective-permute-start.2 = (f32[2,192,128]{2,1,0:T(8,128)S(1)}, f32[2,192,128]{2,1,0:T(8,128)S(1)}, u32[]{:S(2)}, u32[]{:S(2)}) collective-permute-start(f32[2,192,128]{2,1,0:T(8,128)S(1)} %get-tuple-element.823), channel_id=1, source_target_pairs={{0,8},{8,16},{16,24},{24,32},{32,40},{40,48},{48,56},{56,64},{64,7... | collective-permute-start | bytes 589832 | tf_op jit(solution)/shard_map/while/body/eval_jaxpr/ppermute | solution.py:21
  508.3 8.2 %collective-permute-start.2 = (f32[2,192,128]{2,1,0:T(8,128)S(1)}, f32[2,192,128]{2,1,0:T(8,128)S(1)}, u32[]{:S(2)}, u32[]{:S(2)}) collective-permute-start(f32[2,192,128]{2,1,0:T(8,128)S(1)} %get-tuple-element.823), channel_id=1, source_target_pairs={{0,8},{8,16},{16,24},{24,32},{32,40},{40,48},{48,56},{56,64},{64,7... | collective-permute-start | bytes 589832 | tf_op jit(solution)/shard_map/while/body/eval_jaxpr/ppermute | solution.py:21
  518.5 8.2 %collective-permute-start.2 = (f32[2,192,128]{2,1,0:T(8,128)S(1)}, f32[2,192,128]{2,1,0:T(8,128)S(1)}, u32[]{:S(2)}, u32[]{:S(2)}) collective-permute-start(f32[2,192,128]{2,1,0:T(8,128)S(1)} %get-tuple-element.823), channel_id=1, source_target_pairs={{0,8},{8,16},{16,24},{24,32},{32,40},{40,48},{48,56},{56,64},{64,7... | collective-permute-start | bytes 589832 | tf_op jit(solution)/shard_map/while/body/eval_jaxpr/ppermute | solution.py:21
  528.7 8.2 %collective-permute-start.2 = (f32[2,192,128]{2,1,0:T(8,128)S(1)}, f32[2,192,128]{2,1,0:T(8,128)S(1)}, u32[]{:S(2)}, u32[]{:S(2)}) collective-permute-start(f32[2,192,128]{2,1,0:T(8,128)S(1)} %get-tuple-element.823), channel_id=1, source_target_pairs={{0,8},{8,16},{16,24},{24,32},{32,40},{40,48},{48,56},{56,64},{64,7... | collective-permute-start | bytes 589832 | tf_op jit(solution)/shard_map/while/body/eval_jaxpr/ppermute | solution.py:21
  538.9 8.2 %collective-permute-start.2 = (f32[2,192,128]{2,1,0:T(8,128)S(1)}, f32[2,192,128]{2,1,0:T(8,128)S(1)}, u32[]{:S(2)}, u32[]{:S(2)}) collective-permute-start(f32[2,192,128]{2,1,0:T(8,128)S(1)} %get-tuple-element.823), channel_id=1, source_target_pairs={{0,8},{8,16},{16,24},{24,32},{32,40},{40,48},{48,56},{56,64},{64,7... | collective-permute-start | bytes 589832 | tf_op jit(solution)/shard_map/while/body/eval_jaxpr/ppermute | solution.py:21
  549.1 8.2 %collective-permute-start.2 = (f32[2,192,128]{2,1,0:T(8,128)S(1)}, f32[2,192,128]{2,1,0:T(8,128)S(1)}, u32[]{:S(2)}, u32[]{:S(2)}) collective-permute-start(f32[2,192,128]{2,1,0:T(8,128)S(1)} %get-tuple-element.823), channel_id=1, source_target_pairs={{0,8},{8,16},{16,24},{24,32},{32,40},{40,48},{48,56},{56,64},{64,7... | collective-permute-start | bytes 589832 | tf_op jit(solution)/shard_map/while/body/eval_jaxpr/ppermute | solution.py:21
  559.3 8.2 %collective-permute-start.2 = (f32[2,192,128]{2,1,0:T(8,128)S(1)}, f32[2,192,128]{2,1,0:T(8,128)S(1)}, u32[]{:S(2)}, u32[]{:S(2)}) collective-permute-start(f32[2,192,128]{2,1,0:T(8,128)S(1)} %get-tuple-element.823), channel_id=1, source_target_pairs={{0,8},{8,16},{16,24},{24,32},{32,40},{40,48},{48,56},{56,64},{64,7... | collective-permute-start | bytes 589832 | tf_op jit(solution)/shard_map/while/body/eval_jaxpr/ppermute | solution.py:21
  569.5 8.2 %collective-permute-start.2 = (f32[2,192,128]{2,1,0:T(8,128)S(1)}, f32[2,192,128]{2,1,0:T(8,128)S(1)}, u32[]{:S(2)}, u32[]{:S(2)}) collective-permute-start(f32[2,192,128]{2,1,0:T(8,128)S(1)} %get-tuple-element.823), channel_id=1, source_target_pairs={{0,8},{8,16},{16,24},{24,32},{32,40},{40,48},{48,56},{56,64},{64,7... | collective-permute-start | bytes 589832 | tf_op jit(solution)/shard_map/while/body/eval_jaxpr/ppermute | solution.py:21
  579.6 8.2 %collective-permute-start.2 = (f32[2,192,128]{2,1,0:T(8,128)S(1)}, f32[2,192,128]{2,1,0:T(8,128)S(1)}, u32[]{:S(2)}, u32[]{:S(2)}) collective-permute-start(f32[2,192,128]{2,1,0:T(8,128)S(1)} %get-tuple-element.823), channel_id=1, source_target_pairs={{0,8},{8,16},{16,24},{24,32},{32,40},{40,48},{48,56},{56,64},{64,7... | collective-permute-start | bytes 589832 | tf_op jit(solution)/shard_map/while/body/eval_jaxpr/ppermute | solution.py:21
  589.8 8.2 %collective-permute-start.2 = (f32[2,192,128]{2,1,0:T(8,128)S(1)}, f32[2,192,128]{2,1,0:T(8,128)S(1)}, u32[]{:S(2)}, u32[]{:S(2)}) collective-permute-start(f32[2,192,128]{2,1,0:T(8,128)S(1)} %get-tuple-element.823), channel_id=1, source_target_pairs={{0,8},{8,16},{16,24},{24,32},{32,40},{40,48},{48,56},{56,64},{64,7... | collective-permute-start | bytes 589832 | tf_op jit(solution)/shard_map/while/body/eval_jaxpr/ppermute | solution.py:21
  600.0 8.2 %collective-permute-start.2 = (f32[2,192,128]{2,1,0:T(8,128)S(1)}, f32[2,192,128]{2,1,0:T(8,128)S(1)}, u32[]{:S(2)}, u32[]{:S(2)}) collective-permute-start(f32[2,192,128]{2,1,0:T(8,128)S(1)} %get-tuple-element.823), channel_id=1, source_target_pairs={{0,8},{8,16},{16,24},{24,32},{32,40},{40,48},{48,56},{56,64},{64,7... | collective-permute-start | bytes 589832 | tf_op jit(solution)/shard_map/while/body/eval_jaxpr/ppermute | solution.py:21
  610.2 8.2 %collective-permute-start.2 = (f32[2,192,128]{2,1,0:T(8,128)S(1)}, f32[2,192,128]{2,1,0:T(8,128)S(1)}, u32[]{:S(2)}, u32[]{:S(2)}) collective-permute-start(f32[2,192,128]{2,1,0:T(8,128)S(1)} %get-tuple-element.823), channel_id=1, source_target_pairs={{0,8},{8,16},{16,24},{24,32},{32,40},{40,48},{48,56},{56,64},{64,7... | collective-permute-start | bytes 589832 | tf_op jit(solution)/shard_map/while/body/eval_jaxpr/ppermute | solution.py:21
  620.4 8.2 %collective-permute-start.2 = (f32[2,192,128]{2,1,0:T(8,128)S(1)}, f32[2,192,128]{2,1,0:T(8,128)S(1)}, u32[]{:S(2)}, u32[]{:S(2)}) collective-permute-start(f32[2,192,128]{2,1,0:T(8,128)S(1)} %get-tuple-element.823), channel_id=1, source_target_pairs={{0,8},{8,16},{16,24},{24,32},{32,40},{40,48},{48,56},{56,64},{64,7... | collective-permute-start | bytes 589832 | tf_op jit(solution)/shard_map/while/body/eval_jaxpr/ppermute | solution.py:21
  630.6 8.2 %collective-permute-start.2 = (f32[2,192,128]{2,1,0:T(8,128)S(1)}, f32[2,192,128]{2,1,0:T(8,128)S(1)}, u32[]{:S(2)}, u32[]{:S(2)}) collective-permute-start(f32[2,192,128]{2,1,0:T(8,128)S(1)} %get-tuple-element.823), channel_id=1, source_target_pairs={{0,8},{8,16},{16,24},{24,32},{32,40},{40,48},{48,56},{56,64},{64,7... | collective-permute-start | bytes 589832 | tf_op jit(solution)/shard_map/while/body/eval_jaxpr/ppermute | solution.py:21
  640.8 8.2 %collective-permute-start.2 = (f32[2,192,128]{2,1,0:T(8,128)S(1)}, f32[2,192,128]{2,1,0:T(8,128)S(1)}, u32[]{:S(2)}, u32[]{:S(2)}) collective-permute-start(f32[2,192,128]{2,1,0:T(8,128)S(1)} %get-tuple-element.823), channel_id=1, source_target_pairs={{0,8},{8,16},{16,24},{24,32},{32,40},{40,48},{48,56},{56,64},{64,7... | collective-permute-start | bytes 589832 | tf_op jit(solution)/shard_map/while/body/eval_jaxpr/ppermute | solution.py:21
  651.0 8.2 %collective-permute-start.2 = (f32[2,192,128]{2,1,0:T(8,128)S(1)}, f32[2,192,128]{2,1,0:T(8,128)S(1)}, u32[]{:S(2)}, u32[]{:S(2)}) collective-permute-start(f32[2,192,128]{2,1,0:T(8,128)S(1)} %get-tuple-element.823), channel_id=1, source_target_pairs={{0,8},{8,16},{16,24},{24,32},{32,40},{40,48},{48,56},{56,64},{64,7... | collective-permute-start | bytes 589832 | tf_op jit(solution)/shard_map/while/body/eval_jaxpr/ppermute | solution.py:21
  661.2 8.2 %collective-permute-start.2 = (f32[2,192,128]{2,1,0:T(8,128)S(1)}, f32[2,192,128]{2,1,0:T(8,128)S(1)}, u32[]{:S(2)}, u32[]{:S(2)}) collective-permute-start(f32[2,192,128]{2,1,0:T(8,128)S(1)} %get-tuple-element.823), channel_id=1, source_target_pairs={{0,8},{8,16},{16,24},{24,32},{32,40},{40,48},{48,56},{56,64},{64,7... | collective-permute-start | bytes 589832 | tf_op jit(solution)/shard_map/while/body/eval_jaxpr/ppermute | solution.py:21
  (66 other events, 1123.6 us)
Sparse Core Ops, SparseCore 0:
  10.5 59.2 all-gather.1
where the time goes:
time: 685 us; the launch traced here: 683 us
  waiting for transfers between devices  440 us (64%)
  starting transfers between devices  122 us (18%)
  matrix products  75.2 us (11%)
  other arithmetic  22.5 us (3%)
  between operations  14.2 us (2%)
    ppermute x62, waiting for transfers between devices, from_behind(): return lax.ppermute(x, axis, pairs)  361 us
    ppermute x62, starting transfers between devices, from_behind(): return lax.ppermute(x, axis, pairs)  119 us
    all_gather x1, waiting for transfers between devices, local(): lax.all_gather(grad_out, 'head', axis=1, tiled=True)  57.6 us
    dot_general x63, matrix products, masked_scores(): jnp.einsum('qgsd,kgd->gsqk', query_four, key_rows, preferred_element_type...  22 us
    ppermute x32, waiting for transfers between devices, shifted(): return lax.ppermute(value, axis, pairs)  20.9 us
  transfers between devices with their start and end apart: 95, of which 95 were waited for; matrix products, arithmetic and copies ran while one was open for 10% of the time, Pallas kernels for 0%

commit v1 on v0

v1 whole, which is shorter than its diff:
```python
import functools

import jax
import jax.numpy as jnp
from jax import lax
from jax.experimental import pallas as pl
from jax.experimental.pallas import tpu as pltpu
from jax.sharding import PartitionSpec as P

D = 128
HEADS = 4
ROWS = 192
LANES = HEADS * ROWS
REACH = 4
SLOTS = REACH + 1
NEG = -1e30
SCALE = D**-0.5
LOG2E = 1.4426950408889634
MIB = 1 << 20


def dot(a, b, ca, cb):
    return lax.dot_general(a, b, (((ca,), (cb,)), ((), ())), preferred_element_type=jnp.float32)


def stack_heads(src, dst):
    for h in range(HEADS):
        dst[h * ROWS : (h + 1) * ROWS, :] = src[:, h * D : (h + 1) * D]


def first_kernel(place_ref, lengths_ref, q_ref, own_ref, par_ref, p_own_ref, p_par_ref, o_ref, q4, s_own, s_par):
    me = place_ref[0]
    core = lax.rem(me, 2)
    chip = me - core
    stack_heads(q_ref, q4)
    lane = lax.broadcasted_iota(jnp.int32, (1, LANES), 1)
    pos = lane + me * ROWS
    for h in range(1, HEADS):
        pos = pos - jnp.where(lane >= h * ROWS, ROWS, 0)
    start = jnp.zeros((1, LANES), jnp.int32)
    end = jnp.int32(0)
    for d in range(lengths_ref.shape[0]):
        end = end + lengths_ref[d]
        start = jnp.where(end <= pos, end, start)
    queries = q4[...]
    row = lax.broadcasted_iota(jnp.int32, (ROWS, LANES), 0)

    def score(kv_ref, slot, core_of, diagonal):
        keys = kv_ref[pl.ds(pl.multiple_of(slot * ROWS, ROWS), ROWS), :D]
        s = dot(keys, queries, 1, 1) * (SCALE * LOG2E)
        key = row + ((chip + core_of) + 2 * (slot - REACH)) * ROWS
        visible = key >= start
        if diagonal:
            visible = visible & (key <= pos)
        return jnp.where(visible, s, NEG)

    def online(s, state):
        top, total = state
        new = jnp.maximum(top, jnp.max(s, axis=0, keepdims=True))
        total = total * jnp.exp2(top - new) + jnp.sum(jnp.exp2(s - new), axis=0, keepdims=True)
        return new, total

    s = score(own_ref, REACH, core, True)
    s_own[REACH * ROWS :, :] = s
    top = jnp.max(s, axis=0, keepdims=True)
    state = (top, jnp.sum(jnp.exp2(s - top), axis=0, keepdims=True))

    def sweep(i, state):
        at = pl.ds(pl.multiple_of(i * ROWS, ROWS), ROWS)
        s = score(own_ref, i, core, False)
        s_own[at, :] = s
        state = online(s, state)
        s = score(par_ref, i + core, 1 - core, False)
        s_par[at, :] = s
        return online(s, state)

    top, total = lax.fori_loop(0, REACH, sweep, state)
    log_total = top + jnp.log2(total)

    def weigh(s_ref, p_ref, kv_ref, i, slot, state):
        acc, mass = state
        at = pl.ds(pl.multiple_of(i * ROWS, ROWS), ROWS)
        prob = jnp.exp2(s_ref[at, :] - log_total).astype(jnp.bfloat16)
        p_ref[at, :] = prob
        values = kv_ref[pl.ds(pl.multiple_of(slot * ROWS, ROWS), ROWS), D:]
        acc = acc + dot(values, prob, 0, 0)
        mass = mass + jnp.sum(prob.astype(jnp.float32), axis=0, keepdims=True)
        return acc, mass

    def second(i, state):
        state = weigh(s_own, p_own_ref, own_ref, i, i, state)
        return weigh(s_par, p_par_ref, par_ref, i, i + core, state)

    state = (jnp.zeros((D, LANES), jnp.float32), jnp.zeros((1, LANES), jnp.float32))
    state = lax.fori_loop(0, REACH, second, state)
    acc, mass = weigh(s_own, p_own_ref, own_ref, REACH, REACH, state)
    o_ref[...] = acc / mass


def back_block(kv_ref, slot, p_ref, i, g4, q4, rd):
    kv_at = pl.ds(pl.multiple_of(slot * ROWS, ROWS), ROWS)
    prob = p_ref[pl.ds(pl.multiple_of(i * ROWS, ROWS), ROWS), :]
    dprob = dot(kv_ref[kv_at, D:], g4, 1, 1)
    ds = (prob.astype(jnp.float32) * (dprob - rd)).astype(jnp.bfloat16)
    dv = dot(prob, g4, 1, 0)
    dk = dot(ds, q4, 1, 0) * SCALE
    dq = dot(kv_ref[kv_at, :D], ds, 0, 0)
    return dk, dv, dq


def second_kernel(place_ref, head_ref, *refs):
    pieces, (w_ref, q_ref, par_ref, p_ref, o_ref, out_ref, g_ref, rd_ref, dq_ref, q4) = refs[:8], refs[8:]
    me = place_ref[0]
    core = lax.rem(me, 2)
    head = head_ref[0]
    stack_heads(q_ref, q4)

    def flip(i):
        return i + 1 - 2 * lax.rem(i, 2)

    def ring(by):
        return lax.rem(head + by + 8, 8)

    sources = (head, flip(head), ring(-2), ring(2), flip(ring(-2)), flip(ring(2)), ring(4), flip(ring(4)))
    acc = jnp.zeros((ROWS, HEADS * D), jnp.float32)
    for piece, source in zip(pieces, sources):
        acc = acc + dot(piece[...], w_ref[:, pl.ds(pl.multiple_of(source * 512, 512), 512)], 1, 1)
    acc = acc.astype(jnp.bfloat16)
    for h in range(HEADS):
        g_ref[h * ROWS : (h + 1) * ROWS, :] = acc[:, h * D : (h + 1) * D]
    g4 = g_ref[...]
    gt = jnp.transpose(g4.astype(jnp.float32))
    rd = jnp.sum(gt * o_ref[...], axis=0, keepdims=True)
    rd_ref[...] = rd
    dq_ref[...] = jnp.zeros((D, LANES), jnp.float32)
    out_ref[...] = jnp.zeros(out_ref.shape, out_ref.dtype)

    def step(i, _):
        dk, dv, dq = back_block(par_ref, i + core, p_ref, i, g4, q4[...], rd)
        at = pl.ds(pl.multiple_of((i + core) * ROWS, ROWS), ROWS)
        out_ref[at, :D] = dk.astype(jnp.bfloat16)
        out_ref[at, D:] = dv.astype(jnp.bfloat16)
        dq_ref[...] += dq
        return 0

    lax.fori_loop(0, REACH, step, 0)


def third_kernel(q_ref, own_ref, p_ref, g_ref, rd_ref, dq_in_ref, out_ref, dq_out_ref, q4, acc):
    stack_heads(q_ref, q4)
    g4 = g_ref[...]
    rd = rd_ref[...]
    acc[...] = dq_in_ref[...]

    def step(i, _):
        dk, dv, dq = back_block(own_ref, i, p_ref, i, g4, q4[...], rd)
        at = pl.ds(pl.multiple_of(i * ROWS, ROWS), ROWS)
        out_ref[at, :D] = dk
        out_ref[at, D:] = dv
        acc[...] += dq
        return 0

    lax.fori_loop(0, SLOTS, step, 0)
    dq = jnp.transpose(acc[...]) * SCALE
    for h in range(HEADS):
        dq_out_ref[:, h * D : (h + 1) * D] = dq[h * ROWS : (h + 1) * ROWS, :].astype(jnp.bfloat16)


def vmem(n):
    return [pl.BlockSpec(memory_space=pltpu.VMEM)] * n


def smem(n):
    return [pl.BlockSpec(memory_space=pltpu.SMEM)] * n


def params(mib):
    return pltpu.CompilerParams(vmem_limit_bytes=mib * MIB)


def cost(flops, nbytes, exps=0):
    return pl.CostEstimate(flops=int(flops), bytes_accessed=int(nbytes), transcendentals=int(exps))


def moved(x, axis, to):
    return lax.ppermute(x, axis, [(i, to(i)) for i in range(lax.axis_size(axis))])


def turned(x, axis, by):
    count = lax.axis_size(axis)
    return moved(x, axis, lambda i: (i + by) % count)


def local(queries, keys, values, grad_out, out_weight, lengths):
    bf16, f32 = jnp.bfloat16, jnp.float32
    place = lax.axis_index("ctx").astype(jnp.int32).reshape(1)
    head = lax.axis_index("head").astype(jnp.int32).reshape(1)
    kv = jnp.concatenate([keys, values], axis=1)

    other = moved(grad_out, "head", lambda i: i ^ 1)
    right = turned(grad_out, "head", 2)
    left = turned(grad_out, "head", -2)
    earlier = [turned(kv, "ctx", 2 * k) for k in range(REACH, 0, -1)]
    other_right = turned(other, "head", 2)
    other_left = turned(other, "head", -2)
    far = turned(right, "head", 2)
    other_far = turned(other_left, "head", -2)
    pieces = (grad_out, other, right, left, other_right, other_left, far, other_far)

    own = jnp.concatenate(earlier + [kv], axis=0)
    par = moved(own, "ctx", lambda i: i ^ 1)

    pair = ROWS * LANES * D * 2
    p_own, p_par, out_t = pl.pallas_call(
        first_kernel,
        out_shape=(
            jax.ShapeDtypeStruct((SLOTS * ROWS, LANES), bf16),
            jax.ShapeDtypeStruct((REACH * ROWS, LANES), bf16),
            jax.ShapeDtypeStruct((D, LANES), f32),
        ),
        in_specs=smem(2) + vmem(3),
        out_specs=tuple(vmem(3)),
        scratch_shapes=[
            pltpu.VMEM((LANES, D), bf16),
            pltpu.VMEM((SLOTS * ROWS, LANES), f32),
            pltpu.VMEM((REACH * ROWS, LANES), f32),
        ],
        compiler_params=params(24),
        cost_estimate=cost(18 * pair, 5 * MIB, 18 * ROWS * LANES),
        name="softmax",
    )(place, lengths, queries, own, par)

    par_grad, g4, rd, dq = pl.pallas_call(
        second_kernel,
        out_shape=(
            jax.ShapeDtypeStruct((SLOTS * ROWS, 2 * D), bf16),
            jax.ShapeDtypeStruct((LANES, D), bf16),
            jax.ShapeDtypeStruct((1, LANES), f32),
            jax.ShapeDtypeStruct((D, LANES), f32),
        ),
        in_specs=smem(2) + vmem(8 + 5),
        out_specs=tuple(vmem(4)),
        scratch_shapes=[pltpu.VMEM((LANES, D), bf16)],
        compiler_params=params(24),
        cost_estimate=cost(16 * pair, 8 * MIB),
        name="partner_grads",
    )(place, head, *pieces, out_weight, queries, par, p_par, out_t)

    back = moved(par_grad, "ctx", lambda i: i ^ 1)

    own_grad, grad_queries = pl.pallas_call(
        third_kernel,
        out_shape=(
            jax.ShapeDtypeStruct((SLOTS * ROWS, 2 * D), f32),
            jax.ShapeDtypeStruct((ROWS, HEADS * D), bf16),
        ),
        in_specs=vmem(6),
        out_specs=tuple(vmem(2)),
        scratch_shapes=[pltpu.VMEM((LANES, D), bf16), pltpu.VMEM((D, LANES), f32)],
        compiler_params=params(24),
        cost_estimate=cost(20 * pair, 5 * MIB),
        name="own_grads",
    )(queries, own, p_own, g4, rd, dq)

    both = own_grad + back.astype(f32)
    total = both[REACH * ROWS :]
    for m in range(REACH):
        part = both[m * ROWS : (m + 1) * ROWS].astype(bf16)
        total = total + turned(part, "ctx", -2 * (REACH - m)).astype(f32)
    total = total.astype(bf16)
    return grad_queries, total[:, :D], total[:, D:]


def solution(mesh):
    return jax.shard_map(
        local,
        mesh=mesh,
        in_specs=(
            P("ctx", "head"),
            P("ctx", "head"),
            P("ctx", "head"),
            P("ctx", "head"),
            P("head", None),
            P(),
        ),
        out_specs=(P("ctx", "head"), P("ctx", "head"), P("ctx", "head")),
        check_vma=False,
    )
```

time: 685 us -> 68.4 us (0.10)
  the two profiles are of different devices: /device:TPU:128 before, /device:TPU:64 now
where the time goes in v1:
time: 68.4 us; the launch traced here: 67.2 us
  starting transfers between devices  28.7 us (42%)
  waiting for transfers between devices  20.1 us (29%)
  Pallas kernels  11.8 us (17%)
  local copies, waits for them, and re-layouts  5.56 us (8%)
  between operations  0.79 us (1%)
    ppermute x17, starting transfers between devices, moved(): lax.ppermute(x, axis, [(i, to(i)) for i in range(lax.axis_size(axis))])  28.7 us
    ppermute x17, waiting for transfers between devices, moved(): lax.ppermute(x, axis, [(i, to(i)) for i in range(lax.axis_size(axis))])  20.1 us
    pallas_call x1, Pallas kernels, local(): pl.pallas_call(first_kernel, out_shape=(jax.ShapeDtypeStruct((SLOTS * ROW...  5.09 us
    pallas_call x1, Pallas kernels, local(): pl.pallas_call(second_kernel, out_shape=(jax.ShapeDtypeStruct((SLOTS * RO...  3.57 us
    unnamed x16, local copies, waits for them, and re-layouts  3.25 us
    pallas_call x1, Pallas kernels, local(): pl.pallas_call(third_kernel, out_shape=(jax.ShapeDtypeStruct((SLOTS * ROW...  3.18 us
  transfers between devices with their start and end apart: 17, of which 6 were waited for; matrix products, arithmetic and copies ran while one was open for 2% of the time, Pallas kernels for 12%

profile of v1, /device:TPU:64, one launch (start us, length us, event | category | flops | bytes accessed | tf_op | source)
XLA Modules:
  0.0 67.2 jit_solution(18383577064153516731)
XLA Ops:
  0.6 0.8 %constant_dynamic-update-slice_fusion.1 = bf16[192,256]{1,0:T(8,128)(2,1)S(1)} fusion(bf16[192,128]{1,0:T(8,128)(2,1)} %param.7), kind=kLoop, calls=%fused_computation.7 | loop fusion | bytes 98304
  1.4 0.8 %constant_dynamic-update-slice_fusion = bf16[192,256]{1,0:T(8,128)(2,1)S(1)} fusion(bf16[192,256]{1,0:T(8,128)(2,1)S(1)} %constant_dynamic-update-slice_fusion.1, bf16[192,128]{1,0:T(8,128)(2,1)} %param.8), kind=kLoop, calls=%fused_computation.6 | loop fusion | bytes 98304 | tf_op jit(solution)/shard_map/concatenate | solution.py:198
  2.3 4.6 %collective-permute-start = (bf16[192,256]{1,0:T(8,128)(2,1)S(1)}, bf16[192,256]{1,0:T(8,128)(2,1)S(1)}, u32[]{:S(2)}, u32[]{:S(2)}) collective-permute-start(bf16[192,256]{1,0:T(8,128)(2,1)S(1)} %constant_dynamic-update-slice_fusion), channel_id=1, source_target_pairs={{0,64},{8,72},{16,80},{24,88},{32,96},{40,104},{48,112},{56,120},{... | collective-permute-start | bytes 294920 | tf_op jit(solution)/shard_map/ppermute | solution.py:186
  6.8 2.0 %collective-permute-start.1 = (bf16[192,256]{1,0:T(8,128)(2,1)S(1)}, bf16[192,256]{1,0:T(8,128)(2,1)S(1)}, u32[]{:S(2)}, u32[]{:S(2)}) collective-permute-start(bf16[192,256]{1,0:T(8,128)(2,1)S(1)} %constant_dynamic-update-slice_fusion), channel_id=1, source_target_pairs={{0,48},{8,56},{16,64},{24,72},{32,80},{40,88},{48,96},{56,104},{64... | collective-permute-start | bytes 294920 | tf_op jit(solution)/shard_map/ppermute | solution.py:186
  8.9 1.0 %collective-permute-start.2 = (bf16[192,256]{1,0:T(8,128)(2,1)S(1)}, bf16[192,256]{1,0:T(8,128)(2,1)S(1)}, u32[]{:S(2)}, u32[]{:S(2)}) collective-permute-start(bf16[192,256]{1,0:T(8,128)(2,1)S(1)} %constant_dynamic-update-slice_fusion), channel_id=1, source_target_pairs={{0,32},{8,40},{16,48},{24,56},{32,64},{40,72},{48,80},{56,88},{64,... | collective-permute-start | bytes 294920 | tf_op jit(solution)/shard_map/ppermute | solution.py:186
  9.9 0.9 %collective-permute-start.3 = (bf16[192,256]{1,0:T(8,128)(2,1)S(1)}, bf16[192,256]{1,0:T(8,128)(2,1)S(1)}, u32[]{:S(2)}, u32[]{:S(2)}) collective-permute-start(bf16[192,256]{1,0:T(8,128)(2,1)S(1)} %constant_dynamic-update-slice_fusion), channel_id=1, source_target_pairs={{0,16},{8,24},{16,32},{24,40},{32,48},{40,56},{48,64},{56,72},{64,... | collective-permute-start | bytes 294920 | tf_op jit(solution)/shard_map/ppermute | solution.py:186
  10.8 3.2 %collective-permute-start.5 = (bf16[192,512]{1,0:T(8,128)(2,1)}, bf16[192,512]{1,0:T(8,128)(2,1)S(1)}, u32[]{:S(2)}, u32[]{:S(2)}) collective-permute-start(bf16[192,512]{1,0:T(8,128)(2,1)} %refs_0_.1), channel_id=1, source_target_pairs={{0,1},{1,0},{2,3},{3,2},{4,5},{5,4},{6,7},{7,6},{8,9},{9,8},{10,11... | collective-permute-start | bytes 589832 | tf_op jit(solution)/shard_map/ppermute | solution.py:186
  14.0 3.4 %collective-permute-done.1 = bf16[192,256]{1,0:T(8,128)(2,1)S(1)} collective-permute-done((bf16[192,256]{1,0:T(8,128)(2,1)S(1)}, bf16[192,256]{1,0:T(8,128)(2,1)S(1)}, u32[]{:S(2)}, u32[]{:S(2)}) %collective-permute-start.1) | collective-permute-done | bytes 98336 | tf_op jit(solution)/shard_map/ppermute | solution.py:186
  17.4 2.0 %collective-permute-done.3 = bf16[192,256]{1,0:T(8,128)(2,1)S(1)} collective-permute-done((bf16[192,256]{1,0:T(8,128)(2,1)S(1)}, bf16[192,256]{1,0:T(8,128)(2,1)S(1)}, u32[]{:S(2)}, u32[]{:S(2)}) %collective-permute-start.3) | collective-permute-done | bytes 98336 | tf_op jit(solution)/shard_map/ppermute | solution.py:186
  19.4 0.8 %constant_dynamic-update-slice_fusion.2 = bf16[960,256]{1,0:T(8,128)(2,1)S(1)} fusion(bf16[960,256]{1,0:T(8,128)(2,1)S(1)} %constant_dynamic-update-slice_fusion.3, bf16[192,128]{1,0:T(8,128)(2,1)} %param.7), kind=kLoop, calls=%fused_computation.8 | loop fusion | bytes 98304
  20.2 0.8 %constant_dynamic-update-slice_fusion.7.own_ref = bf16[960,256]{1,0:T(8,128)(2,1)S(1)} fusion(bf16[960,256]{1,0:T(8,128)(2,1)S(1)} %constant_dynamic-update-slice_fusion.2, bf16[192,128]{1,0:T(8,128)(2,1)} %param.8), kind=kLoop, calls=%fused_computation.13 | loop fusion | bytes 98304 | tf_op jit(solution)/shard_map/concatenate | solution.py:210
  21.1 1.6 %collective-permute-start.6 = (bf16[192,512]{1,0:T(8,128)(2,1)}, bf16[192,512]{1,0:T(8,128)(2,1)S(1)}, u32[]{:S(2)}, u32[]{:S(2)}) collective-permute-start(bf16[192,512]{1,0:T(8,128)(2,1)} %refs_0_.1), channel_id=1, source_target_pairs={{0,2},{1,3},{2,4},{3,5},{4,6},{5,7},{6,0},{7,1},{8,10},{9,11},{10,... | collective-permute-start | bytes 589832 | tf_op jit(solution)/shard_map/ppermute | solution.py:186
  22.7 1.7 %collective-permute-start.9 = (bf16[192,512]{1,0:T(8,128)(2,1)S(1)}, bf16[192,512]{1,0:T(8,128)(2,1)S(1)}, u32[]{:S(2)}, u32[]{:S(2)}) collective-permute-start(bf16[192,512]{1,0:T(8,128)(2,1)S(1)} %collective-permute-done.5.refs_1_), channel_id=1, source_target_pairs={{0,6},{1,7},{2,0},{3,1},{4,2},{5,3},{6,4},{7,5},{8,14},{9,15},{10,... | collective-permute-start | bytes 589832 | tf_op jit(solution)/shard_map/ppermute | solution.py:186
  24.4 1.5 %collective-permute-start.7 = (bf16[192,512]{1,0:T(8,128)(2,1)}, bf16[192,512]{1,0:T(8,128)(2,1)S(1)}, u32[]{:S(2)}, u32[]{:S(2)}) collective-permute-start(bf16[192,512]{1,0:T(8,128)(2,1)} %refs_0_.1), channel_id=1, source_target_pairs={{0,6},{1,7},{2,0},{3,1},{4,2},{5,3},{6,4},{7,5},{8,14},{9,15},{10,... | collective-permute-start | bytes 589832 | tf_op jit(solution)/shard_map/ppermute | solution.py:186
  26.0 0.5 collective-permute-start.8
  26.5 3.9 %collective-permute-done.6.refs_2_ = bf16[192,512]{1,0:T(8,128)(2,1)S(1)} collective-permute-done((bf16[192,512]{1,0:T(8,128)(2,1)}, bf16[192,512]{1,0:T(8,128)(2,1)S(1)}, u32[]{:S(2)}, u32[]{:S(2)}) %collective-permute-start.6) | collective-permute-done | bytes 196640 | tf_op jit(solution)/shard_map/ppermute | solution.py:186
  30.3 0.3 collective-permute-start.10
  30.6 3.0 %collective-permute-start.11 = (bf16[192,512]{1,0:T(8,128)(2,1)S(1)}, bf16[192,512]{1,0:T(8,128)(2,1)S(1)}, u32[]{:S(2)}, u32[]{:S(2)}) collective-permute-start(bf16[192,512]{1,0:T(8,128)(2,1)S(1)} %collective-permute-done.9.refs_5_), channel_id=1, source_target_pairs={{0,6},{1,7},{2,0},{3,1},{4,2},{5,3},{6,4},{7,5},{8,14},{9,15},{10,... | collective-permute-start | bytes 589832 | tf_op jit(solution)/shard_map/ppermute | solution.py:186
  33.6 0.9 %copy-done.2 = bf16[192,512]{1,0:T(8,128)(2,1)S(1)} copy-done((bf16[192,512]{1,0:T(8,128)(2,1)S(1)}, bf16[192,512]{1,0:T(8,128)(2,1)}, u32[]{:S(2)}) %copy-start.2) | copy-done | bytes 196632
  34.5 0.7 copy-done.4
  35.2 5.1 %softmax.1 = (bf16[960,768]{1,0:T(8,128)(2,1)S(1)}, bf16[768,768]{1,0:T(8,128)(2,1)S(1)}, f32[128,768]{1,0:T(8,128)S(1)}) custom-call(s32[1]{0:T(128)} %bitcast.place_ref, s32[8]{0:T(128)S(1)} %copy-done.4, bf16[192,512]{1,0:T(8,128)(2,1)S(1)} %copy-done.2, bf16[960,256]{1,0:T(8,128)(2,1)S(1)} %constant_dynamic-update-slice_fusion.7.own_ref, ...), custom_call_target="tpu_custom_call" | custom-call | flops 679477248 | bytes 5242880 | tf_op jit(solution)/shard_map/softmax/pallas_call | solution.py:214
  40.3 3.6 %partner_grads.1 = (bf16[960,256]{1,0:T(8,128)(2,1)S(1)}, bf16[768,128]{1,0:T(8,128)(2,1)S(1)}, f32[1,768]{1,0:T(1,128)S(1)}, f32[128,768]{1,0:T(8,128)S(1)}) custom-call(s32[1]{0:T(128)} %bitcast.place_ref, s32[1]{0:T(128)} %bitcast.1.head_ref, bf16[192,512]{1,0:T(8,128)(2,1)S(1)} %copy-done.1, bf16[192,512]{1,0:T(8,128)(2,1)S(1)} %collective-permute-done.5.refs_1_, ...), custom_call_target="tpu_custom_call" | custom-call | flops 603979776 | bytes 8388608 | tf_op jit(solution)/shard_map/partner_grads/pallas_call | solution.py:233
  43.9 0.3 collective-permute-start.12
  44.2 3.2 %own_grads.1 = (f32[960,256]{1,0:T(8,128)S(1)}, bf16[192,512]{1,0:T(8,128)(2,1)}) custom-call(bf16[192,512]{1,0:T(8,128)(2,1)S(1)} %copy-done.3, bf16[960,256]{1,0:T(8,128)(2,1)S(1)} %constant_dynamic-update-slice_fusion.7.own_ref, bf16[960,768]{1,0:T(8,128)(2,1)S(1)} %get-tuple-element.12.p_ref, bf16[768,128]{1,0:T(8,128)(2,1)S(1)} %get-tuple-element.15.g_ref, ...), custom_call_target="tpu_custom_call" | custom-call | flops 754974720 | bytes 5242880 | tf_op jit(solution)/shard_map/own_grads/pallas_call | solution.py:251
  47.4 0.2 fusion.4
  47.6 2.1 %collective-permute-start.16 = (bf16[192,256]{1,0:T(8,128)(2,1)S(1)}, bf16[192,256]{1,0:T(8,128)(2,1)S(1)}, u32[]{:S(2)}, u32[]{:S(2)}) collective-permute-start(bf16[192,256]{1,0:T(8,128)(2,1)S(1)} %get-tuple-element.24), channel_id=1, source_target_pairs={{0,240},{8,248},{16,0},{24,8},{32,16},{40,24},{48,32},{56,40},{64,... | collective-permute-start | bytes 294920 | tf_op jit(solution)/shard_map/ppermute | solution.py:186
  49.7 3.3 %collective-permute-start.14 = (bf16[192,256]{1,0:T(8,128)(2,1)S(1)}, bf16[192,256]{1,0:T(8,128)(2,1)S(1)}, u32[]{:S(2)}, u32[]{:S(2)}) collective-permute-start(bf16[192,256]{1,0:T(8,128)(2,1)S(1)} %get-tuple-element.26), channel_id=1, source_target_pairs={{0,208},{8,216},{16,224},{24,232},{32,240},{40,248},{48,0},{56,8},... | collective-permute-start | bytes 294920 | tf_op jit(solution)/shard_map/ppermute | solution.py:186
  53.0 2.6 %collective-permute-start.13 = (bf16[192,256]{1,0:T(8,128)(2,1)S(1)}, bf16[192,256]{1,0:T(8,128)(2,1)S(1)}, u32[]{:S(2)}, u32[]{:S(2)}) collective-permute-start(bf16[192,256]{1,0:T(8,128)(2,1)S(1)} %get-tuple-element.23), channel_id=1, source_target_pairs={{0,192},{8,200},{16,208},{24,216},{32,224},{40,232},{48,240},{56,2... | collective-permute-start | bytes 294920 | tf_op jit(solution)/shard_map/ppermute | solution.py:186
  55.7 1.2 %collective-permute-done.15 = bf16[192,256]{1,0:T(8,128)(2,1)S(1)} collective-permute-done((bf16[192,256]{1,0:T(8,128)(2,1)S(1)}, bf16[192,256]{1,0:T(8,128)(2,1)S(1)}, u32[]{:S(2)}, u32[]{:S(2)}) %collective-permute-start.15) | collective-permute-done | bytes 98336 | tf_op jit(solution)/shard_map/ppermute | solution.py:186
  56.9 3.2 %collective-permute-done.14 = bf16[192,256]{1,0:T(8,128)(2,1)S(1)} collective-permute-done((bf16[192,256]{1,0:T(8,128)(2,1)S(1)}, bf16[192,256]{1,0:T(8,128)(2,1)S(1)}, u32[]{:S(2)}, u32[]{:S(2)}) %collective-permute-start.14) | collective-permute-done | bytes 98336 | tf_op jit(solution)/shard_map/ppermute | solution.py:186
  60.1 6.4 %collective-permute-done.13 = bf16[192,256]{1,0:T(8,128)(2,1)S(1)} collective-permute-done((bf16[192,256]{1,0:T(8,128)(2,1)S(1)}, bf16[192,256]{1,0:T(8,128)(2,1)S(1)}, u32[]{:S(2)}, u32[]{:S(2)}) %collective-permute-start.13) | collective-permute-done | bytes 98336 | tf_op jit(solution)/shard_map/ppermute | solution.py:186
  66.6 0.6 fusion.6
  (27 shorter events, 0.3 us)
Async XLA Ops:
  2.3 11.7 %collective-permute-start = (bf16[192,256]{1,0:T(8,128)(2,1)S(1)}, bf16[192,256]{1,0:T(8,128)(2,1)S(1)}, u32[]{:S(2)}, u32[]{:S(2)}) collective-permute-start(bf16[192,256]{1,0:T(8,128)(2,1)S(1)} %constant_dynamic-update-slice_fusion), channel_id=1, source_target_pairs={{0,64},{8,72},{16,80},{24,88},{32,96},{40,104},{48,112},{56,120},{... | collective-permute-start | bytes 294920 | tf_op jit(solution)/shard_map/ppermute | solution.py:186
  6.8 10.5 %collective-permute-start.1 = (bf16[192,256]{1,0:T(8,128)(2,1)S(1)}, bf16[192,256]{1,0:T(8,128)(2,1)S(1)}, u32[]{:S(2)}, u32[]{:S(2)}) collective-permute-start(bf16[192,256]{1,0:T(8,128)(2,1)S(1)} %constant_dynamic-update-slice_fusion), channel_id=1, source_target_pairs={{0,48},{8,56},{16,64},{24,72},{32,80},{40,88},{48,96},{56,104},{64... | collective-permute-start | bytes 294920 | tf_op jit(solution)/shard_map/ppermute | solution.py:186
  8.9 8.5 %collective-permute-start.2 = (bf16[192,256]{1,0:T(8,128)(2,1)S(1)}, bf16[192,256]{1,0:T(8,128)(2,1)S(1)}, u32[]{:S(2)}, u32[]{:S(2)}) collective-permute-start(bf16[192,256]{1,0:T(8,128)(2,1)S(1)} %constant_dynamic-update-slice_fusion), channel_id=1, source_target_pairs={{0,32},{8,40},{16,48},{24,56},{32,64},{40,72},{48,80},{56,88},{64,... | collective-permute-start | bytes 294920 | tf_op jit(solution)/shard_map/ppermute | solution.py:186
  9.9 9.5 %collective-permute-start.3 = (bf16[192,256]{1,0:T(8,128)(2,1)S(1)}, bf16[192,256]{1,0:T(8,128)(2,1)S(1)}, u32[]{:S(2)}, u32[]{:S(2)}) collective-permute-start(bf16[192,256]{1,0:T(8,128)(2,1)S(1)} %constant_dynamic-update-slice_fusion), channel_id=1, source_target_pairs={{0,16},{8,24},{16,32},{24,40},{32,48},{40,56},{48,64},{56,72},{64,... | collective-permute-start | bytes 294920 | tf_op jit(solution)/shard_map/ppermute | solution.py:186
  10.8 11.9 %collective-permute-start.5 = (bf16[192,512]{1,0:T(8,128)(2,1)}, bf16[192,512]{1,0:T(8,128)(2,1)S(1)}, u32[]{:S(2)}, u32[]{:S(2)}) collective-permute-start(bf16[192,512]{1,0:T(8,128)(2,1)} %refs_0_.1), channel_id=1, source_target_pairs={{0,1},{1,0},{2,3},{3,2},{4,5},{5,4},{6,7},{7,6},{8,9},{9,8},{10,11... | collective-permute-start | bytes 589832 | tf_op jit(solution)/shard_map/ppermute | solution.py:186
  21.0 12.6 %collective-permute-start.4 = (bf16[960,256]{1,0:T(8,128)(2,1)S(1)}, bf16[960,256]{1,0:T(8,128)(2,1)S(1)}, u32[]{:S(2)}, u32[]{:S(2)}) collective-permute-start(bf16[960,256]{1,0:T(8,128)(2,1)S(1)} %constant_dynamic-update-slice_fusion.7.own_ref), channel_id=1, source_target_pairs={{0,8},{8,0},{16,24},{24,16},{32,40},{40,32},{48,56},{56,48},{64,72... | collective-permute-start | bytes 1474568 | tf_op jit(solution)/shard_map/ppermute | solution.py:186
  21.1 9.2 %collective-permute-start.6 = (bf16[192,512]{1,0:T(8,128)(2,1)}, bf16[192,512]{1,0:T(8,128)(2,1)S(1)}, u32[]{:S(2)}, u32[]{:S(2)}) collective-permute-start(bf16[192,512]{1,0:T(8,128)(2,1)} %refs_0_.1), channel_id=1, source_target_pairs={{0,2},{1,3},{2,4},{3,5},{4,6},{5,7},{6,0},{7,1},{8,10},{9,11},{10,... | collective-permute-start | bytes 589832 | tf_op jit(solution)/shard_map/ppermute | solution.py:186
  22.7 7.9 %collective-permute-start.9 = (bf16[192,512]{1,0:T(8,128)(2,1)S(1)}, bf16[192,512]{1,0:T(8,128)(2,1)S(1)}, u32[]{:S(2)}, u32[]{:S(2)}) collective-permute-start(bf16[192,512]{1,0:T(8,128)(2,1)S(1)} %collective-permute-done.5.refs_1_), channel_id=1, source_target_pairs={{0,6},{1,7},{2,0},{3,1},{4,2},{5,3},{6,4},{7,5},{8,14},{9,15},{10,... | collective-permute-start | bytes 589832 | tf_op jit(solution)/shard_map/ppermute | solution.py:186
  24.4 15.8 %collective-permute-start.7 = (bf16[192,512]{1,0:T(8,128)(2,1)}, bf16[192,512]{1,0:T(8,128)(2,1)S(1)}, u32[]{:S(2)}, u32[]{:S(2)}) collective-permute-start(bf16[192,512]{1,0:T(8,128)(2,1)} %refs_0_.1), channel_id=1, source_target_pairs={{0,6},{1,7},{2,0},{3,1},{4,2},{5,3},{6,4},{7,5},{8,14},{9,15},{10,... | collective-permute-start | bytes 589832 | tf_op jit(solution)/shard_map/ppermute | solution.py:186
  26.0 14.3 %collective-permute-start.8 = (bf16[192,512]{1,0:T(8,128)(2,1)S(1)}, bf16[192,512]{1,0:T(8,128)(2,1)S(1)}, u32[]{:S(2)}, u32[]{:S(2)}) collective-permute-start(bf16[192,512]{1,0:T(8,128)(2,1)S(1)} %collective-permute-done.5.refs_1_), channel_id=1, source_target_pairs={{0,2},{1,3},{2,4},{3,5},{4,6},{5,7},{6,0},{7,1},{8,10},{9,11},{10,... | collective-permute-start | bytes 589832 | tf_op jit(solution)/shard_map/ppermute | solution.py:186
  30.3 10.0 %collective-permute-start.10 = (bf16[192,512]{1,0:T(8,128)(2,1)S(1)}, bf16[192,512]{1,0:T(8,128)(2,1)S(1)}, u32[]{:S(2)}, u32[]{:S(2)}) collective-permute-start(bf16[192,512]{1,0:T(8,128)(2,1)S(1)} %collective-permute-done.6.refs_2_), channel_id=1, source_target_pairs={{0,2},{1,3},{2,4},{3,5},{4,6},{5,7},{6,0},{7,1},{8,10},{9,11},{10,... | collective-permute-start | bytes 589832 | tf_op jit(solution)/shard_map/ppermute | solution.py:186
  30.6 9.7 %collective-permute-start.11 = (bf16[192,512]{1,0:T(8,128)(2,1)S(1)}, bf16[192,512]{1,0:T(8,128)(2,1)S(1)}, u32[]{:S(2)}, u32[]{:S(2)}) collective-permute-start(bf16[192,512]{1,0:T(8,128)(2,1)S(1)} %collective-permute-done.9.refs_5_), channel_id=1, source_target_pairs={{0,6},{1,7},{2,0},{3,1},{4,2},{5,3},{6,4},{7,5},{8,14},{9,15},{10,... | collective-permute-start | bytes 589832 | tf_op jit(solution)/shard_map/ppermute | solution.py:186
  33.6 0.9 %copy-start.2 = (bf16[192,512]{1,0:T(8,128)(2,1)S(1)}, bf16[192,512]{1,0:T(8,128)(2,1)}, u32[]{:S(2)}) copy-start(bf16[192,512]{1,0:T(8,128)(2,1)} %q_ref.3) | copy-start | bytes 589828
  34.5 0.7 copy-start.4
  35.2 5.2 %copy-start = (bf16[512,4096]{1,0:T(8,128)(2,1)S(1)}, bf16[512,4096]{1,0:T(8,128)(2,1)}, u32[]{:S(2)}) copy-start(bf16[512,4096]{1,0:T(8,128)(2,1)} %refs_8_.1) | copy-start | bytes 12582916
  35.2 5.2 %copy-start.1 = (bf16[192,512]{1,0:T(8,128)(2,1)S(1)}, bf16[192,512]{1,0:T(8,128)(2,1)}, u32[]{:S(2)}) copy-start(bf16[192,512]{1,0:T(8,128)(2,1)} %refs_0_.1) | copy-start | bytes 589828
  40.3 3.9 %copy-start.3 = (bf16[192,512]{1,0:T(8,128)(2,1)S(1)}, bf16[192,512]{1,0:T(8,128)(2,1)}, u32[]{:S(2)}) copy-start(bf16[192,512]{1,0:T(8,128)(2,1)} %q_ref.3) | copy-start | bytes 589828
  43.9 3.5 %collective-permute-start.12 = (bf16[960,256]{1,0:T(8,128)(2,1)S(1)}, bf16[960,256]{1,0:T(8,128)(2,1)S(1)}, u32[]{:S(2)}, u32[]{:S(2)}) collective-permute-start(bf16[960,256]{1,0:T(8,128)(2,1)S(1)} %get-tuple-element.20), channel_id=1, source_target_pairs={{0,8},{8,0},{16,24},{24,16},{32,40},{40,32},{48,56},{56,48},{64,72... | collective-permute-start | bytes 1474568 | tf_op jit(solution)/shard_map/ppermute | solution.py:186
  47.6 8.0 %collective-permute-start.16 = (bf16[192,256]{1,0:T(8,128)(2,1)S(1)}, bf16[192,256]{1,0:T(8,128)(2,1)S(1)}, u32[]{:S(2)}, u32[]{:S(2)}) collective-permute-start(bf16[192,256]{1,0:T(8,128)(2,1)S(1)} %get-tuple-element.24), channel_id=1, source_target_pairs={{0,240},{8,248},{16,0},{24,8},{32,16},{40,24},{48,32},{56,40},{64,... | collective-permute-start | bytes 294920 | tf_op jit(solution)/shard_map/ppermute | solution.py:186
  49.7 7.2 %collective-permute-start.15 = (bf16[192,256]{1,0:T(8,128)(2,1)S(1)}, bf16[192,256]{1,0:T(8,128)(2,1)S(1)}, u32[]{:S(2)}, u32[]{:S(2)}) collective-permute-start(bf16[192,256]{1,0:T(8,128)(2,1)S(1)} %get-tuple-element.25), channel_id=1, source_target_pairs={{0,224},{8,232},{16,240},{24,248},{32,0},{40,8},{48,16},{56,24},{6... | collective-permute-start | bytes 294920 | tf_op jit(solution)/shard_map/ppermute | solution.py:186
  49.7 10.4 %collective-permute-start.14 = (bf16[192,256]{1,0:T(8,128)(2,1)S(1)}, bf16[192,256]{1,0:T(8,128)(2,1)S(1)}, u32[]{:S(2)}, u32[]{:S(2)}) collective-permute-start(bf16[192,256]{1,0:T(8,128)(2,1)S(1)} %get-tuple-element.26), channel_id=1, source_target_pairs={{0,208},{8,216},{16,224},{24,232},{32,240},{40,248},{48,0},{56,8},... | collective-permute-start | bytes 294920 | tf_op jit(solution)/shard_map/ppermute | solution.py:186
  53.0 13.5 %collective-permute-start.13 = (bf16[192,256]{1,0:T(8,128)(2,1)S(1)}, bf16[192,256]{1,0:T(8,128)(2,1)S(1)}, u32[]{:S(2)}, u32[]{:S(2)}) collective-permute-start(bf16[192,256]{1,0:T(8,128)(2,1)S(1)} %get-tuple-element.23), channel_id=1, source_target_pairs={{0,192},{8,200},{16,208},{24,216},{32,224},{40,232},{48,240},{56,2... | collective-permute-start | bytes 294920 | tf_op jit(solution)/shard_map/ppermute | solution.py:186

commit v2 on v1

v2 whole, which is shorter than its diff:
```python
import functools

import jax
import jax.numpy as jnp
from jax import lax
from jax.experimental import pallas as pl
from jax.experimental.pallas import tpu as pltpu
from jax.sharding import PartitionSpec as P

D = 128
HEADS = 4
ROWS = 192
LANES = HEADS * ROWS
REACH = 4
SLOTS = REACH + 1
PLANE = 4
NEG = -1e30
SCALE = D**-0.5
LOG2E = 1.4426950408889634
MIB = 1 << 20


def dot(a, b, ca, cb):
    return lax.dot_general(a, b, (((ca,), (cb,)), ((), ())), preferred_element_type=jnp.float32)


def stack_heads(src, dst):
    for h in range(HEADS):
        dst[h * ROWS : (h + 1) * ROWS, :] = src[:, h * D : (h + 1) * D]


def prepare(place_ref, len_ref, q_ref, q4_ref, bound_ref):
    stack_heads(q_ref, q4_ref)
    lane = lax.broadcasted_iota(jnp.int32, (1, LANES), 1)
    pos = lane + place_ref[0] * ROWS
    for h in range(1, HEADS):
        pos = pos - jnp.where(lane >= h * ROWS, ROWS, 0)
    start = jnp.zeros((1, LANES), jnp.int32)
    end = jnp.int32(0)
    for d in range(len_ref.shape[0]):
        end = end + len_ref[d]
        start = jnp.where(end <= pos, end, start)
    bound_ref[0:1, :] = pos
    bound_ref[1:2, :] = start


def pick_kernel(place_ref, z2_ref, z1_ref, z0_ref, *refs):
    out_ref = refs[-1]
    upper = lax.rem(lax.div(place_ref[0], 2), 2) == 1

    @pl.when(upper)
    def _():
        out_ref[:ROWS, :] = z2_ref[...]
        out_ref[ROWS:, :] = z1_ref[...]

    @pl.when(jnp.logical_not(upper))
    def _():
        out_ref[:ROWS, :] = z1_ref[...]
        out_ref[ROWS:, :] = z0_ref[...]


def join_kernel(z2_ref, z1_ref, z0_ref, side_ref, *refs):
    out_ref = refs[-1]
    parts = (z2_ref[...], side_ref[:ROWS, :], z1_ref[...], side_ref[ROWS:, :], z0_ref[...])
    for m, part in enumerate(parts):
        out_ref[m * ROWS : (m + 1) * ROWS, :] = part


def score(kv, queries, row, base, bound_ref, diagonal):
    s = dot(kv[:, :D], queries, 1, 1) * (SCALE * LOG2E)
    key = row + base * ROWS
    visible = key >= bound_ref[1:2, :]
    if diagonal:
        visible = visible & (key <= bound_ref[0:1, :])
    return jnp.where(visible, s, NEG)


def online(s, state):
    top, total = state
    new = jnp.maximum(top, jnp.max(s, axis=0, keepdims=True))
    total = total * jnp.exp2(top - new) + jnp.sum(jnp.exp2(s - new), axis=0, keepdims=True)
    return new, total


def near_kernel(place_ref, z2_ref, z1_ref, z0_ref, q4_ref, bound_ref, after, s_ref, stat_ref):
    me = place_ref[0]
    queries = q4_ref[...]
    row = lax.broadcasted_iota(jnp.int32, (ROWS, LANES), 0)
    s = score(z0_ref[...], queries, row, me, bound_ref, True)
    s_ref[2 * ROWS :, :] = s
    top = jnp.max(s, axis=0, keepdims=True)
    state = (top, jnp.sum(jnp.exp2(s - top), axis=0, keepdims=True))
    for i, ref in ((1, z1_ref), (0, z2_ref)):
        s = score(ref[...], queries, row, me - PLANE * (2 - i), bound_ref, False)
        s_ref[i * ROWS : (i + 1) * ROWS, :] = s
        state = online(s, state)
    stat_ref[0:1, :] = state[0]
    stat_ref[1:2, :] = state[1]


def rest_kernel(place_ref, own_ref, par_ref, q4_ref, bound_ref, s_ref, stat_ref, after, p_own_ref, p_par_ref, o_ref, s_side, s_par):
    me = place_ref[0]
    core = lax.rem(me, 2)
    chip = me - core
    queries = q4_ref[...]
    row = lax.broadcasted_iota(jnp.int32, (ROWS, LANES), 0)

    def rows(i):
        return pl.ds(pl.multiple_of(i * ROWS, ROWS), ROWS)

    def side(i, state):
        slot = 2 * i + 1
        s = score(own_ref[rows(slot), :], queries, row, me + 2 * (slot - REACH), bound_ref, False)
        s_side[rows(i), :] = s
        return online(s, state)

    def across(i, state):
        slot = i + core
        s = score(par_ref[rows(slot), :], queries, row, chip + 1 - core + 2 * (slot - REACH), bound_ref, False)
        s_par[rows(i), :] = s
        return online(s, state)

    state = (stat_ref[0:1, :], stat_ref[1:2, :])
    state = lax.fori_loop(0, 2, side, state)
    top, total = lax.fori_loop(0, REACH, across, state)
    log_total = top + jnp.log2(total)

    def weigh(s, kv_ref, slot, state):
        acc, mass = state
        prob = jnp.exp2(s - log_total).astype(jnp.bfloat16)
        acc = acc + dot(kv_ref[rows(slot), D:], prob, 0, 0)
        mass = mass + jnp.sum(prob.astype(jnp.float32), axis=0, keepdims=True)
        return prob, (acc, mass)

    def weigh_main(i, state):
        prob, state = weigh(s_ref[rows(i), :], own_ref, 2 * i, state)
        p_own_ref[rows(2 * i), :] = prob
        return state

    def weigh_side(i, state):
        prob, state = weigh(s_side[rows(i), :], own_ref, 2 * i + 1, state)
        p_own_ref[rows(2 * i + 1), :] = prob
        return state

    def weigh_across(i, state):
        prob, state = weigh(s_par[rows(i), :], par_ref, i + core, state)
        p_par_ref[rows(i), :] = prob
        return state

    state = (jnp.zeros((D, LANES), jnp.float32), jnp.zeros((1, LANES), jnp.float32))
    state = lax.fori_loop(0, 3, weigh_main, state)
    state = lax.fori_loop(0, 2, weigh_side, state)
    acc, mass = lax.fori_loop(0, REACH, weigh_across, state)
    o_ref[...] = acc / mass


def project(acc, pieces, sources, w_ref):
    for piece, source in zip(pieces, sources):
        part = dot(piece[...], w_ref[:, pl.ds(pl.multiple_of(source * 512, 512), 512)], 1, 1)
        acc = part if acc is None else acc + part
    return acc


def source_of(head, by, flip):
    at = lax.rem(head + by + 8, 8)
    return at + 1 - 2 * lax.rem(at, 2) if flip else at


def early_kernel(head_ref, a_ref, b_ref, c_ref, d_ref, e_ref, f_ref, w_ref, after, out_ref):
    head = head_ref[0]
    sources = (head, source_of(head, 0, True), source_of(head, -2, False), source_of(head, 2, False))
    sources += (source_of(head, -2, True), source_of(head, 2, True))
    out_ref[...] = project(None, (a_ref, b_ref, c_ref, d_ref, e_ref, f_ref), sources, w_ref)


def back_block(kv_ref, slot, p_ref, i, g4, q4, rd):
    kv_at = pl.ds(pl.multiple_of(slot * ROWS, ROWS), ROWS)
    prob = p_ref[pl.ds(pl.multiple_of(i * ROWS, ROWS), ROWS), :]
    dprob = dot(kv_ref[kv_at, D:], g4, 1, 1)
    ds = (prob.astype(jnp.float32) * (dprob - rd)).astype(jnp.bfloat16)
    dv = dot(prob, g4, 1, 0)
    dk = dot(ds, q4, 1, 0) * SCALE
    dq = dot(kv_ref[kv_at, :D], ds, 0, 0)
    return dk, dv, dq


def second_kernel(place_ref, head_ref, a_ref, b_ref, early_ref, w_ref, q4_ref, par_ref, p_ref, o_ref, out_ref, g_ref, rd_ref, dq_ref):
    me = place_ref[0]
    core = lax.rem(me, 2)
    head = head_ref[0]
    sources = (source_of(head, 4, False), source_of(head, 4, True))
    acc = project(early_ref[...], (a_ref, b_ref), sources, w_ref)
    acc = acc.astype(jnp.bfloat16)
    for h in range(HEADS):
        g_ref[h * ROWS : (h + 1) * ROWS, :] = acc[:, h * D : (h + 1) * D]
    g4 = g_ref[...]
    gt = jnp.transpose(g4.astype(jnp.float32))
    rd = jnp.sum(gt * o_ref[...], axis=0, keepdims=True)
    rd_ref[...] = rd
    dq_ref[...] = jnp.zeros((D, LANES), jnp.float32)
    out_ref[...] = jnp.zeros(out_ref.shape, out_ref.dtype)

    def step(i, _):
        dk, dv, dq = back_block(par_ref, i + core, p_ref, i, g4, q4_ref[...], rd)
        at = pl.ds(pl.multiple_of((i + core) * ROWS, ROWS), ROWS)
        out_ref[at, :D] = dk.astype(jnp.bfloat16)
        out_ref[at, D:] = dv.astype(jnp.bfloat16)
        dq_ref[...] += dq
        return 0

    lax.fori_loop(0, REACH, step, 0)


def third_kernel(q4_ref, own_ref, p_ref, g_ref, rd_ref, dq_in_ref, out_ref, dq_out_ref, acc):
    g4 = g_ref[...]
    rd = rd_ref[...]
    acc[...] = dq_in_ref[...]

    def step(i, _):
        dk, dv, dq = back_block(own_ref, i, p_ref, i, g4, q4_ref[...], rd)
        at = pl.ds(pl.multiple_of(i * ROWS, ROWS), ROWS)
        out_ref[at, :D] = dk
        out_ref[at, D:] = dv
        acc[...] += dq
        return 0

    lax.fori_loop(0, SLOTS, step, 0)
    dq = jnp.transpose(acc[...]) * SCALE
    for h in range(HEADS):
        dq_out_ref[:, h * D : (h + 1) * D] = dq[h * ROWS : (h + 1) * ROWS, :].astype(jnp.bfloat16)


def vmem(n):
    return [pl.BlockSpec(memory_space=pltpu.VMEM)] * n


def smem(n):
    return [pl.BlockSpec(memory_space=pltpu.SMEM)] * n


def hbm(n):
    return [pl.BlockSpec(memory_space=pltpu.HBM)] * n


def token(n):
    return [pl.BlockSpec(memory_space=pl.ANY)] * n


def params(mib):
    return pltpu.CompilerParams(vmem_limit_bytes=mib * MIB)


def cost(flops, nbytes, exps=0):
    return pl.CostEstimate(flops=int(flops), bytes_accessed=int(nbytes), transcendentals=int(exps))


def moved(x, axis, to):
    return lax.ppermute(x, axis, [(i, to(i)) for i in range(lax.axis_size(axis))])


def turned(x, axis, by):
    count = lax.axis_size(axis)
    return moved(x, axis, lambda i: (i + by) % count)


def shape(rows, cols, dtype):
    return jax.ShapeDtypeStruct((rows, cols), dtype)


def local(queries, keys, values, grad_out, out_weight, lengths):
    bf16, f32 = jnp.bfloat16, jnp.float32
    ctx = lax.axis_index("ctx").astype(jnp.int32)
    place = ctx.reshape(1)
    head = lax.axis_index("head").astype(jnp.int32).reshape(1)
    upper = lax.rem(ctx // 2, 2) == 1
    pair = ROWS * LANES * D * 2

    other = moved(grad_out, "head", lambda i: i ^ 1)
    right = turned(grad_out, "head", 2)
    left = turned(grad_out, "head", -2)

    kv = jnp.pad(keys, ((0, 0), (0, D))) + jnp.pad(values, ((0, 0), (D, 0)))
    q4, bound = pl.pallas_call(
        prepare,
        out_shape=(shape(LANES, D, bf16), shape(8, LANES, jnp.int32)),
        in_specs=smem(2) + vmem(1),
        out_specs=tuple(vmem(2)),
        compiler_params=params(8),
        cost_estimate=cost(1, 1),
        name="prepare",
    )(place, lengths, queries)

    z2 = turned(kv, "ctx", 2 * PLANE)
    z1 = turned(kv, "ctx", PLANE)

    other_right = turned(other, "head", 2)
    other_left = turned(other, "head", -2)
    far = turned(right, "head", 2)
    other_far = turned(other_left, "head", -2)

    picked = pl.pallas_call(
        pick_kernel,
        out_shape=shape(2 * ROWS, 2 * D, bf16),
        in_specs=smem(1) + vmem(3) + token(4),
        out_specs=vmem(1)[0],
        compiler_params=params(8),
        cost_estimate=cost(1, 1),
        name="pick_side",
    )(place, z2, z1, kv, other, right, left, q4)
    side = moved(picked, "ctx", lambda i: i ^ 2)

    s_near, stat = pl.pallas_call(
        near_kernel,
        out_shape=(shape(3 * ROWS, LANES, f32), shape(8, LANES, f32)),
        in_specs=smem(1) + vmem(5) + token(1),
        out_specs=tuple(vmem(2)),
        compiler_params=params(16),
        cost_estimate=cost(1, 1),
        name="near_scores",
    )(place, z2, z1, kv, q4, bound, picked)

    own = pl.pallas_call(
        join_kernel,
        out_shape=shape(SLOTS * ROWS, 2 * D, bf16),
        in_specs=vmem(4) + token(3),
        out_specs=vmem(1)[0],
        compiler_params=params(8),
        cost_estimate=cost(1, 1),
        name="join_slots",
    )(z2, z1, kv, side, stat, other_right, other_left)
    par = moved(own, "ctx", lambda i: i ^ 1)

    early = pl.pallas_call(
        early_kernel,
        out_shape=shape(ROWS, HEADS * D, f32),
        in_specs=smem(1) + vmem(7) + token(1),
        out_specs=vmem(1)[0],
        compiler_params=params(16),
        cost_estimate=cost(1, 1),
        name="early_projection",
    )(head, grad_out, other, right, left, other_right, other_left, out_weight, own)

    p_own, p_par, out_t = pl.pallas_call(
        rest_kernel,
        out_shape=(shape(SLOTS * ROWS, LANES, bf16), shape(REACH * ROWS, LANES, bf16), shape(D, LANES, f32)),
        in_specs=smem(1) + vmem(6) + token(1),
        out_specs=tuple(vmem(3)),
        scratch_shapes=[pltpu.VMEM((2 * ROWS, LANES), f32), pltpu.VMEM((REACH * ROWS, LANES), f32)],
        compiler_params=params(24),
        cost_estimate=cost(1, 1),
        name="softmax",
    )(place, own, par, q4, bound, s_near, stat, early)

    par_grad, g4, rd, dq = pl.pallas_call(
        second_kernel,
        out_shape=(shape(SLOTS * ROWS, 2 * D, bf16), shape(LANES, D, bf16), shape(1, LANES, f32), shape(D, LANES, f32)),
        in_specs=smem(2) + vmem(8),
        out_specs=tuple(vmem(4)),
        compiler_params=params(24),
        cost_estimate=cost(1, 1),
        name="partner_grads",
    )(place, head, far, other_far, early, out_weight, q4, par, p_par, out_t)

    back = moved(par_grad, "ctx", lambda i: i ^ 1)

    own_grad, grad_queries = pl.pallas_call(
        third_kernel,
        out_shape=(shape(SLOTS * ROWS, 2 * D, f32), shape(ROWS, HEADS * D, bf16)),
        in_specs=vmem(6),
        out_specs=tuple(vmem(2)),
        scratch_shapes=[pltpu.VMEM((D, LANES), f32)],
        compiler_params=params(24),
        cost_estimate=cost(1, 1),
        name="own_grads",
    )(q4, own, p_own, g4, rd, dq)

    both = own_grad + back.astype(f32)
    slots = [both[m * ROWS : (m + 1) * ROWS] for m in range(SLOTS)]
    crossed = moved(jnp.concatenate([slots[1], slots[3]]).astype(bf16), "ctx", lambda i: i ^ 2).astype(f32)
    first, second = crossed[:ROWS], crossed[ROWS:]
    zero = jnp.zeros_like(first)
    to_two = slots[0] + jnp.where(upper, first, zero)
    to_one = slots[2] + jnp.where(upper, second, first)
    total = slots[4] + jnp.where(upper, zero, second)
    got_two = turned(to_two.astype(bf16), "ctx", -2 * PLANE)
    got_one = turned(to_one.astype(bf16), "ctx", -PLANE)
    total = (total + got_one.astype(f32) + got_two.astype(f32)).astype(bf16)
    return grad_queries, total[:, :D], total[:, D:]


def solution(mesh):
    return jax.shard_map(
        local,
        mesh=mesh,
        in_specs=(
            P("ctx", "head"),
            P("ctx", "head"),
            P("ctx", "head"),
            P("ctx", "head"),
            P("head", None),
            P(),
        ),
        out_specs=(P("ctx", "head"), P("ctx", "head"), P("ctx", "head")),
        check_vma=False,
    )
```

time: 68.4 us -> 69.5 us (1.016)
  starting transfers between devices: 28.7 us -> 24 us
  Pallas kernels: 11.8 us -> 15.3 us
  local copies, waits for them, and re-layouts: 5.56 us -> 6.94 us
  other arithmetic: 0.25 us -> 1.16 us
    ppermute x17 -> x15, starting transfers between devices: 28.7 us -> 24 us  [moved(): lax.ppermute(x, axis, [(i, to(i)) for i in range(lax.axis_size(axis))])]
    pallas_call x3 -> x8, Pallas kernels: 11.8 us -> 15.3 us  [the longest x1 4.99 us: local(): pl.pallas_call(rest_kernel, out_shape=(shape(SLOTS * ROWS, LANES, bf16),...]
    unnamed x16 -> x22, local copies, waits for them, and re-layouts: 3.25 us -> 6.28 us
    concatenate x2 -> x0, local copies, waits for them, and re-layouts: 1.63 us -> none  [the longest x1 0.82 us: local(): kv = jnp.concatenate([keys, values], axis=1)]
    add x0 -> x1, other arithmetic: none -> 0.83 us  [local(): kv = jnp.pad(keys, ((0, 0), (0, D))) + jnp.pad(values, ((0, 0), (D, 0)))]
    ppermute x17 -> x15, waiting for transfers between devices: 20.1 us -> 20.4 us  [moved(): lax.ppermute(x, axis, [(i, to(i)) for i in range(lax.axis_size(axis))])]
  transfers between devices with their start and end apart: 17 -> 15, of which waited for: 6 -> 8; matrix products, arithmetic and copies ran while one was open for 2% -> 1% of each run, Pallas kernels for 12% -> 17%
where the time goes in v2:
time: 69.5 us; the launch traced here: 68.6 us
  starting transfers between devices  24 us (35%)
  waiting for transfers between devices  20.4 us (29%)
  Pallas kernels  15.3 us (22%)
  local copies, waits for them, and re-layouts  6.94 us (10%)
  other arithmetic  1.16 us (2%)
  between operations  0.81 us (1%)
    ppermute x15, starting transfers between devices, moved(): lax.ppermute(x, axis, [(i, to(i)) for i in range(lax.axis_size(axis))])  24 us
    ppermute x15, waiting for transfers between devices, moved(): lax.ppermute(x, axis, [(i, to(i)) for i in range(lax.axis_size(axis))])  20.4 us
    unnamed x22, local copies, waits for them, and re-layouts  6.28 us
    pallas_call x1, Pallas kernels, local(): pl.pallas_call(rest_kernel, out_shape=(shape(SLOTS * ROWS, LANES, bf16),...  4.99 us
    pallas_call x1, Pallas kernels, local(): pl.pallas_call(second_kernel, out_shape=(shape(SLOTS * ROWS, 2 * D, bf16)...  3.47 us
    pallas_call x1, Pallas kernels, local(): pl.pallas_call(third_kernel, out_shape=(shape(SLOTS * ROWS, 2 * D, f32),...  3.14 us
    pallas_call x1, Pallas kernels, local(): pl.pallas_call(early_kernel, out_shape=shape(ROWS, HEADS * D, f32), in_sp...  2.25 us
  transfers between devices with their start and end apart: 15, of which 8 were waited for; matrix products, arithmetic and copies ran while one was open for 1% of the time, Pallas kernels for 17%

profile of v2, /device:TPU:64, one launch (start us, length us, event | category | flops | bytes accessed | tf_op | source)
XLA Modules:
  0.0 68.6 jit_solution(9062083704593862580)
XLA Ops:
  0.6 3.3 %collective-permute-start.2 = (bf16[192,512]{1,0:T(8,128)(2,1)}, bf16[192,512]{1,0:T(8,128)(2,1)S(1)}, u32[]{:S(2)}, u32[]{:S(2)}) collective-permute-start(bf16[192,512]{1,0:T(8,128)(2,1)} %a_ref.1), channel_id=1, source_target_pairs={{0,1},{1,0},{2,3},{3,2},{4,5},{5,4},{6,7},{7,6},{8,9},{9,8},{10,11... | collective-permute-start | bytes 589832 | tf_op jit(solution)/shard_map/ppermute | solution.py:258
  3.9 1.5 %collective-permute-start.3 = (bf16[192,512]{1,0:T(8,128)(2,1)}, bf16[192,512]{1,0:T(8,128)(2,1)S(1)}, u32[]{:S(2)}, u32[]{:S(2)}) collective-permute-start(bf16[192,512]{1,0:T(8,128)(2,1)} %a_ref.1), channel_id=1, source_target_pairs={{0,2},{1,3},{2,4},{3,5},{4,6},{5,7},{6,0},{7,1},{8,10},{9,11},{10,... | collective-permute-start | bytes 589832 | tf_op jit(solution)/shard_map/ppermute | solution.py:258
  5.4 1.7 %collective-permute-start.4 = (bf16[192,512]{1,0:T(8,128)(2,1)}, bf16[192,512]{1,0:T(8,128)(2,1)S(1)}, u32[]{:S(2)}, u32[]{:S(2)}) collective-permute-start(bf16[192,512]{1,0:T(8,128)(2,1)} %a_ref.1), channel_id=1, source_target_pairs={{0,6},{1,7},{2,0},{3,1},{4,2},{5,3},{6,4},{7,5},{8,14},{9,15},{10,... | collective-permute-start | bytes 589832 | tf_op jit(solution)/shard_map/ppermute | solution.py:258
  7.1 0.8 %pad_add_fusion.z0_ref = bf16[192,256]{1,0:T(8,128)(2,1)S(1)} fusion(bf16[192,128]{1,0:T(8,128)(2,1)} %param.8, bf16[192,128]{1,0:T(8,128)(2,1)} %param.7), kind=kLoop, calls=%fused_computation.10 | loop fusion | flops 196608 | bytes 196608 | tf_op jit(solution)/shard_map/add | solution.py:282
  8.0 4.6 %collective-permute-start = (bf16[192,256]{1,0:T(8,128)(2,1)S(1)}, bf16[192,256]{1,0:T(8,128)(2,1)S(1)}, u32[]{:S(2)}, u32[]{:S(2)}) collective-permute-start(bf16[192,256]{1,0:T(8,128)(2,1)S(1)} %pad_add_fusion.z0_ref), channel_id=1, source_target_pairs={{0,64},{8,72},{16,80},{24,88},{32,96},{40,104},{48,112},{56,120},{... | collective-permute-start | bytes 294920 | tf_op jit(solution)/shard_map/ppermute | solution.py:258
  12.5 1.0 %collective-permute-start.1 = (bf16[192,256]{1,0:T(8,128)(2,1)S(1)}, bf16[192,256]{1,0:T(8,128)(2,1)S(1)}, u32[]{:S(2)}, u32[]{:S(2)}) collective-permute-start(bf16[192,256]{1,0:T(8,128)(2,1)S(1)} %pad_add_fusion.z0_ref), channel_id=1, source_target_pairs={{0,32},{8,40},{16,48},{24,56},{32,64},{40,72},{48,80},{56,88},{64,... | collective-permute-start | bytes 294920 | tf_op jit(solution)/shard_map/ppermute | solution.py:258
  13.6 0.9 %copy-done.5 = bf16[192,512]{1,0:T(8,128)(2,1)S(1)} copy-done((bf16[192,512]{1,0:T(8,128)(2,1)S(1)}, bf16[192,512]{1,0:T(8,128)(2,1)}, u32[]{:S(2)}) %copy-start.5) | copy-done | bytes 196632
  14.5 0.7 copy-done.10
  15.1 0.6 prepare.1
  15.9 1.2 %collective-permute-done.1.z1_ref = bf16[192,256]{1,0:T(8,128)(2,1)S(1)} collective-permute-done((bf16[192,256]{1,0:T(8,128)(2,1)S(1)}, bf16[192,256]{1,0:T(8,128)(2,1)S(1)}, u32[]{:S(2)}, u32[]{:S(2)}) %collective-permute-start.1) | collective-permute-done | bytes 98336 | tf_op jit(solution)/shard_map/ppermute | solution.py:258
  17.2 0.8 %collective-permute-start.5 = (bf16[384,256]{1,0:T(8,128)(2,1)S(1)}, bf16[384,256]{1,0:T(8,128)(2,1)S(1)}, u32[]{:S(2)}, u32[]{:S(2)}) collective-permute-start(bf16[384,256]{1,0:T(8,128)(2,1)S(1)} %pick_side.1.after), channel_id=1, source_target_pairs={{0,16},{8,24},{16,0},{24,8},{32,48},{40,56},{48,32},{56,40},{64,80... | collective-permute-start | bytes 589832 | tf_op jit(solution)/shard_map/ppermute | solution.py:258
  18.0 1.5 %collective-permute-start.7 = (bf16[192,512]{1,0:T(8,128)(2,1)S(1)}, bf16[192,512]{1,0:T(8,128)(2,1)}, u32[]{:S(2)}, u32[]{:S(2)}) collective-permute-start(bf16[192,512]{1,0:T(8,128)(2,1)S(1)} %collective-permute-done.2.refs_0_.b_ref), channel_id=1, source_target_pairs={{0,6},{1,7},{2,0},{3,1},{4,2},{5,3},{6,4},{7,5},{8,14},{9,15},{10,... | collective-permute-start | bytes 589832 | tf_op jit(solution)/shard_map/ppermute | solution.py:258
  20.0 0.8 %near_scores.1 = (f32[576,768]{1,0:T(8,128)S(1)}, f32[8,768]{1,0:T(8,128)S(1)}) custom-call(s32[1]{0:T(128)} %bitcast.place_ref, bf16[192,256]{1,0:T(8,128)(2,1)S(1)} %collective-permute-done.z2_ref, bf16[192,256]{1,0:T(8,128)(2,1)S(1)} %collective-permute-done.1.z1_ref, bf16[192,256]{1,0:T(8,128)(2,1)S(1)} %pad_add_fusion.z0_ref, ...), custom_call_target="tpu_custom_call" | custom-call | flops 1 | bytes 1 | tf_op jit(solution)/shard_map/near_scores/pallas_call | solution.py:312
  20.8 2.2 %collective-permute-done.5.side_ref = bf16[384,256]{1,0:T(8,128)(2,1)S(1)} collective-permute-done((bf16[384,256]{1,0:T(8,128)(2,1)S(1)}, bf16[384,256]{1,0:T(8,128)(2,1)S(1)}, u32[]{:S(2)}, u32[]{:S(2)}) %collective-permute-start.5) | collective-permute-done | bytes 196640 | tf_op jit(solution)/shard_map/ppermute | solution.py:258
  23.0 0.8 %collective-permute-done.7.refs_2_.f_ref = bf16[192,512]{1,0:T(8,128)(2,1)} collective-permute-done((bf16[192,512]{1,0:T(8,128)(2,1)S(1)}, bf16[192,512]{1,0:T(8,128)(2,1)}, u32[]{:S(2)}, u32[]{:S(2)}) %collective-permute-start.7) | collective-permute-done | bytes 196640 | tf_op jit(solution)/shard_map/ppermute | solution.py:258
  23.8 2.7 %collective-permute-done.6.refs_1_.e_ref = bf16[192,512]{1,0:T(8,128)(2,1)S(1)} collective-permute-done((bf16[192,512]{1,0:T(8,128)(2,1)S(1)}, bf16[192,512]{1,0:T(8,128)(2,1)S(1)}, u32[]{:S(2)}, u32[]{:S(2)}) %collective-permute-start.6) | collective-permute-done | bytes 196640 | tf_op jit(solution)/shard_map/ppermute | solution.py:258
  26.4 0.6 copy-done.2
  27.1 3.2 %collective-permute-start.10 = (bf16[192,512]{1,0:T(8,128)(2,1)}, bf16[192,512]{1,0:T(8,128)(2,1)}, u32[]{:S(2)}, u32[]{:S(2)}) collective-permute-start(bf16[192,512]{1,0:T(8,128)(2,1)} %collective-permute-done.7.refs_2_.f_ref), channel_id=1, source_target_pairs={{0,6},{1,7},{2,0},{3,1},{4,2},{5,3},{6,4},{7,5},{8,14},{9,15},{10,... | collective-permute-start | bytes 589832 | tf_op jit(solution)/shard_map/ppermute | solution.py:258
  30.3 2.2 %copy-done = bf16[512,4096]{1,0:T(8,128)(2,1)S(1)} copy-done((bf16[512,4096]{1,0:T(8,128)(2,1)S(1)}, bf16[512,4096]{1,0:T(8,128)(2,1)}, u32[]{:S(2)}) %copy-start) | copy-done | bytes 4194328
  32.5 0.9 %copy-done.3 = bf16[192,512]{1,0:T(8,128)(2,1)S(1)} copy-done((bf16[192,512]{1,0:T(8,128)(2,1)S(1)}, bf16[192,512]{1,0:T(8,128)(2,1)}, u32[]{:S(2)}) %copy-start.3) | copy-done | bytes 196632
  33.5 0.9 %copy-done.4 = bf16[192,512]{1,0:T(8,128)(2,1)S(1)} copy-done((bf16[192,512]{1,0:T(8,128)(2,1)S(1)}, bf16[192,512]{1,0:T(8,128)(2,1)}, u32[]{:S(2)}) %copy-start.4) | copy-done | bytes 196632
  34.4 2.3 %early_projection.1.after.early_ref = f32[192,512]{1,0:T(8,128)S(1)} custom-call(s32[1]{0:T(128)} %bitcast.1.head_ref, bf16[192,512]{1,0:T(8,128)(2,1)S(1)} %copy-done.4, bf16[192,512]{1,0:T(8,128)(2,1)S(1)} %collective-permute-done.2.refs_0_.b_ref, bf16[192,512]{1,0:T(8,128)(2,1)S(1)} %collective-permute-done.3.refs_1_.c_ref, ...), custom_call_target="tpu_custom_call" | custom-call | flops 1 | bytes 1 | tf_op jit(solution)/shard_map/early_projection/pallas_call | solution.py:333
  36.7 5.0 %softmax.1 = (bf16[960,768]{1,0:T(8,128)(2,1)S(1)}, bf16[768,768]{1,0:T(8,128)(2,1)S(1)}, f32[128,768]{1,0:T(8,128)S(1)}) custom-call(s32[1]{0:T(128)} %bitcast.place_ref, bf16[960,256]{1,0:T(8,128)(2,1)S(1)} %join_slots.1.after.own_ref, bf16[960,256]{1,0:T(8,128)(2,1)S(1)} %collective-permute-done.8.par_ref, ...), custom_call_target="tpu_custom_call" | custom-call | flops 1 | bytes 1 | tf_op jit(solution)/shard_map/softmax/pallas_call | solution.py:343
  41.7 3.5 %partner_grads.1 = (bf16[960,256]{1,0:T(8,128)(2,1)S(1)}, bf16[768,128]{1,0:T(8,128)(2,1)S(1)}, f32[1,768]{1,0:T(1,128)S(1)}, f32[128,768]{1,0:T(8,128)S(1)}) custom-call(s32[1]{0:T(128)} %bitcast.place_ref, s32[1]{0:T(128)} %bitcast.1.head_ref, bf16[192,512]{1,0:T(8,128)(2,1)} %collective-permute-done.9.a_ref, ...), custom_call_target="tpu_custom_call" | custom-call | flops 1 | bytes 1 | tf_op jit(solution)/shard_map/partner_grads/pallas_call | solution.py:354
  45.5 3.1 %own_grads.1 = (f32[960,256]{1,0:T(8,128)S(1)}, bf16[192,512]{1,0:T(8,128)(2,1)}) custom-call(bf16[768,128]{1,0:T(8,128)(2,1)S(1)} %get-tuple-element.16.refs_3_.q4_ref, bf16[960,256]{1,0:T(8,128)(2,1)S(1)} %join_slots.1.after.own_ref, bf16[960,768]{1,0:T(8,128)(2,1)S(1)} %get-tuple-element.20.p_ref, bf16[768,128]{1,0:T(8,128)(2,1)S(1)} %get-tuple-element.23.g_ref, ...), custom_call_target="tpu_custom_call" | custom-call | flops 1 | bytes 1 | tf_op jit(solution)/shard_map/own_grads/pallas_call | solution.py:366
  48.8 1.4 %collective-permute-start.12 = (bf16[384,256]{1,0:T(8,128)(2,1)S(1)}, bf16[384,256]{1,0:T(8,128)(2,1)S(1)}, u32[]{:S(2)}, u32[]{:S(2)}) collective-permute-start(bf16[384,256]{1,0:T(8,128)(2,1)S(1)} %pad_maximum_fusion), channel_id=1, source_target_pairs={{0,16},{8,24},{16,0},{24,8},{32,48},{40,56},{48,32},{56,40},{64,80... | collective-permute-start | bytes 589832 | tf_op jit(solution)/shard_map/ppermute | solution.py:258
  50.3 6.0 %collective-permute-done.12 = bf16[384,256]{1,0:T(8,128)(2,1)S(1)} collective-permute-done((bf16[384,256]{1,0:T(8,128)(2,1)S(1)}, bf16[384,256]{1,0:T(8,128)(2,1)S(1)}, u32[]{:S(2)}, u32[]{:S(2)}) %collective-permute-start.12) | collective-permute-done | bytes 196640 | tf_op jit(solution)/shard_map/ppermute | solution.py:258
  56.3 0.9 %collective-permute-start.13 = (bf16[192,256]{1,0:T(8,128)(2,1)S(1)}, bf16[192,256]{1,0:T(8,128)(2,1)S(1)}, u32[]{:S(2)}, u32[]{:S(2)}) collective-permute-start(bf16[192,256]{1,0:T(8,128)(2,1)S(1)} %get-tuple-element.31), channel_id=1, source_target_pairs={{0,224},{8,232},{16,240},{24,248},{32,0},{40,8},{48,16},{56,24},{6... | collective-permute-start | bytes 294920 | tf_op jit(solution)/shard_map/ppermute | solution.py:258
  57.3 3.3 %collective-permute-start.14 = (bf16[192,256]{1,0:T(8,128)(2,1)S(1)}, bf16[192,256]{1,0:T(8,128)(2,1)S(1)}, u32[]{:S(2)}, u32[]{:S(2)}) collective-permute-start(bf16[192,256]{1,0:T(8,128)(2,1)S(1)} %get-tuple-element.32), channel_id=1, source_target_pairs={{0,192},{8,200},{16,208},{24,216},{32,224},{40,232},{48,240},{56,2... | collective-permute-start | bytes 294920 | tf_op jit(solution)/shard_map/ppermute | solution.py:258
  60.5 1.3 %collective-permute-done.13 = bf16[192,256]{1,0:T(8,128)(2,1)S(1)} collective-permute-done((bf16[192,256]{1,0:T(8,128)(2,1)S(1)}, bf16[192,256]{1,0:T(8,128)(2,1)S(1)}, u32[]{:S(2)}, u32[]{:S(2)}) %collective-permute-start.13) | collective-permute-done | bytes 98336 | tf_op jit(solution)/shard_map/ppermute | solution.py:258
  61.8 6.2 %collective-permute-done.14 = bf16[192,256]{1,0:T(8,128)(2,1)S(1)} collective-permute-done((bf16[192,256]{1,0:T(8,128)(2,1)S(1)}, bf16[192,256]{1,0:T(8,128)(2,1)S(1)}, u32[]{:S(2)}, u32[]{:S(2)}) %collective-permute-start.14) | collective-permute-done | bytes 98336 | tf_op jit(solution)/shard_map/ppermute | solution.py:258
  68.0 0.6 fusion.7
  (36 shorter events, 1.4 us)
Async XLA Ops:
  0.6 16.5 %collective-permute-start.2 = (bf16[192,512]{1,0:T(8,128)(2,1)}, bf16[192,512]{1,0:T(8,128)(2,1)S(1)}, u32[]{:S(2)}, u32[]{:S(2)}) collective-permute-start(bf16[192,512]{1,0:T(8,128)(2,1)} %a_ref.1), channel_id=1, source_target_pairs={{0,1},{1,0},{2,3},{3,2},{4,5},{5,4},{6,7},{7,6},{8,9},{9,8},{10,11... | collective-permute-start | bytes 589832 | tf_op jit(solution)/shard_map/ppermute | solution.py:258
  3.9 13.3 %collective-permute-start.3 = (bf16[192,512]{1,0:T(8,128)(2,1)}, bf16[192,512]{1,0:T(8,128)(2,1)S(1)}, u32[]{:S(2)}, u32[]{:S(2)}) collective-permute-start(bf16[192,512]{1,0:T(8,128)(2,1)} %a_ref.1), channel_id=1, source_target_pairs={{0,2},{1,3},{2,4},{3,5},{4,6},{5,7},{6,0},{7,1},{8,10},{9,11},{10,... | collective-permute-start | bytes 589832 | tf_op jit(solution)/shard_map/ppermute | solution.py:258
  5.4 11.8 %collective-permute-start.4 = (bf16[192,512]{1,0:T(8,128)(2,1)}, bf16[192,512]{1,0:T(8,128)(2,1)S(1)}, u32[]{:S(2)}, u32[]{:S(2)}) collective-permute-start(bf16[192,512]{1,0:T(8,128)(2,1)} %a_ref.1), channel_id=1, source_target_pairs={{0,6},{1,7},{2,0},{3,1},{4,2},{5,3},{6,4},{7,5},{8,14},{9,15},{10,... | collective-permute-start | bytes 589832 | tf_op jit(solution)/shard_map/ppermute | solution.py:258
  8.0 8.0 %collective-permute-start = (bf16[192,256]{1,0:T(8,128)(2,1)S(1)}, bf16[192,256]{1,0:T(8,128)(2,1)S(1)}, u32[]{:S(2)}, u32[]{:S(2)}) collective-permute-start(bf16[192,256]{1,0:T(8,128)(2,1)S(1)} %pad_add_fusion.z0_ref), channel_id=1, source_target_pairs={{0,64},{8,72},{16,80},{24,88},{32,96},{40,104},{48,112},{56,120},{... | collective-permute-start | bytes 294920 | tf_op jit(solution)/shard_map/ppermute | solution.py:258
  12.5 4.6 %collective-permute-start.1 = (bf16[192,256]{1,0:T(8,128)(2,1)S(1)}, bf16[192,256]{1,0:T(8,128)(2,1)S(1)}, u32[]{:S(2)}, u32[]{:S(2)}) collective-permute-start(bf16[192,256]{1,0:T(8,128)(2,1)S(1)} %pad_add_fusion.z0_ref), channel_id=1, source_target_pairs={{0,32},{8,40},{16,48},{24,56},{32,64},{40,72},{48,80},{56,88},{64,... | collective-permute-start | bytes 294920 | tf_op jit(solution)/shard_map/ppermute | solution.py:258
  13.6 0.9 %copy-start.5 = (bf16[192,512]{1,0:T(8,128)(2,1)S(1)}, bf16[192,512]{1,0:T(8,128)(2,1)}, u32[]{:S(2)}) copy-start(bf16[192,512]{1,0:T(8,128)(2,1)} %q_ref.1) | copy-start | bytes 589828
  14.5 0.7 copy-start.10
  15.8 11.3 %copy-start.6 = (s32[8,768]{1,0:T(8,128)}, s32[8,768]{1,0:T(8,128)S(1)}, u32[]{:S(2)}) copy-start(s32[8,768]{1,0:T(8,128)S(1)} %get-tuple-element.17.bound_ref) | copy-start | bytes 73732
  17.2 5.8 %collective-permute-start.5 = (bf16[384,256]{1,0:T(8,128)(2,1)S(1)}, bf16[384,256]{1,0:T(8,128)(2,1)S(1)}, u32[]{:S(2)}, u32[]{:S(2)}) collective-permute-start(bf16[384,256]{1,0:T(8,128)(2,1)S(1)} %pick_side.1.after), channel_id=1, source_target_pairs={{0,16},{8,24},{16,0},{24,8},{32,48},{40,56},{48,32},{56,40},{64,80... | collective-permute-start | bytes 589832 | tf_op jit(solution)/shard_map/ppermute | solution.py:258
  18.0 5.8 %collective-permute-start.7 = (bf16[192,512]{1,0:T(8,128)(2,1)S(1)}, bf16[192,512]{1,0:T(8,128)(2,1)}, u32[]{:S(2)}, u32[]{:S(2)}) collective-permute-start(bf16[192,512]{1,0:T(8,128)(2,1)S(1)} %collective-permute-done.2.refs_0_.b_ref), channel_id=1, source_target_pairs={{0,6},{1,7},{2,0},{3,1},{4,2},{5,3},{6,4},{7,5},{8,14},{9,15},{10,... | collective-permute-start | bytes 589832 | tf_op jit(solution)/shard_map/ppermute | solution.py:258
  19.5 6.9 %collective-permute-start.6 = (bf16[192,512]{1,0:T(8,128)(2,1)S(1)}, bf16[192,512]{1,0:T(8,128)(2,1)S(1)}, u32[]{:S(2)}, u32[]{:S(2)}) collective-permute-start(bf16[192,512]{1,0:T(8,128)(2,1)S(1)} %collective-permute-done.2.refs_0_.b_ref), channel_id=1, source_target_pairs={{0,2},{1,3},{2,4},{3,5},{4,6},{5,7},{6,0},{7,1},{8,10},{9,11},{10,... | collective-permute-start | bytes 589832 | tf_op jit(solution)/shard_map/ppermute | solution.py:258
  20.8 6.3 %copy-start.8 = (f32[8,768]{1,0:T(8,128)}, f32[8,768]{1,0:T(8,128)S(1)}, u32[]{:S(2)}) copy-start(f32[8,768]{1,0:T(8,128)S(1)} %get-tuple-element.18.refs_0_.stat_ref) | copy-start | bytes 73732
  26.4 0.7 copy-start.2
  27.1 9.6 %collective-permute-start.8 = (bf16[960,256]{1,0:T(8,128)(2,1)S(1)}, bf16[960,256]{1,0:T(8,128)(2,1)S(1)}, u32[]{:S(2)}, u32[]{:S(2)}) collective-permute-start(bf16[960,256]{1,0:T(8,128)(2,1)S(1)} %join_slots.1.after.own_ref), channel_id=1, source_target_pairs={{0,8},{8,0},{16,24},{24,16},{32,40},{40,32},{48,56},{56,48},{64,72... | collective-permute-start | bytes 1474568 | tf_op jit(solution)/shard_map/ppermute | solution.py:258
  27.1 14.6 %collective-permute-start.9 = (bf16[192,512]{1,0:T(8,128)(2,1)S(1)}, bf16[192,512]{1,0:T(8,128)(2,1)}, u32[]{:S(2)}, u32[]{:S(2)}) collective-permute-start(bf16[192,512]{1,0:T(8,128)(2,1)S(1)} %collective-permute-done.3.refs_1_.c_ref), channel_id=1, source_target_pairs={{0,2},{1,3},{2,4},{3,5},{4,6},{5,7},{6,0},{7,1},{8,10},{9,11},{10,... | collective-permute-start | bytes 589832 | tf_op jit(solution)/shard_map/ppermute | solution.py:258
  27.1 14.6 %collective-permute-start.10 = (bf16[192,512]{1,0:T(8,128)(2,1)}, bf16[192,512]{1,0:T(8,128)(2,1)}, u32[]{:S(2)}, u32[]{:S(2)}) collective-permute-start(bf16[192,512]{1,0:T(8,128)(2,1)} %collective-permute-done.7.refs_2_.f_ref), channel_id=1, source_target_pairs={{0,6},{1,7},{2,0},{3,1},{4,2},{5,3},{6,4},{7,5},{8,14},{9,15},{10,... | collective-permute-start | bytes 589832 | tf_op jit(solution)/shard_map/ppermute | solution.py:258
  30.3 2.2 %copy-start = (bf16[512,4096]{1,0:T(8,128)(2,1)S(1)}, bf16[512,4096]{1,0:T(8,128)(2,1)}, u32[]{:S(2)}) copy-start(bf16[512,4096]{1,0:T(8,128)(2,1)} %w_ref.3) | copy-start | bytes 12582916
  32.5 0.9 %copy-start.3 = (bf16[192,512]{1,0:T(8,128)(2,1)S(1)}, bf16[192,512]{1,0:T(8,128)(2,1)}, u32[]{:S(2)}) copy-start(bf16[192,512]{1,0:T(8,128)(2,1)} %copy-done.2) | copy-start | bytes 589828
  33.4 0.9 %copy-start.4 = (bf16[192,512]{1,0:T(8,128)(2,1)S(1)}, bf16[192,512]{1,0:T(8,128)(2,1)}, u32[]{:S(2)}) copy-start(bf16[192,512]{1,0:T(8,128)(2,1)} %a_ref.1) | copy-start | bytes 589828
  34.4 2.3 %copy-start.7 = (s32[8,768]{1,0:T(8,128)S(1)}, s32[8,768]{1,0:T(8,128)}, u32[]{:S(2)}) copy-start(s32[8,768]{1,0:T(8,128)} %copy-done.6) | copy-start | bytes 73732
  34.4 2.3 %copy-start.9 = (f32[8,768]{1,0:T(8,128)S(1)}, f32[8,768]{1,0:T(8,128)}, u32[]{:S(2)}) copy-start(f32[8,768]{1,0:T(8,128)} %copy-done.8) | copy-start | bytes 73732
  34.4 7.3 %copy-start.1 = (bf16[512,4096]{1,0:T(8,128)(2,1)S(1)}, bf16[512,4096]{1,0:T(8,128)(2,1)}, u32[]{:S(2)}) copy-start(bf16[512,4096]{1,0:T(8,128)(2,1)} %w_ref.3) | copy-start | bytes 12582916
  45.2 3.4 %collective-permute-start.11 = (bf16[960,256]{1,0:T(8,128)(2,1)S(1)}, bf16[960,256]{1,0:T(8,128)(2,1)S(1)}, u32[]{:S(2)}, u32[]{:S(2)}) collective-permute-start(bf16[960,256]{1,0:T(8,128)(2,1)S(1)} %get-tuple-element.28), channel_id=1, source_target_pairs={{0,8},{8,0},{16,24},{24,16},{32,40},{40,32},{48,56},{56,48},{64,72... | collective-permute-start | bytes 1474568 | tf_op jit(solution)/shard_map/ppermute | solution.py:258
  48.8 7.4 %collective-permute-start.12 = (bf16[384,256]{1,0:T(8,128)(2,1)S(1)}, bf16[384,256]{1,0:T(8,128)(2,1)S(1)}, u32[]{:S(2)}, u32[]{:S(2)}) collective-permute-start(bf16[384,256]{1,0:T(8,128)(2,1)S(1)} %pad_maximum_fusion), channel_id=1, source_target_pairs={{0,16},{8,24},{16,0},{24,8},{32,48},{40,56},{48,32},{56,40},{64,80... | collective-permute-start | bytes 589832 | tf_op jit(solution)/shard_map/ppermute | solution.py:258
  56.3 5.5 %collective-permute-start.13 = (bf16[192,256]{1,0:T(8,128)(2,1)S(1)}, bf16[192,256]{1,0:T(8,128)(2,1)S(1)}, u32[]{:S(2)}, u32[]{:S(2)}) collective-permute-start(bf16[192,256]{1,0:T(8,128)(2,1)S(1)} %get-tuple-element.31), channel_id=1, source_target_pairs={{0,224},{8,232},{16,240},{24,248},{32,0},{40,8},{48,16},{56,24},{6... | collective-permute-start | bytes 294920 | tf_op jit(solution)/shard_map/ppermute | solution.py:258
  57.3 10.7 %collective-permute-start.14 = (bf16[192,256]{1,0:T(8,128)(2,1)S(1)}, bf16[192,256]{1,0:T(8,128)(2,1)S(1)}, u32[]{:S(2)}, u32[]{:S(2)}) collective-permute-start(bf16[192,256]{1,0:T(8,128)(2,1)S(1)} %get-tuple-element.32), channel_id=1, source_target_pairs={{0,192},{8,200},{16,208},{24,216},{32,224},{40,232},{48,240},{56,2... | collective-permute-start | bytes 294920 | tf_op jit(solution)/shard_map/ppermute | solution.py:258

commit v3 on v2

--- a/solution.py
+++ b/solution.py
@@ -82,7 +82,8 @@
     return new, total
 
 
-def near_kernel(place_ref, z2_ref, z1_ref, z0_ref, q4_ref, bound_ref, after, s_ref, stat_ref):
+def near_kernel(place_ref, z2_ref, z1_ref, z0_ref, q4_ref, bound_ref, *refs):
+    s_ref, stat_ref = refs[-2:]
     me = place_ref[0]
     queries = q4_ref[...]
     row = lax.broadcasted_iota(jnp.int32, (ROWS, LANES), 0)
@@ -166,11 +167,15 @@
     return at + 1 - 2 * lax.rem(at, 2) if flip else at
 
 
-def early_kernel(head_ref, a_ref, b_ref, c_ref, d_ref, e_ref, f_ref, w_ref, after, out_ref):
+def first_projection(head_ref, a_ref, w_ref, out_ref):
+    out_ref[...] = project(None, (a_ref,), (head_ref[0],), w_ref)
+
+
+def early_kernel(head_ref, acc_ref, b_ref, c_ref, d_ref, e_ref, f_ref, w_ref, after, out_ref):
     head = head_ref[0]
-    sources = (head, source_of(head, 0, True), source_of(head, -2, False), source_of(head, 2, False))
+    sources = (source_of(head, 0, True), source_of(head, -2, False), source_of(head, 2, False))
     sources += (source_of(head, -2, True), source_of(head, 2, True))
-    out_ref[...] = project(None, (a_ref, b_ref, c_ref, d_ref, e_ref, f_ref), sources, w_ref)
+    out_ref[...] = project(acc_ref[...], (b_ref, c_ref, d_ref, e_ref, f_ref), sources, w_ref)
 
 
 def back_block(kv_ref, slot, p_ref, i, g4, q4, rd):
@@ -184,9 +189,14 @@
     return dk, dv, dq
 
 
-def second_kernel(place_ref, head_ref, a_ref, b_ref, early_ref, w_ref, q4_ref, par_ref, p_ref, o_ref, out_ref, g_ref, rd_ref, dq_ref):
-    me = place_ref[0]
-    core = lax.rem(me, 2)
+def put(out_ref, slot, dk, dv):
+    at = pl.ds(pl.multiple_of(slot * ROWS, ROWS), ROWS)
+    out_ref[at, :D] = dk.astype(out_ref.dtype)
+    out_ref[at, D:] = dv.astype(out_ref.dtype)
+
+
+def cross_far(place_ref, head_ref, a_ref, b_ref, early_ref, w_ref, q4_ref, par_ref, p_ref, o_ref, out_ref, g_ref, rd_ref, dq_ref):
+    core = lax.rem(place_ref[0], 2)
     head = head_ref[0]
     sources = (source_of(head, 4, False), source_of(head, 4, True))
     acc = project(early_ref[...], (a_ref, b_ref), sources, w_ref)
@@ -198,36 +208,74 @@
     rd = jnp.sum(gt * o_ref[...], axis=0, keepdims=True)
     rd_ref[...] = rd
     dq_ref[...] = jnp.zeros((D, LANES), jnp.float32)
-    out_ref[...] = jnp.zeros(out_ref.shape, out_ref.dtype)
-
-    def step(i, _):
-        dk, dv, dq = back_block(par_ref, i + core, p_ref, i, g4, q4_ref[...], rd)
-        at = pl.ds(pl.multiple_of((i + core) * ROWS, ROWS), ROWS)
-        out_ref[at, :D] = dk.astype(jnp.bfloat16)
-        out_ref[at, D:] = dv.astype(jnp.bfloat16)
+
+    @pl.when(core == 1)
+    def _():
+        out_ref[:ROWS, :] = jnp.zeros((ROWS, 2 * D), out_ref.dtype)
+
+    def step(slot, _):
+        dk, dv, dq = back_block(par_ref, slot, p_ref, slot - core, g4, q4_ref[...], rd)
+        put(out_ref, slot, dk, dv)
         dq_ref[...] += dq
         return 0
 
-    lax.fori_loop(0, REACH, step, 0)
-
-
-def third_kernel(q4_ref, own_ref, p_ref, g_ref, rd_ref, dq_in_ref, out_ref, dq_out_ref, acc):
+    lax.fori_loop(core, 2, step, 0)
+
+
+def cross_near(place_ref, q4_ref, par_ref, p_ref, g_ref, rd_ref, dq_in_ref, out_ref, dq_ref):
+    core = lax.rem(place_ref[0], 2)
+    g4 = g_ref[...]
+    rd = rd_ref[...]
+    dq_ref[...] = dq_in_ref[...]
+
+    @pl.when(core == 0)
+    def _():
+        out_ref[2 * ROWS :, :] = jnp.zeros((ROWS, 2 * D), out_ref.dtype)
+
+    def step(slot, _):
+        dk, dv, dq = back_block(par_ref, slot, p_ref, slot - core, g4, q4_ref[...], rd)
+        put(out_ref, slot - 2, dk, dv)
+        dq_ref[...] += dq
+        return 0
+
+    lax.fori_loop(2, REACH + core, step, 0)
+
+
+def own_far(q4_ref, own_ref, p_ref, g_ref, rd_ref, dq_in_ref, out_ref, dq_ref):
+    g4 = g_ref[...]
+    rd = rd_ref[...]
+    dq_ref[...] = dq_in_ref[...]
+
+    def step(slot, _):
+        dk, dv, dq = back_block(own_ref, slot, p_ref, slot, g4, q4_ref[...], rd)
+        put(out_ref, slot, dk, dv)
+        dq_ref[...] += dq
+        return 0
+
+    lax.fori_loop(0, 2, step, 0)
+
+
+def own_near(q4_ref, own_ref, p_ref, g_ref, rd_ref, dq_in_ref, after, out_ref, dq_out_ref, acc):
     g4 = g_ref[...]
     rd = rd_ref[...]
     acc[...] = dq_in_ref[...]
 
-    def step(i, _):
-        dk, dv, dq = back_block(own_ref, i, p_ref, i, g4, q4_ref[...], rd)
-        at = pl.ds(pl.multiple_of(i * ROWS, ROWS), ROWS)
-        out_ref[at, :D] = dk
-        out_ref[at, D:] = dv
+    def step(slot, _):
+        dk, dv, dq = back_block(own_ref, slot, p_ref, slot, g4, q4_ref[...], rd)
+        put(out_ref, slot - 2, dk, dv)
         acc[...] += dq
         return 0
 
-    lax.fori_loop(0, SLOTS, step, 0)
+    lax.fori_loop(2, SLOTS, step, 0)
     dq = jnp.transpose(acc[...]) * SCALE
     for h in range(HEADS):
         dq_out_ref[:, h * D : (h + 1) * D] = dq[h * ROWS : (h + 1) * ROWS, :].astype(jnp.bfloat16)
+
+
+def settle_kernel(own_ref, back_ref, after, both_ref, side_ref):
+    both = own_ref[...] + back_ref[...].astype(jnp.float32)
+    both_ref[...] = both
+    side_ref[...] = both[ROWS : 2 * ROWS].astype(jnp.bfloat16)
 
 
 def vmem(n):
@@ -290,6 +338,16 @@
         name="prepare",
     )(place, lengths, queries)
 
+    begun = pl.pallas_call(
+        first_projection,
+        out_shape=shape(ROWS, HEADS * D, f32),
+        in_specs=smem(1) + vmem(2),
+        out_specs=vmem(1)[0],
+        compiler_params=params(8),
+        cost_estimate=cost(1, 1),
+        name="first_projection",
+    )(head, grad_out, out_weight)
+
     z2 = turned(kv, "ctx", 2 * PLANE)
     z1 = turned(kv, "ctx", PLANE)
 
@@ -301,23 +359,23 @@
     picked = pl.pallas_call(
         pick_kernel,
         out_shape=shape(2 * ROWS, 2 * D, bf16),
-        in_specs=smem(1) + vmem(3) + token(4),
+        in_specs=smem(1) + vmem(3) + token(2),
         out_specs=vmem(1)[0],
         compiler_params=params(8),
         cost_estimate=cost(1, 1),
         name="pick_side",
-    )(place, z2, z1, kv, other, right, left, q4)
+    )(place, z2, z1, kv, q4, begun)
     side = moved(picked, "ctx", lambda i: i ^ 2)
 
     s_near, stat = pl.pallas_call(
         near_kernel,
         out_shape=(shape(3 * ROWS, LANES, f32), shape(8, LANES, f32)),
-        in_specs=smem(1) + vmem(5) + token(1),
-        out_specs=tuple(vmem(2)),
-        compiler_params=params(16),
+        in_specs=smem(1) + vmem(5) + token(3),
+        out_specs=tuple(vmem(2)),
+        compiler_params=params(10),
         cost_estimate=cost(1, 1),
         name="near_scores",
-    )(place, z2, z1, kv, q4, bound, picked)
+    )(place, z2, z1, kv, q4, bound, picked, right, left)
 
     own = pl.pallas_call(
         join_kernel,
@@ -335,10 +393,10 @@
         out_shape=shape(ROWS, HEADS * D, f32),
         in_specs=smem(1) + vmem(7) + token(1),
         out_specs=vmem(1)[0],
-        compiler_params=params(16),
+        compiler_params=params(10),
         cost_estimate=cost(1, 1),
         name="early_projection",
-    )(head, grad_out, other, right, left, other_right, other_left, out_weight, own)
+    )(head, begun, other, right, left, other_right, other_left, out_weight, own)
 
     p_own, p_par, out_t = pl.pallas_call(
         rest_kernel,
@@ -346,44 +404,74 @@
         in_specs=smem(1) + vmem(6) + token(1),
         out_specs=tuple(vmem(3)),
         scratch_shapes=[pltpu.VMEM((2 * ROWS, LANES), f32), pltpu.VMEM((REACH * ROWS, LANES), f32)],
-        compiler_params=params(24),
+        compiler_params=params(12),
         cost_estimate=cost(1, 1),
         name="softmax",
     )(place, own, par, q4, bound, s_near, stat, early)
 
-    par_grad, g4, rd, dq = pl.pallas_call(
-        second_kernel,
-        out_shape=(shape(SLOTS * ROWS, 2 * D, bf16), shape(LANES, D, bf16), shape(1, LANES, f32), shape(D, LANES, f32)),
+    far_cross, g4, rd, dq = pl.pallas_call(
+        cross_far,
+        out_shape=(shape(2 * ROWS, 2 * D, bf16), shape(LANES, D, bf16), shape(1, LANES, f32), shape(D, LANES, f32)),
         in_specs=smem(2) + vmem(8),
         out_specs=tuple(vmem(4)),
-        compiler_params=params(24),
-        cost_estimate=cost(1, 1),
-        name="partner_grads",
+        compiler_params=params(10),
+        cost_estimate=cost(1, 1),
+        name="cross_far",
     )(place, head, far, other_far, early, out_weight, q4, par, p_par, out_t)
-
-    back = moved(par_grad, "ctx", lambda i: i ^ 1)
-
-    own_grad, grad_queries = pl.pallas_call(
-        third_kernel,
-        out_shape=(shape(SLOTS * ROWS, 2 * D, f32), shape(ROWS, HEADS * D, bf16)),
+    far_back = moved(far_cross, "ctx", lambda i: i ^ 1)
+
+    near_cross, dq = pl.pallas_call(
+        cross_near,
+        out_shape=(shape(3 * ROWS, 2 * D, bf16), shape(D, LANES, f32)),
+        in_specs=smem(1) + vmem(6),
+        out_specs=tuple(vmem(2)),
+        compiler_params=params(10),
+        cost_estimate=cost(1, 1),
+        name="cross_near",
+    )(place, q4, par, p_par, g4, rd, dq)
+    near_back = moved(near_cross, "ctx", lambda i: i ^ 1)
+
+    far_own, dq = pl.pallas_call(
+        own_far,
+        out_shape=(shape(2 * ROWS, 2 * D, f32), shape(D, LANES, f32)),
         in_specs=vmem(6),
         out_specs=tuple(vmem(2)),
+        compiler_params=params(10),
+        cost_estimate=cost(1, 1),
+        name="own_far",
+    )(q4, own, p_own, g4, rd, dq)
+    far_both = far_own + far_back.astype(f32)
+    far_side = moved(far_both[ROWS:].astype(bf16), "ctx", lambda i: i ^ 2)
+
+    near_own, grad_queries = pl.pallas_call(
+        own_near,
+        out_shape=(shape(3 * ROWS, 2 * D, f32), shape(ROWS, HEADS * D, bf16)),
+        in_specs=vmem(6) + token(1),
+        out_specs=tuple(vmem(2)),
         scratch_shapes=[pltpu.VMEM((D, LANES), f32)],
-        compiler_params=params(24),
-        cost_estimate=cost(1, 1),
-        name="own_grads",
-    )(q4, own, p_own, g4, rd, dq)
-
-    both = own_grad + back.astype(f32)
-    slots = [both[m * ROWS : (m + 1) * ROWS] for m in range(SLOTS)]
-    crossed = moved(jnp.concatenate([slots[1], slots[3]]).astype(bf16), "ctx", lambda i: i ^ 2).astype(f32)
-    first, second = crossed[:ROWS], crossed[ROWS:]
-    zero = jnp.zeros_like(first)
-    to_two = slots[0] + jnp.where(upper, first, zero)
-    to_one = slots[2] + jnp.where(upper, second, first)
-    total = slots[4] + jnp.where(upper, zero, second)
-    got_two = turned(to_two.astype(bf16), "ctx", -2 * PLANE)
+        compiler_params=params(10),
+        cost_estimate=cost(1, 1),
+        name="own_near",
+    )(q4, own, p_own, g4, rd, dq, far_back)
+    zero = jnp.zeros((ROWS, 2 * D), f32)
+    far_side = far_side.astype(f32)
+    to_two = (far_both[:ROWS] + jnp.where(upper, far_side, zero)).astype(bf16)
+    got_two = turned(to_two, "ctx", -2 * PLANE)
+
+    near_both, near_side = pl.pallas_call(
+        settle_kernel,
+        out_shape=(shape(3 * ROWS, 2 * D, f32), shape(ROWS, 2 * D, bf16)),
+        in_specs=vmem(2) + token(1),
+        out_specs=tuple(vmem(2)),
+        compiler_params=params(8),
+        cost_estimate=cost(1, 1),
+        name="settle",
+    )(near_own, near_back, to_two)
+    near_side = moved(near_side, "ctx", lambda i: i ^ 2).astype(f32)
+
+    to_one = near_both[:ROWS] + jnp.where(upper, near_side, far_side)
     got_one = turned(to_one.astype(bf16), "ctx", -PLANE)
+    total = near_both[2 * ROWS :] + jnp.where(upper, zero, near_side)
     total = (total + got_one.astype(f32) + got_two.astype(f32)).astype(bf16)
     return grad_queries, total[:, :D], total[:, D:]
 

time: 69.5 us -> 63.1 us (0.908)
  waiting for transfers between devices: 20.4 us -> 15 us
  Pallas kernels: 15.3 us -> 13.6 us
  other arithmetic: 1.16 us -> 2.78 us
  starting transfers between devices: 24 us -> 23.2 us
    ppermute x15 -> x17, waiting for transfers between devices: 20.4 us -> 15 us  [moved(): lax.ppermute(x, axis, [(i, to(i)) for i in range(lax.axis_size(axis))])]
    pallas_call x1, Pallas kernels: 2.25 us -> 1.01 us  [local(): pl.pallas_call(early_kernel, out_shape=shape(ROWS, HEADS * D, f32), in_sp...]
    convert_element_type x1, other arithmetic: 0.03 us -> 0.92 us  [local(): to_two = (far_both[:ROWS] + jnp.where(upper, far_side, zero)).astype(bf16)]
    convert_element_type x1, other arithmetic: 0.06 us -> 0.93 us  [local(): got_one = turned(to_one.astype(bf16), 'ctx', -PLANE)]
    ppermute x15 -> x17, starting transfers between devices: 24 us -> 23.2 us  [moved(): lax.ppermute(x, axis, [(i, to(i)) for i in range(lax.axis_size(axis))])]
    pallas_call x2 -> x6, Pallas kernels: 6.61 us -> 6.12 us  [the longest x1 2.23 us: local(): pl.pallas_call(own_near, out_shape=(shape(3 * ROWS, 2 * D, f32), shape(RO...]
    unnamed x22 -> x16, local copies, waits for them, and re-layouts: 6.28 us -> 5.91 us
  transfers between devices with their start and end apart: 15 -> 17, of which waited for: 8 -> 7; matrix products, arithmetic and copies ran while one was open for 1% -> 4% of each run, Pallas kernels for 17% -> 19%
where the time goes in v3:
time: 63.1 us; the launch traced here: 62.6 us
  starting transfers between devices  23.2 us (37%)
  waiting for transfers between devices  15 us (24%)
  Pallas kernels  13.6 us (22%)
  local copies, waits for them, and re-layouts  7.25 us (11%)
  other arithmetic  2.78 us (4%)
  between operations  0.83 us (1%)
    ppermute x17, starting transfers between devices, moved(): lax.ppermute(x, axis, [(i, to(i)) for i in range(lax.axis_size(axis))])  23.2 us
    ppermute x17, waiting for transfers between devices, moved(): lax.ppermute(x, axis, [(i, to(i)) for i in range(lax.axis_size(axis))])  15 us
    unnamed x16, local copies, waits for them, and re-layouts  5.91 us
    pallas_call x1, Pallas kernels, local(): pl.pallas_call(rest_kernel, out_shape=(shape(SLOTS * ROWS, LANES, bf16),...  5.02 us
    pallas_call x1, Pallas kernels, local(): pl.pallas_call(own_near, out_shape=(shape(3 * ROWS, 2 * D, f32), shape(RO...  2.23 us
    pallas_call x1, Pallas kernels, local(): pl.pallas_call(cross_far, out_shape=(shape(2 * ROWS, 2 * D, bf16), shape(...  1.59 us
  transfers between devices with their start and end apart: 17, of which 7 were waited for; matrix products, arithmetic and copies ran while one was open for 4% of the time, Pallas kernels for 19%

profile of v3, /device:TPU:64, one launch (start us, length us, event | category | flops | bytes accessed | tf_op | source)
XLA Modules:
  0.0 62.6 jit_solution(17472770014883721624)
XLA Ops:
  0.6 3.3 %collective-permute-start.5 = (bf16[192,512]{1,0:T(8,128)(2,1)}, bf16[192,512]{1,0:T(8,128)(2,1)S(1)}, u32[]{:S(2)}, u32[]{:S(2)}) collective-permute-start(bf16[192,512]{1,0:T(8,128)(2,1)} %a_ref.1), channel_id=1, source_target_pairs={{0,1},{1,0},{2,3},{3,2},{4,5},{5,4},{6,7},{7,6},{8,9},{9,8},{10,11... | collective-permute-start | bytes 589832 | tf_op jit(solution)/shard_map/ppermute | solution.py:306
  3.9 0.8 %pad_add_fusion.z0_ref = bf16[192,256]{1,0:T(8,128)(2,1)S(1)} fusion(bf16[192,128]{1,0:T(8,128)(2,1)} %param.8, bf16[192,128]{1,0:T(8,128)(2,1)} %param.7), kind=kLoop, calls=%fused_computation.13 | loop fusion | flops 196608 | bytes 196608 | tf_op jit(solution)/shard_map/add | solution.py:330
  4.7 4.6 %collective-permute-start = (bf16[192,256]{1,0:T(8,128)(2,1)S(1)}, bf16[192,256]{1,0:T(8,128)(2,1)S(1)}, u32[]{:S(2)}, u32[]{:S(2)}) collective-permute-start(bf16[192,256]{1,0:T(8,128)(2,1)S(1)} %pad_add_fusion.z0_ref), channel_id=1, source_target_pairs={{0,64},{8,72},{16,80},{24,88},{32,96},{40,104},{48,112},{56,120},{... | collective-permute-start | bytes 294920 | tf_op jit(solution)/shard_map/ppermute | solution.py:306
  9.3 1.0 %collective-permute-start.1 = (bf16[192,256]{1,0:T(8,128)(2,1)S(1)}, bf16[192,256]{1,0:T(8,128)(2,1)S(1)}, u32[]{:S(2)}, u32[]{:S(2)}) collective-permute-start(bf16[192,256]{1,0:T(8,128)(2,1)S(1)} %pad_add_fusion.z0_ref), channel_id=1, source_target_pairs={{0,32},{8,40},{16,48},{24,56},{32,64},{40,72},{48,80},{56,88},{64,... | collective-permute-start | bytes 294920 | tf_op jit(solution)/shard_map/ppermute | solution.py:306
  10.3 1.5 %collective-permute-start.3 = (bf16[192,512]{1,0:T(8,128)(2,1)}, bf16[192,512]{1,0:T(8,128)(2,1)S(1)}, u32[]{:S(2)}, u32[]{:S(2)}) collective-permute-start(bf16[192,512]{1,0:T(8,128)(2,1)} %a_ref.1), channel_id=1, source_target_pairs={{0,2},{1,3},{2,4},{3,5},{4,6},{5,7},{6,0},{7,1},{8,10},{9,11},{10,... | collective-permute-start | bytes 589832 | tf_op jit(solution)/shard_map/ppermute | solution.py:306
  11.8 1.7 %collective-permute-start.4 = (bf16[192,512]{1,0:T(8,128)(2,1)}, bf16[192,512]{1,0:T(8,128)(2,1)S(1)}, u32[]{:S(2)}, u32[]{:S(2)}) collective-permute-start(bf16[192,512]{1,0:T(8,128)(2,1)} %a_ref.1), channel_id=1, source_target_pairs={{0,6},{1,7},{2,0},{3,1},{4,2},{5,3},{6,4},{7,5},{8,14},{9,15},{10,... | collective-permute-start | bytes 589832 | tf_op jit(solution)/shard_map/ppermute | solution.py:306
  13.6 2.2 %copy-done = bf16[512,4096]{1,0:T(8,128)(2,1)S(1)} copy-done((bf16[512,4096]{1,0:T(8,128)(2,1)S(1)}, bf16[512,4096]{1,0:T(8,128)(2,1)}, u32[]{:S(2)}) %copy-start) | copy-done | bytes 4194328
  15.8 0.9 %copy-done.3 = bf16[192,512]{1,0:T(8,128)(2,1)S(1)} copy-done((bf16[192,512]{1,0:T(8,128)(2,1)S(1)}, bf16[192,512]{1,0:T(8,128)(2,1)}, u32[]{:S(2)}) %copy-start.3) | copy-done | bytes 196632
  18.3 0.8 %collective-permute-start.2 = (bf16[384,256]{1,0:T(8,128)(2,1)S(1)}, bf16[384,256]{1,0:T(8,128)(2,1)S(1)}, u32[]{:S(2)}, u32[]{:S(2)}) collective-permute-start(bf16[384,256]{1,0:T(8,128)(2,1)S(1)} %pick_side.1.refs_0_), channel_id=1, source_target_pairs={{0,16},{8,24},{16,0},{24,8},{32,48},{40,56},{48,32},{56,40},{64,80... | collective-permute-start | bytes 589832 | tf_op jit(solution)/shard_map/ppermute | solution.py:306
  19.0 1.5 %collective-permute-start.7 = (bf16[192,512]{1,0:T(8,128)(2,1)S(1)}, bf16[192,512]{1,0:T(8,128)(2,1)S(1)}, u32[]{:S(2)}, u32[]{:S(2)}) collective-permute-start(bf16[192,512]{1,0:T(8,128)(2,1)S(1)} %collective-permute-done.5.b_ref), channel_id=1, source_target_pairs={{0,6},{1,7},{2,0},{3,1},{4,2},{5,3},{6,4},{7,5},{8,14},{9,15},{10,... | collective-permute-start | bytes 589832 | tf_op jit(solution)/shard_map/ppermute | solution.py:306
  21.1 0.8 %near_scores.1 = (f32[576,768]{1,0:T(8,128)S(1)}, f32[8,768]{1,0:T(8,128)S(1)}) custom-call(s32[1]{0:T(128)} %bitcast.place_ref, bf16[192,256]{1,0:T(8,128)(2,1)S(1)} %collective-permute-done.z2_ref, bf16[192,256]{1,0:T(8,128)(2,1)S(1)} %collective-permute-done.1.z1_ref, bf16[192,256]{1,0:T(8,128)(2,1)S(1)} %pad_add_fusion.z0_ref, ...), custom_call_target="tpu_custom_call" | custom-call | flops 1 | bytes 1 | tf_op jit(solution)/shard_map/near_scores/pallas_call | solution.py:370
  21.9 2.2 %collective-permute-done.2.side_ref = bf16[384,256]{1,0:T(8,128)(2,1)S(1)} collective-permute-done((bf16[384,256]{1,0:T(8,128)(2,1)S(1)}, bf16[384,256]{1,0:T(8,128)(2,1)S(1)}, u32[]{:S(2)}, u32[]{:S(2)}) %collective-permute-start.2) | collective-permute-done | bytes 196640 | tf_op jit(solution)/shard_map/ppermute | solution.py:306
  24.0 0.7 %collective-permute-done.7.refs_2_.f_ref = bf16[192,512]{1,0:T(8,128)(2,1)S(1)} collective-permute-done((bf16[192,512]{1,0:T(8,128)(2,1)S(1)}, bf16[192,512]{1,0:T(8,128)(2,1)S(1)}, u32[]{:S(2)}, u32[]{:S(2)}) %collective-permute-start.7) | collective-permute-done | bytes 196640 | tf_op jit(solution)/shard_map/ppermute | solution.py:306
  24.7 2.8 %collective-permute-done.6.refs_1_.e_ref = bf16[192,512]{1,0:T(8,128)(2,1)S(1)} collective-permute-done((bf16[192,512]{1,0:T(8,128)(2,1)S(1)}, bf16[192,512]{1,0:T(8,128)(2,1)S(1)}, u32[]{:S(2)}, u32[]{:S(2)}) %collective-permute-start.6) | collective-permute-done | bytes 196640 | tf_op jit(solution)/shard_map/ppermute | solution.py:306
  27.7 3.2 %collective-permute-start.10 = (bf16[192,512]{1,0:T(8,128)(2,1)S(1)}, bf16[192,512]{1,0:T(8,128)(2,1)S(1)}, u32[]{:S(2)}, u32[]{:S(2)}) collective-permute-start(bf16[192,512]{1,0:T(8,128)(2,1)S(1)} %collective-permute-done.7.refs_2_.f_ref), channel_id=1, source_target_pairs={{0,6},{1,7},{2,0},{3,1},{4,2},{5,3},{6,4},{7,5},{8,14},{9,15},{10,... | collective-permute-start | bytes 589832 | tf_op jit(solution)/shard_map/ppermute | solution.py:306
  30.9 2.2 %copy-done.1 = bf16[512,4096]{1,0:T(8,128)(2,1)S(1)} copy-done((bf16[512,4096]{1,0:T(8,128)(2,1)S(1)}, bf16[512,4096]{1,0:T(8,128)(2,1)}, u32[]{:S(2)}) %copy-start.1) | copy-done | bytes 4194328
  33.1 1.0 %early_projection.1.after.early_ref = f32[192,512]{1,0:T(8,128)S(1)} custom-call(s32[1]{0:T(128)} %bitcast.1.head_ref, f32[192,512]{1,0:T(8,128)S(1)} %first_projection.1.refs_1_.acc_ref, bf16[192,512]{1,0:T(8,128)(2,1)S(1)} %collective-permute-done.5.b_ref, bf16[192,512]{1,0:T(8,128)(2,1)S(1)} %collective-permute-done.3.refs_1_.c_ref, ...), custom_call_target="tpu_custom_call" | custom-call | flops 1 | bytes 1 | tf_op jit(solution)/shard_map/early_projection/pallas_call | solution.py:391
  34.1 5.0 %softmax.1 = (bf16[960,768]{1,0:T(8,128)(2,1)S(1)}, bf16[768,768]{1,0:T(8,128)(2,1)S(1)}, f32[128,768]{1,0:T(8,128)S(1)}) custom-call(s32[1]{0:T(128)} %bitcast.place_ref, bf16[960,256]{1,0:T(8,128)(2,1)S(1)} %join_slots.1.after.own_ref, bf16[960,256]{1,0:T(8,128)(2,1)S(1)} %collective-permute-done.8.par_ref, ...), custom_call_target="tpu_custom_call" | custom-call | flops 1 | bytes 1 | tf_op jit(solution)/shard_map/softmax/pallas_call | solution.py:401
  39.2 1.6 %cross_far.1 = (bf16[384,256]{1,0:T(8,128)(2,1)S(1)}, bf16[768,128]{1,0:T(8,128)(2,1)S(1)}, f32[1,768]{1,0:T(1,128)S(1)}, f32[128,768]{1,0:T(8,128)S(1)}) custom-call(s32[1]{0:T(128)} %bitcast.place_ref, s32[1]{0:T(128)} %bitcast.1.head_ref, bf16[192,512]{1,0:T(8,128)(2,1)S(1)} %collective-permute-done.9.a_ref, ...), custom_call_target="tpu_custom_call" | custom-call | flops 1 | bytes 1 | tf_op jit(solution)/shard_map/cross_far/pallas_call | solution.py:412
  41.1 1.0 %cross_near.1 = (bf16[576,256]{1,0:T(8,128)(2,1)S(1)}, f32[128,768]{1,0:T(8,128)S(1)}) custom-call(s32[1]{0:T(128)} %bitcast.place_ref, bf16[768,128]{1,0:T(8,128)(2,1)S(1)} %get-tuple-element.22.refs_0_.q4_ref, bf16[960,256]{1,0:T(8,128)(2,1)S(1)} %collective-permute-done.8.par_ref, bf16[768,768]{1,0:T(8,128)(2,1)S(1)} %get-tuple-element.27.p_ref, ...), custom_call_target="tpu_custom_call" | custom-call | flops 1 | bytes 1 | tf_op jit(solution)/shard_map/cross_near/pallas_call | solution.py:423
  42.0 0.9 %own_far.1 = (f32[384,256]{1,0:T(8,128)S(1)}, f32[128,768]{1,0:T(8,128)S(1)}) custom-call(bf16[768,128]{1,0:T(8,128)(2,1)S(1)} %get-tuple-element.22.refs_0_.q4_ref, bf16[960,256]{1,0:T(8,128)(2,1)S(1)} %join_slots.1.after.own_ref, bf16[960,768]{1,0:T(8,128)(2,1)S(1)} %get-tuple-element.26.p_ref, bf16[768,128]{1,0:T(8,128)(2,1)S(1)} %get-tuple-element.29.g_ref, ...), custom_call_target="tpu_custom_call" | custom-call | flops 1 | bytes 1 | tf_op jit(solution)/shard_map/own_far/pallas_call | solution.py:434
  43.1 0.7 %slice.33 = bf16[192,256]{1,0:T(8,128)(2,1)} slice(f32[384,256]{1,0:T(8,128)S(1)} %convert_add_fusion), slice={[192:384], [0:256]} | slice | bytes 196608 | tf_op jit(solution)/shard_map/slice | solution.py:444
  43.8 1.3 %collective-permute-start.13 = (bf16[192,256]{1,0:T(8,128)(2,1)}, bf16[192,256]{1,0:T(8,128)(2,1)}, u32[]{:S(2)}, u32[]{:S(2)}) collective-permute-start(bf16[192,256]{1,0:T(8,128)(2,1)} %slice.33), channel_id=1, source_target_pairs={{0,16},{8,24},{16,0},{24,8},{32,48},{40,56},{48,32},{56,40},{64,80... | collective-permute-start | bytes 294920 | tf_op jit(solution)/shard_map/ppermute | solution.py:306
  45.8 2.2 %own_near.1 = (f32[576,256]{1,0:T(8,128)S(1)}, bf16[192,512]{1,0:T(8,128)(2,1)}) custom-call(bf16[768,128]{1,0:T(8,128)(2,1)S(1)} %get-tuple-element.22.refs_0_.q4_ref, bf16[960,256]{1,0:T(8,128)(2,1)S(1)} %join_slots.1.after.own_ref, bf16[960,768]{1,0:T(8,128)(2,1)S(1)} %get-tuple-element.26.p_ref, bf16[768,128]{1,0:T(8,128)(2,1)S(1)} %get-tuple-element.29.g_ref, ...), custom_call_target="tpu_custom_call" | custom-call | flops 1 | bytes 1 | tf_op jit(solution)/shard_map/own_near/pallas_call | solution.py:446
  48.0 1.7 %collective-permute-done.13 = bf16[192,256]{1,0:T(8,128)(2,1)} collective-permute-done((bf16[192,256]{1,0:T(8,128)(2,1)}, bf16[192,256]{1,0:T(8,128)(2,1)}, u32[]{:S(2)}, u32[]{:S(2)}) %collective-permute-start.13) | collective-permute-done | bytes 98336 | tf_op jit(solution)/shard_map/ppermute | solution.py:306
  49.7 0.9 %fusion.1.after = bf16[192,256]{1,0:T(8,128)(2,1)S(1)} fusion(bf16[192,256]{1,0:T(8,128)(2,1)} %collective-permute-done.13, f32[384,256]{1,0:T(8,128)S(1)} %copy-done.7, pred[]{:T(512)S(6)} %eq.3), kind=kLoop, calls=%fused_computation.5 | loop fusion | flops 196608 | bytes 393217 | tf_op jit(solution)/shard_map/convert_element_type | solution.py:458
  50.7 1.4 %collective-permute-start.14 = (bf16[192,256]{1,0:T(8,128)(2,1)S(1)}, bf16[192,256]{1,0:T(8,128)(2,1)S(1)}, u32[]{:S(2)}, u32[]{:S(2)}) collective-permute-start(bf16[192,256]{1,0:T(8,128)(2,1)S(1)} %get-tuple-element.40), channel_id=1, source_target_pairs={{0,16},{8,24},{16,0},{24,8},{32,48},{40,56},{48,32},{56,40},{64,80... | collective-permute-start | bytes 294920 | tf_op jit(solution)/shard_map/ppermute | solution.py:306
  52.3 3.3 %collective-permute-done.14 = bf16[192,256]{1,0:T(8,128)(2,1)S(1)} collective-permute-done((bf16[192,256]{1,0:T(8,128)(2,1)S(1)}, bf16[192,256]{1,0:T(8,128)(2,1)S(1)}, u32[]{:S(2)}, u32[]{:S(2)}) %collective-permute-start.14) | collective-permute-done | bytes 98336 | tf_op jit(solution)/shard_map/ppermute | solution.py:306
  55.6 0.9 %fusion.7 = bf16[192,256]{1,0:T(8,128)(2,1)S(1)} fusion(bf16[192,256]{1,0:T(8,128)(2,1)} %collective-permute-done.13, bf16[192,256]{1,0:T(8,128)(2,1)S(1)} %collective-permute-done.14, f32[576,256]{1,0:T(8,128)S(1)} %get-tuple-element.39, pred[]{:T(512)S(6)} %eq.3), kind=kLoop, calls=%fused_computation.11 | loop fusion | flops 245760 | bytes 491521 | tf_op jit(solution)/shard_map/convert_element_type | solution.py:473
  56.5 1.1 %collective-permute-start.15 = (bf16[192,256]{1,0:T(8,128)(2,1)S(1)}, bf16[192,256]{1,0:T(8,128)(2,1)S(1)}, u32[]{:S(2)}, u32[]{:S(2)}) collective-permute-start(bf16[192,256]{1,0:T(8,128)(2,1)S(1)} %fusion.7), channel_id=1, source_target_pairs={{0,224},{8,232},{16,240},{24,248},{32,0},{40,8},{48,16},{56,24},{6... | collective-permute-start | bytes 294920 | tf_op jit(solution)/shard_map/ppermute | solution.py:306
  57.6 2.4 %collective-permute-done.16 = bf16[192,256]{1,0:T(8,128)(2,1)S(1)} collective-permute-done((bf16[192,256]{1,0:T(8,128)(2,1)S(1)}, bf16[192,256]{1,0:T(8,128)(2,1)S(1)}, u32[]{:S(2)}, u32[]{:S(2)}) %collective-permute-start.16) | collective-permute-done | bytes 98336 | tf_op jit(solution)/shard_map/ppermute | solution.py:306
  60.0 1.9 %collective-permute-done.15 = bf16[192,256]{1,0:T(8,128)(2,1)S(1)} collective-permute-done((bf16[192,256]{1,0:T(8,128)(2,1)S(1)}, bf16[192,256]{1,0:T(8,128)(2,1)S(1)}, u32[]{:S(2)}, u32[]{:S(2)}) %collective-permute-start.15) | collective-permute-done | bytes 98336 | tf_op jit(solution)/shard_map/ppermute | solution.py:306
  (37 shorter events, 4.2 us)
Async XLA Ops:
  0.6 18.4 %collective-permute-start.5 = (bf16[192,512]{1,0:T(8,128)(2,1)}, bf16[192,512]{1,0:T(8,128)(2,1)S(1)}, u32[]{:S(2)}, u32[]{:S(2)}) collective-permute-start(bf16[192,512]{1,0:T(8,128)(2,1)} %a_ref.1), channel_id=1, source_target_pairs={{0,1},{1,0},{2,3},{3,2},{4,5},{5,4},{6,7},{7,6},{8,9},{9,8},{10,11... | collective-permute-start | bytes 589832 | tf_op jit(solution)/shard_map/ppermute | solution.py:306
  4.7 13.5 %collective-permute-start = (bf16[192,256]{1,0:T(8,128)(2,1)S(1)}, bf16[192,256]{1,0:T(8,128)(2,1)S(1)}, u32[]{:S(2)}, u32[]{:S(2)}) collective-permute-start(bf16[192,256]{1,0:T(8,128)(2,1)S(1)} %pad_add_fusion.z0_ref), channel_id=1, source_target_pairs={{0,64},{8,72},{16,80},{24,88},{32,96},{40,104},{48,112},{56,120},{... | collective-permute-start | bytes 294920 | tf_op jit(solution)/shard_map/ppermute | solution.py:306
  9.3 8.9 %collective-permute-start.1 = (bf16[192,256]{1,0:T(8,128)(2,1)S(1)}, bf16[192,256]{1,0:T(8,128)(2,1)S(1)}, u32[]{:S(2)}, u32[]{:S(2)}) collective-permute-start(bf16[192,256]{1,0:T(8,128)(2,1)S(1)} %pad_add_fusion.z0_ref), channel_id=1, source_target_pairs={{0,32},{8,40},{16,48},{24,56},{32,64},{40,72},{48,80},{56,88},{64,... | collective-permute-start | bytes 294920 | tf_op jit(solution)/shard_map/ppermute | solution.py:306
  10.3 10.7 %collective-permute-start.3 = (bf16[192,512]{1,0:T(8,128)(2,1)}, bf16[192,512]{1,0:T(8,128)(2,1)S(1)}, u32[]{:S(2)}, u32[]{:S(2)}) collective-permute-start(bf16[192,512]{1,0:T(8,128)(2,1)} %a_ref.1), channel_id=1, source_target_pairs={{0,2},{1,3},{2,4},{3,5},{4,6},{5,7},{6,0},{7,1},{8,10},{9,11},{10,... | collective-permute-start | bytes 589832 | tf_op jit(solution)/shard_map/ppermute | solution.py:306
  11.8 9.3 %collective-permute-start.4 = (bf16[192,512]{1,0:T(8,128)(2,1)}, bf16[192,512]{1,0:T(8,128)(2,1)S(1)}, u32[]{:S(2)}, u32[]{:S(2)}) collective-permute-start(bf16[192,512]{1,0:T(8,128)(2,1)} %a_ref.1), channel_id=1, source_target_pairs={{0,6},{1,7},{2,0},{3,1},{4,2},{5,3},{6,4},{7,5},{8,14},{9,15},{10,... | collective-permute-start | bytes 589832 | tf_op jit(solution)/shard_map/ppermute | solution.py:306
  13.6 2.2 %copy-start = (bf16[512,4096]{1,0:T(8,128)(2,1)S(1)}, bf16[512,4096]{1,0:T(8,128)(2,1)}, u32[]{:S(2)}) copy-start(bf16[512,4096]{1,0:T(8,128)(2,1)} %w_ref.5) | copy-start | bytes 12582916
  15.8 0.9 %copy-start.3 = (bf16[192,512]{1,0:T(8,128)(2,1)S(1)}, bf16[192,512]{1,0:T(8,128)(2,1)}, u32[]{:S(2)}) copy-start(bf16[192,512]{1,0:T(8,128)(2,1)} %a_ref.1) | copy-start | bytes 589828
  16.7 0.9 %copy-start.4 = (bf16[192,512]{1,0:T(8,128)(2,1)S(1)}, bf16[192,512]{1,0:T(8,128)(2,1)}, u32[]{:S(2)}) copy-start(bf16[192,512]{1,0:T(8,128)(2,1)} %q_ref.1) | copy-start | bytes 589828
  16.7 0.9 %copy-start.5 = (s32[8]{0:T(128)S(1)}, s32[8]{0:T(128)}, u32[]{:S(2)}) copy-start(s32[8]{0:T(128)} %len_ref.1) | copy-start | bytes 100
  18.3 5.8 %collective-permute-start.2 = (bf16[384,256]{1,0:T(8,128)(2,1)S(1)}, bf16[384,256]{1,0:T(8,128)(2,1)S(1)}, u32[]{:S(2)}, u32[]{:S(2)}) collective-permute-start(bf16[384,256]{1,0:T(8,128)(2,1)S(1)} %pick_side.1.refs_0_), channel_id=1, source_target_pairs={{0,16},{8,24},{16,0},{24,8},{32,48},{40,56},{48,32},{56,40},{64,80... | collective-permute-start | bytes 589832 | tf_op jit(solution)/shard_map/ppermute | solution.py:306
  19.0 5.7 %collective-permute-start.7 = (bf16[192,512]{1,0:T(8,128)(2,1)S(1)}, bf16[192,512]{1,0:T(8,128)(2,1)S(1)}, u32[]{:S(2)}, u32[]{:S(2)}) collective-permute-start(bf16[192,512]{1,0:T(8,128)(2,1)S(1)} %collective-permute-done.5.b_ref), channel_id=1, source_target_pairs={{0,6},{1,7},{2,0},{3,1},{4,2},{5,3},{6,4},{7,5},{8,14},{9,15},{10,... | collective-permute-start | bytes 589832 | tf_op jit(solution)/shard_map/ppermute | solution.py:306
  20.6 6.9 %collective-permute-start.6 = (bf16[192,512]{1,0:T(8,128)(2,1)S(1)}, bf16[192,512]{1,0:T(8,128)(2,1)S(1)}, u32[]{:S(2)}, u32[]{:S(2)}) collective-permute-start(bf16[192,512]{1,0:T(8,128)(2,1)S(1)} %collective-permute-done.5.b_ref), channel_id=1, source_target_pairs={{0,2},{1,3},{2,4},{3,5},{4,6},{5,7},{6,0},{7,1},{8,10},{9,11},{10,... | collective-permute-start | bytes 589832 | tf_op jit(solution)/shard_map/ppermute | solution.py:306
  27.5 6.6 %collective-permute-start.8 = (bf16[960,256]{1,0:T(8,128)(2,1)S(1)}, bf16[960,256]{1,0:T(8,128)(2,1)S(1)}, u32[]{:S(2)}, u32[]{:S(2)}) collective-permute-start(bf16[960,256]{1,0:T(8,128)(2,1)S(1)} %join_slots.1.after.own_ref), channel_id=1, source_target_pairs={{0,8},{8,0},{16,24},{24,16},{32,40},{40,32},{48,56},{56,48},{64,72... | collective-permute-start | bytes 1474568 | tf_op jit(solution)/shard_map/ppermute | solution.py:306
  27.6 11.6 %collective-permute-start.9 = (bf16[192,512]{1,0:T(8,128)(2,1)S(1)}, bf16[192,512]{1,0:T(8,128)(2,1)S(1)}, u32[]{:S(2)}, u32[]{:S(2)}) collective-permute-start(bf16[192,512]{1,0:T(8,128)(2,1)S(1)} %collective-permute-done.3.refs_1_.c_ref), channel_id=1, source_target_pairs={{0,2},{1,3},{2,4},{3,5},{4,6},{5,7},{6,0},{7,1},{8,10},{9,11},{10,... | collective-permute-start | bytes 589832 | tf_op jit(solution)/shard_map/ppermute | solution.py:306
  27.7 11.5 %collective-permute-start.10 = (bf16[192,512]{1,0:T(8,128)(2,1)S(1)}, bf16[192,512]{1,0:T(8,128)(2,1)S(1)}, u32[]{:S(2)}, u32[]{:S(2)}) collective-permute-start(bf16[192,512]{1,0:T(8,128)(2,1)S(1)} %collective-permute-done.7.refs_2_.f_ref), channel_id=1, source_target_pairs={{0,6},{1,7},{2,0},{3,1},{4,2},{5,3},{6,4},{7,5},{8,14},{9,15},{10,... | collective-permute-start | bytes 589832 | tf_op jit(solution)/shard_map/ppermute | solution.py:306
  30.9 2.2 %copy-start.1 = (bf16[512,4096]{1,0:T(8,128)(2,1)S(1)}, bf16[512,4096]{1,0:T(8,128)(2,1)}, u32[]{:S(2)}) copy-start(bf16[512,4096]{1,0:T(8,128)(2,1)} %w_ref.5) | copy-start | bytes 12582916
  33.1 6.1 %copy-start.2 = (bf16[512,4096]{1,0:T(8,128)(2,1)S(1)}, bf16[512,4096]{1,0:T(8,128)(2,1)}, u32[]{:S(2)}) copy-start(bf16[512,4096]{1,0:T(8,128)(2,1)} %w_ref.5) | copy-start | bytes 12582916
  40.8 2.2 %collective-permute-start.11 = (bf16[384,256]{1,0:T(8,128)(2,1)S(1)}, bf16[384,256]{1,0:T(8,128)(2,1)S(1)}, u32[]{:S(2)}, u32[]{:S(2)}) collective-permute-start(bf16[384,256]{1,0:T(8,128)(2,1)S(1)} %get-tuple-element.34), channel_id=1, source_target_pairs={{0,8},{8,0},{16,24},{24,16},{32,40},{40,32},{48,56},{56,48},{64,72... | collective-permute-start | bytes 589832 | tf_op jit(solution)/shard_map/ppermute | solution.py:306
  43.1 2.1 %copy-start.6 = (f32[384,256]{1,0:T(8,128)}, f32[384,256]{1,0:T(8,128)S(1)}, u32[]{:S(2)}) copy-start(f32[384,256]{1,0:T(8,128)S(1)} %convert_add_fusion) | copy-start | bytes 1179652
  43.8 5.9 %collective-permute-start.13 = (bf16[192,256]{1,0:T(8,128)(2,1)}, bf16[192,256]{1,0:T(8,128)(2,1)}, u32[]{:S(2)}, u32[]{:S(2)}) collective-permute-start(bf16[192,256]{1,0:T(8,128)(2,1)} %slice.33), channel_id=1, source_target_pairs={{0,16},{8,24},{16,0},{24,8},{32,48},{40,56},{48,32},{56,40},{64,80... | collective-permute-start | bytes 294920 | tf_op jit(solution)/shard_map/ppermute | solution.py:306
  45.1 5.5 %collective-permute-start.12 = (bf16[576,256]{1,0:T(8,128)(2,1)S(1)}, bf16[576,256]{1,0:T(8,128)(2,1)S(1)}, u32[]{:S(2)}, u32[]{:S(2)}) collective-permute-start(bf16[576,256]{1,0:T(8,128)(2,1)S(1)} %get-tuple-element.37), channel_id=1, source_target_pairs={{0,8},{8,0},{16,24},{24,16},{32,40},{40,32},{48,56},{56,48},{64,72... | collective-permute-start | bytes 884744 | tf_op jit(solution)/shard_map/ppermute | solution.py:306
  45.8 4.0 %copy-start.7 = (f32[384,256]{1,0:T(8,128)S(1)}, f32[384,256]{1,0:T(8,128)}, u32[]{:S(2)}) copy-start(f32[384,256]{1,0:T(8,128)} %copy-done.6) | copy-start | bytes 1179652
  50.7 4.9 %collective-permute-start.14 = (bf16[192,256]{1,0:T(8,128)(2,1)S(1)}, bf16[192,256]{1,0:T(8,128)(2,1)S(1)}, u32[]{:S(2)}, u32[]{:S(2)}) collective-permute-start(bf16[192,256]{1,0:T(8,128)(2,1)S(1)} %get-tuple-element.40), channel_id=1, source_target_pairs={{0,16},{8,24},{16,0},{24,8},{32,48},{40,56},{48,32},{56,40},{64,80... | collective-permute-start | bytes 294920 | tf_op jit(solution)/shard_map/ppermute | solution.py:306
  52.2 7.8 %collective-permute-start.16 = (bf16[192,256]{1,0:T(8,128)(2,1)S(1)}, bf16[192,256]{1,0:T(8,128)(2,1)S(1)}, u32[]{:S(2)}, u32[]{:S(2)}) collective-permute-start(bf16[192,256]{1,0:T(8,128)(2,1)S(1)} %fusion.1.after), channel_id=1, source_target_pairs={{0,192},{8,200},{16,208},{24,216},{32,224},{40,232},{48,240},{56,2... | collective-permute-start | bytes 294920 | tf_op jit(solution)/shard_map/ppermute | solution.py:306
  56.5 5.4 %collective-permute-start.15 = (bf16[192,256]{1,0:T(8,128)(2,1)S(1)}, bf16[192,256]{1,0:T(8,128)(2,1)S(1)}, u32[]{:S(2)}, u32[]{:S(2)}) collective-permute-start(bf16[192,256]{1,0:T(8,128)(2,1)S(1)} %fusion.7), channel_id=1, source_target_pairs={{0,224},{8,232},{16,240},{24,248},{32,0},{40,8},{48,16},{56,24},{6... | collective-permute-start | bytes 294920 | tf_op jit(solution)/shard_map/ppermute | solution.py:306

commit v4 on v3

v4 whole, which is shorter than its diff:
```python
import functools

import jax
import jax.numpy as jnp
from jax import lax
from jax.experimental import pallas as pl
from jax.experimental.pallas import tpu as pltpu
from jax.sharding import PartitionSpec as P

D = 128
HEADS = 4
ROWS = 192
LANES = HEADS * ROWS
REACH = 4
SLOTS = REACH + 1
PLANE = 4
BLOCK = 512
NEG = -1e30
FLOOR = -1e20
SCALE = D**-0.5
LOG2E = 1.4426950408889634
MIB = 1 << 20


def dot(a, b, ca, cb):
    return lax.dot_general(a, b, (((ca,), (cb,)), ((), ())), preferred_element_type=jnp.float32)


def stack_heads(src, dst):
    for h in range(HEADS):
        dst[h * ROWS : (h + 1) * ROWS, :] = src[:, h * D : (h + 1) * D]


def prepare(place_ref, len_hbm, q_hbm, q4_ref, bound_ref, len_ref, sems):
    copies = [pltpu.make_async_copy(len_hbm, len_ref, sems.at[0])]
    for h in range(HEADS):
        rows, cols = pl.ds(h * ROWS, ROWS), pl.ds(h * D, D)
        copies.append(pltpu.make_async_copy(q_hbm.at[:, cols], q4_ref.at[rows, :], sems.at[1 + h]))
    for copy in copies:
        copy.start()
    lane = lax.broadcasted_iota(jnp.int32, (1, LANES), 1)
    pos = lane + place_ref[0] * ROWS
    for h in range(1, HEADS):
        pos = pos - jnp.where(lane >= h * ROWS, ROWS, 0)
    start = jnp.zeros((1, LANES), jnp.int32)
    end = jnp.int32(0)
    copies[0].wait()
    for d in range(len_ref.shape[0]):
        end = end + len_ref[d]
        start = jnp.where(end <= pos, end, start)
    bound_ref[0:1, :] = pos
    bound_ref[1:2, :] = start
    for copy in copies[1:]:
        copy.wait()


def pick_kernel(place_ref, z2_ref, z1_ref, z0_ref, *refs):
    out_ref = refs[-1]
    upper = lax.rem(lax.div(place_ref[0], 2), 2) == 1

    @pl.when(upper)
    def _():
        out_ref[:ROWS, :] = z2_ref[...]
        out_ref[ROWS:, :] = z1_ref[...]

    @pl.when(jnp.logical_not(upper))
    def _():
        out_ref[:ROWS, :] = z1_ref[...]
        out_ref[ROWS:, :] = z0_ref[...]


def join_kernel(z2_ref, z1_ref, z0_ref, side_ref, *refs):
    out_ref = refs[-1]
    parts = (z2_ref[...], side_ref[:ROWS, :], z1_ref[...], side_ref[ROWS:, :], z0_ref[...])
    for m, part in enumerate(parts):
        out_ref[m * ROWS : (m + 1) * ROWS, :] = part


def score(kv, queries, row, base, bound_ref, diagonal):
    s = dot(kv[:, :D], queries, 1, 1) * (SCALE * LOG2E)
    key = row + base * ROWS
    visible = key >= bound_ref[1:2, :]
    if diagonal:
        visible = visible & (key <= bound_ref[0:1, :])
    return jnp.where(visible, s, NEG)


def online(s, state):
    top, total = state
    new = jnp.maximum(top, jnp.max(s, axis=0, keepdims=True))
    total = total * jnp.exp2(top - new) + jnp.sum(jnp.exp2(s - new), axis=0, keepdims=True)
    return new, total


def near_kernel(place_ref, z2_ref, z1_ref, z0_ref, q4_ref, bound_ref, *refs):
    s_ref, stat_ref = refs[-2:]
    me = place_ref[0]
    queries = q4_ref[...]
    row = lax.broadcasted_iota(jnp.int32, (ROWS, LANES), 0)
    s = score(z0_ref[...], queries, row, me, bound_ref, True)
    s_ref[2 * ROWS :, :] = s
    top = jnp.max(s, axis=0, keepdims=True)
    state = (top, jnp.sum(jnp.exp2(s - top), axis=0, keepdims=True))
    for i, ref in ((1, z1_ref), (0, z2_ref)):
        s = score(ref[...], queries, row, me - PLANE * (2 - i), bound_ref, False)
        s_ref[i * ROWS : (i + 1) * ROWS, :] = s
        state = online(s, state)
    stat_ref[0:1, :] = state[0]
    stat_ref[1:2, :] = state[1]


def rows(i):
    return pl.ds(pl.multiple_of(i * ROWS, ROWS), ROWS)


def close(state):
    top, total = state
    return top + jnp.log2(jnp.maximum(total, 1e-30))


def weigh(s, log_total, values, state):
    acc, mass = state
    prob = jnp.exp2(s - log_total).astype(jnp.bfloat16)
    acc = acc + dot(values, prob, 0, 0)
    mass = mass + jnp.sum(prob.astype(jnp.float32), axis=0, keepdims=True)
    return prob, (acc, mass)


def no_weight():
    return jnp.zeros((D, LANES), jnp.float32), jnp.zeros((1, LANES), jnp.float32)


def project(acc, pieces, sources, w_ref):
    for piece, source in zip(pieces, sources):
        part = dot(piece[...], w_ref[:, pl.ds(pl.multiple_of(source * BLOCK, BLOCK), BLOCK)], 1, 1)
        acc = part if acc is None else acc + part
    return acc


def source_of(head, by, flip):
    at = lax.rem(head + by + 8, 8)
    return at + 1 - 2 * lax.rem(at, 2) if flip else at


def middle_kernel(place_ref, head_ref, own_ref, q4_ref, bound_ref, s_ref, stat_ref, g_hbm, w_hbm, y_ref, r_ref, l_ref, or_ref, ol_ref, p_ref, o_ref, log_ref, acc_ref, tail_ref, s_side, g_ref, w_ref, sems):
    head = head_ref[0]
    tails = (source_of(head, 4, False), source_of(head, 4, True))
    copies = [pltpu.make_async_copy(w_hbm, w_ref, sems.at[0]), pltpu.make_async_copy(g_hbm, g_ref, sems.at[1])]
    for i, source in enumerate(tails):
        cols = pl.ds(pl.multiple_of(source * BLOCK, BLOCK), BLOCK)
        copies.append(pltpu.make_async_copy(w_hbm.at[:, cols], tail_ref.at[:, pl.ds(i * BLOCK, BLOCK)], sems.at[2 + i]))
    for copy in copies:
        copy.start()

    queries = q4_ref[...]
    row = lax.broadcasted_iota(jnp.int32, (ROWS, LANES), 0)

    def side(i, state):
        slot = 2 * i + 1
        s = score(own_ref[rows(slot), :], queries, row, place_ref[0] + 2 * (slot - REACH), bound_ref, False)
        s_side[rows(i), :] = s
        return online(s, state)

    log_total = close(lax.fori_loop(0, 2, side, (stat_ref[0:1, :], stat_ref[1:2, :])))
    log_ref[0:1, :] = log_total

    def weigh_main(i, state):
        prob, state = weigh(s_ref[rows(i), :], log_total, own_ref[rows(2 * i), D:], state)
        p_ref[rows(2 * i), :] = prob
        return state

    def weigh_side(i, state):
        prob, state = weigh(s_side[rows(i), :], log_total, own_ref[rows(2 * i + 1), D:], state)
        p_ref[rows(2 * i + 1), :] = prob
        return state

    acc, mass = lax.fori_loop(0, 2, weigh_side, lax.fori_loop(0, 3, weigh_main, no_weight()))
    o_ref[...] = acc / mass
    for copy in copies:
        copy.wait()
    sources = (head, source_of(head, 0, True), source_of(head, -2, False), source_of(head, 2, False))
    sources += (source_of(head, -2, True), source_of(head, 2, True))
    acc_ref[...] = project(None, (g_ref, y_ref, r_ref, l_ref, or_ref, ol_ref), sources, w_ref)


def across_kernel(place_ref, par_ref, q4_ref, bound_ref, o_own_ref, log_ref, p_ref, o_ref, f_ref, s_par):
    me = place_ref[0]
    core = lax.rem(me, 2)
    chip = me - core
    queries = q4_ref[...]
    row = lax.broadcasted_iota(jnp.int32, (ROWS, LANES), 0)

    def across(i, state):
        slot = i + core
        s = score(par_ref[rows(slot), :], queries, row, chip + 1 - core + 2 * (slot - REACH), bound_ref, False)
        s_par[rows(i), :] = s
        return online(s, state)

    state = (jnp.full((1, LANES), FLOOR, jnp.float32), jnp.zeros((1, LANES), jnp.float32))
    log_par = close(lax.fori_loop(0, REACH, across, state))

    def weigh_across(i, state):
        prob, state = weigh(s_par[rows(i), :], log_par, par_ref[rows(i + core), D:], state)
        p_ref[rows(i), :] = prob
        return state

    acc, mass = lax.fori_loop(0, REACH, weigh_across, no_weight())
    log_own = log_ref[0:1, :]
    top = jnp.maximum(log_own, log_par)
    own, par = jnp.exp2(log_own - top), jnp.exp2(log_par - top)
    both = own + par
    own, par = own / both, par / both
    f_ref[0:1, :] = own
    f_ref[1:2, :] = par
    o_ref[...] = o_own_ref[...] * own + acc * (par / jnp.maximum(mass, 0.5))


def back_block(kv_ref, slot, p_ref, i, g4, q4, rd, share):
    prob = p_ref[rows(i), :].astype(jnp.float32) * share
    dprob = dot(kv_ref[rows(slot), D:], g4, 1, 1)
    ds = (prob * (dprob - rd)).astype(jnp.bfloat16)
    dv = dot(prob.astype(jnp.bfloat16), g4, 1, 0)
    dk = dot(ds, q4, 1, 0) * SCALE
    dq = dot(kv_ref[rows(slot), :D], ds, 0, 0)
    return dk, dv, dq


def put(out_ref, slot, dk, dv):
    at = pl.ds(pl.multiple_of(slot * ROWS, ROWS), ROWS)
    out_ref[at, :D] = dk.astype(out_ref.dtype)
    out_ref[at, D:] = dv.astype(out_ref.dtype)


def cross_far(place_ref, a_ref, b_ref, early_ref, w_ref, q4_ref, par_ref, p_ref, o_ref, f_ref, out_ref, g_ref, rd_ref, dq_ref):
    core = lax.rem(place_ref[0], 2)
    acc = project(early_ref[...], (a_ref, b_ref), (0, 1), w_ref)
    acc = acc.astype(jnp.bfloat16)
    for h in range(HEADS):
        g_ref[h * ROWS : (h + 1) * ROWS, :] = acc[:, h * D : (h + 1) * D]
    g4 = g_ref[...]
    gt = jnp.transpose(g4.astype(jnp.float32))
    rd = jnp.sum(gt * o_ref[...], axis=0, keepdims=True)
    rd_ref[...] = rd
    dq_ref[...] = jnp.zeros((D, LANES), jnp.float32)

    @pl.when(core == 1)
    def _():
        out_ref[:ROWS, :] = jnp.zeros((ROWS, 2 * D), out_ref.dtype)

    def step(slot, _):
        dk, dv, dq = back_block(par_ref, slot, p_ref, slot - core, g4, q4_ref[...], rd, f_ref[1:2, :])
        put(out_ref, slot, dk, dv)
        dq_ref[...] += dq
        return 0

    lax.fori_loop(core, 2, step, 0)


def cross_near(place_ref, q4_ref, par_ref, p_ref, g_ref, rd_ref, f_ref, dq_in_ref, out_ref, dq_ref):
    core = lax.rem(place_ref[0], 2)
    g4 = g_ref[...]
    rd = rd_ref[...]
    dq_ref[...] = dq_in_ref[...]

    @pl.when(core == 0)
    def _():
        out_ref[2 * ROWS :, :] = jnp.zeros((ROWS, 2 * D), out_ref.dtype)

    def step(slot, _):
        dk, dv, dq = back_block(par_ref, slot, p_ref, slot - core, g4, q4_ref[...], rd, f_ref[1:2, :])
        put(out_ref, slot - 2, dk, dv)
        dq_ref[...] += dq
        return 0

    lax.fori_loop(2, REACH + core, step, 0)


def own_far(q4_ref, own_ref, p_ref, g_ref, rd_ref, f_ref, dq_in_ref, out_ref, dq_ref):
    g4 = g_ref[...]
    rd = rd_ref[...]
    dq_ref[...] = dq_in_ref[...]

    def step(slot, _):
        dk, dv, dq = back_block(own_ref, slot, p_ref, slot, g4, q4_ref[...], rd, f_ref[0:1, :])
        put(out_ref, slot, dk, dv)
        dq_ref[...] += dq
        return 0

    lax.fori_loop(0, 2, step, 0)


def own_near(q4_ref, own_ref, p_ref, g_ref, rd_ref, f_ref, dq_in_ref, after, out_ref, dq_out_ref, acc):
    g4 = g_ref[...]
    rd = rd_ref[...]
    acc[...] = dq_in_ref[...]

    def step(slot, _):
        dk, dv, dq = back_block(own_ref, slot, p_ref, slot, g4, q4_ref[...], rd, f_ref[0:1, :])
        put(out_ref, slot - 2, dk, dv)
        acc[...] += dq
        return 0

    lax.fori_loop(2, SLOTS, step, 0)
    dq = jnp.transpose(acc[...]) * SCALE
    for h in range(HEADS):
        dq_out_ref[:, h * D : (h + 1) * D] = dq[h * ROWS : (h + 1) * ROWS, :].astype(jnp.bfloat16)


def is_upper(place_ref):
    return (lax.rem(lax.div(place_ref[0], 2), 2) == 1).astype(jnp.float32)


def settle_far(own_ref, back_ref, keep_ref, side_ref):
    both = own_ref[...] + back_ref[...].astype(jnp.float32)
    keep_ref[...] = both[:ROWS]
    side_ref[...] = both[ROWS:].astype(jnp.bfloat16)


def relay_far(place_ref, keep_ref, side_ref, out_ref):
    out_ref[...] = (keep_ref[...] + side_ref[...].astype(jnp.float32) * is_upper(place_ref)).astype(jnp.bfloat16)


def settle_near(own_ref, back_ref, after, both_ref, side_ref):
    both = own_ref[...] + back_ref[...].astype(jnp.float32)
    both_ref[...] = both
    side_ref[...] = both[ROWS : 2 * ROWS].astype(jnp.bfloat16)


def relay_near(place_ref, both_ref, near_ref, far_ref, out_ref, keep_ref):
    upper = is_upper(place_ref)
    near, far = near_ref[...].astype(jnp.float32), far_ref[...].astype(jnp.float32)
    out_ref[...] = (both_ref[:ROWS, :] + near * upper + far * (1 - upper)).astype(jnp.bfloat16)
    keep_ref[...] = both_ref[2 * ROWS :, :] + near * (1 - upper)


def vmem(n):
    return [pl.BlockSpec(memory_space=pltpu.VMEM)] * n


def smem(n):
    return [pl.BlockSpec(memory_space=pltpu.SMEM)] * n


def hbm(n):
    return [pl.BlockSpec(memory_space=pltpu.HBM)] * n


def token(n):
    return [pl.BlockSpec(memory_space=pl.ANY)] * n


def params(mib):
    return pltpu.CompilerParams(vmem_limit_bytes=mib * MIB)


def moved(x, axis, to):
    return lax.ppermute(x, axis, [(i, to(i)) for i in range(lax.axis_size(axis))])


def turned(x, axis, by):
    count = lax.axis_size(axis)
    return moved(x, axis, lambda i: (i + by) % count)


def shape(rows, cols, dtype):
    return jax.ShapeDtypeStruct((rows, cols), dtype)


def call(name, kernel, outs, ins, mib, args, scratch=()):
    one = not isinstance(outs, tuple)
    return pl.pallas_call(
        kernel,
        out_shape=outs,
        in_specs=ins,
        out_specs=vmem(1)[0] if one else tuple(vmem(len(outs))),
        scratch_shapes=list(scratch),
        compiler_params=params(mib),
        cost_estimate=pl.CostEstimate(flops=1, bytes_accessed=1, transcendentals=0),
        name=name,
    )(*args)


def local(queries, keys, values, grad_out, out_weight, lengths):
    bf16, f32 = jnp.bfloat16, jnp.float32
    place = lax.axis_index("ctx").astype(jnp.int32).reshape(1)
    head = lax.axis_index("head").astype(jnp.int32).reshape(1)
    dma = pltpu.SemaphoreType.DMA
    pinned = functools.partial(pltpu.with_memory_space_constraint, memory_space=pltpu.HBM)

    other = moved(grad_out, "head", lambda i: i ^ 1)
    right = turned(grad_out, "head", 2)
    left = turned(grad_out, "head", -2)
    kv = jnp.pad(keys, ((0, 0), (0, D))) + jnp.pad(values, ((0, 0), (D, 0)))
    z2 = turned(kv, "ctx", 2 * PLANE)
    z1 = turned(kv, "ctx", PLANE)
    other_right = turned(other, "head", 2)
    other_left = turned(other, "head", -2)
    far = turned(right, "head", 2)
    other_far = turned(other_left, "head", -2)

    q4, bound = call(
        "prepare",
        prepare,
        (shape(LANES, D, bf16), shape(8, LANES, jnp.int32)),
        smem(1) + hbm(2),
        4,
        (place, pinned(lengths), pinned(queries)),
        [pltpu.SMEM((lengths.shape[0],), jnp.int32), dma((1 + HEADS,))],
    )
    picked = call("pick_side", pick_kernel, shape(2 * ROWS, 2 * D, bf16), smem(1) + vmem(3) + token(1), 4, (place, z2, z1, kv, q4))
    side = moved(picked, "ctx", lambda i: i ^ 2)
    s_near, stat = call(
        "near_scores",
        near_kernel,
        (shape(3 * ROWS, LANES, f32), shape(8, LANES, f32)),
        smem(1) + vmem(5) + token(4),
        8,
        (place, z2, z1, kv, q4, bound, picked, other, right, left),
    )
    own = call("join_slots", join_kernel, shape(SLOTS * ROWS, 2 * D, bf16), vmem(4) + token(3), 4, (z2, z1, kv, side, stat, other_right, other_left))
    par = moved(own, "ctx", lambda i: i ^ 1)

    p_own, o_own, log_own, early, tail = call(
        "middle",
        middle_kernel,
        (
            shape(SLOTS * ROWS, LANES, bf16),
            shape(D, LANES, f32),
            shape(8, LANES, f32),
            shape(ROWS, HEADS * D, f32),
            shape(HEADS * D, 2 * BLOCK, bf16),
        ),
        smem(2) + vmem(5) + hbm(2) + vmem(5),
        16,
        (place, head, own, q4, bound, s_near, stat, pinned(grad_out), pinned(out_weight), other, right, left, other_right, other_left),
        [
            pltpu.VMEM((2 * ROWS, LANES), f32),
            pltpu.VMEM((ROWS, BLOCK), bf16),
            pltpu.VMEM((HEADS * D, 8 * BLOCK), bf16),
            dma((4,)),
        ],
    )
    p_par, out_t, share = call(
        "across",
        across_kernel,
        (shape(REACH * ROWS, LANES, bf16), shape(D, LANES, f32), shape(8, LANES, f32)),
        smem(1) + vmem(5),
        12,
        (place, par, q4, bound, o_own, log_own),
        [pltpu.VMEM((REACH * ROWS, LANES), f32)],
    )

    far_cross, g4, rd, dq = call(
        "cross_far",
        cross_far,
        (shape(2 * ROWS, 2 * D, bf16), shape(LANES, D, bf16), shape(1, LANES, f32), shape(D, LANES, f32)),
        smem(1) + vmem(9),
        10,
        (place, far, other_far, early, tail, q4, par, p_par, out_t, share),
    )
    far_back = moved(far_cross, "ctx", lambda i: i ^ 1)
    near_cross, dq = call(
        "cross_near",
        cross_near,
        (shape(3 * ROWS, 2 * D, bf16), shape(D, LANES, f32)),
        smem(1) + vmem(7),
        10,
        (place, q4, par, p_par, g4, rd, share, dq),
    )
    near_back = moved(near_cross, "ctx", lambda i: i ^ 1)
    far_own, dq = call(
        "own_far",
        own_far,
        (shape(2 * ROWS, 2 * D, f32), shape(D, LANES, f32)),
        vmem(7),
        10,
        (q4, own, p_own, g4, rd, share, dq),
    )
    far_keep, far_side = call(
        "settle_far", settle_far, (shape(ROWS, 2 * D, f32), shape(ROWS, 2 * D, bf16)), vmem(2), 4, (far_own, far_back)
    )
    far_side = moved(far_side, "ctx", lambda i: i ^ 2)
    near_own, grad_queries = call(
        "own_near",
        own_near,
        (shape(3 * ROWS, 2 * D, f32), shape(ROWS, HEADS * D, bf16)),
        vmem(7) + token(1),
        10,
        (q4, own, p_own, g4, rd, share, dq, far_keep),
        [pltpu.VMEM((D, LANES), f32)],
    )
    to_two = call("relay_far", relay_far, shape(ROWS, 2 * D, bf16), smem(1) + vmem(2), 4, (place, far_keep, far_side))
    got_two = turned(to_two, "ctx", -2 * PLANE)
    near_both, near_side = call(
        "settle_near",
        settle_near,
        (shape(3 * ROWS, 2 * D, f32), shape(ROWS, 2 * D, bf16)),
        vmem(2) + token(1),
        4,
        (near_own, near_back, to_two),
    )
    near_side = moved(near_side, "ctx", lambda i: i ^ 2)
    to_one, keep = call(
        "relay_near",
        relay_near,
        (shape(ROWS, 2 * D, bf16), shape(ROWS, 2 * D, f32)),
        smem(1) + vmem(3),
        4,
        (place, near_both, near_side, far_side),
    )
    got_one = turned(to_one, "ctx", -PLANE)
    total = (keep + got_one.astype(f32) + got_two.astype(f32)).astype(bf16)
    return grad_queries, total[:, :D], total[:, D:]


def solution(mesh):
    return jax.shard_map(
        local,
        mesh=mesh,
        in_specs=(
            P("ctx", "head"),
            P("ctx", "head"),
            P("ctx", "head"),
            P("ctx", "head"),
            P("head", None),
            P(),
        ),
        out_specs=(P("ctx", "head"), P("ctx", "head"), P("ctx", "head")),
        check_vma=False,
    )
```

time: 63.1 us -> 61.5 us (0.975)
  the two profiles are of different devices: /device:TPU:64 before, /device:TPU:1 now
where the time goes in v4:
time: 61.5 us; the launch traced here: 61.1 us
  starting transfers between devices  26.5 us (43%)
  Pallas kernels  16.2 us (26%)
  waiting for transfers between devices  12.9 us (21%)
  local copies, waits for them, and re-layouts  3.73 us (6%)
  other arithmetic  0.87 us (1%)
  between operations  0.82 us (1%)
    ppermute x17, starting transfers between devices, moved(): lax.ppermute(x, axis, [(i, to(i)) for i in range(lax.axis_size(axis))])  26.5 us
    pallas_call x14, Pallas kernels, call(): pl.pallas_call(kernel, out_shape=outs, in_specs=ins, out_specs=vmem(1)[0]...  16.2 us
    ppermute x17, waiting for transfers between devices, moved(): lax.ppermute(x, axis, [(i, to(i)) for i in range(lax.axis_size(axis))])  12.9 us
    unnamed x12, local copies, waits for them, and re-layouts  3.08 us
  transfers between devices with their start and end apart: 17, of which 7 were waited for; matrix products, arithmetic and copies ran while one was open for 1% of the time, Pallas kernels for 23%

profile of v4, /device:TPU:1, one launch (start us, length us, event | category | flops | bytes accessed | tf_op | source)
XLA Modules:
  0.0 61.1 jit_solution(6922283749227700190)
XLA Ops:
  0.6 3.8 %collective-permute-start.3 = (bf16[192,512]{1,0:T(8,128)(2,1)}, bf16[192,512]{1,0:T(8,128)(2,1)S(1)}, u32[]{:S(2)}, u32[]{:S(2)}) collective-permute-start(bf16[192,512]{1,0:T(8,128)(2,1)} %g_hbm.1), channel_id=1, source_target_pairs={{0,1},{1,0},{2,3},{3,2},{4,5},{5,4},{6,7},{7,6},{8,9},{9,8},{10,11... | collective-permute-start | bytes 589832 | tf_op jit(solution)/shard_map/ppermute | solution.py:357
  4.5 0.8 %pad_add_fusion.z0_ref = bf16[192,256]{1,0:T(8,128)(2,1)S(1)} fusion(bf16[192,128]{1,0:T(8,128)(2,1)} %param.8, bf16[192,128]{1,0:T(8,128)(2,1)} %param.7), kind=kLoop, calls=%fused_computation.1 | loop fusion | flops 196608 | bytes 196608 | tf_op jit(solution)/shard_map/add | solution.py:393
  5.3 3.1 %collective-permute-start = (bf16[192,256]{1,0:T(8,128)(2,1)S(1)}, bf16[192,256]{1,0:T(8,128)(2,1)S(1)}, u32[]{:S(2)}, u32[]{:S(2)}) collective-permute-start(bf16[192,256]{1,0:T(8,128)(2,1)S(1)} %pad_add_fusion.z0_ref), channel_id=1, source_target_pairs={{0,64},{8,72},{16,80},{24,88},{32,96},{40,104},{48,112},{56,120},{... | collective-permute-start | bytes 294920 | tf_op jit(solution)/shard_map/ppermute | solution.py:357
  8.4 1.6 %collective-permute-start.1 = (bf16[192,256]{1,0:T(8,128)(2,1)S(1)}, bf16[192,256]{1,0:T(8,128)(2,1)S(1)}, u32[]{:S(2)}, u32[]{:S(2)}) collective-permute-start(bf16[192,256]{1,0:T(8,128)(2,1)S(1)} %pad_add_fusion.z0_ref), channel_id=1, source_target_pairs={{0,32},{8,40},{16,48},{24,56},{32,64},{40,72},{48,80},{56,88},{64,... | collective-permute-start | bytes 294920 | tf_op jit(solution)/shard_map/ppermute | solution.py:357
  10.0 1.2 %collective-permute-start.4 = (bf16[192,512]{1,0:T(8,128)(2,1)}, bf16[192,512]{1,0:T(8,128)(2,1)S(1)}, u32[]{:S(2)}, u32[]{:S(2)}) collective-permute-start(bf16[192,512]{1,0:T(8,128)(2,1)} %g_hbm.1), channel_id=1, source_target_pairs={{0,2},{1,3},{2,4},{3,5},{4,6},{5,7},{6,0},{7,1},{8,10},{9,11},{10,... | collective-permute-start | bytes 589832 | tf_op jit(solution)/shard_map/ppermute | solution.py:357
  11.2 1.5 %collective-permute-start.5 = (bf16[192,512]{1,0:T(8,128)(2,1)}, bf16[192,512]{1,0:T(8,128)(2,1)S(1)}, u32[]{:S(2)}, u32[]{:S(2)}) collective-permute-start(bf16[192,512]{1,0:T(8,128)(2,1)} %g_hbm.1), channel_id=1, source_target_pairs={{0,6},{1,7},{2,0},{3,1},{4,2},{5,3},{6,4},{7,5},{8,14},{9,15},{10,... | collective-permute-start | bytes 589832 | tf_op jit(solution)/shard_map/ppermute | solution.py:357
  12.7 0.9 %prepare.1 = (bf16[768,128]{1,0:T(8,128)(2,1)S(1)}, s32[8,768]{1,0:T(8,128)S(1)}) custom-call(s32[1]{0:T(128)} %bitcast.place_ref, s32[8]{0:T(128)} %len_hbm.1, bf16[192,512]{1,0:T(8,128)(2,1)} %q_hbm.1), custom_call_target="tpu_custom_call" | custom-call | flops 1 | bytes 1 | tf_op jit(solution)/shard_map/prepare/pallas_call | solution.py:371
  13.6 4.3 %collective-permute-done.1.z1_ref = bf16[192,256]{1,0:T(8,128)(2,1)S(1)} collective-permute-done((bf16[192,256]{1,0:T(8,128)(2,1)S(1)}, bf16[192,256]{1,0:T(8,128)(2,1)S(1)}, u32[]{:S(2)}, u32[]{:S(2)}) %collective-permute-start.1) | collective-permute-done | bytes 98336 | tf_op jit(solution)/shard_map/ppermute | solution.py:357
  18.5 1.2 %collective-permute-start.6 = (bf16[192,512]{1,0:T(8,128)(2,1)S(1)}, bf16[192,512]{1,0:T(8,128)(2,1)S(1)}, u32[]{:S(2)}, u32[]{:S(2)}) collective-permute-start(bf16[192,512]{1,0:T(8,128)(2,1)S(1)} %collective-permute-done.3.refs_1_.y_ref), channel_id=1, source_target_pairs={{0,2},{1,3},{2,4},{3,5},{4,6},{5,7},{6,0},{7,1},{8,10},{9,11},{10,... | collective-permute-start | bytes 589832 | tf_op jit(solution)/shard_map/ppermute | solution.py:357
  19.7 1.5 %collective-permute-start.7 = (bf16[192,512]{1,0:T(8,128)(2,1)S(1)}, bf16[192,512]{1,0:T(8,128)(2,1)}, u32[]{:S(2)}, u32[]{:S(2)}) collective-permute-start(bf16[192,512]{1,0:T(8,128)(2,1)S(1)} %collective-permute-done.3.refs_1_.y_ref), channel_id=1, source_target_pairs={{0,6},{1,7},{2,0},{3,1},{4,2},{5,3},{6,4},{7,5},{8,14},{9,15},{10,... | collective-permute-start | bytes 589832 | tf_op jit(solution)/shard_map/ppermute | solution.py:357
  21.1 0.8 %near_scores.1 = (f32[576,768]{1,0:T(8,128)S(1)}, f32[8,768]{1,0:T(8,128)S(1)}) custom-call(s32[1]{0:T(128)} %bitcast.place_ref, bf16[192,256]{1,0:T(8,128)(2,1)S(1)} %collective-permute-done.z2_ref, bf16[192,256]{1,0:T(8,128)(2,1)S(1)} %collective-permute-done.1.z1_ref, bf16[192,256]{1,0:T(8,128)(2,1)S(1)} %pad_add_fusion.z0_ref, ...), custom_call_target="tpu_custom_call" | custom-call | flops 1 | bytes 1 | tf_op jit(solution)/shard_map/near_scores/pallas_call | solution.py:371
  21.9 1.6 %collective-permute-done.2.side_ref = bf16[384,256]{1,0:T(8,128)(2,1)S(1)} collective-permute-done((bf16[384,256]{1,0:T(8,128)(2,1)S(1)}, bf16[384,256]{1,0:T(8,128)(2,1)S(1)}, u32[]{:S(2)}, u32[]{:S(2)}) %collective-permute-start.2) | collective-permute-done | bytes 196640 | tf_op jit(solution)/shard_map/ppermute | solution.py:357
  23.5 1.3 %collective-permute-done.6.refs_1_.or_ref = bf16[192,512]{1,0:T(8,128)(2,1)S(1)} collective-permute-done((bf16[192,512]{1,0:T(8,128)(2,1)S(1)}, bf16[192,512]{1,0:T(8,128)(2,1)S(1)}, u32[]{:S(2)}, u32[]{:S(2)}) %collective-permute-start.6) | collective-permute-done | bytes 196640 | tf_op jit(solution)/shard_map/ppermute | solution.py:357
  25.6 2.3 %collective-permute-start.10 = (bf16[960,256]{1,0:T(8,128)(2,1)S(1)}, bf16[960,256]{1,0:T(8,128)(2,1)S(1)}, u32[]{:S(2)}, u32[]{:S(2)}) collective-permute-start(bf16[960,256]{1,0:T(8,128)(2,1)S(1)} %join_slots.1.own_ref), channel_id=1, source_target_pairs={{0,8},{8,0},{16,24},{24,16},{32,40},{40,32},{48,56},{56,48},{64,72... | collective-permute-start | bytes 1474568 | tf_op jit(solution)/shard_map/ppermute | solution.py:357
  27.8 1.2 %collective-permute-start.8 = (bf16[192,512]{1,0:T(8,128)(2,1)S(1)}, bf16[192,512]{1,0:T(8,128)(2,1)}, u32[]{:S(2)}, u32[]{:S(2)}) collective-permute-start(bf16[192,512]{1,0:T(8,128)(2,1)S(1)} %collective-permute-done.4.refs_2_.r_ref), channel_id=1, source_target_pairs={{0,2},{1,3},{2,4},{3,5},{4,6},{5,7},{6,0},{7,1},{8,10},{9,11},{10,... | collective-permute-start | bytes 589832 | tf_op jit(solution)/shard_map/ppermute | solution.py:357
  29.0 1.5 %collective-permute-start.9 = (bf16[192,512]{1,0:T(8,128)(2,1)}, bf16[192,512]{1,0:T(8,128)(2,1)}, u32[]{:S(2)}, u32[]{:S(2)}) collective-permute-start(bf16[192,512]{1,0:T(8,128)(2,1)} %collective-permute-done.7.refs_2_.ol_ref), channel_id=1, source_target_pairs={{0,6},{1,7},{2,0},{3,1},{4,2},{5,3},{6,4},{7,5},{8,14},{9,15},{10,... | collective-permute-start | bytes 589832 | tf_op jit(solution)/shard_map/ppermute | solution.py:357
  30.5 0.9 %copy-done.1 = bf16[192,512]{1,0:T(8,128)(2,1)S(1)} copy-done((bf16[192,512]{1,0:T(8,128)(2,1)S(1)}, bf16[192,512]{1,0:T(8,128)(2,1)}, u32[]{:S(2)}) %copy-start.1) | copy-done | bytes 196632
  31.4 0.7 %copy-done.3 = s32[8,768]{1,0:T(8,128)S(1)} copy-done((s32[8,768]{1,0:T(8,128)S(1)}, s32[8,768]{1,0:T(8,128)}, u32[]{:S(2)}) %copy-start.3) | copy-done | bytes 24600
  32.2 0.7 %copy-done.5 = f32[8,768]{1,0:T(8,128)S(1)} copy-done((f32[8,768]{1,0:T(8,128)S(1)}, f32[8,768]{1,0:T(8,128)}, u32[]{:S(2)}) %copy-start.5) | copy-done | bytes 24600
  32.9 4.7 %middle.1 = (bf16[960,768]{1,0:T(8,128)(2,1)S(1)}, f32[128,768]{1,0:T(8,128)S(1)}, f32[8,768]{1,0:T(8,128)S(1)}, f32[192,512]{1,0:T(8,128)S(1)}, bf16[512,1024]{1,0:T(8,128)(2,1)S(1)}) custom-call(s32[1]{0:T(128)} %bitcast.place_ref, s32[1]{0:T(128)} %bitcast.1.head_ref, bf16[960,256]{1,0:T(8,128)(2,1)S(1)} %join_slots.1.own_ref, ...), custom_call_target="tpu_custom_call" | custom-call | flops 1 | bytes 1 | tf_op jit(solution)/shard_map/middle/pallas_call | solution.py:371
  37.6 2.7 %across.1 = (bf16[768,768]{1,0:T(8,128)(2,1)S(1)}, f32[128,768]{1,0:T(8,128)S(1)}, f32[8,768]{1,0:T(8,128)S(1)}) custom-call(s32[1]{0:T(128)} %bitcast.place_ref, bf16[960,256]{1,0:T(8,128)(2,1)S(1)} %collective-permute-done.10.par_ref, bf16[768,128]{1,0:T(8,128)(2,1)S(1)} %get-tuple-element.31.refs_0_.q4_ref, s32[8,768]{1,0:T(8,128)S(1)} %copy-done.3, ...), custom_call_target="tpu_custom_call" | custom-call | flops 1 | bytes 1 | tf_op jit(solution)/shard_map/across/pallas_call | solution.py:371
  40.4 2.1 %cross_far.1 = (bf16[384,256]{1,0:T(8,128)(2,1)S(1)}, bf16[768,128]{1,0:T(8,128)(2,1)S(1)}, f32[1,768]{1,0:T(1,128)S(1)}, f32[128,768]{1,0:T(8,128)S(1)}) custom-call(s32[1]{0:T(128)} %bitcast.place_ref, bf16[192,512]{1,0:T(8,128)(2,1)} %collective-permute-done.8.a_ref, bf16[192,512]{1,0:T(8,128)(2,1)} %collective-permute-done.9.b_ref, ...), custom_call_target="tpu_custom_call" | custom-call | flops 1 | bytes 1 | tf_op jit(solution)/shard_map/cross_far/pallas_call | solution.py:371
  42.5 1.3 %collective-permute-start.11 = (bf16[384,256]{1,0:T(8,128)(2,1)S(1)}, bf16[384,256]{1,0:T(8,128)(2,1)S(1)}, u32[]{:S(2)}, u32[]{:S(2)}) collective-permute-start(bf16[384,256]{1,0:T(8,128)(2,1)S(1)} %get-tuple-element.49), channel_id=1, source_target_pairs={{0,8},{8,0},{16,24},{24,16},{32,40},{40,32},{48,56},{56,48},{64,72... | collective-permute-start | bytes 589832 | tf_op jit(solution)/shard_map/ppermute | solution.py:357
  43.8 1.4 %cross_near.1 = (bf16[576,256]{1,0:T(8,128)(2,1)S(1)}, f32[128,768]{1,0:T(8,128)S(1)}) custom-call(s32[1]{0:T(128)} %bitcast.place_ref, bf16[768,128]{1,0:T(8,128)(2,1)S(1)} %get-tuple-element.31.refs_0_.q4_ref, bf16[960,256]{1,0:T(8,128)(2,1)S(1)} %collective-permute-done.10.par_ref, bf16[768,768]{1,0:T(8,128)(2,1)S(1)} %get-tuple-element.40.p_ref, ...), custom_call_target="tpu_custom_call" | custom-call | flops 1 | bytes 1 | tf_op jit(solution)/shard_map/cross_near/pallas_call | solution.py:371
  45.3 1.0 %own_far.1 = (f32[384,256]{1,0:T(8,128)S(1)}, f32[128,768]{1,0:T(8,128)S(1)}) custom-call(bf16[768,128]{1,0:T(8,128)(2,1)S(1)} %get-tuple-element.31.refs_0_.q4_ref, bf16[960,256]{1,0:T(8,128)(2,1)S(1)} %join_slots.1.own_ref, bf16[960,768]{1,0:T(8,128)(2,1)S(1)} %get-tuple-element.35.p_ref, bf16[768,128]{1,0:T(8,128)(2,1)S(1)} %get-tuple-element.43.g_ref, ...), custom_call_target="tpu_custom_call" | custom-call | flops 1 | bytes 1 | tf_op jit(solution)/shard_map/own_far/pallas_call | solution.py:371
  46.4 1.1 %collective-permute-start.13 = (bf16[192,256]{1,0:T(8,128)(2,1)S(1)}, bf16[192,256]{1,0:T(8,128)(2,1)S(1)}, u32[]{:S(2)}, u32[]{:S(2)}) collective-permute-start(bf16[192,256]{1,0:T(8,128)(2,1)S(1)} %get-tuple-element.54), channel_id=1, source_target_pairs={{0,16},{8,24},{16,0},{24,8},{32,48},{40,56},{48,32},{56,40},{64,80... | collective-permute-start | bytes 294920 | tf_op jit(solution)/shard_map/ppermute | solution.py:357
  47.5 2.3 %own_near.1 = (f32[576,256]{1,0:T(8,128)S(1)}, bf16[192,512]{1,0:T(8,128)(2,1)}) custom-call(bf16[768,128]{1,0:T(8,128)(2,1)S(1)} %get-tuple-element.31.refs_0_.q4_ref, bf16[960,256]{1,0:T(8,128)(2,1)S(1)} %join_slots.1.own_ref, bf16[960,768]{1,0:T(8,128)(2,1)S(1)} %get-tuple-element.35.p_ref, bf16[768,128]{1,0:T(8,128)(2,1)S(1)} %get-tuple-element.43.g_ref, ...), custom_call_target="tpu_custom_call" | custom-call | flops 1 | bytes 1 | tf_op jit(solution)/shard_map/own_near/pallas_call | solution.py:371
  50.5 1.1 %collective-permute-start.14 = (bf16[192,256]{1,0:T(8,128)(2,1)S(1)}, bf16[192,256]{1,0:T(8,128)(2,1)S(1)}, u32[]{:S(2)}, u32[]{:S(2)}) collective-permute-start(bf16[192,256]{1,0:T(8,128)(2,1)S(1)} %get-tuple-element.56), channel_id=1, source_target_pairs={{0,16},{8,24},{16,0},{24,8},{32,48},{40,56},{48,32},{56,40},{64,80... | collective-permute-start | bytes 294920 | tf_op jit(solution)/shard_map/ppermute | solution.py:357
  51.6 2.3 %collective-permute-start.16 = (bf16[192,256]{1,0:T(8,128)(2,1)S(1)}, bf16[192,256]{1,0:T(8,128)(2,1)S(1)}, u32[]{:S(2)}, u32[]{:S(2)}) collective-permute-start(bf16[192,256]{1,0:T(8,128)(2,1)S(1)} %relay_far.1.after), channel_id=1, source_target_pairs={{0,192},{8,200},{16,208},{24,216},{32,224},{40,232},{48,240},{56,2... | collective-permute-start | bytes 294920 | tf_op jit(solution)/shard_map/ppermute | solution.py:357
  54.1 1.2 %collective-permute-start.15 = (bf16[192,256]{1,0:T(8,128)(2,1)S(1)}, bf16[192,256]{1,0:T(8,128)(2,1)S(1)}, u32[]{:S(2)}, u32[]{:S(2)}) collective-permute-start(bf16[192,256]{1,0:T(8,128)(2,1)S(1)} %get-tuple-element.58), channel_id=1, source_target_pairs={{0,224},{8,232},{16,240},{24,248},{32,0},{40,8},{48,16},{56,24},{6... | collective-permute-start | bytes 294920 | tf_op jit(solution)/shard_map/ppermute | solution.py:357
  55.3 2.4 %collective-permute-done.16 = bf16[192,256]{1,0:T(8,128)(2,1)S(1)} collective-permute-done((bf16[192,256]{1,0:T(8,128)(2,1)S(1)}, bf16[192,256]{1,0:T(8,128)(2,1)S(1)}, u32[]{:S(2)}, u32[]{:S(2)}) %collective-permute-start.16) | collective-permute-done | bytes 98336 | tf_op jit(solution)/shard_map/ppermute | solution.py:357
  57.7 2.6 %collective-permute-done.15 = bf16[192,256]{1,0:T(8,128)(2,1)S(1)} collective-permute-done((bf16[192,256]{1,0:T(8,128)(2,1)S(1)}, bf16[192,256]{1,0:T(8,128)(2,1)S(1)}, u32[]{:S(2)}, u32[]{:S(2)}) %collective-permute-start.15) | collective-permute-done | bytes 98336 | tf_op jit(solution)/shard_map/ppermute | solution.py:357
  (31 shorter events, 2.9 us)
Async XLA Ops:
  0.6 17.8 %collective-permute-start.3 = (bf16[192,512]{1,0:T(8,128)(2,1)}, bf16[192,512]{1,0:T(8,128)(2,1)S(1)}, u32[]{:S(2)}, u32[]{:S(2)}) collective-permute-start(bf16[192,512]{1,0:T(8,128)(2,1)} %g_hbm.1), channel_id=1, source_target_pairs={{0,1},{1,0},{2,3},{3,2},{4,5},{5,4},{6,7},{7,6},{8,9},{9,8},{10,11... | collective-permute-start | bytes 589832 | tf_op jit(solution)/shard_map/ppermute | solution.py:357
  5.3 8.3 %collective-permute-start = (bf16[192,256]{1,0:T(8,128)(2,1)S(1)}, bf16[192,256]{1,0:T(8,128)(2,1)S(1)}, u32[]{:S(2)}, u32[]{:S(2)}) collective-permute-start(bf16[192,256]{1,0:T(8,128)(2,1)S(1)} %pad_add_fusion.z0_ref), channel_id=1, source_target_pairs={{0,64},{8,72},{16,80},{24,88},{32,96},{40,104},{48,112},{56,120},{... | collective-permute-start | bytes 294920 | tf_op jit(solution)/shard_map/ppermute | solution.py:357
  8.4 9.6 %collective-permute-start.1 = (bf16[192,256]{1,0:T(8,128)(2,1)S(1)}, bf16[192,256]{1,0:T(8,128)(2,1)S(1)}, u32[]{:S(2)}, u32[]{:S(2)}) collective-permute-start(bf16[192,256]{1,0:T(8,128)(2,1)S(1)} %pad_add_fusion.z0_ref), channel_id=1, source_target_pairs={{0,32},{8,40},{16,48},{24,56},{32,64},{40,72},{48,80},{56,88},{64,... | collective-permute-start | bytes 294920 | tf_op jit(solution)/shard_map/ppermute | solution.py:357
  10.0 11.1 %collective-permute-start.4 = (bf16[192,512]{1,0:T(8,128)(2,1)}, bf16[192,512]{1,0:T(8,128)(2,1)S(1)}, u32[]{:S(2)}, u32[]{:S(2)}) collective-permute-start(bf16[192,512]{1,0:T(8,128)(2,1)} %g_hbm.1), channel_id=1, source_target_pairs={{0,2},{1,3},{2,4},{3,5},{4,6},{5,7},{6,0},{7,1},{8,10},{9,11},{10,... | collective-permute-start | bytes 589832 | tf_op jit(solution)/shard_map/ppermute | solution.py:357
  11.2 9.9 %collective-permute-start.5 = (bf16[192,512]{1,0:T(8,128)(2,1)}, bf16[192,512]{1,0:T(8,128)(2,1)S(1)}, u32[]{:S(2)}, u32[]{:S(2)}) collective-permute-start(bf16[192,512]{1,0:T(8,128)(2,1)} %g_hbm.1), channel_id=1, source_target_pairs={{0,6},{1,7},{2,0},{3,1},{4,2},{5,3},{6,4},{7,5},{8,14},{9,15},{10,... | collective-permute-start | bytes 589832 | tf_op jit(solution)/shard_map/ppermute | solution.py:357
  13.6 11.2 %copy-start.2 = (s32[8,768]{1,0:T(8,128)}, s32[8,768]{1,0:T(8,128)S(1)}, u32[]{:S(2)}) copy-start(s32[8,768]{1,0:T(8,128)S(1)} %get-tuple-element.32.bound_ref) | copy-start | bytes 73732
  18.0 5.5 %collective-permute-start.2 = (bf16[384,256]{1,0:T(8,128)(2,1)S(1)}, bf16[384,256]{1,0:T(8,128)(2,1)S(1)}, u32[]{:S(2)}, u32[]{:S(2)}) collective-permute-start(bf16[384,256]{1,0:T(8,128)(2,1)S(1)} %pick_side.1.refs_0_), channel_id=1, source_target_pairs={{0,16},{8,24},{16,0},{24,8},{32,48},{40,56},{48,32},{56,40},{64,80... | collective-permute-start | bytes 589832 | tf_op jit(solution)/shard_map/ppermute | solution.py:357
  18.5 6.4 %collective-permute-start.6 = (bf16[192,512]{1,0:T(8,128)(2,1)S(1)}, bf16[192,512]{1,0:T(8,128)(2,1)S(1)}, u32[]{:S(2)}, u32[]{:S(2)}) collective-permute-start(bf16[192,512]{1,0:T(8,128)(2,1)S(1)} %collective-permute-done.3.refs_1_.y_ref), channel_id=1, source_target_pairs={{0,2},{1,3},{2,4},{3,5},{4,6},{5,7},{6,0},{7,1},{8,10},{9,11},{10,... | collective-permute-start | bytes 589832 | tf_op jit(solution)/shard_map/ppermute | solution.py:357
  19.7 5.2 %collective-permute-start.7 = (bf16[192,512]{1,0:T(8,128)(2,1)S(1)}, bf16[192,512]{1,0:T(8,128)(2,1)}, u32[]{:S(2)}, u32[]{:S(2)}) collective-permute-start(bf16[192,512]{1,0:T(8,128)(2,1)S(1)} %collective-permute-done.3.refs_1_.y_ref), channel_id=1, source_target_pairs={{0,6},{1,7},{2,0},{3,1},{4,2},{5,3},{6,4},{7,5},{8,14},{9,15},{10,... | collective-permute-start | bytes 589832 | tf_op jit(solution)/shard_map/ppermute | solution.py:357
  21.9 2.9 %copy-start.4 = (f32[8,768]{1,0:T(8,128)}, f32[8,768]{1,0:T(8,128)S(1)}, u32[]{:S(2)}) copy-start(f32[8,768]{1,0:T(8,128)S(1)} %get-tuple-element.33.refs_0_.stat_ref) | copy-start | bytes 73732
  24.9 0.7 %copy-start = (bf16[192,512]{1,0:T(8,128)(2,1)}, bf16[192,512]{1,0:T(8,128)(2,1)S(1)}, u32[]{:S(2)}) copy-start(bf16[192,512]{1,0:T(8,128)(2,1)S(1)} %collective-permute-done.6.refs_1_.or_ref) | copy-start | bytes 589828
  25.6 12.0 %collective-permute-start.10 = (bf16[960,256]{1,0:T(8,128)(2,1)S(1)}, bf16[960,256]{1,0:T(8,128)(2,1)S(1)}, u32[]{:S(2)}, u32[]{:S(2)}) collective-permute-start(bf16[960,256]{1,0:T(8,128)(2,1)S(1)} %join_slots.1.own_ref), channel_id=1, source_target_pairs={{0,8},{8,0},{16,24},{24,16},{32,40},{40,32},{48,56},{56,48},{64,72... | collective-permute-start | bytes 1474568 | tf_op jit(solution)/shard_map/ppermute | solution.py:357
  27.8 12.5 %collective-permute-start.8 = (bf16[192,512]{1,0:T(8,128)(2,1)S(1)}, bf16[192,512]{1,0:T(8,128)(2,1)}, u32[]{:S(2)}, u32[]{:S(2)}) collective-permute-start(bf16[192,512]{1,0:T(8,128)(2,1)S(1)} %collective-permute-done.4.refs_2_.r_ref), channel_id=1, source_target_pairs={{0,2},{1,3},{2,4},{3,5},{4,6},{5,7},{6,0},{7,1},{8,10},{9,11},{10,... | collective-permute-start | bytes 589832 | tf_op jit(solution)/shard_map/ppermute | solution.py:357
  29.0 11.3 %collective-permute-start.9 = (bf16[192,512]{1,0:T(8,128)(2,1)}, bf16[192,512]{1,0:T(8,128)(2,1)}, u32[]{:S(2)}, u32[]{:S(2)}) collective-permute-start(bf16[192,512]{1,0:T(8,128)(2,1)} %collective-permute-done.7.refs_2_.ol_ref), channel_id=1, source_target_pairs={{0,6},{1,7},{2,0},{3,1},{4,2},{5,3},{6,4},{7,5},{8,14},{9,15},{10,... | collective-permute-start | bytes 589832 | tf_op jit(solution)/shard_map/ppermute | solution.py:357
  30.5 0.9 %copy-start.1 = (bf16[192,512]{1,0:T(8,128)(2,1)S(1)}, bf16[192,512]{1,0:T(8,128)(2,1)}, u32[]{:S(2)}) copy-start(bf16[192,512]{1,0:T(8,128)(2,1)} %copy-done) | copy-start | bytes 589828
  31.4 0.7 %copy-start.3 = (s32[8,768]{1,0:T(8,128)S(1)}, s32[8,768]{1,0:T(8,128)}, u32[]{:S(2)}) copy-start(s32[8,768]{1,0:T(8,128)} %copy-done.2) | copy-start | bytes 73732
  32.2 0.7 %copy-start.5 = (f32[8,768]{1,0:T(8,128)S(1)}, f32[8,768]{1,0:T(8,128)}, u32[]{:S(2)}) copy-start(f32[8,768]{1,0:T(8,128)} %copy-done.4) | copy-start | bytes 73732
  42.5 3.8 %collective-permute-start.11 = (bf16[384,256]{1,0:T(8,128)(2,1)S(1)}, bf16[384,256]{1,0:T(8,128)(2,1)S(1)}, u32[]{:S(2)}, u32[]{:S(2)}) collective-permute-start(bf16[384,256]{1,0:T(8,128)(2,1)S(1)} %get-tuple-element.49), channel_id=1, source_target_pairs={{0,8},{8,0},{16,24},{24,16},{32,40},{40,32},{48,56},{56,48},{64,72... | collective-permute-start | bytes 589832 | tf_op jit(solution)/shard_map/ppermute | solution.py:357
  45.2 5.1 %collective-permute-start.12 = (bf16[576,256]{1,0:T(8,128)(2,1)S(1)}, bf16[576,256]{1,0:T(8,128)(2,1)S(1)}, u32[]{:S(2)}, u32[]{:S(2)}) collective-permute-start(bf16[576,256]{1,0:T(8,128)(2,1)S(1)} %get-tuple-element.53), channel_id=1, source_target_pairs={{0,8},{8,0},{16,24},{24,16},{32,40},{40,32},{48,56},{56,48},{64,72... | collective-permute-start | bytes 884744 | tf_op jit(solution)/shard_map/ppermute | solution.py:357
  46.4 4.0 %collective-permute-start.13 = (bf16[192,256]{1,0:T(8,128)(2,1)S(1)}, bf16[192,256]{1,0:T(8,128)(2,1)S(1)}, u32[]{:S(2)}, u32[]{:S(2)}) collective-permute-start(bf16[192,256]{1,0:T(8,128)(2,1)S(1)} %get-tuple-element.54), channel_id=1, source_target_pairs={{0,16},{8,24},{16,0},{24,8},{32,48},{40,56},{48,32},{56,40},{64,80... | collective-permute-start | bytes 294920 | tf_op jit(solution)/shard_map/ppermute | solution.py:357
  50.5 3.6 %collective-permute-start.14 = (bf16[192,256]{1,0:T(8,128)(2,1)S(1)}, bf16[192,256]{1,0:T(8,128)(2,1)S(1)}, u32[]{:S(2)}, u32[]{:S(2)}) collective-permute-start(bf16[192,256]{1,0:T(8,128)(2,1)S(1)} %get-tuple-element.56), channel_id=1, source_target_pairs={{0,16},{8,24},{16,0},{24,8},{32,48},{40,56},{48,32},{56,40},{64,80... | collective-permute-start | bytes 294920 | tf_op jit(solution)/shard_map/ppermute | solution.py:357
  51.6 6.1 %collective-permute-start.16 = (bf16[192,256]{1,0:T(8,128)(2,1)S(1)}, bf16[192,256]{1,0:T(8,128)(2,1)S(1)}, u32[]{:S(2)}, u32[]{:S(2)}) collective-permute-start(bf16[192,256]{1,0:T(8,128)(2,1)S(1)} %relay_far.1.after), channel_id=1, source_target_pairs={{0,192},{8,200},{16,208},{24,216},{32,224},{40,232},{48,240},{56,2... | collective-permute-start | bytes 294920 | tf_op jit(solution)/shard_map/ppermute | solution.py:357
  54.1 6.3 %collective-permute-start.15 = (bf16[192,256]{1,0:T(8,128)(2,1)S(1)}, bf16[192,256]{1,0:T(8,128)(2,1)S(1)}, u32[]{:S(2)}, u32[]{:S(2)}) collective-permute-start(bf16[192,256]{1,0:T(8,128)(2,1)S(1)} %get-tuple-element.58), channel_id=1, source_target_pairs={{0,224},{8,232},{16,240},{24,248},{32,0},{40,8},{48,16},{56,24},{6... | collective-permute-start | bytes 294920 | tf_op jit(solution)/shard_map/ppermute | solution.py:357

commit v5 on v4

--- a/solution.py
+++ b/solution.py
@@ -350,7 +350,7 @@
 
 
 def params(mib):
-    return pltpu.CompilerParams(vmem_limit_bytes=mib * MIB)
+    return pltpu.CompilerParams(vmem_limit_bytes=max(mib, 16) * MIB)
 
 
 def moved(x, axis, to):
@@ -366,7 +366,7 @@
     return jax.ShapeDtypeStruct((rows, cols), dtype)
 
 
-def call(name, kernel, outs, ins, mib, args, scratch=()):
+def call(name, kernel, outs, ins, mib, args, scratch=(), flops=1):
     one = not isinstance(outs, tuple)
     return pl.pallas_call(
         kernel,
@@ -375,7 +375,7 @@
         out_specs=vmem(1)[0] if one else tuple(vmem(len(outs))),
         scratch_shapes=list(scratch),
         compiler_params=params(mib),
-        cost_estimate=pl.CostEstimate(flops=1, bytes_accessed=1, transcendentals=0),
+        cost_estimate=pl.CostEstimate(flops=flops, bytes_accessed=1, transcendentals=0),
         name=name,
     )(*args)
 
@@ -413,11 +413,12 @@
         "near_scores",
         near_kernel,
         (shape(3 * ROWS, LANES, f32), shape(8, LANES, f32)),
-        smem(1) + vmem(5) + token(4),
+        smem(1) + vmem(5) + token(6),
         8,
-        (place, z2, z1, kv, q4, bound, picked, other, right, left),
-    )
-    own = call("join_slots", join_kernel, shape(SLOTS * ROWS, 2 * D, bf16), vmem(4) + token(3), 4, (z2, z1, kv, side, stat, other_right, other_left))
+        (place, z2, z1, kv, q4, bound, picked, other, right, left, other_right, other_left),
+        flops=10**10,
+    )
+    own = call("join_slots", join_kernel, shape(SLOTS * ROWS, 2 * D, bf16), vmem(4) + token(1), 4, (z2, z1, kv, side, stat))
     par = moved(own, "ctx", lambda i: i ^ 1)
 
     p_own, o_own, log_own, early, tail = call(

time: 61.5 us -> 63.1 us (1.026)
  starting transfers between devices: 26.5 us -> 31.1 us
  waiting for transfers between devices: 12.9 us -> 9.79 us
  local copies, waits for them, and re-layouts: 3.73 us -> 4.92 us
  Pallas kernels: 16.2 us -> 15.2 us
    ppermute x17, starting transfers between devices: 26.5 us -> 31.1 us  [moved(): lax.ppermute(x, axis, [(i, to(i)) for i in range(lax.axis_size(axis))])]
    ppermute x17, waiting for transfers between devices: 12.9 us -> 9.79 us  [moved(): lax.ppermute(x, axis, [(i, to(i)) for i in range(lax.axis_size(axis))])]
    unnamed x12 -> x22, local copies, waits for them, and re-layouts: 3.08 us -> 4.28 us
    pallas_call x14, Pallas kernels: 16.2 us -> 15.2 us  [call(): pl.pallas_call(kernel, out_shape=outs, in_specs=ins, out_specs=vmem(1)[0]...]
  transfers between devices with their start and end apart: 17 -> 17, of which waited for: 7 -> 5; matrix products, arithmetic and copies ran while one was open for 1% -> 1% of each run, Pallas kernels for 23% -> 22%
where the time goes in v5:
time: 63.1 us; the launch traced here: 62.7 us
  starting transfers between devices  31.1 us (49%)
  Pallas kernels  15.2 us (24%)
  waiting for transfers between devices  9.79 us (16%)
  local copies, waits for them, and re-layouts  4.92 us (8%)
  other arithmetic  0.87 us (1%)
  between operations  0.87 us (1%)
    ppermute x17, starting transfers between devices, moved(): lax.ppermute(x, axis, [(i, to(i)) for i in range(lax.axis_size(axis))])  31.1 us
    pallas_call x14, Pallas kernels, call(): pl.pallas_call(kernel, out_shape=outs, in_specs=ins, out_specs=vmem(1)[0]...  15.2 us
    ppermute x17, waiting for transfers between devices, moved(): lax.ppermute(x, axis, [(i, to(i)) for i in range(lax.axis_size(axis))])  9.79 us
    unnamed x22, local copies, waits for them, and re-layouts  4.28 us
  transfers between devices with their start and end apart: 17, of which 5 were waited for; matrix products, arithmetic and copies ran while one was open for 1% of the time, Pallas kernels for 22%

profile of v5, /device:TPU:1, one launch (start us, length us, event | category | flops | bytes accessed | tf_op | source)
XLA Modules:
  0.0 62.7 jit_solution(11704827445303211979)
XLA Ops:
  0.6 3.8 %collective-permute-start.3 = (bf16[192,512]{1,0:T(8,128)(2,1)}, bf16[192,512]{1,0:T(8,128)(2,1)S(1)}, u32[]{:S(2)}, u32[]{:S(2)}) collective-permute-start(bf16[192,512]{1,0:T(8,128)(2,1)} %g_hbm.1), channel_id=1, source_target_pairs={{0,1},{1,0},{2,3},{3,2},{4,5},{5,4},{6,7},{7,6},{8,9},{9,8},{10,11... | collective-permute-start | bytes 589832 | tf_op jit(solution)/shard_map/ppermute | solution.py:357
  4.5 0.8 %pad_add_fusion.z0_ref = bf16[192,256]{1,0:T(8,128)(2,1)S(1)} fusion(bf16[192,128]{1,0:T(8,128)(2,1)} %param.8, bf16[192,128]{1,0:T(8,128)(2,1)} %param.7), kind=kLoop, calls=%fused_computation.1 | loop fusion | flops 196608 | bytes 196608 | tf_op jit(solution)/shard_map/add | solution.py:393
  5.3 3.1 %collective-permute-start = (bf16[192,256]{1,0:T(8,128)(2,1)S(1)}, bf16[192,256]{1,0:T(8,128)(2,1)S(1)}, u32[]{:S(2)}, u32[]{:S(2)}) collective-permute-start(bf16[192,256]{1,0:T(8,128)(2,1)S(1)} %pad_add_fusion.z0_ref), channel_id=1, source_target_pairs={{0,64},{8,72},{16,80},{24,88},{32,96},{40,104},{48,112},{56,120},{... | collective-permute-start | bytes 294920 | tf_op jit(solution)/shard_map/ppermute | solution.py:357
  8.4 1.2 %collective-permute-start.4 = (bf16[192,512]{1,0:T(8,128)(2,1)}, bf16[192,512]{1,0:T(8,128)(2,1)S(1)}, u32[]{:S(2)}, u32[]{:S(2)}) collective-permute-start(bf16[192,512]{1,0:T(8,128)(2,1)} %g_hbm.1), channel_id=1, source_target_pairs={{0,2},{1,3},{2,4},{3,5},{4,6},{5,7},{6,0},{7,1},{8,10},{9,11},{10,... | collective-permute-start | bytes 589832 | tf_op jit(solution)/shard_map/ppermute | solution.py:357
  9.6 1.5 %collective-permute-start.5 = (bf16[192,512]{1,0:T(8,128)(2,1)}, bf16[192,512]{1,0:T(8,128)(2,1)S(1)}, u32[]{:S(2)}, u32[]{:S(2)}) collective-permute-start(bf16[192,512]{1,0:T(8,128)(2,1)} %g_hbm.1), channel_id=1, source_target_pairs={{0,6},{1,7},{2,0},{3,1},{4,2},{5,3},{6,4},{7,5},{8,14},{9,15},{10,... | collective-permute-start | bytes 589832 | tf_op jit(solution)/shard_map/ppermute | solution.py:357
  11.1 2.7 %collective-permute-start.7 = (bf16[192,512]{1,0:T(8,128)(2,1)S(1)}, bf16[192,512]{1,0:T(8,128)(2,1)}, u32[]{:S(2)}, u32[]{:S(2)}) collective-permute-start(bf16[192,512]{1,0:T(8,128)(2,1)S(1)} %collective-permute-done.3.refs_1_.y_ref), channel_id=1, source_target_pairs={{0,6},{1,7},{2,0},{3,1},{4,2},{5,3},{6,4},{7,5},{8,14},{9,15},{10,... | collective-permute-start | bytes 589832 | tf_op jit(solution)/shard_map/ppermute | solution.py:357
  13.7 3.3 %collective-permute-start.1 = (bf16[192,256]{1,0:T(8,128)(2,1)S(1)}, bf16[192,256]{1,0:T(8,128)(2,1)S(1)}, u32[]{:S(2)}, u32[]{:S(2)}) collective-permute-start(bf16[192,256]{1,0:T(8,128)(2,1)S(1)} %pad_add_fusion.z0_ref), channel_id=1, source_target_pairs={{0,32},{8,40},{16,48},{24,56},{32,64},{40,72},{48,80},{56,88},{64,... | collective-permute-start | bytes 294920 | tf_op jit(solution)/shard_map/ppermute | solution.py:357
  17.0 0.9 %prepare.1 = (bf16[768,128]{1,0:T(8,128)(2,1)S(1)}, s32[8,768]{1,0:T(8,128)S(1)}) custom-call(s32[1]{0:T(128)} %bitcast.place_ref, s32[8]{0:T(128)} %len_hbm.1, bf16[192,512]{1,0:T(8,128)(2,1)} %q_hbm.1), custom_call_target="tpu_custom_call" | custom-call | flops 1 | bytes 1 | tf_op jit(solution)/shard_map/prepare/pallas_call | solution.py:371
  18.0 2.0 %collective-permute-done.1.z1_ref = bf16[192,256]{1,0:T(8,128)(2,1)S(1)} collective-permute-done((bf16[192,256]{1,0:T(8,128)(2,1)S(1)}, bf16[192,256]{1,0:T(8,128)(2,1)S(1)}, u32[]{:S(2)}, u32[]{:S(2)}) %collective-permute-start.1) | collective-permute-done | bytes 98336 | tf_op jit(solution)/shard_map/ppermute | solution.py:357
  20.0 1.0 %collective-permute-start.2 = (bf16[384,256]{1,0:T(8,128)(2,1)S(1)}, bf16[384,256]{1,0:T(8,128)(2,1)S(1)}, u32[]{:S(2)}, u32[]{:S(2)}) collective-permute-start(bf16[384,256]{1,0:T(8,128)(2,1)S(1)} %pick_side.1.refs_0_), channel_id=1, source_target_pairs={{0,16},{8,24},{16,0},{24,8},{32,48},{40,56},{48,32},{56,40},{64,80... | collective-permute-start | bytes 589832 | tf_op jit(solution)/shard_map/ppermute | solution.py:357
  21.0 0.8 %near_scores.1 = (f32[576,768]{1,0:T(8,128)S(1)}, f32[8,768]{1,0:T(8,128)S(1)}) custom-call(s32[1]{0:T(128)} %bitcast.place_ref, bf16[192,256]{1,0:T(8,128)(2,1)S(1)} %collective-permute-done.z2_ref, bf16[192,256]{1,0:T(8,128)(2,1)S(1)} %collective-permute-done.1.z1_ref, bf16[192,256]{1,0:T(8,128)(2,1)S(1)} %pad_add_fusion.z0_ref, ...), custom_call_target="tpu_custom_call" | custom-call | flops 10000000000 | bytes 1 | tf_op jit(solution)/shard_map/near_scores/pallas_call | solution.py:371
  21.9 2.7 %collective-permute-done.2.side_ref = bf16[384,256]{1,0:T(8,128)(2,1)S(1)} collective-permute-done((bf16[384,256]{1,0:T(8,128)(2,1)S(1)}, bf16[384,256]{1,0:T(8,128)(2,1)S(1)}, u32[]{:S(2)}, u32[]{:S(2)}) %collective-permute-start.2) | collective-permute-done | bytes 196640 | tf_op jit(solution)/shard_map/ppermute | solution.py:357
  24.6 3.6 %collective-permute-start.10 = (bf16[960,256]{1,0:T(8,128)(2,1)S(1)}, bf16[960,256]{1,0:T(8,128)(2,1)S(1)}, u32[]{:S(2)}, u32[]{:S(2)}) collective-permute-start(bf16[960,256]{1,0:T(8,128)(2,1)S(1)} %join_slots.1.own_ref), channel_id=1, source_target_pairs={{0,8},{8,0},{16,24},{24,16},{32,40},{40,32},{48,56},{56,48},{64,72... | collective-permute-start | bytes 1474568 | tf_op jit(solution)/shard_map/ppermute | solution.py:357
  28.7 2.1 %collective-permute-start.9 = (bf16[192,512]{1,0:T(8,128)(2,1)}, bf16[192,512]{1,0:T(8,128)(2,1)S(1)}, u32[]{:S(2)}, u32[]{:S(2)}) collective-permute-start(bf16[192,512]{1,0:T(8,128)(2,1)} %collective-permute-done.7.refs_5_.ol_ref), channel_id=1, source_target_pairs={{0,6},{1,7},{2,0},{3,1},{4,2},{5,3},{6,4},{7,5},{8,14},{9,15},{10,... | collective-permute-start | bytes 589832 | tf_op jit(solution)/shard_map/ppermute | solution.py:357
  30.9 0.9 %copy-done.1 = bf16[192,512]{1,0:T(8,128)(2,1)S(1)} copy-done((bf16[192,512]{1,0:T(8,128)(2,1)S(1)}, bf16[192,512]{1,0:T(8,128)(2,1)}, u32[]{:S(2)}) %copy-start.1) | copy-done | bytes 196632
  31.8 0.9 %copy-done.3 = bf16[192,512]{1,0:T(8,128)(2,1)S(1)} copy-done((bf16[192,512]{1,0:T(8,128)(2,1)S(1)}, bf16[192,512]{1,0:T(8,128)(2,1)}, u32[]{:S(2)}) %copy-start.3) | copy-done | bytes 196632
  32.7 0.9 %copy-done.5 = bf16[192,512]{1,0:T(8,128)(2,1)S(1)} copy-done((bf16[192,512]{1,0:T(8,128)(2,1)S(1)}, bf16[192,512]{1,0:T(8,128)(2,1)}, u32[]{:S(2)}) %copy-start.5) | copy-done | bytes 196632
  33.7 0.7 %copy-done.7 = s32[8,768]{1,0:T(8,128)S(1)} copy-done((s32[8,768]{1,0:T(8,128)S(1)}, s32[8,768]{1,0:T(8,128)}, u32[]{:S(2)}) %copy-start.7) | copy-done | bytes 24600
  34.4 0.7 %copy-done.10 = f32[8,768]{1,0:T(8,128)S(1)} copy-done((f32[8,768]{1,0:T(8,128)S(1)}, f32[8,768]{1,0:T(8,128)}, u32[]{:S(2)}) %copy-start.10) | copy-done | bytes 24600
  35.1 4.7 %middle.1 = (bf16[960,768]{1,0:T(8,128)(2,1)S(1)}, f32[128,768]{1,0:T(8,128)S(1)}, f32[8,768]{1,0:T(8,128)S(1)}, f32[192,512]{1,0:T(8,128)S(1)}, bf16[512,1024]{1,0:T(8,128)(2,1)S(1)}) custom-call(s32[1]{0:T(128)} %bitcast.place_ref, s32[1]{0:T(128)} %bitcast.1.head_ref, bf16[960,256]{1,0:T(8,128)(2,1)S(1)} %join_slots.1.own_ref, ...), custom_call_target="tpu_custom_call" | custom-call | flops 1 | bytes 1 | tf_op jit(solution)/shard_map/middle/pallas_call | solution.py:371
  39.8 2.8 %across.1 = (bf16[768,768]{1,0:T(8,128)(2,1)S(1)}, f32[128,768]{1,0:T(8,128)S(1)}, f32[8,768]{1,0:T(8,128)S(1)}) custom-call(s32[1]{0:T(128)} %bitcast.place_ref, bf16[960,256]{1,0:T(8,128)(2,1)S(1)} %collective-permute-done.10.par_ref, bf16[768,128]{1,0:T(8,128)(2,1)S(1)} %get-tuple-element.31.refs_0_.q4_ref, s32[8,768]{1,0:T(8,128)S(1)} %copy-done.8, ...), custom_call_target="tpu_custom_call" | custom-call | flops 1 | bytes 1 | tf_op jit(solution)/shard_map/across/pallas_call | solution.py:371
  42.6 1.1 %cross_far.1 = (bf16[384,256]{1,0:T(8,128)(2,1)S(1)}, bf16[768,128]{1,0:T(8,128)(2,1)S(1)}, f32[1,768]{1,0:T(1,128)S(1)}, f32[128,768]{1,0:T(8,128)S(1)}) custom-call(s32[1]{0:T(128)} %bitcast.place_ref, bf16[192,512]{1,0:T(8,128)(2,1)S(1)} %collective-permute-done.8.a_ref, bf16[192,512]{1,0:T(8,128)(2,1)S(1)} %collective-permute-done.9.b_ref, ...), custom_call_target="tpu_custom_call" | custom-call | flops 1 | bytes 1 | tf_op jit(solution)/shard_map/cross_far/pallas_call | solution.py:371
  43.8 1.4 %collective-permute-start.11 = (bf16[384,256]{1,0:T(8,128)(2,1)S(1)}, bf16[384,256]{1,0:T(8,128)(2,1)S(1)}, u32[]{:S(2)}, u32[]{:S(2)}) collective-permute-start(bf16[384,256]{1,0:T(8,128)(2,1)S(1)} %get-tuple-element.49), channel_id=1, source_target_pairs={{0,8},{8,0},{16,24},{24,16},{32,40},{40,32},{48,56},{56,48},{64,72... | collective-permute-start | bytes 589832 | tf_op jit(solution)/shard_map/ppermute | solution.py:357
  45.1 1.4 %cross_near.1 = (bf16[576,256]{1,0:T(8,128)(2,1)S(1)}, f32[128,768]{1,0:T(8,128)S(1)}) custom-call(s32[1]{0:T(128)} %bitcast.place_ref, bf16[768,128]{1,0:T(8,128)(2,1)S(1)} %get-tuple-element.31.refs_0_.q4_ref, bf16[960,256]{1,0:T(8,128)(2,1)S(1)} %collective-permute-done.10.par_ref, bf16[768,768]{1,0:T(8,128)(2,1)S(1)} %get-tuple-element.40.p_ref, ...), custom_call_target="tpu_custom_call" | custom-call | flops 1 | bytes 1 | tf_op jit(solution)/shard_map/cross_near/pallas_call | solution.py:371
  46.7 1.0 %own_far.1 = (f32[384,256]{1,0:T(8,128)S(1)}, f32[128,768]{1,0:T(8,128)S(1)}) custom-call(bf16[768,128]{1,0:T(8,128)(2,1)S(1)} %get-tuple-element.31.refs_0_.q4_ref, bf16[960,256]{1,0:T(8,128)(2,1)S(1)} %join_slots.1.own_ref, bf16[960,768]{1,0:T(8,128)(2,1)S(1)} %get-tuple-element.35.p_ref, bf16[768,128]{1,0:T(8,128)(2,1)S(1)} %get-tuple-element.43.g_ref, ...), custom_call_target="tpu_custom_call" | custom-call | flops 1 | bytes 1 | tf_op jit(solution)/shard_map/own_far/pallas_call | solution.py:371
  47.7 1.4 %collective-permute-start.13 = (bf16[192,256]{1,0:T(8,128)(2,1)S(1)}, bf16[192,256]{1,0:T(8,128)(2,1)S(1)}, u32[]{:S(2)}, u32[]{:S(2)}) collective-permute-start(bf16[192,256]{1,0:T(8,128)(2,1)S(1)} %get-tuple-element.54), channel_id=1, source_target_pairs={{0,16},{8,24},{16,0},{24,8},{32,48},{40,56},{48,32},{56,40},{64,80... | collective-permute-start | bytes 294920 | tf_op jit(solution)/shard_map/ppermute | solution.py:357
  49.1 2.3 %own_near.1 = (f32[576,256]{1,0:T(8,128)S(1)}, bf16[192,512]{1,0:T(8,128)(2,1)}) custom-call(bf16[768,128]{1,0:T(8,128)(2,1)S(1)} %get-tuple-element.31.refs_0_.q4_ref, bf16[960,256]{1,0:T(8,128)(2,1)S(1)} %join_slots.1.own_ref, bf16[960,768]{1,0:T(8,128)(2,1)S(1)} %get-tuple-element.35.p_ref, bf16[768,128]{1,0:T(8,128)(2,1)S(1)} %get-tuple-element.43.g_ref, ...), custom_call_target="tpu_custom_call" | custom-call | flops 1 | bytes 1 | tf_op jit(solution)/shard_map/own_near/pallas_call | solution.py:371
  51.8 1.4 %collective-permute-start.14 = (bf16[192,256]{1,0:T(8,128)(2,1)S(1)}, bf16[192,256]{1,0:T(8,128)(2,1)S(1)}, u32[]{:S(2)}, u32[]{:S(2)}) collective-permute-start(bf16[192,256]{1,0:T(8,128)(2,1)S(1)} %get-tuple-element.56), channel_id=1, source_target_pairs={{0,16},{8,24},{16,0},{24,8},{32,48},{40,56},{48,32},{56,40},{64,80... | collective-permute-start | bytes 294920 | tf_op jit(solution)/shard_map/ppermute | solution.py:357
  53.1 2.2 %collective-permute-start.16 = (bf16[192,256]{1,0:T(8,128)(2,1)S(1)}, bf16[192,256]{1,0:T(8,128)(2,1)S(1)}, u32[]{:S(2)}, u32[]{:S(2)}) collective-permute-start(bf16[192,256]{1,0:T(8,128)(2,1)S(1)} %relay_far.1.after), channel_id=1, source_target_pairs={{0,192},{8,200},{16,208},{24,216},{32,224},{40,232},{48,240},{56,2... | collective-permute-start | bytes 294920 | tf_op jit(solution)/shard_map/ppermute | solution.py:357
  55.4 1.8 %collective-permute-start.15 = (bf16[192,256]{1,0:T(8,128)(2,1)S(1)}, bf16[192,256]{1,0:T(8,128)(2,1)S(1)}, u32[]{:S(2)}, u32[]{:S(2)}) collective-permute-start(bf16[192,256]{1,0:T(8,128)(2,1)S(1)} %get-tuple-element.58), channel_id=1, source_target_pairs={{0,224},{8,232},{16,240},{24,248},{32,0},{40,8},{48,16},{56,24},{6... | collective-permute-start | bytes 294920 | tf_op jit(solution)/shard_map/ppermute | solution.py:357
  57.2 2.6 %collective-permute-done.16 = bf16[192,256]{1,0:T(8,128)(2,1)S(1)} collective-permute-done((bf16[192,256]{1,0:T(8,128)(2,1)S(1)}, bf16[192,256]{1,0:T(8,128)(2,1)S(1)}, u32[]{:S(2)}, u32[]{:S(2)}) %collective-permute-start.16) | collective-permute-done | bytes 98336 | tf_op jit(solution)/shard_map/ppermute | solution.py:357
  59.8 2.2 %collective-permute-done.15 = bf16[192,256]{1,0:T(8,128)(2,1)S(1)} collective-permute-done((bf16[192,256]{1,0:T(8,128)(2,1)S(1)}, bf16[192,256]{1,0:T(8,128)(2,1)S(1)}, u32[]{:S(2)}, u32[]{:S(2)}) %collective-permute-start.15) | collective-permute-done | bytes 98336 | tf_op jit(solution)/shard_map/ppermute | solution.py:357
  (41 shorter events, 2.0 us)
Async XLA Ops:
  0.6 10.4 %collective-permute-start.3 = (bf16[192,512]{1,0:T(8,128)(2,1)}, bf16[192,512]{1,0:T(8,128)(2,1)S(1)}, u32[]{:S(2)}, u32[]{:S(2)}) collective-permute-start(bf16[192,512]{1,0:T(8,128)(2,1)} %g_hbm.1), channel_id=1, source_target_pairs={{0,1},{1,0},{2,3},{3,2},{4,5},{5,4},{6,7},{7,6},{8,9},{9,8},{10,11... | collective-permute-start | bytes 589832 | tf_op jit(solution)/shard_map/ppermute | solution.py:357
  5.3 8.4 %collective-permute-start = (bf16[192,256]{1,0:T(8,128)(2,1)S(1)}, bf16[192,256]{1,0:T(8,128)(2,1)S(1)}, u32[]{:S(2)}, u32[]{:S(2)}) collective-permute-start(bf16[192,256]{1,0:T(8,128)(2,1)S(1)} %pad_add_fusion.z0_ref), channel_id=1, source_target_pairs={{0,64},{8,72},{16,80},{24,88},{32,96},{40,104},{48,112},{56,120},{... | collective-permute-start | bytes 294920 | tf_op jit(solution)/shard_map/ppermute | solution.py:357
  8.4 12.6 %collective-permute-start.4 = (bf16[192,512]{1,0:T(8,128)(2,1)}, bf16[192,512]{1,0:T(8,128)(2,1)S(1)}, u32[]{:S(2)}, u32[]{:S(2)}) collective-permute-start(bf16[192,512]{1,0:T(8,128)(2,1)} %g_hbm.1), channel_id=1, source_target_pairs={{0,2},{1,3},{2,4},{3,5},{4,6},{5,7},{6,0},{7,1},{8,10},{9,11},{10,... | collective-permute-start | bytes 589832 | tf_op jit(solution)/shard_map/ppermute | solution.py:357
  9.6 11.4 %collective-permute-start.5 = (bf16[192,512]{1,0:T(8,128)(2,1)}, bf16[192,512]{1,0:T(8,128)(2,1)S(1)}, u32[]{:S(2)}, u32[]{:S(2)}) collective-permute-start(bf16[192,512]{1,0:T(8,128)(2,1)} %g_hbm.1), channel_id=1, source_target_pairs={{0,6},{1,7},{2,0},{3,1},{4,2},{5,3},{6,4},{7,5},{8,14},{9,15},{10,... | collective-permute-start | bytes 589832 | tf_op jit(solution)/shard_map/ppermute | solution.py:357
  11.0 10.8 %copy-start = (bf16[192,512]{1,0:T(8,128)(2,1)}, bf16[192,512]{1,0:T(8,128)(2,1)S(1)}, u32[]{:S(2)}) copy-start(bf16[192,512]{1,0:T(8,128)(2,1)S(1)} %collective-permute-done.3.refs_1_.y_ref) | copy-start | bytes 589828
  11.0 10.0 %collective-permute-start.6 = (bf16[192,512]{1,0:T(8,128)(2,1)S(1)}, bf16[192,512]{1,0:T(8,128)(2,1)S(1)}, u32[]{:S(2)}, u32[]{:S(2)}) collective-permute-start(bf16[192,512]{1,0:T(8,128)(2,1)S(1)} %collective-permute-done.3.refs_1_.y_ref), channel_id=1, source_target_pairs={{0,2},{1,3},{2,4},{3,5},{4,6},{5,7},{6,0},{7,1},{8,10},{9,11},{10,... | collective-permute-start | bytes 589832 | tf_op jit(solution)/shard_map/ppermute | solution.py:357
  11.1 10.0 %collective-permute-start.7 = (bf16[192,512]{1,0:T(8,128)(2,1)S(1)}, bf16[192,512]{1,0:T(8,128)(2,1)}, u32[]{:S(2)}, u32[]{:S(2)}) collective-permute-start(bf16[192,512]{1,0:T(8,128)(2,1)S(1)} %collective-permute-done.3.refs_1_.y_ref), channel_id=1, source_target_pairs={{0,6},{1,7},{2,0},{3,1},{4,2},{5,3},{6,4},{7,5},{8,14},{9,15},{10,... | collective-permute-start | bytes 589832 | tf_op jit(solution)/shard_map/ppermute | solution.py:357
  13.7 6.2 %collective-permute-start.1 = (bf16[192,256]{1,0:T(8,128)(2,1)S(1)}, bf16[192,256]{1,0:T(8,128)(2,1)S(1)}, u32[]{:S(2)}, u32[]{:S(2)}) collective-permute-start(bf16[192,256]{1,0:T(8,128)(2,1)S(1)} %pad_add_fusion.z0_ref), channel_id=1, source_target_pairs={{0,32},{8,40},{16,48},{24,56},{32,64},{40,72},{48,80},{56,88},{64,... | collective-permute-start | bytes 294920 | tf_op jit(solution)/shard_map/ppermute | solution.py:357
  18.0 3.9 %copy-start.6 = (s32[8,768]{1,0:T(8,128)}, s32[8,768]{1,0:T(8,128)S(1)}, u32[]{:S(2)}) copy-start(s32[8,768]{1,0:T(8,128)S(1)} %get-tuple-element.32.bound_ref) | copy-start | bytes 73732
  20.0 4.6 %collective-permute-start.2 = (bf16[384,256]{1,0:T(8,128)(2,1)S(1)}, bf16[384,256]{1,0:T(8,128)(2,1)S(1)}, u32[]{:S(2)}, u32[]{:S(2)}) collective-permute-start(bf16[384,256]{1,0:T(8,128)(2,1)S(1)} %pick_side.1.refs_0_), channel_id=1, source_target_pairs={{0,16},{8,24},{16,0},{24,8},{32,48},{40,56},{48,32},{56,40},{64,80... | collective-permute-start | bytes 589832 | tf_op jit(solution)/shard_map/ppermute | solution.py:357
  21.0 0.8 %copy-start.2 = (bf16[192,512]{1,0:T(8,128)(2,1)}, bf16[192,512]{1,0:T(8,128)(2,1)S(1)}, u32[]{:S(2)}) copy-start(bf16[192,512]{1,0:T(8,128)(2,1)S(1)} %collective-permute-done.5.refs_3_.l_ref) | copy-start | bytes 589828
  21.0 0.8 %copy-start.4 = (bf16[192,512]{1,0:T(8,128)(2,1)}, bf16[192,512]{1,0:T(8,128)(2,1)S(1)}, u32[]{:S(2)}) copy-start(bf16[192,512]{1,0:T(8,128)(2,1)S(1)} %collective-permute-done.6.refs_4_.or_ref) | copy-start | bytes 589828
  21.9 6.3 %copy-start.9 = (f32[8,768]{1,0:T(8,128)}, f32[8,768]{1,0:T(8,128)S(1)}, u32[]{:S(2)}) copy-start(f32[8,768]{1,0:T(8,128)S(1)} %get-tuple-element.33.refs_0_.stat_ref) | copy-start | bytes 73732
  24.6 15.2 %collective-permute-start.10 = (bf16[960,256]{1,0:T(8,128)(2,1)S(1)}, bf16[960,256]{1,0:T(8,128)(2,1)S(1)}, u32[]{:S(2)}, u32[]{:S(2)}) collective-permute-start(bf16[960,256]{1,0:T(8,128)(2,1)S(1)} %join_slots.1.own_ref), channel_id=1, source_target_pairs={{0,8},{8,0},{16,24},{24,16},{32,40},{40,32},{48,56},{56,48},{64,72... | collective-permute-start | bytes 1474568 | tf_op jit(solution)/shard_map/ppermute | solution.py:357
  28.2 14.4 %collective-permute-start.8 = (bf16[192,512]{1,0:T(8,128)(2,1)S(1)}, bf16[192,512]{1,0:T(8,128)(2,1)S(1)}, u32[]{:S(2)}, u32[]{:S(2)}) collective-permute-start(bf16[192,512]{1,0:T(8,128)(2,1)S(1)} %collective-permute-done.4.refs_2_.r_ref), channel_id=1, source_target_pairs={{0,2},{1,3},{2,4},{3,5},{4,6},{5,7},{6,0},{7,1},{8,10},{9,11},{10,... | collective-permute-start | bytes 589832 | tf_op jit(solution)/shard_map/ppermute | solution.py:357
  28.7 13.9 %collective-permute-start.9 = (bf16[192,512]{1,0:T(8,128)(2,1)}, bf16[192,512]{1,0:T(8,128)(2,1)S(1)}, u32[]{:S(2)}, u32[]{:S(2)}) collective-permute-start(bf16[192,512]{1,0:T(8,128)(2,1)} %collective-permute-done.7.refs_5_.ol_ref), channel_id=1, source_target_pairs={{0,6},{1,7},{2,0},{3,1},{4,2},{5,3},{6,4},{7,5},{8,14},{9,15},{10,... | collective-permute-start | bytes 589832 | tf_op jit(solution)/shard_map/ppermute | solution.py:357
  30.9 0.9 %copy-start.1 = (bf16[192,512]{1,0:T(8,128)(2,1)S(1)}, bf16[192,512]{1,0:T(8,128)(2,1)}, u32[]{:S(2)}) copy-start(bf16[192,512]{1,0:T(8,128)(2,1)} %copy-done) | copy-start | bytes 589828
  31.8 0.9 %copy-start.3 = (bf16[192,512]{1,0:T(8,128)(2,1)S(1)}, bf16[192,512]{1,0:T(8,128)(2,1)}, u32[]{:S(2)}) copy-start(bf16[192,512]{1,0:T(8,128)(2,1)} %copy-done.2) | copy-start | bytes 589828
  32.7 0.9 %copy-start.5 = (bf16[192,512]{1,0:T(8,128)(2,1)S(1)}, bf16[192,512]{1,0:T(8,128)(2,1)}, u32[]{:S(2)}) copy-start(bf16[192,512]{1,0:T(8,128)(2,1)} %copy-done.4) | copy-start | bytes 589828
  33.6 0.7 %copy-start.7 = (s32[8,768]{1,0:T(8,128)S(1)}, s32[8,768]{1,0:T(8,128)}, u32[]{:S(2)}) copy-start(s32[8,768]{1,0:T(8,128)} %copy-done.6) | copy-start | bytes 73732
  34.4 0.7 %copy-start.10 = (f32[8,768]{1,0:T(8,128)S(1)}, f32[8,768]{1,0:T(8,128)}, u32[]{:S(2)}) copy-start(f32[8,768]{1,0:T(8,128)} %copy-done.9) | copy-start | bytes 73732
  35.1 4.7 %copy-start.8 = (s32[8,768]{1,0:T(8,128)S(1)}, s32[8,768]{1,0:T(8,128)}, u32[]{:S(2)}) copy-start(s32[8,768]{1,0:T(8,128)} %copy-done.6) | copy-start | bytes 73732
  43.8 3.9 %collective-permute-start.11 = (bf16[384,256]{1,0:T(8,128)(2,1)S(1)}, bf16[384,256]{1,0:T(8,128)(2,1)S(1)}, u32[]{:S(2)}, u32[]{:S(2)}) collective-permute-start(bf16[384,256]{1,0:T(8,128)(2,1)S(1)} %get-tuple-element.49), channel_id=1, source_target_pairs={{0,8},{8,0},{16,24},{24,16},{32,40},{40,32},{48,56},{56,48},{64,72... | collective-permute-start | bytes 589832 | tf_op jit(solution)/shard_map/ppermute | solution.py:357
  46.6 5.1 %collective-permute-start.12 = (bf16[576,256]{1,0:T(8,128)(2,1)S(1)}, bf16[576,256]{1,0:T(8,128)(2,1)S(1)}, u32[]{:S(2)}, u32[]{:S(2)}) collective-permute-start(bf16[576,256]{1,0:T(8,128)(2,1)S(1)} %get-tuple-element.53), channel_id=1, source_target_pairs={{0,8},{8,0},{16,24},{24,16},{32,40},{40,32},{48,56},{56,48},{64,72... | collective-permute-start | bytes 884744 | tf_op jit(solution)/shard_map/ppermute | solution.py:357
  47.7 4.0 %collective-permute-start.13 = (bf16[192,256]{1,0:T(8,128)(2,1)S(1)}, bf16[192,256]{1,0:T(8,128)(2,1)S(1)}, u32[]{:S(2)}, u32[]{:S(2)}) collective-permute-start(bf16[192,256]{1,0:T(8,128)(2,1)S(1)} %get-tuple-element.54), channel_id=1, source_target_pairs={{0,16},{8,24},{16,0},{24,8},{32,48},{40,56},{48,32},{56,40},{64,80... | collective-permute-start | bytes 294920 | tf_op jit(solution)/shard_map/ppermute | solution.py:357
  51.8 3.6 %collective-permute-start.14 = (bf16[192,256]{1,0:T(8,128)(2,1)S(1)}, bf16[192,256]{1,0:T(8,128)(2,1)S(1)}, u32[]{:S(2)}, u32[]{:S(2)}) collective-permute-start(bf16[192,256]{1,0:T(8,128)(2,1)S(1)} %get-tuple-element.56), channel_id=1, source_target_pairs={{0,16},{8,24},{16,0},{24,8},{32,48},{40,56},{48,32},{56,40},{64,80... | collective-permute-start | bytes 294920 | tf_op jit(solution)/shard_map/ppermute | solution.py:357
  53.1 6.7 %collective-permute-start.16 = (bf16[192,256]{1,0:T(8,128)(2,1)S(1)}, bf16[192,256]{1,0:T(8,128)(2,1)S(1)}, u32[]{:S(2)}, u32[]{:S(2)}) collective-permute-start(bf16[192,256]{1,0:T(8,128)(2,1)S(1)} %relay_far.1.after), channel_id=1, source_target_pairs={{0,192},{8,200},{16,208},{24,216},{32,224},{40,232},{48,240},{56,2... | collective-permute-start | bytes 294920 | tf_op jit(solution)/shard_map/ppermute | solution.py:357
  55.4 6.6 %collective-permute-start.15 = (bf16[192,256]{1,0:T(8,128)(2,1)S(1)}, bf16[192,256]{1,0:T(8,128)(2,1)S(1)}, u32[]{:S(2)}, u32[]{:S(2)}) collective-permute-start(bf16[192,256]{1,0:T(8,128)(2,1)S(1)} %get-tuple-element.58), channel_id=1, source_target_pairs={{0,224},{8,232},{16,240},{24,248},{32,0},{40,8},{48,16},{56,24},{6... | collective-permute-start | bytes 294920 | tf_op jit(solution)/shard_map/ppermute | solution.py:357

commit v6 on v4

--- a/solution.py
+++ b/solution.py
@@ -15,6 +15,7 @@
 SLOTS = REACH + 1
 PLANE = 4
 BLOCK = 512
+STAT = 3 * ROWS
 NEG = -1e30
 FLOOR = -1e20
 SCALE = D**-0.5
@@ -31,7 +32,8 @@
         dst[h * ROWS : (h + 1) * ROWS, :] = src[:, h * D : (h + 1) * D]
 
 
-def prepare(place_ref, len_hbm, q_hbm, q4_ref, bound_ref, len_ref, sems):
+def prepare(place_ref, len_hbm, q_hbm, *refs):
+    q4_ref, bound_ref, len_ref, sems = refs[-4:]
     copies = [pltpu.make_async_copy(len_hbm, len_ref, sems.at[0])]
     for h in range(HEADS):
         rows, cols = pl.ds(h * ROWS, ROWS), pl.ds(h * D, D)
@@ -48,8 +50,8 @@
     for d in range(len_ref.shape[0]):
         end = end + len_ref[d]
         start = jnp.where(end <= pos, end, start)
-    bound_ref[0:1, :] = pos
-    bound_ref[1:2, :] = start
+    bound_ref[0:1, :] = pos.astype(jnp.float32)
+    bound_ref[1:2, :] = start.astype(jnp.float32)
     for copy in copies[1:]:
         copy.wait()
 
@@ -76,12 +78,11 @@
         out_ref[m * ROWS : (m + 1) * ROWS, :] = part
 
 
-def score(kv, queries, row, base, bound_ref, diagonal):
+def score(kv, queries, row, base, start, pos=None):
     s = dot(kv[:, :D], queries, 1, 1) * (SCALE * LOG2E)
-    key = row + base * ROWS
-    visible = key >= bound_ref[1:2, :]
-    if diagonal:
-        visible = visible & (key <= bound_ref[0:1, :])
+    visible = row >= start - base * ROWS
+    if pos is not None:
+        visible = visible & (row <= pos - base * ROWS)
     return jnp.where(visible, s, NEG)
 
 
@@ -93,20 +94,22 @@
 
 
 def near_kernel(place_ref, z2_ref, z1_ref, z0_ref, q4_ref, bound_ref, *refs):
-    s_ref, stat_ref = refs[-2:]
+    s_ref = refs[-1]
     me = place_ref[0]
     queries = q4_ref[...]
     row = lax.broadcasted_iota(jnp.int32, (ROWS, LANES), 0)
-    s = score(z0_ref[...], queries, row, me, bound_ref, True)
-    s_ref[2 * ROWS :, :] = s
+    pos, start = bound_ref[0:1, :].astype(jnp.int32), bound_ref[1:2, :].astype(jnp.int32)
+    s = score(z0_ref[...], queries, row, me, start, pos)
+    s_ref[2 * ROWS : 3 * ROWS, :] = s
     top = jnp.max(s, axis=0, keepdims=True)
     state = (top, jnp.sum(jnp.exp2(s - top), axis=0, keepdims=True))
     for i, ref in ((1, z1_ref), (0, z2_ref)):
-        s = score(ref[...], queries, row, me - PLANE * (2 - i), bound_ref, False)
+        s = score(ref[...], queries, row, me - PLANE * (2 - i), start)
         s_ref[i * ROWS : (i + 1) * ROWS, :] = s
         state = online(s, state)
-    stat_ref[0:1, :] = state[0]
-    stat_ref[1:2, :] = state[1]
+    s_ref[STAT : STAT + 1, :] = state[0]
+    s_ref[STAT + 1 : STAT + 2, :] = state[1]
+    s_ref[STAT + 2 : STAT + 3, :] = bound_ref[1:2, :]
 
 
 def rows(i):
@@ -142,27 +145,31 @@
     return at + 1 - 2 * lax.rem(at, 2) if flip else at
 
 
-def middle_kernel(place_ref, head_ref, own_ref, q4_ref, bound_ref, s_ref, stat_ref, g_hbm, w_hbm, y_ref, r_ref, l_ref, or_ref, ol_ref, p_ref, o_ref, log_ref, acc_ref, tail_ref, s_side, g_ref, w_ref, sems):
+def middle_kernel(place_ref, head_ref, own_ref, q4_ref, s_ref, g_hbm, w_hbm, y_hbm, l_hbm, r_ref, or_ref, ol_ref, p_ref, o_ref, acc_ref, tail_ref, s_side, g_ref, y_ref, l_ref, w_ref, sems):
     head = head_ref[0]
     tails = (source_of(head, 4, False), source_of(head, 4, True))
     copies = [pltpu.make_async_copy(w_hbm, w_ref, sems.at[0]), pltpu.make_async_copy(g_hbm, g_ref, sems.at[1])]
+    copies += [pltpu.make_async_copy(y_hbm, y_ref, sems.at[2]), pltpu.make_async_copy(l_hbm, l_ref, sems.at[3])]
     for i, source in enumerate(tails):
         cols = pl.ds(pl.multiple_of(source * BLOCK, BLOCK), BLOCK)
-        copies.append(pltpu.make_async_copy(w_hbm.at[:, cols], tail_ref.at[:, pl.ds(i * BLOCK, BLOCK)], sems.at[2 + i]))
+        copies.append(pltpu.make_async_copy(w_hbm.at[:, cols], tail_ref.at[:, pl.ds(i * BLOCK, BLOCK)], sems.at[4 + i]))
     for copy in copies:
         copy.start()
 
     queries = q4_ref[...]
     row = lax.broadcasted_iota(jnp.int32, (ROWS, LANES), 0)
 
+    start = s_ref[STAT + 2 : STAT + 3, :].astype(jnp.int32)
+
     def side(i, state):
         slot = 2 * i + 1
-        s = score(own_ref[rows(slot), :], queries, row, place_ref[0] + 2 * (slot - REACH), bound_ref, False)
+        s = score(own_ref[rows(slot), :], queries, row, place_ref[0] + 2 * (slot - REACH), start)
         s_side[rows(i), :] = s
         return online(s, state)
 
-    log_total = close(lax.fori_loop(0, 2, side, (stat_ref[0:1, :], stat_ref[1:2, :])))
-    log_ref[0:1, :] = log_total
+    log_total = close(lax.fori_loop(0, 2, side, (s_ref[STAT : STAT + 1, :], s_ref[STAT + 1 : STAT + 2, :])))
+    o_ref[D : D + 1, :] = log_total
+    o_ref[D + 1 : D + 2, :] = s_ref[STAT + 2 : STAT + 3, :]
 
     def weigh_main(i, state):
         prob, state = weigh(s_ref[rows(i), :], log_total, own_ref[rows(2 * i), D:], state)
@@ -175,7 +182,7 @@
         return state
 
     acc, mass = lax.fori_loop(0, 2, weigh_side, lax.fori_loop(0, 3, weigh_main, no_weight()))
-    o_ref[...] = acc / mass
+    o_ref[:D, :] = acc / mass
     for copy in copies:
         copy.wait()
     sources = (head, source_of(head, 0, True), source_of(head, -2, False), source_of(head, 2, False))
@@ -183,16 +190,18 @@
     acc_ref[...] = project(None, (g_ref, y_ref, r_ref, l_ref, or_ref, ol_ref), sources, w_ref)
 
 
-def across_kernel(place_ref, par_ref, q4_ref, bound_ref, o_own_ref, log_ref, p_ref, o_ref, f_ref, s_par):
+def across_kernel(place_ref, par_ref, q4_ref, o_own_ref, p_ref, o_ref, s_par):
     me = place_ref[0]
     core = lax.rem(me, 2)
     chip = me - core
     queries = q4_ref[...]
     row = lax.broadcasted_iota(jnp.int32, (ROWS, LANES), 0)
 
+    start = o_own_ref[D + 1 : D + 2, :].astype(jnp.int32)
+
     def across(i, state):
         slot = i + core
-        s = score(par_ref[rows(slot), :], queries, row, chip + 1 - core + 2 * (slot - REACH), bound_ref, False)
+        s = score(par_ref[rows(slot), :], queries, row, chip + 1 - core + 2 * (slot - REACH), start)
         s_par[rows(i), :] = s
         return online(s, state)
 
@@ -205,14 +214,14 @@
         return state
 
     acc, mass = lax.fori_loop(0, REACH, weigh_across, no_weight())
-    log_own = log_ref[0:1, :]
+    log_own = o_own_ref[D : D + 1, :]
     top = jnp.maximum(log_own, log_par)
     own, par = jnp.exp2(log_own - top), jnp.exp2(log_par - top)
     both = own + par
     own, par = own / both, par / both
-    f_ref[0:1, :] = own
-    f_ref[1:2, :] = par
-    o_ref[...] = o_own_ref[...] * own + acc * (par / jnp.maximum(mass, 0.5))
+    o_ref[D : D + 1, :] = own
+    o_ref[D + 1 : D + 2, :] = par
+    o_ref[:D, :] = o_own_ref[:D, :] * own + acc * (par / jnp.maximum(mass, 0.5))
 
 
 def back_block(kv_ref, slot, p_ref, i, g4, q4, rd, share):
@@ -231,7 +240,7 @@
     out_ref[at, D:] = dv.astype(out_ref.dtype)
 
 
-def cross_far(place_ref, a_ref, b_ref, early_ref, w_ref, q4_ref, par_ref, p_ref, o_ref, f_ref, out_ref, g_ref, rd_ref, dq_ref):
+def cross_far(place_ref, a_ref, b_ref, early_ref, w_ref, q4_ref, par_ref, p_ref, o_ref, out_ref, g_ref, dq_ref):
     core = lax.rem(place_ref[0], 2)
     acc = project(early_ref[...], (a_ref, b_ref), (0, 1), w_ref)
     acc = acc.astype(jnp.bfloat16)
@@ -239,27 +248,29 @@
         g_ref[h * ROWS : (h + 1) * ROWS, :] = acc[:, h * D : (h + 1) * D]
     g4 = g_ref[...]
     gt = jnp.transpose(g4.astype(jnp.float32))
-    rd = jnp.sum(gt * o_ref[...], axis=0, keepdims=True)
-    rd_ref[...] = rd
-    dq_ref[...] = jnp.zeros((D, LANES), jnp.float32)
+    rd = jnp.sum(gt * o_ref[:D, :], axis=0, keepdims=True)
+    dq_ref[:D, :] = jnp.zeros((D, LANES), jnp.float32)
+    dq_ref[D : D + 1, :] = o_ref[D : D + 1, :]
+    dq_ref[D + 1 : D + 2, :] = o_ref[D + 1 : D + 2, :]
+    dq_ref[D + 2 : D + 3, :] = rd
 
     @pl.when(core == 1)
     def _():
         out_ref[:ROWS, :] = jnp.zeros((ROWS, 2 * D), out_ref.dtype)
 
     def step(slot, _):
-        dk, dv, dq = back_block(par_ref, slot, p_ref, slot - core, g4, q4_ref[...], rd, f_ref[1:2, :])
+        dk, dv, dq = back_block(par_ref, slot, p_ref, slot - core, g4, q4_ref[...], rd, dq_ref[D + 1 : D + 2, :])
         put(out_ref, slot, dk, dv)
-        dq_ref[...] += dq
+        dq_ref[:D, :] += dq
         return 0
 
     lax.fori_loop(core, 2, step, 0)
 
 
-def cross_near(place_ref, q4_ref, par_ref, p_ref, g_ref, rd_ref, f_ref, dq_in_ref, out_ref, dq_ref):
+def cross_near(place_ref, q4_ref, par_ref, p_ref, g_ref, dq_in_ref, out_ref, dq_ref):
     core = lax.rem(place_ref[0], 2)
     g4 = g_ref[...]
-    rd = rd_ref[...]
+    rd = dq_in_ref[D + 2 : D + 3, :]
     dq_ref[...] = dq_in_ref[...]
 
     @pl.when(core == 0)
@@ -267,35 +278,35 @@
         out_ref[2 * ROWS :, :] = jnp.zeros((ROWS, 2 * D), out_ref.dtype)
 
     def step(slot, _):
-        dk, dv, dq = back_block(par_ref, slot, p_ref, slot - core, g4, q4_ref[...], rd, f_ref[1:2, :])
+        dk, dv, dq = back_block(par_ref, slot, p_ref, slot - core, g4, q4_ref[...], rd, dq_ref[D + 1 : D + 2, :])
         put(out_ref, slot - 2, dk, dv)
-        dq_ref[...] += dq
+        dq_ref[:D, :] += dq
         return 0
 
     lax.fori_loop(2, REACH + core, step, 0)
 
 
-def own_far(q4_ref, own_ref, p_ref, g_ref, rd_ref, f_ref, dq_in_ref, out_ref, dq_ref):
+def own_far(q4_ref, own_ref, p_ref, g_ref, dq_in_ref, out_ref, dq_ref):
     g4 = g_ref[...]
-    rd = rd_ref[...]
+    rd = dq_in_ref[D + 2 : D + 3, :]
     dq_ref[...] = dq_in_ref[...]
 
     def step(slot, _):
-        dk, dv, dq = back_block(own_ref, slot, p_ref, slot, g4, q4_ref[...], rd, f_ref[0:1, :])
+        dk, dv, dq = back_block(own_ref, slot, p_ref, slot, g4, q4_ref[...], rd, dq_ref[D : D + 1, :])
         put(out_ref, slot, dk, dv)
-        dq_ref[...] += dq
+        dq_ref[:D, :] += dq
         return 0
 
     lax.fori_loop(0, 2, step, 0)
 
 
-def own_near(q4_ref, own_ref, p_ref, g_ref, rd_ref, f_ref, dq_in_ref, after, out_ref, dq_out_ref, acc):
+def own_near(q4_ref, own_ref, p_ref, g_ref, dq_in_ref, after, out_ref, dq_out_ref, acc):
     g4 = g_ref[...]
-    rd = rd_ref[...]
-    acc[...] = dq_in_ref[...]
+    rd = dq_in_ref[D + 2 : D + 3, :]
+    acc[...] = dq_in_ref[:D, :]
 
     def step(slot, _):
-        dk, dv, dq = back_block(own_ref, slot, p_ref, slot, g4, q4_ref[...], rd, f_ref[0:1, :])
+        dk, dv, dq = back_block(own_ref, slot, p_ref, slot, g4, q4_ref[...], rd, dq_in_ref[D : D + 1, :])
         put(out_ref, slot - 2, dk, dv)
         acc[...] += dq
         return 0
@@ -350,7 +361,7 @@
 
 
 def params(mib):
-    return pltpu.CompilerParams(vmem_limit_bytes=mib * MIB)
+    return pltpu.CompilerParams(vmem_limit_bytes=10 * MIB)
 
 
 def moved(x, axis, to):
@@ -401,80 +412,81 @@
     q4, bound = call(
         "prepare",
         prepare,
-        (shape(LANES, D, bf16), shape(8, LANES, jnp.int32)),
-        smem(1) + hbm(2),
+        (shape(LANES, D, bf16), shape(8, LANES, f32)),
+        smem(1) + hbm(2) + token(3),
         4,
-        (place, pinned(lengths), pinned(queries)),
+        (place, pinned(lengths), pinned(queries), other, right, left),
         [pltpu.SMEM((lengths.shape[0],), jnp.int32), dma((1 + HEADS,))],
     )
     picked = call("pick_side", pick_kernel, shape(2 * ROWS, 2 * D, bf16), smem(1) + vmem(3) + token(1), 4, (place, z2, z1, kv, q4))
     side = moved(picked, "ctx", lambda i: i ^ 2)
-    s_near, stat = call(
+    s_near = call(
         "near_scores",
         near_kernel,
-        (shape(3 * ROWS, LANES, f32), shape(8, LANES, f32)),
-        smem(1) + vmem(5) + token(4),
+        shape(STAT + 8, LANES, f32),
+        smem(1) + vmem(5) + token(3),
         8,
-        (place, z2, z1, kv, q4, bound, picked, other, right, left),
-    )
-    own = call("join_slots", join_kernel, shape(SLOTS * ROWS, 2 * D, bf16), vmem(4) + token(3), 4, (z2, z1, kv, side, stat, other_right, other_left))
+        (place, z2, z1, kv, q4, bound, picked, other_right, other_left),
+    )
+    own = call("join_slots", join_kernel, shape(SLOTS * ROWS, 2 * D, bf16), vmem(4) + token(1), 4, (z2, z1, kv, side, s_near))
     par = moved(own, "ctx", lambda i: i ^ 1)
 
-    p_own, o_own, log_own, early, tail = call(
+    p_own, o_own, early, tail = call(
         "middle",
         middle_kernel,
         (
             shape(SLOTS * ROWS, LANES, bf16),
-            shape(D, LANES, f32),
-            shape(8, LANES, f32),
+            shape(D + 8, LANES, f32),
             shape(ROWS, HEADS * D, f32),
             shape(HEADS * D, 2 * BLOCK, bf16),
         ),
-        smem(2) + vmem(5) + hbm(2) + vmem(5),
+        smem(2) + vmem(3) + hbm(4) + vmem(3),
         16,
-        (place, head, own, q4, bound, s_near, stat, pinned(grad_out), pinned(out_weight), other, right, left, other_right, other_left),
+        (place, head, own, q4, s_near, pinned(grad_out), pinned(out_weight), pinned(other), pinned(left), right, other_right, other_left),
         [
             pltpu.VMEM((2 * ROWS, LANES), f32),
             pltpu.VMEM((ROWS, BLOCK), bf16),
+            pltpu.VMEM((ROWS, BLOCK), bf16),
+            pltpu.VMEM((ROWS, BLOCK), bf16),
             pltpu.VMEM((HEADS * D, 8 * BLOCK), bf16),
-            dma((4,)),
+            dma((6,)),
         ],
     )
-    p_par, out_t, share = call(
+    p_par, out_t = call(
         "across",
         across_kernel,
-        (shape(REACH * ROWS, LANES, bf16), shape(D, LANES, f32), shape(8, LANES, f32)),
-        smem(1) + vmem(5),
+        (shape(REACH * ROWS, LANES, bf16), shape(D + 8, LANES, f32)),
+        smem(1) + vmem(3),
         12,
-        (place, par, q4, bound, o_own, log_own),
+        (place, par, q4, o_own),
         [pltpu.VMEM((REACH * ROWS, LANES), f32)],
     )
 
-    far_cross, g4, rd, dq = call(
+    far_cross, g4, dq = call(
         "cross_far",
         cross_far,
-        (shape(2 * ROWS, 2 * D, bf16), shape(LANES, D, bf16), shape(1, LANES, f32), shape(D, LANES, f32)),
-        smem(1) + vmem(9),
+        (shape(2 * ROWS, 2 * D, bf16), shape(LANES, D, bf16), shape(D + 8, LANES, f32)),
+        smem(1) + vmem(8),
         10,
-        (place, far, other_far, early, tail, q4, par, p_par, out_t, share),
+        (place, far, other_far, early, tail, q4, par, p_par, out_t),
     )
     far_back = moved(far_cross, "ctx", lambda i: i ^ 1)
     near_cross, dq = call(
         "cross_near",
         cross_near,
-        (shape(3 * ROWS, 2 * D, bf16), shape(D, LANES, f32)),
-        smem(1) + vmem(7),
+        (shape(3 * ROWS, 2 * D, bf16), shape(D + 8, LANES, f32)),
+        smem(1) + vmem(5),
         10,
-        (place, q4, par, p_par, g4, rd, share, dq),
+        (place, q4, par, p_par, g4, dq),
     )
     near_back = moved(near_cross, "ctx", lambda i: i ^ 1)
     far_own, dq = call(
         "own_far",
         own_far,
-        (shape(2 * ROWS, 2 * D, f32), shape(D, LANES, f32)),
-        vmem(7),
+        (shape(2 * ROWS, 2 * D, f32), shape(D + 8, LANES, f32)),
+        vmem(5),
         10,
-        (q4, own, p_own, g4, rd, share, dq),
+        (q4, own, p_own, g4, dq),
     )
     far_keep, far_side = call(
         "settle_far", settle_far, (shape(ROWS, 2 * D, f32), shape(ROWS, 2 * D, bf16)), vmem(2), 4, (far_own, far_back)
@@ -484,9 +496,9 @@
         "own_near",
         own_near,
         (shape(3 * ROWS, 2 * D, f32), shape(ROWS, HEADS * D, bf16)),
-        vmem(7) + token(1),
+        vmem(5) + token(1),
         10,
-        (q4, own, p_own, g4, rd, share, dq, far_keep),
+        (q4, own, p_own, g4, dq, far_keep),
         [pltpu.VMEM((D, LANES), f32)],
     )
     to_two = call("relay_far", relay_far, shape(ROWS, 2 * D, bf16), smem(1) + vmem(2), 4, (place, far_keep, far_side))

time: 61.5 us -> 58 us (0.943)
  the two profiles are of different devices: /device:TPU:1 before, /device:TPU:8 now
where the time goes in v6:
time: 58 us; the launch traced here: 57.8 us
  starting transfers between devices  26.5 us (46%)
  Pallas kernels  16.4 us (28%)
  waiting for transfers between devices  12.5 us (22%)
  other arithmetic  0.87 us (2%)
  between operations  0.8 us (1%)
  local copies, waits for them, and re-layouts  0.65 us (1%)
    ppermute x17, starting transfers between devices, moved(): lax.ppermute(x, axis, [(i, to(i)) for i in range(lax.axis_size(axis))])  26.5 us
    pallas_call x14, Pallas kernels, call(): pl.pallas_call(kernel, out_shape=outs, in_specs=ins, out_specs=vmem(1)[0]...  16.4 us
    ppermute x17, waiting for transfers between devices, moved(): lax.ppermute(x, axis, [(i, to(i)) for i in range(lax.axis_size(axis))])  12.5 us
  transfers between devices with their start and end apart: 17, of which 7 were waited for; matrix products, arithmetic and copies ran while one was open for 1% of the time, Pallas kernels for 24%

profile of v6, /device:TPU:8, one launch (start us, length us, event | category | flops | bytes accessed | tf_op | source)
XLA Modules:
  0.0 57.8 jit_solution(3916355438927647995)
XLA Ops:
  0.6 2.4 %collective-permute-start = (bf16[192,512]{1,0:T(8,128)(2,1)}, bf16[192,512]{1,0:T(8,128)(2,1)S(1)}, u32[]{:S(2)}, u32[]{:S(2)}) collective-permute-start(bf16[192,512]{1,0:T(8,128)(2,1)} %g_hbm.1), channel_id=1, source_target_pairs={{0,1},{1,0},{2,3},{3,2},{4,5},{5,4},{6,7},{7,6},{8,9},{9,8},{10,11... | collective-permute-start | bytes 589832 | tf_op jit(solution)/shard_map/ppermute | solution.py:368
  3.0 1.5 %collective-permute-start.1 = (bf16[192,512]{1,0:T(8,128)(2,1)}, bf16[192,512]{1,0:T(8,128)(2,1)}, u32[]{:S(2)}, u32[]{:S(2)}) collective-permute-start(bf16[192,512]{1,0:T(8,128)(2,1)} %g_hbm.1), channel_id=1, source_target_pairs={{0,2},{1,3},{2,4},{3,5},{4,6},{5,7},{6,0},{7,1},{8,10},{9,11},{10,... | collective-permute-start | bytes 589832 | tf_op jit(solution)/shard_map/ppermute | solution.py:368
  4.5 1.7 %collective-permute-start.2 = (bf16[192,512]{1,0:T(8,128)(2,1)}, bf16[192,512]{1,0:T(8,128)(2,1)S(1)}, u32[]{:S(2)}, u32[]{:S(2)}) collective-permute-start(bf16[192,512]{1,0:T(8,128)(2,1)} %g_hbm.1), channel_id=1, source_target_pairs={{0,6},{1,7},{2,0},{3,1},{4,2},{5,3},{6,4},{7,5},{8,14},{9,15},{10,... | collective-permute-start | bytes 589832 | tf_op jit(solution)/shard_map/ppermute | solution.py:368
  6.2 0.8 %pad_add_fusion.z0_ref = bf16[192,256]{1,0:T(8,128)(2,1)S(1)} fusion(bf16[192,128]{1,0:T(8,128)(2,1)} %param.8, bf16[192,128]{1,0:T(8,128)(2,1)} %param.7), kind=kLoop, calls=%fused_computation.1 | loop fusion | flops 196608 | bytes 196608 | tf_op jit(solution)/shard_map/add | solution.py:404
  7.1 3.3 %collective-permute-start.3 = (bf16[192,256]{1,0:T(8,128)(2,1)S(1)}, bf16[192,256]{1,0:T(8,128)(2,1)S(1)}, u32[]{:S(2)}, u32[]{:S(2)}) collective-permute-start(bf16[192,256]{1,0:T(8,128)(2,1)S(1)} %pad_add_fusion.z0_ref), channel_id=1, source_target_pairs={{0,64},{8,72},{16,80},{24,88},{32,96},{40,104},{48,112},{56,120},{... | collective-permute-start | bytes 294920 | tf_op jit(solution)/shard_map/ppermute | solution.py:368
  10.4 1.9 %collective-permute-start.4 = (bf16[192,256]{1,0:T(8,128)(2,1)S(1)}, bf16[192,256]{1,0:T(8,128)(2,1)S(1)}, u32[]{:S(2)}, u32[]{:S(2)}) collective-permute-start(bf16[192,256]{1,0:T(8,128)(2,1)S(1)} %pad_add_fusion.z0_ref), channel_id=1, source_target_pairs={{0,32},{8,40},{16,48},{24,56},{32,64},{40,72},{48,80},{56,88},{64,... | collective-permute-start | bytes 294920 | tf_op jit(solution)/shard_map/ppermute | solution.py:368
  12.4 0.3 collective-permute-start.6
  12.6 3.0 %collective-permute-start.7 = (bf16[192,512]{1,0:T(8,128)(2,1)S(1)}, bf16[192,512]{1,0:T(8,128)(2,1)S(1)}, u32[]{:S(2)}, u32[]{:S(2)}) collective-permute-start(bf16[192,512]{1,0:T(8,128)(2,1)S(1)} %collective-permute-done.refs_0_.y_hbm), channel_id=1, source_target_pairs={{0,6},{1,7},{2,0},{3,1},{4,2},{5,3},{6,4},{7,5},{8,14},{9,15},{10,... | collective-permute-start | bytes 589832 | tf_op jit(solution)/shard_map/ppermute | solution.py:368
  15.6 1.0 %prepare.1 = (bf16[768,128]{1,0:T(8,128)(2,1)S(1)}, f32[8,768]{1,0:T(8,128)S(1)}) custom-call(s32[1]{0:T(128)} %bitcast.place_ref, s32[8]{0:T(128)} %len_hbm.1, bf16[192,512]{1,0:T(8,128)(2,1)} %q_hbm.1, bf16[192,512]{1,0:T(8,128)(2,1)S(1)} %collective-permute-done.refs_0_.y_hbm, bf16[192,512]{1,0:T(8,128)(2,1)} %collective-permute-done.1.refs_1_.r_ref, ...), custom_call_target="tpu_custom_call" | custom-call | flops 1 | bytes 1 | tf_op jit(solution)/shard_map/prepare/pallas_call | solution.py:382
  16.6 1.5 %collective-permute-done.3.z2_ref = bf16[192,256]{1,0:T(8,128)(2,1)S(1)} collective-permute-done((bf16[192,256]{1,0:T(8,128)(2,1)S(1)}, bf16[192,256]{1,0:T(8,128)(2,1)S(1)}, u32[]{:S(2)}, u32[]{:S(2)}) %collective-permute-start.3) | collective-permute-done | bytes 98336 | tf_op jit(solution)/shard_map/ppermute | solution.py:368
  18.1 1.1 %collective-permute-done.4.z1_ref = bf16[192,256]{1,0:T(8,128)(2,1)S(1)} collective-permute-done((bf16[192,256]{1,0:T(8,128)(2,1)S(1)}, bf16[192,256]{1,0:T(8,128)(2,1)S(1)}, u32[]{:S(2)}, u32[]{:S(2)}) %collective-permute-start.4) | collective-permute-done | bytes 98336 | tf_op jit(solution)/shard_map/ppermute | solution.py:368
  19.2 1.4 %collective-permute-start.5 = (bf16[384,256]{1,0:T(8,128)(2,1)S(1)}, bf16[384,256]{1,0:T(8,128)(2,1)S(1)}, u32[]{:S(2)}, u32[]{:S(2)}) collective-permute-start(bf16[384,256]{1,0:T(8,128)(2,1)S(1)} %pick_side.1.refs_0_), channel_id=1, source_target_pairs={{0,16},{8,24},{16,0},{24,8},{32,48},{40,56},{48,32},{56,40},{64,80... | collective-permute-start | bytes 589832 | tf_op jit(solution)/shard_map/ppermute | solution.py:368
  20.6 0.8 %near_scores.1.refs_0_.s_ref = f32[584,768]{1,0:T(8,128)S(1)} custom-call(s32[1]{0:T(128)} %bitcast.place_ref, bf16[192,256]{1,0:T(8,128)(2,1)S(1)} %collective-permute-done.3.z2_ref, bf16[192,256]{1,0:T(8,128)(2,1)S(1)} %collective-permute-done.4.z1_ref, bf16[192,256]{1,0:T(8,128)(2,1)S(1)} %pad_add_fusion.z0_ref, ...), custom_call_target="tpu_custom_call" | custom-call | flops 1 | bytes 1 | tf_op jit(solution)/shard_map/near_scores/pallas_call | solution.py:382
  21.5 4.0 %collective-permute-done.5.side_ref = bf16[384,256]{1,0:T(8,128)(2,1)S(1)} collective-permute-done((bf16[384,256]{1,0:T(8,128)(2,1)S(1)}, bf16[384,256]{1,0:T(8,128)(2,1)S(1)}, u32[]{:S(2)}, u32[]{:S(2)}) %collective-permute-start.5) | collective-permute-done | bytes 196640 | tf_op jit(solution)/shard_map/ppermute | solution.py:368
  25.6 0.4 collective-permute-start.8
  26.0 3.0 %collective-permute-start.9 = (bf16[192,512]{1,0:T(8,128)(2,1)S(1)}, bf16[192,512]{1,0:T(8,128)(2,1)}, u32[]{:S(2)}, u32[]{:S(2)}) collective-permute-start(bf16[192,512]{1,0:T(8,128)(2,1)S(1)} %collective-permute-done.7.refs_2_.ol_ref), channel_id=1, source_target_pairs={{0,6},{1,7},{2,0},{3,1},{4,2},{5,3},{6,4},{7,5},{8,14},{9,15},{10,... | collective-permute-start | bytes 589832 | tf_op jit(solution)/shard_map/ppermute | solution.py:368
  29.0 4.8 %middle.1 = (bf16[960,768]{1,0:T(8,128)(2,1)S(1)}, f32[136,768]{1,0:T(8,128)S(1)}, f32[192,512]{1,0:T(8,128)S(1)}, bf16[512,1024]{1,0:T(8,128)(2,1)S(1)}) custom-call(s32[1]{0:T(128)} %bitcast.place_ref, s32[1]{0:T(128)} %bitcast.1.head_ref, bf16[960,256]{1,0:T(8,128)(2,1)S(1)} %join_slots.1.own_ref, bf16[768,128]{1,0:T(8,128)(2,1)S(1)} %get-tuple-element.26.refs_0_.q4_ref, ...), custom_call_target="tpu_custom_call" | custom-call | flops 1 | bytes 1 | tf_op jit(solution)/shard_map/middle/pallas_call | solution.py:382
  33.8 2.7 %across.1 = (bf16[768,768]{1,0:T(8,128)(2,1)S(1)}, f32[136,768]{1,0:T(8,128)S(1)}) custom-call(s32[1]{0:T(128)} %bitcast.place_ref, bf16[960,256]{1,0:T(8,128)(2,1)S(1)} %collective-permute-done.10.par_ref, bf16[768,128]{1,0:T(8,128)(2,1)S(1)} %get-tuple-element.26.refs_0_.q4_ref, f32[136,768]{1,0:T(8,128)S(1)} %get-tuple-element.31.o_own_ref), custom_call_target="tpu_custom_call" | custom-call | flops 1 | bytes 1 | tf_op jit(solution)/shard_map/across/pallas_call | solution.py:382
  36.6 2.6 %cross_far.1 = (bf16[384,256]{1,0:T(8,128)(2,1)S(1)}, bf16[768,128]{1,0:T(8,128)(2,1)S(1)}, f32[136,768]{1,0:T(8,128)S(1)}) custom-call(s32[1]{0:T(128)} %bitcast.place_ref, bf16[192,512]{1,0:T(8,128)(2,1)} %collective-permute-done.8.a_ref, bf16[192,512]{1,0:T(8,128)(2,1)} %collective-permute-done.9.b_ref, f32[192,512]{1,0:T(8,128)S(1)} %get-tuple-element.29.early_ref, ...), custom_call_target="tpu_custom_call" | custom-call | flops 1 | bytes 1 | tf_op jit(solution)/shard_map/cross_far/pallas_call | solution.py:382
  39.4 1.0 %cross_near.1 = (bf16[576,256]{1,0:T(8,128)(2,1)S(1)}, f32[136,768]{1,0:T(8,128)S(1)}) custom-call(s32[1]{0:T(128)} %bitcast.place_ref, bf16[768,128]{1,0:T(8,128)(2,1)S(1)} %get-tuple-element.26.refs_0_.q4_ref, bf16[960,256]{1,0:T(8,128)(2,1)S(1)} %collective-permute-done.10.par_ref, bf16[768,768]{1,0:T(8,128)(2,1)S(1)} %get-tuple-element.32.p_ref, ...), custom_call_target="tpu_custom_call" | custom-call | flops 1 | bytes 1 | tf_op jit(solution)/shard_map/cross_near/pallas_call | solution.py:382
  40.4 1.0 %collective-permute-start.12 = (bf16[576,256]{1,0:T(8,128)(2,1)S(1)}, bf16[576,256]{1,0:T(8,128)(2,1)S(1)}, u32[]{:S(2)}, u32[]{:S(2)}) collective-permute-start(bf16[576,256]{1,0:T(8,128)(2,1)S(1)} %get-tuple-element.43), channel_id=1, source_target_pairs={{0,8},{8,0},{16,24},{24,16},{32,40},{40,32},{48,56},{56,48},{64,72... | collective-permute-start | bytes 884744 | tf_op jit(solution)/shard_map/ppermute | solution.py:368
  41.4 1.0 %own_far.1 = (f32[384,256]{1,0:T(8,128)S(1)}, f32[136,768]{1,0:T(8,128)S(1)}) custom-call(bf16[768,128]{1,0:T(8,128)(2,1)S(1)} %get-tuple-element.26.refs_0_.q4_ref, bf16[960,256]{1,0:T(8,128)(2,1)S(1)} %join_slots.1.own_ref, bf16[960,768]{1,0:T(8,128)(2,1)S(1)} %get-tuple-element.28.p_ref, bf16[768,128]{1,0:T(8,128)(2,1)S(1)} %get-tuple-element.34.g_ref, ...), custom_call_target="tpu_custom_call" | custom-call | flops 1 | bytes 1 | tf_op jit(solution)/shard_map/own_far/pallas_call | solution.py:382
  42.5 1.4 %collective-permute-start.13 = (bf16[192,256]{1,0:T(8,128)(2,1)S(1)}, bf16[192,256]{1,0:T(8,128)(2,1)S(1)}, u32[]{:S(2)}, u32[]{:S(2)}) collective-permute-start(bf16[192,256]{1,0:T(8,128)(2,1)S(1)} %get-tuple-element.44), channel_id=1, source_target_pairs={{0,16},{8,24},{16,0},{24,8},{32,48},{40,56},{48,32},{56,40},{64,80... | collective-permute-start | bytes 294920 | tf_op jit(solution)/shard_map/ppermute | solution.py:368
  43.9 2.3 %own_near.1 = (f32[576,256]{1,0:T(8,128)S(1)}, bf16[192,512]{1,0:T(8,128)(2,1)}) custom-call(bf16[768,128]{1,0:T(8,128)(2,1)S(1)} %get-tuple-element.26.refs_0_.q4_ref, bf16[960,256]{1,0:T(8,128)(2,1)S(1)} %join_slots.1.own_ref, bf16[960,768]{1,0:T(8,128)(2,1)S(1)} %get-tuple-element.28.p_ref, bf16[768,128]{1,0:T(8,128)(2,1)S(1)} %get-tuple-element.34.g_ref, ...), custom_call_target="tpu_custom_call" | custom-call | flops 1 | bytes 1 | tf_op jit(solution)/shard_map/own_near/pallas_call | solution.py:382
  46.2 1.1 %collective-permute-done.13.side_ref.far_ref = bf16[192,256]{1,0:T(8,128)(2,1)S(1)} collective-permute-done((bf16[192,256]{1,0:T(8,128)(2,1)S(1)}, bf16[192,256]{1,0:T(8,128)(2,1)S(1)}, u32[]{:S(2)}, u32[]{:S(2)}) %collective-permute-start.13) | collective-permute-done | bytes 98336 | tf_op jit(solution)/shard_map/ppermute | solution.py:368
  47.4 1.4 %collective-permute-start.14 = (bf16[192,256]{1,0:T(8,128)(2,1)S(1)}, bf16[192,256]{1,0:T(8,128)(2,1)S(1)}, u32[]{:S(2)}, u32[]{:S(2)}) collective-permute-start(bf16[192,256]{1,0:T(8,128)(2,1)S(1)} %get-tuple-element.46), channel_id=1, source_target_pairs={{0,16},{8,24},{16,0},{24,8},{32,48},{40,56},{48,32},{56,40},{64,80... | collective-permute-start | bytes 294920 | tf_op jit(solution)/shard_map/ppermute | solution.py:368
  48.8 2.4 %collective-permute-start.16 = (bf16[192,256]{1,0:T(8,128)(2,1)S(1)}, bf16[192,256]{1,0:T(8,128)(2,1)S(1)}, u32[]{:S(2)}, u32[]{:S(2)}) collective-permute-start(bf16[192,256]{1,0:T(8,128)(2,1)S(1)} %relay_far.1.after), channel_id=1, source_target_pairs={{0,192},{8,200},{16,208},{24,216},{32,224},{40,232},{48,240},{56,2... | collective-permute-start | bytes 294920 | tf_op jit(solution)/shard_map/ppermute | solution.py:368
  51.2 0.9 %collective-permute-done.14.near_ref = bf16[192,256]{1,0:T(8,128)(2,1)S(1)} collective-permute-done((bf16[192,256]{1,0:T(8,128)(2,1)S(1)}, bf16[192,256]{1,0:T(8,128)(2,1)S(1)}, u32[]{:S(2)}, u32[]{:S(2)}) %collective-permute-start.14) | collective-permute-done | bytes 98336 | tf_op jit(solution)/shard_map/ppermute | solution.py:368
  52.2 1.1 %collective-permute-start.15 = (bf16[192,256]{1,0:T(8,128)(2,1)S(1)}, bf16[192,256]{1,0:T(8,128)(2,1)S(1)}, u32[]{:S(2)}, u32[]{:S(2)}) collective-permute-start(bf16[192,256]{1,0:T(8,128)(2,1)S(1)} %get-tuple-element.48), channel_id=1, source_target_pairs={{0,224},{8,232},{16,240},{24,248},{32,0},{40,8},{48,16},{56,24},{6... | collective-permute-start | bytes 294920 | tf_op jit(solution)/shard_map/ppermute | solution.py:368
  53.3 2.4 %collective-permute-done.16 = bf16[192,256]{1,0:T(8,128)(2,1)S(1)} collective-permute-done((bf16[192,256]{1,0:T(8,128)(2,1)S(1)}, bf16[192,256]{1,0:T(8,128)(2,1)S(1)}, u32[]{:S(2)}, u32[]{:S(2)}) %collective-permute-start.16) | collective-permute-done | bytes 98336 | tf_op jit(solution)/shard_map/ppermute | solution.py:368
  55.6 1.5 %collective-permute-done.15 = bf16[192,256]{1,0:T(8,128)(2,1)S(1)} collective-permute-done((bf16[192,256]{1,0:T(8,128)(2,1)S(1)}, bf16[192,256]{1,0:T(8,128)(2,1)S(1)}, u32[]{:S(2)}, u32[]{:S(2)}) %collective-permute-start.15) | collective-permute-done | bytes 98336 | tf_op jit(solution)/shard_map/ppermute | solution.py:368
  57.1 0.6 %fusion = (bf16[192,128]{1,0:T(8,128)(2,1)}, bf16[192,128]{1,0:T(8,128)(2,1)}) fusion(bf16[192,256]{1,0:T(8,128)(2,1)S(1)} %add_convert_fusion), kind=kLoop, calls=%fused_computation.2 | loop fusion | bytes 196608 | tf_op jit(solution)/shard_map/slice | solution.py:525
  (23 shorter events, 0.7 us)
Async XLA Ops:
  0.6 11.7 %collective-permute-start = (bf16[192,512]{1,0:T(8,128)(2,1)}, bf16[192,512]{1,0:T(8,128)(2,1)S(1)}, u32[]{:S(2)}, u32[]{:S(2)}) collective-permute-start(bf16[192,512]{1,0:T(8,128)(2,1)} %g_hbm.1), channel_id=1, source_target_pairs={{0,1},{1,0},{2,3},{3,2},{4,5},{5,4},{6,7},{7,6},{8,9},{9,8},{10,11... | collective-permute-start | bytes 589832 | tf_op jit(solution)/shard_map/ppermute | solution.py:368
  3.0 9.6 %collective-permute-start.1 = (bf16[192,512]{1,0:T(8,128)(2,1)}, bf16[192,512]{1,0:T(8,128)(2,1)}, u32[]{:S(2)}, u32[]{:S(2)}) collective-permute-start(bf16[192,512]{1,0:T(8,128)(2,1)} %g_hbm.1), channel_id=1, source_target_pairs={{0,2},{1,3},{2,4},{3,5},{4,6},{5,7},{6,0},{7,1},{8,10},{9,11},{10,... | collective-permute-start | bytes 589832 | tf_op jit(solution)/shard_map/ppermute | solution.py:368
  4.5 11.1 %collective-permute-start.2 = (bf16[192,512]{1,0:T(8,128)(2,1)}, bf16[192,512]{1,0:T(8,128)(2,1)S(1)}, u32[]{:S(2)}, u32[]{:S(2)}) collective-permute-start(bf16[192,512]{1,0:T(8,128)(2,1)} %g_hbm.1), channel_id=1, source_target_pairs={{0,6},{1,7},{2,0},{3,1},{4,2},{5,3},{6,4},{7,5},{8,14},{9,15},{10,... | collective-permute-start | bytes 589832 | tf_op jit(solution)/shard_map/ppermute | solution.py:368
  7.1 11.0 %collective-permute-start.3 = (bf16[192,256]{1,0:T(8,128)(2,1)S(1)}, bf16[192,256]{1,0:T(8,128)(2,1)S(1)}, u32[]{:S(2)}, u32[]{:S(2)}) collective-permute-start(bf16[192,256]{1,0:T(8,128)(2,1)S(1)} %pad_add_fusion.z0_ref), channel_id=1, source_target_pairs={{0,64},{8,72},{16,80},{24,88},{32,96},{40,104},{48,112},{56,120},{... | collective-permute-start | bytes 294920 | tf_op jit(solution)/shard_map/ppermute | solution.py:368
  10.4 8.8 %collective-permute-start.4 = (bf16[192,256]{1,0:T(8,128)(2,1)S(1)}, bf16[192,256]{1,0:T(8,128)(2,1)S(1)}, u32[]{:S(2)}, u32[]{:S(2)}) collective-permute-start(bf16[192,256]{1,0:T(8,128)(2,1)S(1)} %pad_add_fusion.z0_ref), channel_id=1, source_target_pairs={{0,32},{8,40},{16,48},{24,56},{32,64},{40,72},{48,80},{56,88},{64,... | collective-permute-start | bytes 294920 | tf_op jit(solution)/shard_map/ppermute | solution.py:368
  12.4 9.1 %copy-start = (bf16[192,512]{1,0:T(8,128)(2,1)}, bf16[192,512]{1,0:T(8,128)(2,1)S(1)}, u32[]{:S(2)}) copy-start(bf16[192,512]{1,0:T(8,128)(2,1)S(1)} %collective-permute-done.refs_0_.y_hbm) | copy-start | bytes 589828
  12.4 8.3 %collective-permute-start.6 = (bf16[192,512]{1,0:T(8,128)(2,1)S(1)}, bf16[192,512]{1,0:T(8,128)(2,1)S(1)}, u32[]{:S(2)}, u32[]{:S(2)}) collective-permute-start(bf16[192,512]{1,0:T(8,128)(2,1)S(1)} %collective-permute-done.refs_0_.y_hbm), channel_id=1, source_target_pairs={{0,2},{1,3},{2,4},{3,5},{4,6},{5,7},{6,0},{7,1},{8,10},{9,11},{10,... | collective-permute-start | bytes 589832 | tf_op jit(solution)/shard_map/ppermute | solution.py:368
  12.6 8.0 %collective-permute-start.7 = (bf16[192,512]{1,0:T(8,128)(2,1)S(1)}, bf16[192,512]{1,0:T(8,128)(2,1)S(1)}, u32[]{:S(2)}, u32[]{:S(2)}) collective-permute-start(bf16[192,512]{1,0:T(8,128)(2,1)S(1)} %collective-permute-done.refs_0_.y_hbm), channel_id=1, source_target_pairs={{0,6},{1,7},{2,0},{3,1},{4,2},{5,3},{6,4},{7,5},{8,14},{9,15},{10,... | collective-permute-start | bytes 589832 | tf_op jit(solution)/shard_map/ppermute | solution.py:368
  15.6 5.9 %copy-start.1 = (bf16[192,512]{1,0:T(8,128)(2,1)}, bf16[192,512]{1,0:T(8,128)(2,1)S(1)}, u32[]{:S(2)}) copy-start(bf16[192,512]{1,0:T(8,128)(2,1)S(1)} %collective-permute-done.2.refs_2_.l_hbm) | copy-start | bytes 589828
  19.2 6.3 %collective-permute-start.5 = (bf16[384,256]{1,0:T(8,128)(2,1)S(1)}, bf16[384,256]{1,0:T(8,128)(2,1)S(1)}, u32[]{:S(2)}, u32[]{:S(2)}) collective-permute-start(bf16[384,256]{1,0:T(8,128)(2,1)S(1)} %pick_side.1.refs_0_), channel_id=1, source_target_pairs={{0,16},{8,24},{16,0},{24,8},{32,48},{40,56},{48,32},{56,40},{64,80... | collective-permute-start | bytes 589832 | tf_op jit(solution)/shard_map/ppermute | solution.py:368
  25.5 8.2 %collective-permute-start.10 = (bf16[960,256]{1,0:T(8,128)(2,1)S(1)}, bf16[960,256]{1,0:T(8,128)(2,1)S(1)}, u32[]{:S(2)}, u32[]{:S(2)}) collective-permute-start(bf16[960,256]{1,0:T(8,128)(2,1)S(1)} %join_slots.1.own_ref), channel_id=1, source_target_pairs={{0,8},{8,0},{16,24},{24,16},{32,40},{40,32},{48,56},{56,48},{64,72... | collective-permute-start | bytes 1474568 | tf_op jit(solution)/shard_map/ppermute | solution.py:368
  25.6 10.9 %collective-permute-start.8 = (bf16[192,512]{1,0:T(8,128)(2,1)}, bf16[192,512]{1,0:T(8,128)(2,1)}, u32[]{:S(2)}, u32[]{:S(2)}) collective-permute-start(bf16[192,512]{1,0:T(8,128)(2,1)} %collective-permute-done.1.refs_1_.r_ref), channel_id=1, source_target_pairs={{0,2},{1,3},{2,4},{3,5},{4,6},{5,7},{6,0},{7,1},{8,10},{9,11},{10,... | collective-permute-start | bytes 589832 | tf_op jit(solution)/shard_map/ppermute | solution.py:368
  26.0 10.5 %collective-permute-start.9 = (bf16[192,512]{1,0:T(8,128)(2,1)S(1)}, bf16[192,512]{1,0:T(8,128)(2,1)}, u32[]{:S(2)}, u32[]{:S(2)}) collective-permute-start(bf16[192,512]{1,0:T(8,128)(2,1)S(1)} %collective-permute-done.7.refs_2_.ol_ref), channel_id=1, source_target_pairs={{0,6},{1,7},{2,0},{3,1},{4,2},{5,3},{6,4},{7,5},{8,14},{9,15},{10,... | collective-permute-start | bytes 589832 | tf_op jit(solution)/shard_map/ppermute | solution.py:368
  39.2 3.3 %collective-permute-start.11 = (bf16[384,256]{1,0:T(8,128)(2,1)S(1)}, bf16[384,256]{1,0:T(8,128)(2,1)S(1)}, u32[]{:S(2)}, u32[]{:S(2)}) collective-permute-start(bf16[384,256]{1,0:T(8,128)(2,1)S(1)} %get-tuple-element.39), channel_id=1, source_target_pairs={{0,8},{8,0},{16,24},{24,16},{32,40},{40,32},{48,56},{56,48},{64,72... | collective-permute-start | bytes 589832 | tf_op jit(solution)/shard_map/ppermute | solution.py:368
  40.4 6.9 %collective-permute-start.12 = (bf16[576,256]{1,0:T(8,128)(2,1)S(1)}, bf16[576,256]{1,0:T(8,128)(2,1)S(1)}, u32[]{:S(2)}, u32[]{:S(2)}) collective-permute-start(bf16[576,256]{1,0:T(8,128)(2,1)S(1)} %get-tuple-element.43), channel_id=1, source_target_pairs={{0,8},{8,0},{16,24},{24,16},{32,40},{40,32},{48,56},{56,48},{64,72... | collective-permute-start | bytes 884744 | tf_op jit(solution)/shard_map/ppermute | solution.py:368
  42.5 4.8 %collective-permute-start.13 = (bf16[192,256]{1,0:T(8,128)(2,1)S(1)}, bf16[192,256]{1,0:T(8,128)(2,1)S(1)}, u32[]{:S(2)}, u32[]{:S(2)}) collective-permute-start(bf16[192,256]{1,0:T(8,128)(2,1)S(1)} %get-tuple-element.44), channel_id=1, source_target_pairs={{0,16},{8,24},{16,0},{24,8},{32,48},{40,56},{48,32},{56,40},{64,80... | collective-permute-start | bytes 294920 | tf_op jit(solution)/shard_map/ppermute | solution.py:368
  47.4 4.7 %collective-permute-start.14 = (bf16[192,256]{1,0:T(8,128)(2,1)S(1)}, bf16[192,256]{1,0:T(8,128)(2,1)S(1)}, u32[]{:S(2)}, u32[]{:S(2)}) collective-permute-start(bf16[192,256]{1,0:T(8,128)(2,1)S(1)} %get-tuple-element.46), channel_id=1, source_target_pairs={{0,16},{8,24},{16,0},{24,8},{32,48},{40,56},{48,32},{56,40},{64,80... | collective-permute-start | bytes 294920 | tf_op jit(solution)/shard_map/ppermute | solution.py:368
  48.8 6.8 %collective-permute-start.16 = (bf16[192,256]{1,0:T(8,128)(2,1)S(1)}, bf16[192,256]{1,0:T(8,128)(2,1)S(1)}, u32[]{:S(2)}, u32[]{:S(2)}) collective-permute-start(bf16[192,256]{1,0:T(8,128)(2,1)S(1)} %relay_far.1.after), channel_id=1, source_target_pairs={{0,192},{8,200},{16,208},{24,216},{32,224},{40,232},{48,240},{56,2... | collective-permute-start | bytes 294920 | tf_op jit(solution)/shard_map/ppermute | solution.py:368
  52.2 4.9 %collective-permute-start.15 = (bf16[192,256]{1,0:T(8,128)(2,1)S(1)}, bf16[192,256]{1,0:T(8,128)(2,1)S(1)}, u32[]{:S(2)}, u32[]{:S(2)}) collective-permute-start(bf16[192,256]{1,0:T(8,128)(2,1)S(1)} %get-tuple-element.48), channel_id=1, source_target_pairs={{0,224},{8,232},{16,240},{24,248},{32,0},{40,8},{48,16},{56,24},{6... | collective-permute-start | bytes 294920 | tf_op jit(solution)/shard_map/ppermute | solution.py:368

commit v7 on v6

v7 whole, which is shorter than its diff:
```python
import functools

import jax
import jax.numpy as jnp
from jax import lax
from jax.experimental import pallas as pl
from jax.experimental.pallas import tpu as pltpu
from jax.sharding import PartitionSpec as P

D = 128
HEADS = 4
ROWS = 192
LANES = HEADS * ROWS
REACH = 4
SLOTS = REACH + 1
PLANE = 4
BLOCK = 512
MASS, TOP, START, DOT = D, D + 1, D + 2, D + 3
PEAK = D + 8
STATE = PEAK + 16
NEG = -1e30
FLOOR = -1e20
SCALE = D**-0.5
LOG2E = 1.4426950408889634
MIB = 1 << 20
FL = 10**9


def dot(a, b, ca, cb):
    return lax.dot_general(a, b, (((ca,), (cb,)), ((), ())), preferred_element_type=jnp.float32)


def stack_heads(src, dst):
    for h in range(HEADS):
        dst[h * ROWS : (h + 1) * ROWS, :] = src[:, h * D : (h + 1) * D]


def load_kernel(place_ref, len_hbm, q_hbm, q4_ref, bound_ref, len_ref, sems):
    copies = [pltpu.make_async_copy(len_hbm, len_ref, sems.at[0])]
    for h in range(HEADS):
        across, along = pl.ds(h * ROWS, ROWS), pl.ds(h * D, D)
        copies.append(pltpu.make_async_copy(q_hbm.at[:, along], q4_ref.at[across, :], sems.at[1 + h]))
    for copy in copies:
        copy.start()
    lane = lax.broadcasted_iota(jnp.int32, (1, LANES), 1)
    pos = lane + place_ref[0] * ROWS
    for h in range(1, HEADS):
        pos = pos - jnp.where(lane >= h * ROWS, ROWS, 0)
    start = jnp.zeros((1, LANES), jnp.int32)
    end = jnp.int32(0)
    copies[0].wait()
    for d in range(len_ref.shape[0]):
        end = end + len_ref[d]
        start = jnp.where(end <= pos, end, start)
    bound_ref[0:1, :] = pos.astype(jnp.float32)
    bound_ref[1:2, :] = start.astype(jnp.float32)
    for copy in copies[1:]:
        copy.wait()


def gate_kernel(*refs):
    refs[-1][...] = jnp.zeros(refs[-1].shape, refs[-1].dtype)


def pick_kernel(place_ref, z2_ref, z1_ref, z0_ref, *refs):
    out_ref = refs[-1]
    upper = lax.rem(lax.div(place_ref[0], 2), 2) == 1

    @pl.when(upper)
    def _():
        out_ref[:ROWS, :] = z2_ref[...]
        out_ref[ROWS:, :] = z1_ref[...]

    @pl.when(jnp.logical_not(upper))
    def _():
        out_ref[:ROWS, :] = z1_ref[...]
        out_ref[ROWS:, :] = z0_ref[...]


def join_kernel(z2_ref, z1_ref, z0_ref, side_ref, *refs):
    out_ref = refs[-1]
    parts = (z2_ref[...], side_ref[:ROWS, :], z1_ref[...], side_ref[ROWS:, :], z0_ref[...])
    for m, part in enumerate(parts):
        out_ref[m * ROWS : (m + 1) * ROWS, :] = part


def absorb(block, queries, row, base, start, state, pos=None):
    s = dot(block[:, :D], queries, 1, 1) * (SCALE * LOG2E)
    visible = row >= start - base * ROWS
    if pos is not None:
        visible = visible & (row <= pos - base * ROWS)
    s = jnp.where(visible, s, NEG)
    peak = jnp.maximum(jnp.max(s, axis=0, keepdims=True), FLOOR)
    prob = jnp.exp2(s - peak).astype(jnp.bfloat16)
    mass = jnp.sum(prob.astype(jnp.float32), axis=0, keepdims=True)
    out = dot(block[:, D:], prob, 0, 0)
    if state is None:
        return prob, peak, (out, mass, peak)
    old_out, old_mass, old_peak = state
    top = jnp.maximum(old_peak, peak)
    before, now = jnp.exp2(old_peak - top), jnp.exp2(peak - top)
    return prob, peak, (old_out * before + out * now, old_mass * before + mass * now, top)


def read_state(ref):
    return ref[:D, :], ref[MASS : MASS + 1, :], ref[TOP : TOP + 1, :]


def write_state(ref, state):
    ref[:D, :], ref[MASS : MASS + 1, :], ref[TOP : TOP + 1, :] = state


def put_row(ref, at, value):
    ref[at : at + 1, :] = value


def near_kernel(place_ref, head_ref, z2_ref, z1_ref, z0_ref, q4_ref, bound_ref, g_hbm, w_hbm, y_ref, r_ref, l_ref, or_ref, ol_ref, after, p_ref, st_ref, acc_ref, tail_ref, g_ref, w_ref, sems):
    head = head_ref[0]
    copies = [pltpu.make_async_copy(g_hbm, g_ref, sems.at[0])]
    for i, source in enumerate((source_of(head, 4, False), source_of(head, 4, True))):
        cols = pl.ds(pl.multiple_of(source * BLOCK, BLOCK), BLOCK)
        copies.append(pltpu.make_async_copy(w_hbm.at[:, cols], tail_ref.at[:, pl.ds(i * BLOCK, BLOCK)], sems.at[1 + i]))
    sources = (head, source_of(head, 0, True), source_of(head, -2, False), source_of(head, 2, False))
    sources += (source_of(head, -2, True), source_of(head, 2, True))
    for i, source in enumerate(sources):
        cols = pl.ds(pl.multiple_of(source * BLOCK, BLOCK), BLOCK)
        copies.append(pltpu.make_async_copy(w_hbm.at[:, cols], w_ref.at[:, pl.ds(i * BLOCK, BLOCK)], sems.at[3 + i]))
    for copy in copies:
        copy.start()
    me = place_ref[0]
    queries = q4_ref[...]
    row = lax.broadcasted_iota(jnp.int32, (ROWS, LANES), 0)
    pos, start = bound_ref[0:1, :].astype(jnp.int32), bound_ref[1:2, :].astype(jnp.int32)
    state = None
    for i, ref in ((2, z0_ref), (1, z1_ref), (0, z2_ref)):
        at = pos if i == 2 else None
        prob, peak, state = absorb(ref[...], queries, row, me - PLANE * (2 - i), start, state, at)
        p_ref[i * ROWS : (i + 1) * ROWS, :] = prob
        put_row(st_ref, PEAK + 2 * i, peak)
    write_state(st_ref, state)
    put_row(st_ref, START, bound_ref[1:2, :])
    for copy in copies:
        copy.wait()
    acc_ref[...] = project(None, (g_ref, y_ref, r_ref, l_ref, or_ref, ol_ref), range(6), w_ref)


def rows(i):
    return pl.ds(pl.multiple_of(i * ROWS, ROWS), ROWS)


def project(acc, pieces, sources, w_ref):
    for piece, source in zip(pieces, sources):
        part = dot(piece[...], w_ref[:, source * BLOCK : (source + 1) * BLOCK], 1, 1)
        acc = part if acc is None else acc + part
    return acc


def source_of(head, by, flip):
    at = lax.rem(head + by + 8, 8)
    return at + 1 - 2 * lax.rem(at, 2) if flip else at


def middle_kernel(place_ref, own_ref, q4_ref, st_in_ref, p_ref, st_ref):
    queries = q4_ref[...]
    row = lax.broadcasted_iota(jnp.int32, (ROWS, LANES), 0)
    start = st_in_ref[START : START + 1, :].astype(jnp.int32)
    state = read_state(st_in_ref)
    st_ref[PEAK:, :] = st_in_ref[PEAK:, :]
    for i in range(2):
        slot = 2 * i + 1
        block = own_ref[slot * ROWS : (slot + 1) * ROWS, :]
        prob, peak, state = absorb(block, queries, row, place_ref[0] + 2 * (slot - REACH), start, state)
        p_ref[i * ROWS : (i + 1) * ROWS, :] = prob
        put_row(st_ref, PEAK + slot, peak)
    write_state(st_ref, state)
    put_row(st_ref, START, st_in_ref[START : START + 1, :])


def across_kernel(place_ref, par_ref, q4_ref, st_in_ref, p_ref, st_ref):
    me = place_ref[0]
    core = lax.rem(me, 2)
    chip = me - core
    queries = q4_ref[...]
    row = lax.broadcasted_iota(jnp.int32, (ROWS, LANES), 0)
    start = st_in_ref[START : START + 1, :].astype(jnp.int32)
    state = read_state(st_in_ref)
    peaks = [st_in_ref[PEAK + m : PEAK + m + 1, :] for m in range(SLOTS)]
    for i in range(REACH):
        slot = i + core
        prob, peak, state = absorb(par_ref[rows(slot), :], queries, row, chip + 1 - core + 2 * (slot - REACH), start, state)
        p_ref[i * ROWS : (i + 1) * ROWS, :] = prob
        peaks.append(peak)
    out, mass, top = state
    st_ref[:D, :] = out / mass
    log_total = top + jnp.log2(mass)
    for i, peak in enumerate(peaks):
        put_row(st_ref, PEAK + i, jnp.exp2(peak - log_total))


def back_block(block, prob, share, g4, q4, rd):
    prob = prob.astype(jnp.float32) * share
    dprob = dot(block[:, D:], g4, 1, 1)
    ds = (prob * (dprob - rd)).astype(jnp.bfloat16)
    dv = dot(prob.astype(jnp.bfloat16), g4, 1, 0)
    dk = dot(ds, q4, 1, 0) * SCALE
    dq = dot(block[:, :D], ds, 0, 0)
    return dk, dv, dq


def put(out_ref, slot, dk, dv):
    at = pl.ds(pl.multiple_of(slot * ROWS, ROWS), ROWS)
    out_ref[at, :D] = dk.astype(out_ref.dtype)
    out_ref[at, D:] = dv.astype(out_ref.dtype)


def cross_step(slot, core, par_ref, p_ref, st_ref, g4, q4_ref, rd):
    share = st_ref[pl.ds(PEAK + SLOTS + slot - core, 1), :]
    return back_block(par_ref[rows(slot), :], p_ref[rows(slot - core), :], share, g4, q4_ref[...], rd)


def cross_far(place_ref, a_ref, b_ref, early_ref, w_ref, q4_ref, par_ref, p_ref, st_in_ref, out_ref, g_ref, st_ref):
    core = lax.rem(place_ref[0], 2)
    acc = project(early_ref[...], (a_ref, b_ref), range(2), w_ref)
    acc = acc.astype(jnp.bfloat16)
    for h in range(HEADS):
        g_ref[h * ROWS : (h + 1) * ROWS, :] = acc[:, h * D : (h + 1) * D]
    g4 = g_ref[...]
    gt = jnp.transpose(g4.astype(jnp.float32))
    rd = jnp.sum(gt * st_in_ref[:D, :], axis=0, keepdims=True)
    st_ref[PEAK:, :] = st_in_ref[PEAK:, :]
    put_row(st_ref, DOT, rd)

    dk, dv, dq = cross_step(1, core, par_ref, p_ref, st_ref, g4, q4_ref, rd)
    put(out_ref, 1, dk, dv)
    st_ref[:D, :] = dq

    @pl.when(core == 1)
    def _():
        out_ref[:ROWS, :] = jnp.zeros((ROWS, 2 * D), out_ref.dtype)

    @pl.when(core == 0)
    def _():
        dk, dv, dq = cross_step(0, core, par_ref, p_ref, st_ref, g4, q4_ref, rd)
        put(out_ref, 0, dk, dv)
        st_ref[:D, :] += dq


def cross_near(place_ref, q4_ref, par_ref, p_ref, g_ref, st_in_ref, out_ref, st_ref):
    core = lax.rem(place_ref[0], 2)
    g4 = g_ref[...]
    rd = st_in_ref[DOT : DOT + 1, :]
    st_ref[DOT : DOT + 1, :] = rd
    st_ref[PEAK:, :] = st_in_ref[PEAK:, :]
    total = st_in_ref[:D, :]
    for slot in (2, 3):
        dk, dv, dq = cross_step(slot, core, par_ref, p_ref, st_ref, g4, q4_ref, rd)
        put(out_ref, slot - 2, dk, dv)
        total = total + dq
    st_ref[:D, :] = total

    @pl.when(core == 0)
    def _():
        out_ref[2 * ROWS :, :] = jnp.zeros((ROWS, 2 * D), out_ref.dtype)

    @pl.when(core == 1)
    def _():
        dk, dv, dq = cross_step(4, core, par_ref, p_ref, st_ref, g4, q4_ref, rd)
        put(out_ref, 2, dk, dv)
        st_ref[:D, :] += dq


def own_kernel(slots, q4_ref, own_ref, near_ref, side_ref, g_ref, st_in_ref, *refs):
    out_ref, st_ref = refs[-2:]
    g4 = g_ref[...]
    rd = st_in_ref[DOT : DOT + 1, :]
    total = st_in_ref[:D, :]
    for i, slot in enumerate(slots):
        at = slot // 2 * ROWS
        prob = (side_ref if slot % 2 else near_ref)[at : at + ROWS, :]
        share = st_in_ref[PEAK + slot : PEAK + slot + 1, :]
        dk, dv, dq = back_block(own_ref[slot * ROWS : (slot + 1) * ROWS, :], prob, share, g4, q4_ref[...], rd)
        out_ref[i * ROWS : (i + 1) * ROWS, :D] = dk
        out_ref[i * ROWS : (i + 1) * ROWS, D:] = dv
        total = total + dq
    if slots[-1] < REACH:
        st_ref[DOT : DOT + 1, :] = rd
        st_ref[PEAK:, :] = st_in_ref[PEAK:, :]
        st_ref[:D, :] = total
    else:
        dq = jnp.transpose(total) * SCALE
        for h in range(HEADS):
            st_ref[:, h * D : (h + 1) * D] = dq[h * ROWS : (h + 1) * ROWS, :].astype(jnp.bfloat16)


def is_upper(place_ref):
    return (lax.rem(lax.div(place_ref[0], 2), 2) == 1).astype(jnp.float32)


def settle_far(own_ref, back_ref, keep_ref, side_ref):
    both = own_ref[...] + back_ref[...].astype(jnp.float32)
    keep_ref[...] = both[:ROWS]
    side_ref[...] = both[ROWS:].astype(jnp.bfloat16)


def relay_far(place_ref, keep_ref, side_ref, out_ref):
    out_ref[...] = (keep_ref[...] + side_ref[...].astype(jnp.float32) * is_upper(place_ref)).astype(jnp.bfloat16)


def settle_near(own_ref, back_ref, keep_ref, side_ref):
    both = own_ref[...] + back_ref[: 2 * ROWS, :].astype(jnp.float32)
    keep_ref[...] = both[:ROWS]
    side_ref[...] = both[ROWS:].astype(jnp.bfloat16)


def relay_near(place_ref, keep_ref, near_ref, far_ref, *refs):
    out_ref = refs[-1]
    upper = is_upper(place_ref)
    near, far = near_ref[...].astype(jnp.float32), far_ref[...].astype(jnp.float32)
    out_ref[...] = (keep_ref[...] + near * upper + far * (1 - upper)).astype(jnp.bfloat16)


def finish_kernel(place_ref, own_ref, back_ref, near_ref, one_ref, two_ref, k_ref, v_ref):
    def wide(x):
        return x.astype(jnp.float32)

    total = own_ref[...] + wide(back_ref[2 * ROWS :, :]) + wide(near_ref[...]) * (1 - is_upper(place_ref))
    total = (total + wide(one_ref[...]) + wide(two_ref[...])).astype(jnp.bfloat16)
    k_ref[...] = total[:, :D]
    v_ref[...] = total[:, D:]


def vmem(n):
    return [pl.BlockSpec(memory_space=pltpu.VMEM)] * n


def smem(n):
    return [pl.BlockSpec(memory_space=pltpu.SMEM)] * n


def hbm(n):
    return [pl.BlockSpec(memory_space=pltpu.HBM)] * n


def token(n):
    return [pl.BlockSpec(memory_space=pl.ANY)] * n


def moved(x, axis, to):
    return lax.ppermute(x, axis, [(i, to(i)) for i in range(lax.axis_size(axis))])


def turned(x, axis, by):
    count = lax.axis_size(axis)
    return moved(x, axis, lambda i: (i + by) % count)


def shape(rows, cols, dtype):
    return jax.ShapeDtypeStruct((rows, cols), dtype)


def call(name, kernel, outs, ins, args, scratch=(), flops=1):
    one = not isinstance(outs, tuple)
    return pl.pallas_call(
        kernel,
        out_shape=outs,
        in_specs=ins,
        out_specs=vmem(1)[0] if one else tuple(vmem(len(outs))),
        scratch_shapes=list(scratch),
        compiler_params=pltpu.CompilerParams(vmem_limit_bytes=8 * MIB),
        cost_estimate=pl.CostEstimate(flops=flops, bytes_accessed=1, transcendentals=0),
        name=name,
    )(*args)


def local(queries, keys, values, grad_out, out_weight, lengths):
    bf16, f32 = jnp.bfloat16, jnp.float32
    place = lax.axis_index("ctx").astype(jnp.int32).reshape(1)
    head = lax.axis_index("head").astype(jnp.int32).reshape(1)
    dma = pltpu.SemaphoreType.DMA
    pinned = functools.partial(pltpu.with_memory_space_constraint, memory_space=pltpu.HBM)
    state = shape(STATE, LANES, f32)

    first = moved(grad_out, "head", lambda i: i ^ 1)
    right = turned(grad_out, "head", 2)
    left = turned(grad_out, "head", -2)
    kv = jnp.pad(keys, ((0, 0), (0, D))) + jnp.pad(values, ((0, 0), (D, 0)))
    z2 = turned(kv, "ctx", 2 * PLANE)
    z1 = turned(kv, "ctx", PLANE)
    q4, bound = call(
        "load",
        load_kernel,
        (shape(LANES, D, bf16), shape(8, LANES, f32)),
        smem(1) + hbm(2),
        (place, pinned(lengths), pinned(queries)),
        [pltpu.SMEM((lengths.shape[0],), jnp.int32), dma((1 + HEADS,))],
    )
    other = first
    other_right = turned(other, "head", 2)
    other_left = turned(other, "head", -2)
    far = turned(right, "head", 2)
    other_far = turned(other_left, "head", -2)

    gate = call("gate", gate_kernel, shape(8, D, f32), token(4), (other, right, left, q4))
    picked = call(
        "pick_side", pick_kernel, shape(2 * ROWS, 2 * D, bf16), smem(1) + vmem(3) + token(1), (place, z2, z1, kv, gate)
    )
    side = moved(picked, "ctx", lambda i: i ^ 2)
    p_near, st, early, tail = call(
        "near",
        near_kernel,
        (shape(3 * ROWS, LANES, bf16), state, shape(ROWS, HEADS * D, f32), shape(HEADS * D, 2 * BLOCK, bf16)),
        smem(2) + vmem(5) + hbm(2) + vmem(5) + token(1),
        (place, head, z2, z1, kv, q4, bound, pinned(grad_out), pinned(out_weight), other, right, left, other_right, other_left, picked),
        [pltpu.VMEM((ROWS, BLOCK), bf16), pltpu.VMEM((HEADS * D, 6 * BLOCK), bf16), dma((9,))],
    )
    own = call("join_slots", join_kernel, shape(SLOTS * ROWS, 2 * D, bf16), vmem(4) + token(1), (z2, z1, kv, side, st))
    par = moved(own, "ctx", lambda i: i ^ 1)

    p_side, st = call(
        "middle", middle_kernel, (shape(2 * ROWS, LANES, bf16), state), smem(1) + vmem(3), (place, own, q4, st)
    )
    p_par, st = call(
        "across", across_kernel, (shape(REACH * ROWS, LANES, bf16), state), smem(1) + vmem(3), (place, par, q4, st)
    )

    far_cross, g4, st = call(
        "cross_far",
        cross_far,
        (shape(2 * ROWS, 2 * D, bf16), shape(LANES, D, bf16), state),
        smem(1) + vmem(8),
        (place, far, other_far, early, tail, q4, par, p_par, st),
    )
    far_back = moved(far_cross, "ctx", lambda i: i ^ 1)
    near_cross, st = call(
        "cross_near", cross_near, (shape(3 * ROWS, 2 * D, bf16), state), smem(1) + vmem(5), (place, q4, par, p_par, g4, st), flops=FL
    )
    near_back = moved(near_cross, "ctx", lambda i: i ^ 1)
    far_own, st = call(
        "own_far",
        functools.partial(own_kernel, (0, 1)),
        (shape(2 * ROWS, 2 * D, f32), state),
        vmem(6),
        (q4, own, p_near, p_side, g4, st),
        flops=FL,
    )
    far_keep, far_side = call(
        "settle_far", settle_far, (shape(ROWS, 2 * D, f32), shape(ROWS, 2 * D, bf16)), vmem(2), (far_own, far_back)
    )
    far_side = moved(far_side, "ctx", lambda i: i ^ 2)
    near_own, st = call(
        "own_near",
        functools.partial(own_kernel, (2, 3)),
        (shape(2 * ROWS, 2 * D, f32), state),
        vmem(6) + token(1),
        (q4, own, p_near, p_side, g4, st, far_keep),
        flops=FL,
    )
    near_keep, near_side = call(
        "settle_near", settle_near, (shape(ROWS, 2 * D, f32), shape(ROWS, 2 * D, bf16)), vmem(2), (near_own, near_back)
    )
    near_side = moved(near_side, "ctx", lambda i: i ^ 2)
    last_own, grad_queries = call(
        "own_last",
        functools.partial(own_kernel, (4,)),
        (shape(ROWS, 2 * D, f32), shape(ROWS, HEADS * D, bf16)),
        vmem(6) + token(1),
        (q4, own, p_near, p_side, g4, st, near_keep),
    )
    to_two = call("relay_far", relay_far, shape(ROWS, 2 * D, bf16), smem(1) + vmem(2), (place, far_keep, far_side))
    got_two = turned(to_two, "ctx", -2 * PLANE)
    to_one = call(
        "relay_near",
        relay_near,
        shape(ROWS, 2 * D, bf16),
        smem(1) + vmem(3) + token(2),
        (place, near_keep, near_side, far_side, to_two, last_own),
    )
    got_one = turned(to_one, "ctx", -PLANE)
    grad_keys, grad_values = call(
        "finish",
        finish_kernel,
        (shape(ROWS, D, bf16), shape(ROWS, D, bf16)),
        smem(1) + vmem(5),
        (place, last_own, near_back, near_side, got_one, got_two),
    )
    return grad_queries, grad_keys, grad_values


def solution(mesh):
    return jax.shard_map(
        local,
        mesh=mesh,
        in_specs=(
            P("ctx", "head"),
            P("ctx", "head"),
            P("ctx", "head"),
            P("ctx", "head"),
            P("head", None),
            P(),
        ),
        out_specs=(P("ctx", "head"), P("ctx", "head"), P("ctx", "head")),
        check_vma=False,
    )
```

time: 58 us -> 56.1 us (0.967)
  the two profiles are of different devices: /device:TPU:8 before, /device:TPU:64 now
where the time goes in v7:
time: 56.1 us; the launch traced here: 55.7 us
  starting transfers between devices  22.3 us (40%)
  waiting for transfers between devices  17.9 us (32%)
  Pallas kernels  13.9 us (25%)
  other arithmetic  0.83 us (1%)
  between operations  0.8 us (1%)
    ppermute x17, starting transfers between devices, moved(): lax.ppermute(x, axis, [(i, to(i)) for i in range(lax.axis_size(axis))])  22.3 us
    ppermute x17, waiting for transfers between devices, moved(): lax.ppermute(x, axis, [(i, to(i)) for i in range(lax.axis_size(axis))])  17.9 us
    pallas_call x17, Pallas kernels, call(): pl.pallas_call(kernel, out_shape=outs, in_specs=ins, out_specs=vmem(1)[0]...  13.9 us
  transfers between devices with their start and end apart: 17, of which 7 were waited for; matrix products, arithmetic and copies ran while one was open for 1% of the time, Pallas kernels for 20%

profile of v7, /device:TPU:64, one launch (start us, length us, event | category | flops | bytes accessed | tf_op | source)
XLA Modules:
  0.0 55.7 jit_solution(6718197310530763289)
XLA Ops:
  0.6 1.6 %collective-permute-start.3 = (bf16[192,512]{1,0:T(8,128)(2,1)}, bf16[192,512]{1,0:T(8,128)(2,1)S(1)}, u32[]{:S(2)}, u32[]{:S(2)}) collective-permute-start(bf16[192,512]{1,0:T(8,128)(2,1)} %g_hbm.1), channel_id=1, source_target_pairs={{0,2},{1,3},{2,4},{3,5},{4,6},{5,7},{6,0},{7,1},{8,10},{9,11},{10,... | collective-permute-start | bytes 589832 | tf_op jit(solution)/shard_map/ppermute | solution.py:349
  2.2 3.2 %collective-permute-start.2 = (bf16[192,512]{1,0:T(8,128)(2,1)}, bf16[192,512]{1,0:T(8,128)(2,1)S(1)}, u32[]{:S(2)}, u32[]{:S(2)}) collective-permute-start(bf16[192,512]{1,0:T(8,128)(2,1)} %g_hbm.1), channel_id=1, source_target_pairs={{0,1},{1,0},{2,3},{3,2},{4,5},{5,4},{6,7},{7,6},{8,9},{9,8},{10,11... | collective-permute-start | bytes 589832 | tf_op jit(solution)/shard_map/ppermute | solution.py:349
  5.4 1.7 %collective-permute-start.4 = (bf16[192,512]{1,0:T(8,128)(2,1)}, bf16[192,512]{1,0:T(8,128)(2,1)S(1)}, u32[]{:S(2)}, u32[]{:S(2)}) collective-permute-start(bf16[192,512]{1,0:T(8,128)(2,1)} %g_hbm.1), channel_id=1, source_target_pairs={{0,6},{1,7},{2,0},{3,1},{4,2},{5,3},{6,4},{7,5},{8,14},{9,15},{10,... | collective-permute-start | bytes 589832 | tf_op jit(solution)/shard_map/ppermute | solution.py:349
  7.1 0.8 %pad_add_fusion.z0_ref = bf16[192,256]{1,0:T(8,128)(2,1)S(1)} fusion(bf16[192,128]{1,0:T(8,128)(2,1)} %param.8, bf16[192,128]{1,0:T(8,128)(2,1)} %param.7), kind=kLoop, calls=%fused_computation | loop fusion | flops 196608 | bytes 196608 | tf_op jit(solution)/shard_map/add | solution.py:386
  8.0 2.0 %collective-permute-start.1 = (bf16[192,256]{1,0:T(8,128)(2,1)S(1)}, bf16[192,256]{1,0:T(8,128)(2,1)S(1)}, u32[]{:S(2)}, u32[]{:S(2)}) collective-permute-start(bf16[192,256]{1,0:T(8,128)(2,1)S(1)} %pad_add_fusion.z0_ref), channel_id=1, source_target_pairs={{0,32},{8,40},{16,48},{24,56},{32,64},{40,72},{48,80},{56,88},{64,... | collective-permute-start | bytes 294920 | tf_op jit(solution)/shard_map/ppermute | solution.py:349
  10.0 3.6 %collective-permute-start = (bf16[192,256]{1,0:T(8,128)(2,1)S(1)}, bf16[192,256]{1,0:T(8,128)(2,1)S(1)}, u32[]{:S(2)}, u32[]{:S(2)}) collective-permute-start(bf16[192,256]{1,0:T(8,128)(2,1)S(1)} %pad_add_fusion.z0_ref), channel_id=1, source_target_pairs={{0,64},{8,72},{16,80},{24,88},{32,96},{40,104},{48,112},{56,120},{... | collective-permute-start | bytes 294920 | tf_op jit(solution)/shard_map/ppermute | solution.py:349
  13.6 0.9 %load.1 = (bf16[768,128]{1,0:T(8,128)(2,1)S(1)}, f32[8,768]{1,0:T(8,128)S(1)}) custom-call(s32[1]{0:T(128)} %bitcast.place_ref, s32[8]{0:T(128)} %len_hbm.1, bf16[192,512]{1,0:T(8,128)(2,1)} %q_hbm.1), custom_call_target="tpu_custom_call" | custom-call | flops 1 | bytes 1 | tf_op jit(solution)/shard_map/load/pallas_call | solution.py:363
  14.5 1.6 %collective-permute-start.7 = (bf16[192,512]{1,0:T(8,128)(2,1)S(1)}, bf16[192,512]{1,0:T(8,128)(2,1)S(1)}, u32[]{:S(2)}, u32[]{:S(2)}) collective-permute-start(bf16[192,512]{1,0:T(8,128)(2,1)S(1)} %collective-permute-done.2.refs_0_.y_ref), channel_id=1, source_target_pairs={{0,6},{1,7},{2,0},{3,1},{4,2},{5,3},{6,4},{7,5},{8,14},{9,15},{10,... | collective-permute-start | bytes 589832 | tf_op jit(solution)/shard_map/ppermute | solution.py:349
  16.1 0.5 collective-permute-start.6
  16.6 0.2 collective-permute-done.z2_ref
  16.8 0.8 %collective-permute-start.5 = (bf16[384,256]{1,0:T(8,128)(2,1)S(1)}, bf16[384,256]{1,0:T(8,128)(2,1)S(1)}, u32[]{:S(2)}, u32[]{:S(2)}) collective-permute-start(bf16[384,256]{1,0:T(8,128)(2,1)S(1)} %pick_side.1.after), channel_id=1, source_target_pairs={{0,16},{8,24},{16,0},{24,8},{32,48},{40,56},{48,32},{56,40},{64,80... | collective-permute-start | bytes 589832 | tf_op jit(solution)/shard_map/ppermute | solution.py:349
  17.6 2.7 %collective-permute-done.7.ol_ref = bf16[192,512]{1,0:T(8,128)(2,1)S(1)} collective-permute-done((bf16[192,512]{1,0:T(8,128)(2,1)S(1)}, bf16[192,512]{1,0:T(8,128)(2,1)S(1)}, u32[]{:S(2)}, u32[]{:S(2)}) %collective-permute-start.7) | collective-permute-done | bytes 196640 | tf_op jit(solution)/shard_map/ppermute | solution.py:349
  20.2 2.8 %collective-permute-done.6.or_ref = bf16[192,512]{1,0:T(8,128)(2,1)S(1)} collective-permute-done((bf16[192,512]{1,0:T(8,128)(2,1)S(1)}, bf16[192,512]{1,0:T(8,128)(2,1)S(1)}, u32[]{:S(2)}, u32[]{:S(2)}) %collective-permute-start.6) | collective-permute-done | bytes 196640 | tf_op jit(solution)/shard_map/ppermute | solution.py:349
  23.0 4.6 %near.1 = (bf16[576,768]{1,0:T(8,128)(2,1)S(1)}, f32[152,768]{1,0:T(8,128)S(1)}, f32[192,512]{1,0:T(8,128)S(1)}, bf16[512,1024]{1,0:T(8,128)(2,1)S(1)}) custom-call(s32[1]{0:T(128)} %bitcast.place_ref, s32[1]{0:T(128)} %bitcast.1.head_ref, bf16[192,256]{1,0:T(8,128)(2,1)S(1)} %collective-permute-done.z2_ref, ...), custom_call_target="tpu_custom_call" | custom-call | flops 1 | bytes 1 | tf_op jit(solution)/shard_map/near/pallas_call | solution.py:363
  27.6 0.1 collective-permute-start.10
  27.8 3.2 %collective-permute-start.9 = (bf16[192,512]{1,0:T(8,128)(2,1)S(1)}, bf16[192,512]{1,0:T(8,128)(2,1)S(1)}, u32[]{:S(2)}, u32[]{:S(2)}) collective-permute-start(bf16[192,512]{1,0:T(8,128)(2,1)S(1)} %collective-permute-done.7.ol_ref), channel_id=1, source_target_pairs={{0,6},{1,7},{2,0},{3,1},{4,2},{5,3},{6,4},{7,5},{8,14},{9,15},{10,... | collective-permute-start | bytes 589832 | tf_op jit(solution)/shard_map/ppermute | solution.py:349
  31.0 0.9 %middle.1 = (bf16[384,768]{1,0:T(8,128)(2,1)S(1)}, f32[152,768]{1,0:T(8,128)S(1)}) custom-call(s32[1]{0:T(128)} %bitcast.place_ref, bf16[960,256]{1,0:T(8,128)(2,1)S(1)} %join_slots.1.own_ref, bf16[768,128]{1,0:T(8,128)(2,1)S(1)} %get-tuple-element.30.refs_3_.q4_ref, f32[152,768]{1,0:T(8,128)S(1)} %get-tuple-element.32.refs_0_.st_in_ref), custom_call_target="tpu_custom_call" | custom-call | flops 1 | bytes 1 | tf_op jit(solution)/shard_map/middle/pallas_call | solution.py:363
  31.9 1.6 %across.1 = (bf16[768,768]{1,0:T(8,128)(2,1)S(1)}, f32[152,768]{1,0:T(8,128)S(1)}) custom-call(s32[1]{0:T(128)} %bitcast.place_ref, bf16[960,256]{1,0:T(8,128)(2,1)S(1)} %collective-permute-done.10.par_ref, bf16[768,128]{1,0:T(8,128)(2,1)S(1)} %get-tuple-element.30.refs_3_.q4_ref, f32[152,768]{1,0:T(8,128)S(1)} %get-tuple-element.37.st_in_ref), custom_call_target="tpu_custom_call" | custom-call | flops 1 | bytes 1 | tf_op jit(solution)/shard_map/across/pallas_call | solution.py:363
  33.5 2.7 %collective-permute-done.8.a_ref = bf16[192,512]{1,0:T(8,128)(2,1)S(1)} collective-permute-done((bf16[192,512]{1,0:T(8,128)(2,1)S(1)}, bf16[192,512]{1,0:T(8,128)(2,1)S(1)}, u32[]{:S(2)}, u32[]{:S(2)}) %collective-permute-start.8) | collective-permute-done | bytes 196640 | tf_op jit(solution)/shard_map/ppermute | solution.py:349
  36.3 1.4 %cross_far.1 = (bf16[384,256]{1,0:T(8,128)(2,1)S(1)}, bf16[768,128]{1,0:T(8,128)(2,1)S(1)}, f32[152,768]{1,0:T(8,128)S(1)}) custom-call(s32[1]{0:T(128)} %bitcast.place_ref, bf16[192,512]{1,0:T(8,128)(2,1)S(1)} %collective-permute-done.8.a_ref, bf16[192,512]{1,0:T(8,128)(2,1)S(1)} %collective-permute-done.9.b_ref, ...), custom_call_target="tpu_custom_call" | custom-call | flops 1 | bytes 1 | tf_op jit(solution)/shard_map/cross_far/pallas_call | solution.py:363
  37.7 0.8 %cross_near.1 = (bf16[576,256]{1,0:T(8,128)(2,1)S(1)}, f32[152,768]{1,0:T(8,128)S(1)}) custom-call(s32[1]{0:T(128)} %bitcast.place_ref, bf16[768,128]{1,0:T(8,128)(2,1)S(1)} %get-tuple-element.30.refs_3_.q4_ref, bf16[960,256]{1,0:T(8,128)(2,1)S(1)} %collective-permute-done.10.par_ref, bf16[768,768]{1,0:T(8,128)(2,1)S(1)} %get-tuple-element.38.p_ref, ...), custom_call_target="tpu_custom_call" | custom-call | flops 1000000000 | bytes 1 | tf_op jit(solution)/shard_map/cross_near/pallas_call | solution.py:363
  38.6 0.5 collective-permute-start.11
  39.1 0.8 %own_far.1 = (f32[384,256]{1,0:T(8,128)S(1)}, f32[152,768]{1,0:T(8,128)S(1)}) custom-call(bf16[768,128]{1,0:T(8,128)(2,1)S(1)} %get-tuple-element.30.refs_3_.q4_ref, bf16[960,256]{1,0:T(8,128)(2,1)S(1)} %join_slots.1.own_ref, bf16[576,768]{1,0:T(8,128)(2,1)S(1)} %get-tuple-element.33.near_ref, bf16[384,768]{1,0:T(8,128)(2,1)S(1)} %get-tuple-element.34.side_ref, ...), custom_call_target="tpu_custom_call" | custom-call | flops 1000000000 | bytes 1 | tf_op jit(solution)/shard_map/own_far/pallas_call | solution.py:363
  39.9 0.6 collective-permute-done.11.back_ref
  40.5 0.8 %collective-permute-start.14 = (bf16[192,256]{1,0:T(8,128)(2,1)S(1)}, bf16[192,256]{1,0:T(8,128)(2,1)S(1)}, u32[]{:S(2)}, u32[]{:S(2)}) collective-permute-start(bf16[192,256]{1,0:T(8,128)(2,1)S(1)} %get-tuple-element.54), channel_id=1, source_target_pairs={{0,16},{8,24},{16,0},{24,8},{32,48},{40,56},{48,32},{56,40},{64,80... | collective-permute-start | bytes 294920 | tf_op jit(solution)/shard_map/ppermute | solution.py:349
  41.3 0.8 %own_near.1 = (f32[384,256]{1,0:T(8,128)S(1)}, f32[152,768]{1,0:T(8,128)S(1)}) custom-call(bf16[768,128]{1,0:T(8,128)(2,1)S(1)} %get-tuple-element.30.refs_3_.q4_ref, bf16[960,256]{1,0:T(8,128)(2,1)S(1)} %join_slots.1.own_ref, bf16[576,768]{1,0:T(8,128)(2,1)S(1)} %get-tuple-element.33.near_ref, bf16[384,768]{1,0:T(8,128)(2,1)S(1)} %get-tuple-element.34.side_ref, ...), custom_call_target="tpu_custom_call" | custom-call | flops 1000000000 | bytes 1 | tf_op jit(solution)/shard_map/own_near/pallas_call | solution.py:363
  42.1 1.4 %collective-permute-start.13 = (bf16[192,256]{1,0:T(8,128)(2,1)S(1)}, bf16[192,256]{1,0:T(8,128)(2,1)S(1)}, u32[]{:S(2)}, u32[]{:S(2)}) collective-permute-start(bf16[192,256]{1,0:T(8,128)(2,1)S(1)} %get-tuple-element.53), channel_id=1, source_target_pairs={{0,16},{8,24},{16,0},{24,8},{32,48},{40,56},{48,32},{56,40},{64,80... | collective-permute-start | bytes 294920 | tf_op jit(solution)/shard_map/ppermute | solution.py:349
  43.5 2.6 %collective-permute-done.14.side_ref.far_ref = bf16[192,256]{1,0:T(8,128)(2,1)S(1)} collective-permute-done((bf16[192,256]{1,0:T(8,128)(2,1)S(1)}, bf16[192,256]{1,0:T(8,128)(2,1)S(1)}, u32[]{:S(2)}, u32[]{:S(2)}) %collective-permute-start.14) | collective-permute-done | bytes 98336 | tf_op jit(solution)/shard_map/ppermute | solution.py:349
  46.3 1.2 %own_last.1 = (f32[192,256]{1,0:T(8,128)S(1)}, bf16[192,512]{1,0:T(8,128)(2,1)}) custom-call(bf16[768,128]{1,0:T(8,128)(2,1)S(1)} %get-tuple-element.30.refs_3_.q4_ref, bf16[960,256]{1,0:T(8,128)(2,1)S(1)} %join_slots.1.own_ref, bf16[576,768]{1,0:T(8,128)(2,1)S(1)} %get-tuple-element.33.near_ref, bf16[384,768]{1,0:T(8,128)(2,1)S(1)} %get-tuple-element.34.side_ref, ...), custom_call_target="tpu_custom_call" | custom-call | flops 1 | bytes 1 | tf_op jit(solution)/shard_map/own_last/pallas_call | solution.py:363
  47.6 1.1 %collective-permute-start.15 = (bf16[192,256]{1,0:T(8,128)(2,1)S(1)}, bf16[192,256]{1,0:T(8,128)(2,1)S(1)}, u32[]{:S(2)}, u32[]{:S(2)}) collective-permute-start(bf16[192,256]{1,0:T(8,128)(2,1)S(1)} %relay_near.1), channel_id=1, source_target_pairs={{0,224},{8,232},{16,240},{24,248},{32,0},{40,8},{48,16},{56,24},{6... | collective-permute-start | bytes 294920 | tf_op jit(solution)/shard_map/ppermute | solution.py:349
  48.7 6.3 %collective-permute-done.16.two_ref = bf16[192,256]{1,0:T(8,128)(2,1)S(1)} collective-permute-done((bf16[192,256]{1,0:T(8,128)(2,1)S(1)}, bf16[192,256]{1,0:T(8,128)(2,1)S(1)}, u32[]{:S(2)}, u32[]{:S(2)}) %collective-permute-start.16) | collective-permute-done | bytes 98336 | tf_op jit(solution)/shard_map/ppermute | solution.py:349
  55.0 0.7 %finish.1 = (bf16[192,128]{1,0:T(8,128)(2,1)}, bf16[192,128]{1,0:T(8,128)(2,1)}) custom-call(s32[1]{0:T(128)} %bitcast.place_ref, f32[192,256]{1,0:T(8,128)S(1)} %get-tuple-element.52.refs_1_.own_ref, bf16[576,256]{1,0:T(8,128)(2,1)S(1)} %collective-permute-done.12.back_ref, bf16[192,256]{1,0:T(8,128)(2,1)S(1)} %collective-permute-done.13.near_ref, ...), custom_call_target="tpu_custom_call" | custom-call | flops 1 | bytes 1 | tf_op jit(solution)/shard_map/finish/pallas_call | solution.py:363
  (20 shorter events, 0.5 us)
Async XLA Ops:
  0.6 15.5 %collective-permute-start.3 = (bf16[192,512]{1,0:T(8,128)(2,1)}, bf16[192,512]{1,0:T(8,128)(2,1)S(1)}, u32[]{:S(2)}, u32[]{:S(2)}) collective-permute-start(bf16[192,512]{1,0:T(8,128)(2,1)} %g_hbm.1), channel_id=1, source_target_pairs={{0,2},{1,3},{2,4},{3,5},{4,6},{5,7},{6,0},{7,1},{8,10},{9,11},{10,... | collective-permute-start | bytes 589832 | tf_op jit(solution)/shard_map/ppermute | solution.py:349
  2.2 12.3 %collective-permute-start.2 = (bf16[192,512]{1,0:T(8,128)(2,1)}, bf16[192,512]{1,0:T(8,128)(2,1)S(1)}, u32[]{:S(2)}, u32[]{:S(2)}) collective-permute-start(bf16[192,512]{1,0:T(8,128)(2,1)} %g_hbm.1), channel_id=1, source_target_pairs={{0,1},{1,0},{2,3},{3,2},{4,5},{5,4},{6,7},{7,6},{8,9},{9,8},{10,11... | collective-permute-start | bytes 589832 | tf_op jit(solution)/shard_map/ppermute | solution.py:349
  5.4 11.2 %collective-permute-start.4 = (bf16[192,512]{1,0:T(8,128)(2,1)}, bf16[192,512]{1,0:T(8,128)(2,1)S(1)}, u32[]{:S(2)}, u32[]{:S(2)}) collective-permute-start(bf16[192,512]{1,0:T(8,128)(2,1)} %g_hbm.1), channel_id=1, source_target_pairs={{0,6},{1,7},{2,0},{3,1},{4,2},{5,3},{6,4},{7,5},{8,14},{9,15},{10,... | collective-permute-start | bytes 589832 | tf_op jit(solution)/shard_map/ppermute | solution.py:349
  8.0 8.6 %collective-permute-start.1 = (bf16[192,256]{1,0:T(8,128)(2,1)S(1)}, bf16[192,256]{1,0:T(8,128)(2,1)S(1)}, u32[]{:S(2)}, u32[]{:S(2)}) collective-permute-start(bf16[192,256]{1,0:T(8,128)(2,1)S(1)} %pad_add_fusion.z0_ref), channel_id=1, source_target_pairs={{0,32},{8,40},{16,48},{24,56},{32,64},{40,72},{48,80},{56,88},{64,... | collective-permute-start | bytes 294920 | tf_op jit(solution)/shard_map/ppermute | solution.py:349
  10.0 6.8 %collective-permute-start = (bf16[192,256]{1,0:T(8,128)(2,1)S(1)}, bf16[192,256]{1,0:T(8,128)(2,1)S(1)}, u32[]{:S(2)}, u32[]{:S(2)}) collective-permute-start(bf16[192,256]{1,0:T(8,128)(2,1)S(1)} %pad_add_fusion.z0_ref), channel_id=1, source_target_pairs={{0,64},{8,72},{16,80},{24,88},{32,96},{40,104},{48,112},{56,120},{... | collective-permute-start | bytes 294920 | tf_op jit(solution)/shard_map/ppermute | solution.py:349
  14.5 5.7 %collective-permute-start.7 = (bf16[192,512]{1,0:T(8,128)(2,1)S(1)}, bf16[192,512]{1,0:T(8,128)(2,1)S(1)}, u32[]{:S(2)}, u32[]{:S(2)}) collective-permute-start(bf16[192,512]{1,0:T(8,128)(2,1)S(1)} %collective-permute-done.2.refs_0_.y_ref), channel_id=1, source_target_pairs={{0,6},{1,7},{2,0},{3,1},{4,2},{5,3},{6,4},{7,5},{8,14},{9,15},{10,... | collective-permute-start | bytes 589832 | tf_op jit(solution)/shard_map/ppermute | solution.py:349
  16.1 6.9 %collective-permute-start.6 = (bf16[192,512]{1,0:T(8,128)(2,1)S(1)}, bf16[192,512]{1,0:T(8,128)(2,1)S(1)}, u32[]{:S(2)}, u32[]{:S(2)}) collective-permute-start(bf16[192,512]{1,0:T(8,128)(2,1)S(1)} %collective-permute-done.2.refs_0_.y_ref), channel_id=1, source_target_pairs={{0,2},{1,3},{2,4},{3,5},{4,6},{5,7},{6,0},{7,1},{8,10},{9,11},{10,... | collective-permute-start | bytes 589832 | tf_op jit(solution)/shard_map/ppermute | solution.py:349
  16.8 10.8 %collective-permute-start.5 = (bf16[384,256]{1,0:T(8,128)(2,1)S(1)}, bf16[384,256]{1,0:T(8,128)(2,1)S(1)}, u32[]{:S(2)}, u32[]{:S(2)}) collective-permute-start(bf16[384,256]{1,0:T(8,128)(2,1)S(1)} %pick_side.1.after), channel_id=1, source_target_pairs={{0,16},{8,24},{16,0},{24,8},{32,48},{40,56},{48,32},{56,40},{64,80... | collective-permute-start | bytes 589832 | tf_op jit(solution)/shard_map/ppermute | solution.py:349
  27.6 4.3 %collective-permute-start.10 = (bf16[960,256]{1,0:T(8,128)(2,1)S(1)}, bf16[960,256]{1,0:T(8,128)(2,1)S(1)}, u32[]{:S(2)}, u32[]{:S(2)}) collective-permute-start(bf16[960,256]{1,0:T(8,128)(2,1)S(1)} %join_slots.1.own_ref), channel_id=1, source_target_pairs={{0,8},{8,0},{16,24},{24,16},{32,40},{40,32},{48,56},{56,48},{64,72... | collective-permute-start | bytes 1474568 | tf_op jit(solution)/shard_map/ppermute | solution.py:349
  27.7 8.5 %collective-permute-start.8 = (bf16[192,512]{1,0:T(8,128)(2,1)S(1)}, bf16[192,512]{1,0:T(8,128)(2,1)S(1)}, u32[]{:S(2)}, u32[]{:S(2)}) collective-permute-start(bf16[192,512]{1,0:T(8,128)(2,1)S(1)} %collective-permute-done.3.refs_1_.r_ref), channel_id=1, source_target_pairs={{0,2},{1,3},{2,4},{3,5},{4,6},{5,7},{6,0},{7,1},{8,10},{9,11},{10,... | collective-permute-start | bytes 589832 | tf_op jit(solution)/shard_map/ppermute | solution.py:349
  27.8 8.4 %collective-permute-start.9 = (bf16[192,512]{1,0:T(8,128)(2,1)S(1)}, bf16[192,512]{1,0:T(8,128)(2,1)S(1)}, u32[]{:S(2)}, u32[]{:S(2)}) collective-permute-start(bf16[192,512]{1,0:T(8,128)(2,1)S(1)} %collective-permute-done.7.ol_ref), channel_id=1, source_target_pairs={{0,6},{1,7},{2,0},{3,1},{4,2},{5,3},{6,4},{7,5},{8,14},{9,15},{10,... | collective-permute-start | bytes 589832 | tf_op jit(solution)/shard_map/ppermute | solution.py:349
  38.5 3.6 %collective-permute-start.12 = (bf16[576,256]{1,0:T(8,128)(2,1)S(1)}, bf16[576,256]{1,0:T(8,128)(2,1)S(1)}, u32[]{:S(2)}, u32[]{:S(2)}) collective-permute-start(bf16[576,256]{1,0:T(8,128)(2,1)S(1)} %get-tuple-element.49), channel_id=1, source_target_pairs={{0,8},{8,0},{16,24},{24,16},{32,40},{40,32},{48,56},{56,48},{64,72... | collective-permute-start | bytes 884744 | tf_op jit(solution)/shard_map/ppermute | solution.py:349
  38.6 1.9 %collective-permute-start.11 = (bf16[384,256]{1,0:T(8,128)(2,1)S(1)}, bf16[384,256]{1,0:T(8,128)(2,1)S(1)}, u32[]{:S(2)}, u32[]{:S(2)}) collective-permute-start(bf16[384,256]{1,0:T(8,128)(2,1)S(1)} %get-tuple-element.45), channel_id=1, source_target_pairs={{0,8},{8,0},{16,24},{24,16},{32,40},{40,32},{48,56},{56,48},{64,72... | collective-permute-start | bytes 589832 | tf_op jit(solution)/shard_map/ppermute | solution.py:349
  40.5 5.7 %collective-permute-start.14 = (bf16[192,256]{1,0:T(8,128)(2,1)S(1)}, bf16[192,256]{1,0:T(8,128)(2,1)S(1)}, u32[]{:S(2)}, u32[]{:S(2)}) collective-permute-start(bf16[192,256]{1,0:T(8,128)(2,1)S(1)} %get-tuple-element.54), channel_id=1, source_target_pairs={{0,16},{8,24},{16,0},{24,8},{32,48},{40,56},{48,32},{56,40},{64,80... | collective-permute-start | bytes 294920 | tf_op jit(solution)/shard_map/ppermute | solution.py:349
  42.1 5.4 %collective-permute-start.13 = (bf16[192,256]{1,0:T(8,128)(2,1)S(1)}, bf16[192,256]{1,0:T(8,128)(2,1)S(1)}, u32[]{:S(2)}, u32[]{:S(2)}) collective-permute-start(bf16[192,256]{1,0:T(8,128)(2,1)S(1)} %get-tuple-element.53), channel_id=1, source_target_pairs={{0,16},{8,24},{16,0},{24,8},{32,48},{40,56},{48,32},{56,40},{64,80... | collective-permute-start | bytes 294920 | tf_op jit(solution)/shard_map/ppermute | solution.py:349
  46.2 8.8 %collective-permute-start.16 = (bf16[192,256]{1,0:T(8,128)(2,1)S(1)}, bf16[192,256]{1,0:T(8,128)(2,1)S(1)}, u32[]{:S(2)}, u32[]{:S(2)}) collective-permute-start(bf16[192,256]{1,0:T(8,128)(2,1)S(1)} %relay_far.1.refs_0_), channel_id=1, source_target_pairs={{0,192},{8,200},{16,208},{24,216},{32,224},{40,232},{48,240},{56,2... | collective-permute-start | bytes 294920 | tf_op jit(solution)/shard_map/ppermute | solution.py:349
  47.6 7.4 %collective-permute-start.15 = (bf16[192,256]{1,0:T(8,128)(2,1)S(1)}, bf16[192,256]{1,0:T(8,128)(2,1)S(1)}, u32[]{:S(2)}, u32[]{:S(2)}) collective-permute-start(bf16[192,256]{1,0:T(8,128)(2,1)S(1)} %relay_near.1), channel_id=1, source_target_pairs={{0,224},{8,232},{16,240},{24,248},{32,0},{40,8},{48,16},{56,24},{6... | collective-permute-start | bytes 294920 | tf_op jit(solution)/shard_map/ppermute | solution.py:349

commit v8 on v7

--- a/solution.py
+++ b/solution.py
@@ -23,7 +23,7 @@
 SCALE = D**-0.5
 LOG2E = 1.4426950408889634
 MIB = 1 << 20
-FL = 10**9
+FL = 4 * 10**9
 
 
 def dot(a, b, ca, cb):
@@ -114,17 +114,16 @@
     ref[at : at + 1, :] = value
 
 
-def near_kernel(place_ref, head_ref, z2_ref, z1_ref, z0_ref, q4_ref, bound_ref, g_hbm, w_hbm, y_ref, r_ref, l_ref, or_ref, ol_ref, after, p_ref, st_ref, acc_ref, tail_ref, g_ref, w_ref, sems):
+def near_kernel(place_ref, head_ref, z2_ref, z1_ref, z0_ref, q4_ref, bound_ref, w_hbm, *refs):
+    p_ref, st_ref, w_ref, tail_ref, sems = refs[-5:]
     head = head_ref[0]
-    copies = [pltpu.make_async_copy(g_hbm, g_ref, sems.at[0])]
-    for i, source in enumerate((source_of(head, 4, False), source_of(head, 4, True))):
-        cols = pl.ds(pl.multiple_of(source * BLOCK, BLOCK), BLOCK)
-        copies.append(pltpu.make_async_copy(w_hbm.at[:, cols], tail_ref.at[:, pl.ds(i * BLOCK, BLOCK)], sems.at[1 + i]))
     sources = (head, source_of(head, 0, True), source_of(head, -2, False), source_of(head, 2, False))
-    sources += (source_of(head, -2, True), source_of(head, 2, True))
+    sources += (source_of(head, -2, True), source_of(head, 2, True), source_of(head, 4, False), source_of(head, 4, True))
+    copies = []
     for i, source in enumerate(sources):
         cols = pl.ds(pl.multiple_of(source * BLOCK, BLOCK), BLOCK)
-        copies.append(pltpu.make_async_copy(w_hbm.at[:, cols], w_ref.at[:, pl.ds(i * BLOCK, BLOCK)], sems.at[3 + i]))
+        target = w_ref.at[:, pl.ds(i * BLOCK, BLOCK)] if i < 6 else tail_ref.at[:, pl.ds((i - 6) * BLOCK, BLOCK)]
+        copies.append(pltpu.make_async_copy(w_hbm.at[:, cols], target, sems.at[i]))
     for copy in copies:
         copy.start()
     me = place_ref[0]
@@ -141,6 +140,9 @@
     put_row(st_ref, START, bound_ref[1:2, :])
     for copy in copies:
         copy.wait()
+
+
+def early_kernel(g_ref, y_ref, r_ref, l_ref, or_ref, ol_ref, w_ref, after, acc_ref):
     acc_ref[...] = project(None, (g_ref, y_ref, r_ref, l_ref, or_ref, ol_ref), range(6), w_ref)
 
 
@@ -160,7 +162,7 @@
     return at + 1 - 2 * lax.rem(at, 2) if flip else at
 
 
-def middle_kernel(place_ref, own_ref, q4_ref, st_in_ref, p_ref, st_ref):
+def middle_kernel(place_ref, own_ref, q4_ref, st_in_ref, after, p_ref, st_ref):
     queries = q4_ref[...]
     row = lax.broadcasted_iota(jnp.int32, (ROWS, LANES), 0)
     start = st_in_ref[START : START + 1, :].astype(jnp.int32)
@@ -405,19 +407,31 @@
         "pick_side", pick_kernel, shape(2 * ROWS, 2 * D, bf16), smem(1) + vmem(3) + token(1), (place, z2, z1, kv, gate)
     )
     side = moved(picked, "ctx", lambda i: i ^ 2)
-    p_near, st, early, tail = call(
+    p_near, st, weight, tail = call(
         "near",
         near_kernel,
-        (shape(3 * ROWS, LANES, bf16), state, shape(ROWS, HEADS * D, f32), shape(HEADS * D, 2 * BLOCK, bf16)),
-        smem(2) + vmem(5) + hbm(2) + vmem(5) + token(1),
-        (place, head, z2, z1, kv, q4, bound, pinned(grad_out), pinned(out_weight), other, right, left, other_right, other_left, picked),
-        [pltpu.VMEM((ROWS, BLOCK), bf16), pltpu.VMEM((HEADS * D, 6 * BLOCK), bf16), dma((9,))],
+        (
+            shape(3 * ROWS, LANES, bf16),
+            state,
+            shape(HEADS * D, 6 * BLOCK, bf16),
+            shape(HEADS * D, 2 * BLOCK, bf16),
+        ),
+        smem(2) + vmem(5) + hbm(1) + token(3),
+        (place, head, z2, z1, kv, q4, bound, pinned(out_weight), picked, other_right, other_left),
+        [dma((8,))],
     )
     own = call("join_slots", join_kernel, shape(SLOTS * ROWS, 2 * D, bf16), vmem(4) + token(1), (z2, z1, kv, side, st))
     par = moved(own, "ctx", lambda i: i ^ 1)
 
+    early = call(
+        "early",
+        early_kernel,
+        shape(ROWS, HEADS * D, f32),
+        vmem(7) + token(1),
+        (grad_out, other, right, left, other_right, other_left, weight, own),
+    )
     p_side, st = call(
-        "middle", middle_kernel, (shape(2 * ROWS, LANES, bf16), state), smem(1) + vmem(3), (place, own, q4, st)
+        "middle", middle_kernel, (shape(2 * ROWS, LANES, bf16), state), smem(1) + vmem(3) + token(1), (place, own, q4, st, early)
     )
     p_par, st = call(
         "across", across_kernel, (shape(REACH * ROWS, LANES, bf16), state), smem(1) + vmem(3), (place, par, q4, st)

time: 56.1 us -> 54.7 us (0.975)
  waiting for transfers between devices: 17.9 us -> 16 us
  starting transfers between devices: 22.3 us -> 22.9 us
    ppermute x17, waiting for transfers between devices: 17.9 us -> 16 us  [moved(): lax.ppermute(x, axis, [(i, to(i)) for i in range(lax.axis_size(axis))])]
    pallas_call x17 -> x18, Pallas kernels: 13.9 us -> 13.8 us  [call(): pl.pallas_call(kernel, out_shape=outs, in_specs=ins, out_specs=vmem(1)[0]...]
  transfers between devices with their start and end apart: 17 -> 17, of which waited for: 7 -> 6; matrix products, arithmetic and copies ran while one was open for 1% -> 2% of each run, Pallas kernels for 20% -> 22%
where the time goes in v8:
time: 54.7 us; the launch traced here: 54.3 us
  starting transfers between devices  22.9 us (42%)
  waiting for transfers between devices  16 us (29%)
  Pallas kernels  13.8 us (25%)
  other arithmetic  0.83 us (2%)
  between operations  0.82 us (1%)
    ppermute x17, starting transfers between devices, moved(): lax.ppermute(x, axis, [(i, to(i)) for i in range(lax.axis_size(axis))])  22.9 us
    ppermute x17, waiting for transfers between devices, moved(): lax.ppermute(x, axis, [(i, to(i)) for i in range(lax.axis_size(axis))])  16 us
    pallas_call x18, Pallas kernels, call(): pl.pallas_call(kernel, out_shape=outs, in_specs=ins, out_specs=vmem(1)[0]...  13.8 us
  transfers between devices with their start and end apart: 17, of which 6 were waited for; matrix products, arithmetic and copies ran while one was open for 2% of the time, Pallas kernels for 22%

profile of v8, /device:TPU:64, one launch (start us, length us, event | category | flops | bytes accessed | tf_op | source)
XLA Modules:
  0.0 54.3 jit_solution(16435207077716168435)
XLA Ops:
  0.6 3.3 %collective-permute-start.2 = (bf16[192,512]{1,0:T(8,128)(2,1)}, bf16[192,512]{1,0:T(8,128)(2,1)S(1)}, u32[]{:S(2)}, u32[]{:S(2)}) collective-permute-start(bf16[192,512]{1,0:T(8,128)(2,1)} %g_ref.1), channel_id=1, source_target_pairs={{0,1},{1,0},{2,3},{3,2},{4,5},{5,4},{6,7},{7,6},{8,9},{9,8},{10,11... | collective-permute-start | bytes 589832 | tf_op jit(solution)/shard_map/ppermute | solution.py:351
  3.9 1.5 %collective-permute-start.3 = (bf16[192,512]{1,0:T(8,128)(2,1)}, bf16[192,512]{1,0:T(8,128)(2,1)S(1)}, u32[]{:S(2)}, u32[]{:S(2)}) collective-permute-start(bf16[192,512]{1,0:T(8,128)(2,1)} %g_ref.1), channel_id=1, source_target_pairs={{0,2},{1,3},{2,4},{3,5},{4,6},{5,7},{6,0},{7,1},{8,10},{9,11},{10,... | collective-permute-start | bytes 589832 | tf_op jit(solution)/shard_map/ppermute | solution.py:351
  5.4 1.7 %collective-permute-start.4 = (bf16[192,512]{1,0:T(8,128)(2,1)}, bf16[192,512]{1,0:T(8,128)(2,1)S(1)}, u32[]{:S(2)}, u32[]{:S(2)}) collective-permute-start(bf16[192,512]{1,0:T(8,128)(2,1)} %g_ref.1), channel_id=1, source_target_pairs={{0,6},{1,7},{2,0},{3,1},{4,2},{5,3},{6,4},{7,5},{8,14},{9,15},{10,... | collective-permute-start | bytes 589832 | tf_op jit(solution)/shard_map/ppermute | solution.py:351
  7.1 0.8 %pad_add_fusion.z0_ref = bf16[192,256]{1,0:T(8,128)(2,1)S(1)} fusion(bf16[192,128]{1,0:T(8,128)(2,1)} %param.8, bf16[192,128]{1,0:T(8,128)(2,1)} %param.7), kind=kLoop, calls=%fused_computation | loop fusion | flops 196608 | bytes 196608 | tf_op jit(solution)/shard_map/add | solution.py:388
  8.0 4.6 %collective-permute-start = (bf16[192,256]{1,0:T(8,128)(2,1)S(1)}, bf16[192,256]{1,0:T(8,128)(2,1)S(1)}, u32[]{:S(2)}, u32[]{:S(2)}) collective-permute-start(bf16[192,256]{1,0:T(8,128)(2,1)S(1)} %pad_add_fusion.z0_ref), channel_id=1, source_target_pairs={{0,64},{8,72},{16,80},{24,88},{32,96},{40,104},{48,112},{56,120},{... | collective-permute-start | bytes 294920 | tf_op jit(solution)/shard_map/ppermute | solution.py:351
  12.5 1.0 %collective-permute-start.1 = (bf16[192,256]{1,0:T(8,128)(2,1)S(1)}, bf16[192,256]{1,0:T(8,128)(2,1)S(1)}, u32[]{:S(2)}, u32[]{:S(2)}) collective-permute-start(bf16[192,256]{1,0:T(8,128)(2,1)S(1)} %pad_add_fusion.z0_ref), channel_id=1, source_target_pairs={{0,32},{8,40},{16,48},{24,56},{32,64},{40,72},{48,80},{56,88},{64,... | collective-permute-start | bytes 294920 | tf_op jit(solution)/shard_map/ppermute | solution.py:351
  13.6 0.9 %load.1 = (bf16[768,128]{1,0:T(8,128)(2,1)S(1)}, f32[8,768]{1,0:T(8,128)S(1)}) custom-call(s32[1]{0:T(128)} %bitcast.place_ref, s32[8]{0:T(128)} %len_hbm.1, bf16[192,512]{1,0:T(8,128)(2,1)} %q_hbm.1), custom_call_target="tpu_custom_call" | custom-call | flops 1 | bytes 1 | tf_op jit(solution)/shard_map/load/pallas_call | solution.py:365
  14.5 1.6 %collective-permute-start.7 = (bf16[192,512]{1,0:T(8,128)(2,1)S(1)}, bf16[192,512]{1,0:T(8,128)(2,1)S(1)}, u32[]{:S(2)}, u32[]{:S(2)}) collective-permute-start(bf16[192,512]{1,0:T(8,128)(2,1)S(1)} %collective-permute-done.2.refs_0_.y_ref), channel_id=1, source_target_pairs={{0,6},{1,7},{2,0},{3,1},{4,2},{5,3},{6,4},{7,5},{8,14},{9,15},{10,... | collective-permute-start | bytes 589832 | tf_op jit(solution)/shard_map/ppermute | solution.py:351
  16.1 0.5 collective-permute-start.6
  16.6 0.5 %collective-permute-done.1.z1_ref = bf16[192,256]{1,0:T(8,128)(2,1)S(1)} collective-permute-done((bf16[192,256]{1,0:T(8,128)(2,1)S(1)}, bf16[192,256]{1,0:T(8,128)(2,1)S(1)}, u32[]{:S(2)}, u32[]{:S(2)}) %collective-permute-start.1) | collective-permute-done | bytes 98336 | tf_op jit(solution)/shard_map/ppermute | solution.py:351
  17.2 0.8 %collective-permute-start.5 = (bf16[384,256]{1,0:T(8,128)(2,1)S(1)}, bf16[384,256]{1,0:T(8,128)(2,1)S(1)}, u32[]{:S(2)}, u32[]{:S(2)}) collective-permute-start(bf16[384,256]{1,0:T(8,128)(2,1)S(1)} %pick_side.1.refs_0_), channel_id=1, source_target_pairs={{0,16},{8,24},{16,0},{24,8},{32,48},{40,56},{48,32},{56,40},{64,80... | collective-permute-start | bytes 589832 | tf_op jit(solution)/shard_map/ppermute | solution.py:351
  18.0 2.3 %collective-permute-done.7.refs_2_.ol_ref = bf16[192,512]{1,0:T(8,128)(2,1)S(1)} collective-permute-done((bf16[192,512]{1,0:T(8,128)(2,1)S(1)}, bf16[192,512]{1,0:T(8,128)(2,1)S(1)}, u32[]{:S(2)}, u32[]{:S(2)}) %collective-permute-start.7) | collective-permute-done | bytes 196640 | tf_op jit(solution)/shard_map/ppermute | solution.py:351
  20.2 2.8 %collective-permute-done.6.refs_1_.or_ref = bf16[192,512]{1,0:T(8,128)(2,1)S(1)} collective-permute-done((bf16[192,512]{1,0:T(8,128)(2,1)S(1)}, bf16[192,512]{1,0:T(8,128)(2,1)S(1)}, u32[]{:S(2)}, u32[]{:S(2)}) %collective-permute-start.6) | collective-permute-done | bytes 196640 | tf_op jit(solution)/shard_map/ppermute | solution.py:351
  23.0 3.4 %near.1 = (bf16[576,768]{1,0:T(8,128)(2,1)S(1)}, f32[152,768]{1,0:T(8,128)S(1)}, bf16[512,3072]{1,0:T(8,128)(2,1)S(1)}, bf16[512,1024]{1,0:T(8,128)(2,1)S(1)}) custom-call(s32[1]{0:T(128)} %bitcast.place_ref, s32[1]{0:T(128)} %bitcast.1.head_ref, bf16[192,256]{1,0:T(8,128)(2,1)S(1)} %collective-permute-done.z2_ref, ...), custom_call_target="tpu_custom_call" | custom-call | flops 1 | bytes 1 | tf_op jit(solution)/shard_map/near/pallas_call | solution.py:365
  26.6 3.2 %collective-permute-start.9 = (bf16[192,512]{1,0:T(8,128)(2,1)S(1)}, bf16[192,512]{1,0:T(8,128)(2,1)S(1)}, u32[]{:S(2)}, u32[]{:S(2)}) collective-permute-start(bf16[192,512]{1,0:T(8,128)(2,1)S(1)} %collective-permute-done.7.refs_2_.ol_ref), channel_id=1, source_target_pairs={{0,6},{1,7},{2,0},{3,1},{4,2},{5,3},{6,4},{7,5},{8,14},{9,15},{10,... | collective-permute-start | bytes 589832 | tf_op jit(solution)/shard_map/ppermute | solution.py:351
  29.9 1.2 %early.1.after.early_ref = f32[192,512]{1,0:T(8,128)S(1)} custom-call(bf16[192,512]{1,0:T(8,128)(2,1)S(1)} %copy-done, bf16[192,512]{1,0:T(8,128)(2,1)S(1)} %collective-permute-done.2.refs_0_.y_ref, bf16[192,512]{1,0:T(8,128)(2,1)S(1)} %collective-permute-done.3.refs_1_.r_ref, bf16[192,512]{1,0:T(8,128)(2,1)S(1)} %collective-permute-done.4.refs_2_.l_ref, ...), custom_call_target="tpu_custom_call" | custom-call | flops 1 | bytes 1 | tf_op jit(solution)/shard_map/early/pallas_call | solution.py:365
  31.0 0.9 %middle.1 = (bf16[384,768]{1,0:T(8,128)(2,1)S(1)}, f32[152,768]{1,0:T(8,128)S(1)}) custom-call(s32[1]{0:T(128)} %bitcast.place_ref, bf16[960,256]{1,0:T(8,128)(2,1)S(1)} %join_slots.1.after.own_ref, bf16[768,128]{1,0:T(8,128)(2,1)S(1)} %get-tuple-element.30.refs_3_.q4_ref, f32[152,768]{1,0:T(8,128)S(1)} %get-tuple-element.32.refs_0_.st_in_ref, ...), custom_call_target="tpu_custom_call" | custom-call | flops 1 | bytes 1 | tf_op jit(solution)/shard_map/middle/pallas_call | solution.py:365
  31.9 1.6 %across.1 = (bf16[768,768]{1,0:T(8,128)(2,1)S(1)}, f32[152,768]{1,0:T(8,128)S(1)}) custom-call(s32[1]{0:T(128)} %bitcast.place_ref, bf16[960,256]{1,0:T(8,128)(2,1)S(1)} %collective-permute-done.10.par_ref, bf16[768,128]{1,0:T(8,128)(2,1)S(1)} %get-tuple-element.30.refs_3_.q4_ref, f32[152,768]{1,0:T(8,128)S(1)} %get-tuple-element.37.st_in_ref), custom_call_target="tpu_custom_call" | custom-call | flops 1 | bytes 1 | tf_op jit(solution)/shard_map/across/pallas_call | solution.py:365
  33.5 1.6 %collective-permute-done.8.a_ref = bf16[192,512]{1,0:T(8,128)(2,1)S(1)} collective-permute-done((bf16[192,512]{1,0:T(8,128)(2,1)S(1)}, bf16[192,512]{1,0:T(8,128)(2,1)S(1)}, u32[]{:S(2)}, u32[]{:S(2)}) %collective-permute-start.8) | collective-permute-done | bytes 196640 | tf_op jit(solution)/shard_map/ppermute | solution.py:351
  35.1 1.4 %cross_far.1 = (bf16[384,256]{1,0:T(8,128)(2,1)S(1)}, bf16[768,128]{1,0:T(8,128)(2,1)S(1)}, f32[152,768]{1,0:T(8,128)S(1)}) custom-call(s32[1]{0:T(128)} %bitcast.place_ref, bf16[192,512]{1,0:T(8,128)(2,1)S(1)} %collective-permute-done.8.a_ref, bf16[192,512]{1,0:T(8,128)(2,1)S(1)} %collective-permute-done.9.b_ref, f32[192,512]{1,0:T(8,128)S(1)} %early.1.after.early_ref, ...), custom_call_target="tpu_custom_call" | custom-call | flops 1 | bytes 1 | tf_op jit(solution)/shard_map/cross_far/pallas_call | solution.py:365
  36.5 0.1 collective-permute-start.11
  36.6 0.8 %cross_near.1 = (bf16[576,256]{1,0:T(8,128)(2,1)S(1)}, f32[152,768]{1,0:T(8,128)S(1)}) custom-call(s32[1]{0:T(128)} %bitcast.place_ref, bf16[768,128]{1,0:T(8,128)(2,1)S(1)} %get-tuple-element.30.refs_3_.q4_ref, bf16[960,256]{1,0:T(8,128)(2,1)S(1)} %collective-permute-done.10.par_ref, bf16[768,768]{1,0:T(8,128)(2,1)S(1)} %get-tuple-element.38.p_ref, ...), custom_call_target="tpu_custom_call" | custom-call | flops 4000000000 | bytes 1 | tf_op jit(solution)/shard_map/cross_near/pallas_call | solution.py:365
  37.4 1.0 %collective-permute-start.12 = (bf16[576,256]{1,0:T(8,128)(2,1)S(1)}, bf16[576,256]{1,0:T(8,128)(2,1)S(1)}, u32[]{:S(2)}, u32[]{:S(2)}) collective-permute-start(bf16[576,256]{1,0:T(8,128)(2,1)S(1)} %get-tuple-element.49), channel_id=1, source_target_pairs={{0,8},{8,0},{16,24},{24,16},{32,40},{40,32},{48,56},{56,48},{64,72... | collective-permute-start | bytes 884744 | tf_op jit(solution)/shard_map/ppermute | solution.py:351
  38.4 0.8 %own_far.1 = (f32[384,256]{1,0:T(8,128)S(1)}, f32[152,768]{1,0:T(8,128)S(1)}) custom-call(bf16[768,128]{1,0:T(8,128)(2,1)S(1)} %get-tuple-element.30.refs_3_.q4_ref, bf16[960,256]{1,0:T(8,128)(2,1)S(1)} %join_slots.1.after.own_ref, bf16[576,768]{1,0:T(8,128)(2,1)S(1)} %get-tuple-element.33.near_ref, bf16[384,768]{1,0:T(8,128)(2,1)S(1)} %get-tuple-element.35.side_ref, ...), custom_call_target="tpu_custom_call" | custom-call | flops 4000000000 | bytes 1 | tf_op jit(solution)/shard_map/own_far/pallas_call | solution.py:365
  39.3 0.8 %collective-permute-start.14 = (bf16[192,256]{1,0:T(8,128)(2,1)S(1)}, bf16[192,256]{1,0:T(8,128)(2,1)S(1)}, u32[]{:S(2)}, u32[]{:S(2)}) collective-permute-start(bf16[192,256]{1,0:T(8,128)(2,1)S(1)} %get-tuple-element.54), channel_id=1, source_target_pairs={{0,16},{8,24},{16,0},{24,8},{32,48},{40,56},{48,32},{56,40},{64,80... | collective-permute-start | bytes 294920 | tf_op jit(solution)/shard_map/ppermute | solution.py:351
  40.0 0.8 %own_near.1 = (f32[384,256]{1,0:T(8,128)S(1)}, f32[152,768]{1,0:T(8,128)S(1)}) custom-call(bf16[768,128]{1,0:T(8,128)(2,1)S(1)} %get-tuple-element.30.refs_3_.q4_ref, bf16[960,256]{1,0:T(8,128)(2,1)S(1)} %join_slots.1.after.own_ref, bf16[576,768]{1,0:T(8,128)(2,1)S(1)} %get-tuple-element.33.near_ref, bf16[384,768]{1,0:T(8,128)(2,1)S(1)} %get-tuple-element.35.side_ref, ...), custom_call_target="tpu_custom_call" | custom-call | flops 4000000000 | bytes 1 | tf_op jit(solution)/shard_map/own_near/pallas_call | solution.py:365
  40.9 1.4 %collective-permute-start.13 = (bf16[192,256]{1,0:T(8,128)(2,1)S(1)}, bf16[192,256]{1,0:T(8,128)(2,1)S(1)}, u32[]{:S(2)}, u32[]{:S(2)}) collective-permute-start(bf16[192,256]{1,0:T(8,128)(2,1)S(1)} %get-tuple-element.53), channel_id=1, source_target_pairs={{0,16},{8,24},{16,0},{24,8},{32,48},{40,56},{48,32},{56,40},{64,80... | collective-permute-start | bytes 294920 | tf_op jit(solution)/shard_map/ppermute | solution.py:351
  42.3 2.5 %collective-permute-done.14.side_ref.far_ref = bf16[192,256]{1,0:T(8,128)(2,1)S(1)} collective-permute-done((bf16[192,256]{1,0:T(8,128)(2,1)S(1)}, bf16[192,256]{1,0:T(8,128)(2,1)S(1)}, u32[]{:S(2)}, u32[]{:S(2)}) %collective-permute-start.14) | collective-permute-done | bytes 98336 | tf_op jit(solution)/shard_map/ppermute | solution.py:351
  45.0 1.2 %own_last.1 = (f32[192,256]{1,0:T(8,128)S(1)}, bf16[192,512]{1,0:T(8,128)(2,1)}) custom-call(bf16[768,128]{1,0:T(8,128)(2,1)S(1)} %get-tuple-element.30.refs_3_.q4_ref, bf16[960,256]{1,0:T(8,128)(2,1)S(1)} %join_slots.1.after.own_ref, bf16[576,768]{1,0:T(8,128)(2,1)S(1)} %get-tuple-element.33.near_ref, bf16[384,768]{1,0:T(8,128)(2,1)S(1)} %get-tuple-element.35.side_ref, ...), custom_call_target="tpu_custom_call" | custom-call | flops 1 | bytes 1 | tf_op jit(solution)/shard_map/own_last/pallas_call | solution.py:365
  46.3 1.1 %collective-permute-start.15 = (bf16[192,256]{1,0:T(8,128)(2,1)S(1)}, bf16[192,256]{1,0:T(8,128)(2,1)S(1)}, u32[]{:S(2)}, u32[]{:S(2)}) collective-permute-start(bf16[192,256]{1,0:T(8,128)(2,1)S(1)} %relay_near.1), channel_id=1, source_target_pairs={{0,224},{8,232},{16,240},{24,248},{32,0},{40,8},{48,16},{56,24},{6... | collective-permute-start | bytes 294920 | tf_op jit(solution)/shard_map/ppermute | solution.py:351
  47.4 6.3 %collective-permute-done.16.two_ref = bf16[192,256]{1,0:T(8,128)(2,1)S(1)} collective-permute-done((bf16[192,256]{1,0:T(8,128)(2,1)S(1)}, bf16[192,256]{1,0:T(8,128)(2,1)S(1)}, u32[]{:S(2)}, u32[]{:S(2)}) %collective-permute-start.16) | collective-permute-done | bytes 98336 | tf_op jit(solution)/shard_map/ppermute | solution.py:351
  53.6 0.7 %finish.1 = (bf16[192,128]{1,0:T(8,128)(2,1)}, bf16[192,128]{1,0:T(8,128)(2,1)}) custom-call(s32[1]{0:T(128)} %bitcast.place_ref, f32[192,256]{1,0:T(8,128)S(1)} %get-tuple-element.52.refs_1_.own_ref, bf16[576,256]{1,0:T(8,128)(2,1)S(1)} %collective-permute-done.12.back_ref, bf16[192,256]{1,0:T(8,128)(2,1)S(1)} %collective-permute-done.13.near_ref, ...), custom_call_target="tpu_custom_call" | custom-call | flops 1 | bytes 1 | tf_op jit(solution)/shard_map/finish/pallas_call | solution.py:365
  (23 shorter events, 0.5 us)
Async XLA Ops:
  0.6 13.9 %collective-permute-start.2 = (bf16[192,512]{1,0:T(8,128)(2,1)}, bf16[192,512]{1,0:T(8,128)(2,1)S(1)}, u32[]{:S(2)}, u32[]{:S(2)}) collective-permute-start(bf16[192,512]{1,0:T(8,128)(2,1)} %g_ref.1), channel_id=1, source_target_pairs={{0,1},{1,0},{2,3},{3,2},{4,5},{5,4},{6,7},{7,6},{8,9},{9,8},{10,11... | collective-permute-start | bytes 589832 | tf_op jit(solution)/shard_map/ppermute | solution.py:351
  3.9 12.2 %collective-permute-start.3 = (bf16[192,512]{1,0:T(8,128)(2,1)}, bf16[192,512]{1,0:T(8,128)(2,1)S(1)}, u32[]{:S(2)}, u32[]{:S(2)}) collective-permute-start(bf16[192,512]{1,0:T(8,128)(2,1)} %g_ref.1), channel_id=1, source_target_pairs={{0,2},{1,3},{2,4},{3,5},{4,6},{5,7},{6,0},{7,1},{8,10},{9,11},{10,... | collective-permute-start | bytes 589832 | tf_op jit(solution)/shard_map/ppermute | solution.py:351
  5.4 11.2 %collective-permute-start.4 = (bf16[192,512]{1,0:T(8,128)(2,1)}, bf16[192,512]{1,0:T(8,128)(2,1)S(1)}, u32[]{:S(2)}, u32[]{:S(2)}) collective-permute-start(bf16[192,512]{1,0:T(8,128)(2,1)} %g_ref.1), channel_id=1, source_target_pairs={{0,6},{1,7},{2,0},{3,1},{4,2},{5,3},{6,4},{7,5},{8,14},{9,15},{10,... | collective-permute-start | bytes 589832 | tf_op jit(solution)/shard_map/ppermute | solution.py:351
  8.0 8.6 %collective-permute-start = (bf16[192,256]{1,0:T(8,128)(2,1)S(1)}, bf16[192,256]{1,0:T(8,128)(2,1)S(1)}, u32[]{:S(2)}, u32[]{:S(2)}) collective-permute-start(bf16[192,256]{1,0:T(8,128)(2,1)S(1)} %pad_add_fusion.z0_ref), channel_id=1, source_target_pairs={{0,64},{8,72},{16,80},{24,88},{32,96},{40,104},{48,112},{56,120},{... | collective-permute-start | bytes 294920 | tf_op jit(solution)/shard_map/ppermute | solution.py:351
  12.5 4.6 %collective-permute-start.1 = (bf16[192,256]{1,0:T(8,128)(2,1)S(1)}, bf16[192,256]{1,0:T(8,128)(2,1)S(1)}, u32[]{:S(2)}, u32[]{:S(2)}) collective-permute-start(bf16[192,256]{1,0:T(8,128)(2,1)S(1)} %pad_add_fusion.z0_ref), channel_id=1, source_target_pairs={{0,32},{8,40},{16,48},{24,56},{32,64},{40,72},{48,80},{56,88},{64,... | collective-permute-start | bytes 294920 | tf_op jit(solution)/shard_map/ppermute | solution.py:351
  14.5 5.7 %collective-permute-start.7 = (bf16[192,512]{1,0:T(8,128)(2,1)S(1)}, bf16[192,512]{1,0:T(8,128)(2,1)S(1)}, u32[]{:S(2)}, u32[]{:S(2)}) collective-permute-start(bf16[192,512]{1,0:T(8,128)(2,1)S(1)} %collective-permute-done.2.refs_0_.y_ref), channel_id=1, source_target_pairs={{0,6},{1,7},{2,0},{3,1},{4,2},{5,3},{6,4},{7,5},{8,14},{9,15},{10,... | collective-permute-start | bytes 589832 | tf_op jit(solution)/shard_map/ppermute | solution.py:351
  16.1 6.9 %collective-permute-start.6 = (bf16[192,512]{1,0:T(8,128)(2,1)S(1)}, bf16[192,512]{1,0:T(8,128)(2,1)S(1)}, u32[]{:S(2)}, u32[]{:S(2)}) collective-permute-start(bf16[192,512]{1,0:T(8,128)(2,1)S(1)} %collective-permute-done.2.refs_0_.y_ref), channel_id=1, source_target_pairs={{0,2},{1,3},{2,4},{3,5},{4,6},{5,7},{6,0},{7,1},{8,10},{9,11},{10,... | collective-permute-start | bytes 589832 | tf_op jit(solution)/shard_map/ppermute | solution.py:351
  17.2 9.2 %collective-permute-start.5 = (bf16[384,256]{1,0:T(8,128)(2,1)S(1)}, bf16[384,256]{1,0:T(8,128)(2,1)S(1)}, u32[]{:S(2)}, u32[]{:S(2)}) collective-permute-start(bf16[384,256]{1,0:T(8,128)(2,1)S(1)} %pick_side.1.refs_0_), channel_id=1, source_target_pairs={{0,16},{8,24},{16,0},{24,8},{32,48},{40,56},{48,32},{56,40},{64,80... | collective-permute-start | bytes 589832 | tf_op jit(solution)/shard_map/ppermute | solution.py:351
  23.0 6.9 %copy-start = (bf16[192,512]{1,0:T(8,128)(2,1)S(1)}, bf16[192,512]{1,0:T(8,128)(2,1)}, u32[]{:S(2)}) copy-start(bf16[192,512]{1,0:T(8,128)(2,1)} %g_ref.1) | copy-start | bytes 589828
  26.4 5.5 %collective-permute-start.10 = (bf16[960,256]{1,0:T(8,128)(2,1)S(1)}, bf16[960,256]{1,0:T(8,128)(2,1)S(1)}, u32[]{:S(2)}, u32[]{:S(2)}) collective-permute-start(bf16[960,256]{1,0:T(8,128)(2,1)S(1)} %join_slots.1.after.own_ref), channel_id=1, source_target_pairs={{0,8},{8,0},{16,24},{24,16},{32,40},{40,32},{48,56},{56,48},{64,72... | collective-permute-start | bytes 1474568 | tf_op jit(solution)/shard_map/ppermute | solution.py:351
  26.5 8.5 %collective-permute-start.8 = (bf16[192,512]{1,0:T(8,128)(2,1)S(1)}, bf16[192,512]{1,0:T(8,128)(2,1)S(1)}, u32[]{:S(2)}, u32[]{:S(2)}) collective-permute-start(bf16[192,512]{1,0:T(8,128)(2,1)S(1)} %collective-permute-done.3.refs_1_.r_ref), channel_id=1, source_target_pairs={{0,2},{1,3},{2,4},{3,5},{4,6},{5,7},{6,0},{7,1},{8,10},{9,11},{10,... | collective-permute-start | bytes 589832 | tf_op jit(solution)/shard_map/ppermute | solution.py:351
  26.6 8.4 %collective-permute-start.9 = (bf16[192,512]{1,0:T(8,128)(2,1)S(1)}, bf16[192,512]{1,0:T(8,128)(2,1)S(1)}, u32[]{:S(2)}, u32[]{:S(2)}) collective-permute-start(bf16[192,512]{1,0:T(8,128)(2,1)S(1)} %collective-permute-done.7.refs_2_.ol_ref), channel_id=1, source_target_pairs={{0,6},{1,7},{2,0},{3,1},{4,2},{5,3},{6,4},{7,5},{8,14},{9,15},{10,... | collective-permute-start | bytes 589832 | tf_op jit(solution)/shard_map/ppermute | solution.py:351
  36.5 2.7 %collective-permute-start.11 = (bf16[384,256]{1,0:T(8,128)(2,1)S(1)}, bf16[384,256]{1,0:T(8,128)(2,1)S(1)}, u32[]{:S(2)}, u32[]{:S(2)}) collective-permute-start(bf16[384,256]{1,0:T(8,128)(2,1)S(1)} %get-tuple-element.45), channel_id=1, source_target_pairs={{0,8},{8,0},{16,24},{24,16},{32,40},{40,32},{48,56},{56,48},{64,72... | collective-permute-start | bytes 589832 | tf_op jit(solution)/shard_map/ppermute | solution.py:351
  37.4 3.5 %collective-permute-start.12 = (bf16[576,256]{1,0:T(8,128)(2,1)S(1)}, bf16[576,256]{1,0:T(8,128)(2,1)S(1)}, u32[]{:S(2)}, u32[]{:S(2)}) collective-permute-start(bf16[576,256]{1,0:T(8,128)(2,1)S(1)} %get-tuple-element.49), channel_id=1, source_target_pairs={{0,8},{8,0},{16,24},{24,16},{32,40},{40,32},{48,56},{56,48},{64,72... | collective-permute-start | bytes 884744 | tf_op jit(solution)/shard_map/ppermute | solution.py:351
  39.3 5.6 %collective-permute-start.14 = (bf16[192,256]{1,0:T(8,128)(2,1)S(1)}, bf16[192,256]{1,0:T(8,128)(2,1)S(1)}, u32[]{:S(2)}, u32[]{:S(2)}) collective-permute-start(bf16[192,256]{1,0:T(8,128)(2,1)S(1)} %get-tuple-element.54), channel_id=1, source_target_pairs={{0,16},{8,24},{16,0},{24,8},{32,48},{40,56},{48,32},{56,40},{64,80... | collective-permute-start | bytes 294920 | tf_op jit(solution)/shard_map/ppermute | solution.py:351
  40.9 5.3 %collective-permute-start.13 = (bf16[192,256]{1,0:T(8,128)(2,1)S(1)}, bf16[192,256]{1,0:T(8,128)(2,1)S(1)}, u32[]{:S(2)}, u32[]{:S(2)}) collective-permute-start(bf16[192,256]{1,0:T(8,128)(2,1)S(1)} %get-tuple-element.53), channel_id=1, source_target_pairs={{0,16},{8,24},{16,0},{24,8},{32,48},{40,56},{48,32},{56,40},{64,80... | collective-permute-start | bytes 294920 | tf_op jit(solution)/shard_map/ppermute | solution.py:351
  44.9 8.8 %collective-permute-start.16 = (bf16[192,256]{1,0:T(8,128)(2,1)S(1)}, bf16[192,256]{1,0:T(8,128)(2,1)S(1)}, u32[]{:S(2)}, u32[]{:S(2)}) collective-permute-start(bf16[192,256]{1,0:T(8,128)(2,1)S(1)} %relay_far.1.refs_0_), channel_id=1, source_target_pairs={{0,192},{8,200},{16,208},{24,216},{32,224},{40,232},{48,240},{56,2... | collective-permute-start | bytes 294920 | tf_op jit(solution)/shard_map/ppermute | solution.py:351
  46.3 7.4 %collective-permute-start.15 = (bf16[192,256]{1,0:T(8,128)(2,1)S(1)}, bf16[192,256]{1,0:T(8,128)(2,1)S(1)}, u32[]{:S(2)}, u32[]{:S(2)}) collective-permute-start(bf16[192,256]{1,0:T(8,128)(2,1)S(1)} %relay_near.1), channel_id=1, source_target_pairs={{0,224},{8,232},{16,240},{24,248},{32,0},{40,8},{48,16},{56,24},{6... | collective-permute-start | bytes 294920 | tf_op jit(solution)/shard_map/ppermute | solution.py:351

commit v9 on v8

--- a/solution.py
+++ b/solution.py
@@ -115,15 +115,14 @@
 
 
 def near_kernel(place_ref, head_ref, z2_ref, z1_ref, z0_ref, q4_ref, bound_ref, w_hbm, *refs):
-    p_ref, st_ref, w_ref, tail_ref, sems = refs[-5:]
+    p_ref, st_ref, w_ref, sems = refs[-4:]
     head = head_ref[0]
     sources = (head, source_of(head, 0, True), source_of(head, -2, False), source_of(head, 2, False))
     sources += (source_of(head, -2, True), source_of(head, 2, True), source_of(head, 4, False), source_of(head, 4, True))
     copies = []
     for i, source in enumerate(sources):
         cols = pl.ds(pl.multiple_of(source * BLOCK, BLOCK), BLOCK)
-        target = w_ref.at[:, pl.ds(i * BLOCK, BLOCK)] if i < 6 else tail_ref.at[:, pl.ds((i - 6) * BLOCK, BLOCK)]
-        copies.append(pltpu.make_async_copy(w_hbm.at[:, cols], target, sems.at[i]))
+        copies.append(pltpu.make_async_copy(w_hbm.at[:, cols], w_ref.at[:, pl.ds(i * BLOCK, BLOCK)], sems.at[i]))
     for copy in copies:
         copy.start()
     me = place_ref[0]
@@ -142,19 +141,20 @@
         copy.wait()
 
 
-def early_kernel(g_ref, y_ref, r_ref, l_ref, or_ref, ol_ref, w_ref, after, acc_ref):
-    acc_ref[...] = project(None, (g_ref, y_ref, r_ref, l_ref, or_ref, ol_ref), range(6), w_ref)
+def project_kernel(*refs):
+    pieces, (w_ref, after, g4_ref, gt_ref) = refs[:8], refs[8:]
+    acc = None
+    for i, piece in enumerate(pieces):
+        part = dot(piece[...], w_ref[:, i * BLOCK : (i + 1) * BLOCK], 1, 1)
+        acc = part if acc is None else acc + part
+    acc = acc.astype(jnp.bfloat16)
+    for h in range(HEADS):
+        g4_ref[h * ROWS : (h + 1) * ROWS, :] = acc[:, h * D : (h + 1) * D]
+    gt_ref[...] = jnp.transpose(g4_ref[...].astype(jnp.float32))
 
 
 def rows(i):
     return pl.ds(pl.multiple_of(i * ROWS, ROWS), ROWS)
-
-
-def project(acc, pieces, sources, w_ref):
-    for piece, source in zip(pieces, sources):
-        part = dot(piece[...], w_ref[:, source * BLOCK : (source + 1) * BLOCK], 1, 1)
-        acc = part if acc is None else acc + part
-    return acc
 
 
 def source_of(head, by, flip):
@@ -178,7 +178,7 @@
     put_row(st_ref, START, st_in_ref[START : START + 1, :])
 
 
-def across_kernel(place_ref, par_ref, q4_ref, st_in_ref, p_ref, st_ref):
+def across_kernel(place_ref, par_ref, q4_ref, gt_ref, st_in_ref, p_ref, st_ref):
     me = place_ref[0]
     core = lax.rem(me, 2)
     chip = me - core
@@ -193,7 +193,7 @@
         p_ref[i * ROWS : (i + 1) * ROWS, :] = prob
         peaks.append(peak)
     out, mass, top = state
-    st_ref[:D, :] = out / mass
+    put_row(st_ref, DOT, jnp.sum(gt_ref[...] * out, axis=0, keepdims=True) / mass)
     log_total = top + jnp.log2(mass)
     for i, peak in enumerate(peaks):
         put_row(st_ref, PEAK + i, jnp.exp2(peak - log_total))
@@ -220,18 +220,12 @@
     return back_block(par_ref[rows(slot), :], p_ref[rows(slot - core), :], share, g4, q4_ref[...], rd)
 
 
-def cross_far(place_ref, a_ref, b_ref, early_ref, w_ref, q4_ref, par_ref, p_ref, st_in_ref, out_ref, g_ref, st_ref):
+def cross_far(place_ref, q4_ref, par_ref, p_ref, g_ref, st_in_ref, out_ref, st_ref):
     core = lax.rem(place_ref[0], 2)
-    acc = project(early_ref[...], (a_ref, b_ref), range(2), w_ref)
-    acc = acc.astype(jnp.bfloat16)
-    for h in range(HEADS):
-        g_ref[h * ROWS : (h + 1) * ROWS, :] = acc[:, h * D : (h + 1) * D]
     g4 = g_ref[...]
-    gt = jnp.transpose(g4.astype(jnp.float32))
-    rd = jnp.sum(gt * st_in_ref[:D, :], axis=0, keepdims=True)
+    rd = st_in_ref[DOT : DOT + 1, :]
+    st_ref[DOT : DOT + 1, :] = rd
     st_ref[PEAK:, :] = st_in_ref[PEAK:, :]
-    put_row(st_ref, DOT, rd)
-
     dk, dv, dq = cross_step(1, core, par_ref, p_ref, st_ref, g4, q4_ref, rd)
     put(out_ref, 1, dk, dv)
     st_ref[:D, :] = dq
@@ -407,14 +401,13 @@
         "pick_side", pick_kernel, shape(2 * ROWS, 2 * D, bf16), smem(1) + vmem(3) + token(1), (place, z2, z1, kv, gate)
     )
     side = moved(picked, "ctx", lambda i: i ^ 2)
-    p_near, st, weight, tail = call(
+    p_near, st, weight = call(
         "near",
         near_kernel,
         (
             shape(3 * ROWS, LANES, bf16),
             state,
-            shape(HEADS * D, 6 * BLOCK, bf16),
-            shape(HEADS * D, 2 * BLOCK, bf16),
+            shape(HEADS * D, 8 * BLOCK, bf16),
         ),
         smem(2) + vmem(5) + hbm(1) + token(3),
         (place, head, z2, z1, kv, q4, bound, pinned(out_weight), picked, other_right, other_left),
@@ -423,26 +416,22 @@
     own = call("join_slots", join_kernel, shape(SLOTS * ROWS, 2 * D, bf16), vmem(4) + token(1), (z2, z1, kv, side, st))
     par = moved(own, "ctx", lambda i: i ^ 1)
 
-    early = call(
-        "early",
-        early_kernel,
-        shape(ROWS, HEADS * D, f32),
-        vmem(7) + token(1),
-        (grad_out, other, right, left, other_right, other_left, weight, own),
+    g4, gt = call(
+        "project",
+        project_kernel,
+        (shape(LANES, D, bf16), shape(D, LANES, f32)),
+        vmem(9) + token(1),
+        (grad_out, other, right, left, other_right, other_left, far, other_far, weight, own),
     )
     p_side, st = call(
-        "middle", middle_kernel, (shape(2 * ROWS, LANES, bf16), state), smem(1) + vmem(3) + token(1), (place, own, q4, st, early)
+        "middle", middle_kernel, (shape(2 * ROWS, LANES, bf16), state), smem(1) + vmem(3) + token(1), (place, own, q4, st, gt), flops=4 * 10**9
     )
     p_par, st = call(
-        "across", across_kernel, (shape(REACH * ROWS, LANES, bf16), state), smem(1) + vmem(3), (place, par, q4, st)
-    )
-
-    far_cross, g4, st = call(
-        "cross_far",
-        cross_far,
-        (shape(2 * ROWS, 2 * D, bf16), shape(LANES, D, bf16), state),
-        smem(1) + vmem(8),
-        (place, far, other_far, early, tail, q4, par, p_par, st),
+        "across", across_kernel, (shape(REACH * ROWS, LANES, bf16), state), smem(1) + vmem(4), (place, par, q4, gt, st)
+    )
+
+    far_cross, st = call(
+        "cross_far", cross_far, (shape(2 * ROWS, 2 * D, bf16), state), smem(1) + vmem(5), (place, q4, par, p_par, g4, st)
     )
     far_back = moved(far_cross, "ctx", lambda i: i ^ 1)
     near_cross, st = call(

time: 54.7 us -> 52.2 us (0.954)
  the two profiles are of different devices: /device:TPU:64 before, /device:TPU:8 now
where the time goes in v9:
time: 52.2 us; the launch traced here: 52 us
  starting transfers between devices  25.8 us (49%)
  Pallas kernels  13.7 us (26%)
  waiting for transfers between devices  10.8 us (21%)
  other arithmetic  0.83 us (2%)
  between operations  0.81 us (2%)
    ppermute x17, starting transfers between devices, moved(): lax.ppermute(x, axis, [(i, to(i)) for i in range(lax.axis_size(axis))])  25.8 us
    pallas_call x18, Pallas kernels, call(): pl.pallas_call(kernel, out_shape=outs, in_specs=ins, out_specs=vmem(1)[0]...  13.7 us
    ppermute x17, waiting for transfers between devices, moved(): lax.ppermute(x, axis, [(i, to(i)) for i in range(lax.axis_size(axis))])  10.8 us
  transfers between devices with their start and end apart: 17, of which 5 were waited for; matrix products, arithmetic and copies ran while one was open for 2% of the time, Pallas kernels for 20%

profile of v9, /device:TPU:8, one launch (start us, length us, event | category | flops | bytes accessed | tf_op | source)
XLA Modules:
  0.0 52.0 jit_solution(1363307689402280624)
XLA Ops:
  0.6 2.4 %collective-permute-start.2 = (bf16[192,512]{1,0:T(8,128)(2,1)}, bf16[192,512]{1,0:T(8,128)(2,1)S(1)}, u32[]{:S(2)}, u32[]{:S(2)}) collective-permute-start(bf16[192,512]{1,0:T(8,128)(2,1)} %refs_0_.1), channel_id=1, source_target_pairs={{0,1},{1,0},{2,3},{3,2},{4,5},{5,4},{6,7},{7,6},{8,9},{9,8},{10,11... | collective-permute-start | bytes 589832 | tf_op jit(solution)/shard_map/ppermute | solution.py:345
  3.0 1.5 %collective-permute-start.3 = (bf16[192,512]{1,0:T(8,128)(2,1)}, bf16[192,512]{1,0:T(8,128)(2,1)S(1)}, u32[]{:S(2)}, u32[]{:S(2)}) collective-permute-start(bf16[192,512]{1,0:T(8,128)(2,1)} %refs_0_.1), channel_id=1, source_target_pairs={{0,2},{1,3},{2,4},{3,5},{4,6},{5,7},{6,0},{7,1},{8,10},{9,11},{10,... | collective-permute-start | bytes 589832 | tf_op jit(solution)/shard_map/ppermute | solution.py:345
  4.5 1.7 %collective-permute-start.4 = (bf16[192,512]{1,0:T(8,128)(2,1)}, bf16[192,512]{1,0:T(8,128)(2,1)S(1)}, u32[]{:S(2)}, u32[]{:S(2)}) collective-permute-start(bf16[192,512]{1,0:T(8,128)(2,1)} %refs_0_.1), channel_id=1, source_target_pairs={{0,6},{1,7},{2,0},{3,1},{4,2},{5,3},{6,4},{7,5},{8,14},{9,15},{10,... | collective-permute-start | bytes 589832 | tf_op jit(solution)/shard_map/ppermute | solution.py:345
  6.3 0.8 %pad_add_fusion.z0_ref = bf16[192,256]{1,0:T(8,128)(2,1)S(1)} fusion(bf16[192,128]{1,0:T(8,128)(2,1)} %param.8, bf16[192,128]{1,0:T(8,128)(2,1)} %param.7), kind=kLoop, calls=%fused_computation | loop fusion | flops 196608 | bytes 196608 | tf_op jit(solution)/shard_map/add | solution.py:382
  7.1 2.0 %collective-permute-start.1 = (bf16[192,256]{1,0:T(8,128)(2,1)S(1)}, bf16[192,256]{1,0:T(8,128)(2,1)S(1)}, u32[]{:S(2)}, u32[]{:S(2)}) collective-permute-start(bf16[192,256]{1,0:T(8,128)(2,1)S(1)} %pad_add_fusion.z0_ref), channel_id=1, source_target_pairs={{0,32},{8,40},{16,48},{24,56},{32,64},{40,72},{48,80},{56,88},{64,... | collective-permute-start | bytes 294920 | tf_op jit(solution)/shard_map/ppermute | solution.py:345
  9.1 3.3 %collective-permute-start = (bf16[192,256]{1,0:T(8,128)(2,1)S(1)}, bf16[192,256]{1,0:T(8,128)(2,1)S(1)}, u32[]{:S(2)}, u32[]{:S(2)}) collective-permute-start(bf16[192,256]{1,0:T(8,128)(2,1)S(1)} %pad_add_fusion.z0_ref), channel_id=1, source_target_pairs={{0,64},{8,72},{16,80},{24,88},{32,96},{40,104},{48,112},{56,120},{... | collective-permute-start | bytes 294920 | tf_op jit(solution)/shard_map/ppermute | solution.py:345
  12.4 1.5 %collective-permute-start.7 = (bf16[192,512]{1,0:T(8,128)(2,1)S(1)}, bf16[192,512]{1,0:T(8,128)(2,1)S(1)}, u32[]{:S(2)}, u32[]{:S(2)}) collective-permute-start(bf16[192,512]{1,0:T(8,128)(2,1)S(1)} %collective-permute-done.2.refs_0_.refs_1_), channel_id=1, source_target_pairs={{0,6},{1,7},{2,0},{3,1},{4,2},{5,3},{6,4},{7,5},{8,14},{9,15},{10,... | collective-permute-start | bytes 589832 | tf_op jit(solution)/shard_map/ppermute | solution.py:345
  13.9 0.9 %load.1 = (bf16[768,128]{1,0:T(8,128)(2,1)S(1)}, f32[8,768]{1,0:T(8,128)S(1)}) custom-call(s32[1]{0:T(128)} %bitcast.place_ref, s32[8]{0:T(128)} %len_hbm.1, bf16[192,512]{1,0:T(8,128)(2,1)} %q_hbm.1), custom_call_target="tpu_custom_call" | custom-call | flops 1 | bytes 1 | tf_op jit(solution)/shard_map/load/pallas_call | solution.py:359
  14.9 0.6 %collective-permute-start.6 = (bf16[192,512]{1,0:T(8,128)(2,1)S(1)}, bf16[192,512]{1,0:T(8,128)(2,1)S(1)}, u32[]{:S(2)}, u32[]{:S(2)}) collective-permute-start(bf16[192,512]{1,0:T(8,128)(2,1)S(1)} %collective-permute-done.2.refs_0_.refs_1_), channel_id=1, source_target_pairs={{0,2},{1,3},{2,4},{3,5},{4,6},{5,7},{6,0},{7,1},{8,10},{9,11},{10,... | collective-permute-start | bytes 589832 | tf_op jit(solution)/shard_map/ppermute | solution.py:345
  15.4 1.5 %collective-permute-done.1.z1_ref = bf16[192,256]{1,0:T(8,128)(2,1)S(1)} collective-permute-done((bf16[192,256]{1,0:T(8,128)(2,1)S(1)}, bf16[192,256]{1,0:T(8,128)(2,1)S(1)}, u32[]{:S(2)}, u32[]{:S(2)}) %collective-permute-start.1) | collective-permute-done | bytes 98336 | tf_op jit(solution)/shard_map/ppermute | solution.py:345
  16.9 2.9 %collective-permute-done.z2_ref = bf16[192,256]{1,0:T(8,128)(2,1)S(1)} collective-permute-done((bf16[192,256]{1,0:T(8,128)(2,1)S(1)}, bf16[192,256]{1,0:T(8,128)(2,1)S(1)}, u32[]{:S(2)}, u32[]{:S(2)}) %collective-permute-start) | collective-permute-done | bytes 98336 | tf_op jit(solution)/shard_map/ppermute | solution.py:345
  19.8 1.4 %collective-permute-start.5 = (bf16[384,256]{1,0:T(8,128)(2,1)S(1)}, bf16[384,256]{1,0:T(8,128)(2,1)S(1)}, u32[]{:S(2)}, u32[]{:S(2)}) collective-permute-start(bf16[384,256]{1,0:T(8,128)(2,1)S(1)} %pick_side.1.refs_0_), channel_id=1, source_target_pairs={{0,16},{8,24},{16,0},{24,8},{32,48},{40,56},{48,32},{56,40},{64,80... | collective-permute-start | bytes 589832 | tf_op jit(solution)/shard_map/ppermute | solution.py:345
  21.3 0.3 collective-permute-start.8
  21.5 3.0 %collective-permute-start.9 = (bf16[192,512]{1,0:T(8,128)(2,1)S(1)}, bf16[192,512]{1,0:T(8,128)(2,1)S(1)}, u32[]{:S(2)}, u32[]{:S(2)}) collective-permute-start(bf16[192,512]{1,0:T(8,128)(2,1)S(1)} %collective-permute-done.7.refs_2_.refs_5_), channel_id=1, source_target_pairs={{0,6},{1,7},{2,0},{3,1},{4,2},{5,3},{6,4},{7,5},{8,14},{9,15},{10,... | collective-permute-start | bytes 589832 | tf_op jit(solution)/shard_map/ppermute | solution.py:345
  24.5 3.3 %near.1 = (bf16[576,768]{1,0:T(8,128)(2,1)S(1)}, f32[152,768]{1,0:T(8,128)S(1)}, bf16[512,4096]{1,0:T(8,128)(2,1)S(1)}) custom-call(s32[1]{0:T(128)} %bitcast.place_ref, s32[1]{0:T(128)} %bitcast.1.head_ref, bf16[192,256]{1,0:T(8,128)(2,1)S(1)} %collective-permute-done.z2_ref, bf16[192,256]{1,0:T(8,128)(2,1)S(1)} %collective-permute-done.1.z1_ref, ...), custom_call_target="tpu_custom_call" | custom-call | flops 1 | bytes 1 | tf_op jit(solution)/shard_map/near/pallas_call | solution.py:359
  28.1 1.6 %project.1 = (bf16[768,128]{1,0:T(8,128)(2,1)S(1)}, f32[128,768]{1,0:T(8,128)S(1)}) custom-call(bf16[192,512]{1,0:T(8,128)(2,1)S(1)} %copy-done, bf16[192,512]{1,0:T(8,128)(2,1)S(1)} %collective-permute-done.2.refs_0_.refs_1_, bf16[192,512]{1,0:T(8,128)(2,1)S(1)} %collective-permute-done.3.refs_1_.refs_2_, ...), custom_call_target="tpu_custom_call" | custom-call | flops 1 | bytes 1 | tf_op jit(solution)/shard_map/project/pallas_call | solution.py:359
  29.8 0.9 %middle.1 = (bf16[384,768]{1,0:T(8,128)(2,1)S(1)}, f32[152,768]{1,0:T(8,128)S(1)}) custom-call(s32[1]{0:T(128)} %bitcast.place_ref, bf16[960,256]{1,0:T(8,128)(2,1)S(1)} %join_slots.1.refs_9_.own_ref, bf16[768,128]{1,0:T(8,128)(2,1)S(1)} %get-tuple-element.30.refs_3_.q4_ref, f32[152,768]{1,0:T(8,128)S(1)} %get-tuple-element.32.refs_0_.st_in_ref, ...), custom_call_target="tpu_custom_call" | custom-call | flops 4000000000 | bytes 1 | tf_op jit(solution)/shard_map/middle/pallas_call | solution.py:359
  30.7 1.6 %across.1 = (bf16[768,768]{1,0:T(8,128)(2,1)S(1)}, f32[152,768]{1,0:T(8,128)S(1)}) custom-call(s32[1]{0:T(128)} %bitcast.place_ref, bf16[960,256]{1,0:T(8,128)(2,1)S(1)} %collective-permute-done.10.par_ref, bf16[768,128]{1,0:T(8,128)(2,1)S(1)} %get-tuple-element.30.refs_3_.q4_ref, f32[128,768]{1,0:T(8,128)S(1)} %get-tuple-element.35.after.gt_ref, ...), custom_call_target="tpu_custom_call" | custom-call | flops 1 | bytes 1 | tf_op jit(solution)/shard_map/across/pallas_call | solution.py:359
  32.3 0.9 %cross_far.1 = (bf16[384,256]{1,0:T(8,128)(2,1)S(1)}, f32[152,768]{1,0:T(8,128)S(1)}) custom-call(s32[1]{0:T(128)} %bitcast.place_ref, bf16[768,128]{1,0:T(8,128)(2,1)S(1)} %get-tuple-element.30.refs_3_.q4_ref, bf16[960,256]{1,0:T(8,128)(2,1)S(1)} %collective-permute-done.10.par_ref, bf16[768,768]{1,0:T(8,128)(2,1)S(1)} %get-tuple-element.39.p_ref, ...), custom_call_target="tpu_custom_call" | custom-call | flops 1 | bytes 1 | tf_op jit(solution)/shard_map/cross_far/pallas_call | solution.py:359
  33.3 0.8 %cross_near.1 = (bf16[576,256]{1,0:T(8,128)(2,1)S(1)}, f32[152,768]{1,0:T(8,128)S(1)}) custom-call(s32[1]{0:T(128)} %bitcast.place_ref, bf16[768,128]{1,0:T(8,128)(2,1)S(1)} %get-tuple-element.30.refs_3_.q4_ref, bf16[960,256]{1,0:T(8,128)(2,1)S(1)} %collective-permute-done.10.par_ref, bf16[768,768]{1,0:T(8,128)(2,1)S(1)} %get-tuple-element.39.p_ref, ...), custom_call_target="tpu_custom_call" | custom-call | flops 4000000000 | bytes 1 | tf_op jit(solution)/shard_map/cross_near/pallas_call | solution.py:359
  34.1 1.0 %collective-permute-start.12 = (bf16[576,256]{1,0:T(8,128)(2,1)S(1)}, bf16[576,256]{1,0:T(8,128)(2,1)S(1)}, u32[]{:S(2)}, u32[]{:S(2)}) collective-permute-start(bf16[576,256]{1,0:T(8,128)(2,1)S(1)} %get-tuple-element.49), channel_id=1, source_target_pairs={{0,8},{8,0},{16,24},{24,16},{32,40},{40,32},{48,56},{56,48},{64,72... | collective-permute-start | bytes 884744 | tf_op jit(solution)/shard_map/ppermute | solution.py:345
  35.2 0.8 %own_far.1 = (f32[384,256]{1,0:T(8,128)S(1)}, f32[152,768]{1,0:T(8,128)S(1)}) custom-call(bf16[768,128]{1,0:T(8,128)(2,1)S(1)} %get-tuple-element.30.refs_3_.q4_ref, bf16[960,256]{1,0:T(8,128)(2,1)S(1)} %join_slots.1.refs_9_.own_ref, bf16[576,768]{1,0:T(8,128)(2,1)S(1)} %get-tuple-element.33.near_ref, bf16[384,768]{1,0:T(8,128)(2,1)S(1)} %get-tuple-element.36.side_ref, ...), custom_call_target="tpu_custom_call" | custom-call | flops 4000000000 | bytes 1 | tf_op jit(solution)/shard_map/own_far/pallas_call | solution.py:359
  36.0 0.8 %collective-permute-start.14 = (bf16[192,256]{1,0:T(8,128)(2,1)S(1)}, bf16[192,256]{1,0:T(8,128)(2,1)S(1)}, u32[]{:S(2)}, u32[]{:S(2)}) collective-permute-start(bf16[192,256]{1,0:T(8,128)(2,1)S(1)} %get-tuple-element.54), channel_id=1, source_target_pairs={{0,16},{8,24},{16,0},{24,8},{32,48},{40,56},{48,32},{56,40},{64,80... | collective-permute-start | bytes 294920 | tf_op jit(solution)/shard_map/ppermute | solution.py:345
  36.8 0.8 %own_near.1 = (f32[384,256]{1,0:T(8,128)S(1)}, f32[152,768]{1,0:T(8,128)S(1)}) custom-call(bf16[768,128]{1,0:T(8,128)(2,1)S(1)} %get-tuple-element.30.refs_3_.q4_ref, bf16[960,256]{1,0:T(8,128)(2,1)S(1)} %join_slots.1.refs_9_.own_ref, bf16[576,768]{1,0:T(8,128)(2,1)S(1)} %get-tuple-element.33.near_ref, bf16[384,768]{1,0:T(8,128)(2,1)S(1)} %get-tuple-element.36.side_ref, ...), custom_call_target="tpu_custom_call" | custom-call | flops 4000000000 | bytes 1 | tf_op jit(solution)/shard_map/own_near/pallas_call | solution.py:359
  37.6 1.4 %collective-permute-start.13 = (bf16[192,256]{1,0:T(8,128)(2,1)S(1)}, bf16[192,256]{1,0:T(8,128)(2,1)S(1)}, u32[]{:S(2)}, u32[]{:S(2)}) collective-permute-start(bf16[192,256]{1,0:T(8,128)(2,1)S(1)} %get-tuple-element.53), channel_id=1, source_target_pairs={{0,16},{8,24},{16,0},{24,8},{32,48},{40,56},{48,32},{56,40},{64,80... | collective-permute-start | bytes 294920 | tf_op jit(solution)/shard_map/ppermute | solution.py:345
  39.1 2.5 %collective-permute-done.14.side_ref.far_ref = bf16[192,256]{1,0:T(8,128)(2,1)S(1)} collective-permute-done((bf16[192,256]{1,0:T(8,128)(2,1)S(1)}, bf16[192,256]{1,0:T(8,128)(2,1)S(1)}, u32[]{:S(2)}, u32[]{:S(2)}) %collective-permute-start.14) | collective-permute-done | bytes 98336 | tf_op jit(solution)/shard_map/ppermute | solution.py:345
  41.6 3.7 %collective-permute-start.16 = (bf16[192,256]{1,0:T(8,128)(2,1)S(1)}, bf16[192,256]{1,0:T(8,128)(2,1)S(1)}, u32[]{:S(2)}, u32[]{:S(2)}) collective-permute-start(bf16[192,256]{1,0:T(8,128)(2,1)S(1)} %relay_far.1.refs_0_), channel_id=1, source_target_pairs={{0,192},{8,200},{16,208},{24,216},{32,224},{40,232},{48,240},{56,2... | collective-permute-start | bytes 294920 | tf_op jit(solution)/shard_map/ppermute | solution.py:345
  45.3 1.2 %own_last.1 = (f32[192,256]{1,0:T(8,128)S(1)}, bf16[192,512]{1,0:T(8,128)(2,1)}) custom-call(bf16[768,128]{1,0:T(8,128)(2,1)S(1)} %get-tuple-element.30.refs_3_.q4_ref, bf16[960,256]{1,0:T(8,128)(2,1)S(1)} %join_slots.1.refs_9_.own_ref, bf16[576,768]{1,0:T(8,128)(2,1)S(1)} %get-tuple-element.33.near_ref, bf16[384,768]{1,0:T(8,128)(2,1)S(1)} %get-tuple-element.36.side_ref, ...), custom_call_target="tpu_custom_call" | custom-call | flops 1 | bytes 1 | tf_op jit(solution)/shard_map/own_last/pallas_call | solution.py:359
  46.6 0.8 %collective-permute-start.15 = (bf16[192,256]{1,0:T(8,128)(2,1)S(1)}, bf16[192,256]{1,0:T(8,128)(2,1)S(1)}, u32[]{:S(2)}, u32[]{:S(2)}) collective-permute-start(bf16[192,256]{1,0:T(8,128)(2,1)S(1)} %relay_near.1), channel_id=1, source_target_pairs={{0,224},{8,232},{16,240},{24,248},{32,0},{40,8},{48,16},{56,24},{6... | collective-permute-start | bytes 294920 | tf_op jit(solution)/shard_map/ppermute | solution.py:345
  47.4 1.5 %collective-permute-done.16.two_ref = bf16[192,256]{1,0:T(8,128)(2,1)S(1)} collective-permute-done((bf16[192,256]{1,0:T(8,128)(2,1)S(1)}, bf16[192,256]{1,0:T(8,128)(2,1)S(1)}, u32[]{:S(2)}, u32[]{:S(2)}) %collective-permute-start.16) | collective-permute-done | bytes 98336 | tf_op jit(solution)/shard_map/ppermute | solution.py:345
  48.9 2.3 %collective-permute-done.15.one_ref = bf16[192,256]{1,0:T(8,128)(2,1)S(1)} collective-permute-done((bf16[192,256]{1,0:T(8,128)(2,1)S(1)}, bf16[192,256]{1,0:T(8,128)(2,1)S(1)}, u32[]{:S(2)}, u32[]{:S(2)}) %collective-permute-start.15) | collective-permute-done | bytes 98336 | tf_op jit(solution)/shard_map/ppermute | solution.py:345
  51.3 0.7 %finish.1 = (bf16[192,128]{1,0:T(8,128)(2,1)}, bf16[192,128]{1,0:T(8,128)(2,1)}) custom-call(s32[1]{0:T(128)} %bitcast.place_ref, f32[192,256]{1,0:T(8,128)S(1)} %get-tuple-element.52.refs_1_.own_ref, bf16[576,256]{1,0:T(8,128)(2,1)S(1)} %collective-permute-done.12.back_ref, bf16[192,256]{1,0:T(8,128)(2,1)S(1)} %collective-permute-done.13.near_ref, ...), custom_call_target="tpu_custom_call" | custom-call | flops 1 | bytes 1 | tf_op jit(solution)/shard_map/finish/pallas_call | solution.py:359
  (23 shorter events, 0.6 us)
Async XLA Ops:
  0.6 27.5 %copy-start = (bf16[192,512]{1,0:T(8,128)(2,1)S(1)}, bf16[192,512]{1,0:T(8,128)(2,1)}, u32[]{:S(2)}) copy-start(bf16[192,512]{1,0:T(8,128)(2,1)} %refs_0_.1) | copy-start | bytes 589828
  0.6 11.7 %collective-permute-start.2 = (bf16[192,512]{1,0:T(8,128)(2,1)}, bf16[192,512]{1,0:T(8,128)(2,1)S(1)}, u32[]{:S(2)}, u32[]{:S(2)}) collective-permute-start(bf16[192,512]{1,0:T(8,128)(2,1)} %refs_0_.1), channel_id=1, source_target_pairs={{0,1},{1,0},{2,3},{3,2},{4,5},{5,4},{6,7},{7,6},{8,9},{9,8},{10,11... | collective-permute-start | bytes 589832 | tf_op jit(solution)/shard_map/ppermute | solution.py:345
  3.0 11.8 %collective-permute-start.3 = (bf16[192,512]{1,0:T(8,128)(2,1)}, bf16[192,512]{1,0:T(8,128)(2,1)S(1)}, u32[]{:S(2)}, u32[]{:S(2)}) collective-permute-start(bf16[192,512]{1,0:T(8,128)(2,1)} %refs_0_.1), channel_id=1, source_target_pairs={{0,2},{1,3},{2,4},{3,5},{4,6},{5,7},{6,0},{7,1},{8,10},{9,11},{10,... | collective-permute-start | bytes 589832 | tf_op jit(solution)/shard_map/ppermute | solution.py:345
  4.5 10.9 %collective-permute-start.4 = (bf16[192,512]{1,0:T(8,128)(2,1)}, bf16[192,512]{1,0:T(8,128)(2,1)S(1)}, u32[]{:S(2)}, u32[]{:S(2)}) collective-permute-start(bf16[192,512]{1,0:T(8,128)(2,1)} %refs_0_.1), channel_id=1, source_target_pairs={{0,6},{1,7},{2,0},{3,1},{4,2},{5,3},{6,4},{7,5},{8,14},{9,15},{10,... | collective-permute-start | bytes 589832 | tf_op jit(solution)/shard_map/ppermute | solution.py:345
  7.1 9.8 %collective-permute-start.1 = (bf16[192,256]{1,0:T(8,128)(2,1)S(1)}, bf16[192,256]{1,0:T(8,128)(2,1)S(1)}, u32[]{:S(2)}, u32[]{:S(2)}) collective-permute-start(bf16[192,256]{1,0:T(8,128)(2,1)S(1)} %pad_add_fusion.z0_ref), channel_id=1, source_target_pairs={{0,32},{8,40},{16,48},{24,56},{32,64},{40,72},{48,80},{56,88},{64,... | collective-permute-start | bytes 294920 | tf_op jit(solution)/shard_map/ppermute | solution.py:345
  9.1 10.7 %collective-permute-start = (bf16[192,256]{1,0:T(8,128)(2,1)S(1)}, bf16[192,256]{1,0:T(8,128)(2,1)S(1)}, u32[]{:S(2)}, u32[]{:S(2)}) collective-permute-start(bf16[192,256]{1,0:T(8,128)(2,1)S(1)} %pad_add_fusion.z0_ref), channel_id=1, source_target_pairs={{0,64},{8,72},{16,80},{24,88},{32,96},{40,104},{48,112},{56,120},{... | collective-permute-start | bytes 294920 | tf_op jit(solution)/shard_map/ppermute | solution.py:345
  12.4 9.2 %collective-permute-start.7 = (bf16[192,512]{1,0:T(8,128)(2,1)S(1)}, bf16[192,512]{1,0:T(8,128)(2,1)S(1)}, u32[]{:S(2)}, u32[]{:S(2)}) collective-permute-start(bf16[192,512]{1,0:T(8,128)(2,1)S(1)} %collective-permute-done.2.refs_0_.refs_1_), channel_id=1, source_target_pairs={{0,6},{1,7},{2,0},{3,1},{4,2},{5,3},{6,4},{7,5},{8,14},{9,15},{10,... | collective-permute-start | bytes 589832 | tf_op jit(solution)/shard_map/ppermute | solution.py:345
  14.9 9.6 %collective-permute-start.6 = (bf16[192,512]{1,0:T(8,128)(2,1)S(1)}, bf16[192,512]{1,0:T(8,128)(2,1)S(1)}, u32[]{:S(2)}, u32[]{:S(2)}) collective-permute-start(bf16[192,512]{1,0:T(8,128)(2,1)S(1)} %collective-permute-done.2.refs_0_.refs_1_), channel_id=1, source_target_pairs={{0,2},{1,3},{2,4},{3,5},{4,6},{5,7},{6,0},{7,1},{8,10},{9,11},{10,... | collective-permute-start | bytes 589832 | tf_op jit(solution)/shard_map/ppermute | solution.py:345
  19.8 7.9 %collective-permute-start.5 = (bf16[384,256]{1,0:T(8,128)(2,1)S(1)}, bf16[384,256]{1,0:T(8,128)(2,1)S(1)}, u32[]{:S(2)}, u32[]{:S(2)}) collective-permute-start(bf16[384,256]{1,0:T(8,128)(2,1)S(1)} %pick_side.1.refs_0_), channel_id=1, source_target_pairs={{0,16},{8,24},{16,0},{24,8},{32,48},{40,56},{48,32},{56,40},{64,80... | collective-permute-start | bytes 589832 | tf_op jit(solution)/shard_map/ppermute | solution.py:345
  21.3 6.9 %collective-permute-start.8 = (bf16[192,512]{1,0:T(8,128)(2,1)S(1)}, bf16[192,512]{1,0:T(8,128)(2,1)S(1)}, u32[]{:S(2)}, u32[]{:S(2)}) collective-permute-start(bf16[192,512]{1,0:T(8,128)(2,1)S(1)} %collective-permute-done.3.refs_1_.refs_2_), channel_id=1, source_target_pairs={{0,2},{1,3},{2,4},{3,5},{4,6},{5,7},{6,0},{7,1},{8,10},{9,11},{10,... | collective-permute-start | bytes 589832 | tf_op jit(solution)/shard_map/ppermute | solution.py:345
  21.5 6.6 %collective-permute-start.9 = (bf16[192,512]{1,0:T(8,128)(2,1)S(1)}, bf16[192,512]{1,0:T(8,128)(2,1)S(1)}, u32[]{:S(2)}, u32[]{:S(2)}) collective-permute-start(bf16[192,512]{1,0:T(8,128)(2,1)S(1)} %collective-permute-done.7.refs_2_.refs_5_), channel_id=1, source_target_pairs={{0,6},{1,7},{2,0},{3,1},{4,2},{5,3},{6,4},{7,5},{8,14},{9,15},{10,... | collective-permute-start | bytes 589832 | tf_op jit(solution)/shard_map/ppermute | solution.py:345
  27.8 2.9 %collective-permute-start.10 = (bf16[960,256]{1,0:T(8,128)(2,1)S(1)}, bf16[960,256]{1,0:T(8,128)(2,1)S(1)}, u32[]{:S(2)}, u32[]{:S(2)}) collective-permute-start(bf16[960,256]{1,0:T(8,128)(2,1)S(1)} %join_slots.1.refs_9_.own_ref), channel_id=1, source_target_pairs={{0,8},{8,0},{16,24},{24,16},{32,40},{40,32},{48,56},{56,48},{64,72... | collective-permute-start | bytes 1474568 | tf_op jit(solution)/shard_map/ppermute | solution.py:345
  33.2 2.7 %collective-permute-start.11 = (bf16[384,256]{1,0:T(8,128)(2,1)S(1)}, bf16[384,256]{1,0:T(8,128)(2,1)S(1)}, u32[]{:S(2)}, u32[]{:S(2)}) collective-permute-start(bf16[384,256]{1,0:T(8,128)(2,1)S(1)} %get-tuple-element.45), channel_id=1, source_target_pairs={{0,8},{8,0},{16,24},{24,16},{32,40},{40,32},{48,56},{56,48},{64,72... | collective-permute-start | bytes 589832 | tf_op jit(solution)/shard_map/ppermute | solution.py:345
  34.1 3.5 %collective-permute-start.12 = (bf16[576,256]{1,0:T(8,128)(2,1)S(1)}, bf16[576,256]{1,0:T(8,128)(2,1)S(1)}, u32[]{:S(2)}, u32[]{:S(2)}) collective-permute-start(bf16[576,256]{1,0:T(8,128)(2,1)S(1)} %get-tuple-element.49), channel_id=1, source_target_pairs={{0,8},{8,0},{16,24},{24,16},{32,40},{40,32},{48,56},{56,48},{64,72... | collective-permute-start | bytes 884744 | tf_op jit(solution)/shard_map/ppermute | solution.py:345
  36.0 5.6 %collective-permute-start.14 = (bf16[192,256]{1,0:T(8,128)(2,1)S(1)}, bf16[192,256]{1,0:T(8,128)(2,1)S(1)}, u32[]{:S(2)}, u32[]{:S(2)}) collective-permute-start(bf16[192,256]{1,0:T(8,128)(2,1)S(1)} %get-tuple-element.54), channel_id=1, source_target_pairs={{0,16},{8,24},{16,0},{24,8},{32,48},{40,56},{48,32},{56,40},{64,80... | collective-permute-start | bytes 294920 | tf_op jit(solution)/shard_map/ppermute | solution.py:345
  37.6 8.9 %collective-permute-start.13 = (bf16[192,256]{1,0:T(8,128)(2,1)S(1)}, bf16[192,256]{1,0:T(8,128)(2,1)S(1)}, u32[]{:S(2)}, u32[]{:S(2)}) collective-permute-start(bf16[192,256]{1,0:T(8,128)(2,1)S(1)} %get-tuple-element.53), channel_id=1, source_target_pairs={{0,16},{8,24},{16,0},{24,8},{32,48},{40,56},{48,32},{56,40},{64,80... | collective-permute-start | bytes 294920 | tf_op jit(solution)/shard_map/ppermute | solution.py:345
  41.6 7.3 %collective-permute-start.16 = (bf16[192,256]{1,0:T(8,128)(2,1)S(1)}, bf16[192,256]{1,0:T(8,128)(2,1)S(1)}, u32[]{:S(2)}, u32[]{:S(2)}) collective-permute-start(bf16[192,256]{1,0:T(8,128)(2,1)S(1)} %relay_far.1.refs_0_), channel_id=1, source_target_pairs={{0,192},{8,200},{16,208},{24,216},{32,224},{40,232},{48,240},{56,2... | collective-permute-start | bytes 294920 | tf_op jit(solution)/shard_map/ppermute | solution.py:345
  46.6 4.7 %collective-permute-start.15 = (bf16[192,256]{1,0:T(8,128)(2,1)S(1)}, bf16[192,256]{1,0:T(8,128)(2,1)S(1)}, u32[]{:S(2)}, u32[]{:S(2)}) collective-permute-start(bf16[192,256]{1,0:T(8,128)(2,1)S(1)} %relay_near.1), channel_id=1, source_target_pairs={{0,224},{8,232},{16,240},{24,248},{32,0},{40,8},{48,16},{56,24},{6... | collective-permute-start | bytes 294920 | tf_op jit(solution)/shard_map/ppermute | solution.py:345

commit v10 on v9

--- a/solution.py
+++ b/solution.py
@@ -35,8 +35,14 @@
         dst[h * ROWS : (h + 1) * ROWS, :] = src[:, h * D : (h + 1) * D]
 
 
-def load_kernel(place_ref, len_hbm, q_hbm, q4_ref, bound_ref, len_ref, sems):
+def load_kernel(place_ref, head_ref, len_hbm, q_hbm, w_hbm, q4_ref, bound_ref, w_ref, len_ref, sems):
+    head = head_ref[0]
     copies = [pltpu.make_async_copy(len_hbm, len_ref, sems.at[0])]
+    sources = (head, source_of(head, 0, True), source_of(head, -2, False), source_of(head, 2, False))
+    sources += (source_of(head, -2, True), source_of(head, 2, True), source_of(head, 4, False), source_of(head, 4, True))
+    for i, source in enumerate(sources):
+        cols = pl.ds(pl.multiple_of(source * BLOCK, BLOCK), BLOCK)
+        copies.append(pltpu.make_async_copy(w_hbm.at[:, cols], w_ref.at[:, pl.ds(i * BLOCK, BLOCK)], sems.at[1 + HEADS + i]))
     for h in range(HEADS):
         across, along = pl.ds(h * ROWS, ROWS), pl.ds(h * D, D)
         copies.append(pltpu.make_async_copy(q_hbm.at[:, along], q4_ref.at[across, :], sems.at[1 + h]))
@@ -58,6 +64,10 @@
         copy.wait()
 
 
+def stage_kernel(piece_ref, after, out_ref):
+    out_ref[...] = piece_ref[...]
+
+
 def gate_kernel(*refs):
     refs[-1][...] = jnp.zeros(refs[-1].shape, refs[-1].dtype)
 
@@ -114,17 +124,8 @@
     ref[at : at + 1, :] = value
 
 
-def near_kernel(place_ref, head_ref, z2_ref, z1_ref, z0_ref, q4_ref, bound_ref, w_hbm, *refs):
-    p_ref, st_ref, w_ref, sems = refs[-4:]
-    head = head_ref[0]
-    sources = (head, source_of(head, 0, True), source_of(head, -2, False), source_of(head, 2, False))
-    sources += (source_of(head, -2, True), source_of(head, 2, True), source_of(head, 4, False), source_of(head, 4, True))
-    copies = []
-    for i, source in enumerate(sources):
-        cols = pl.ds(pl.multiple_of(source * BLOCK, BLOCK), BLOCK)
-        copies.append(pltpu.make_async_copy(w_hbm.at[:, cols], w_ref.at[:, pl.ds(i * BLOCK, BLOCK)], sems.at[i]))
-    for copy in copies:
-        copy.start()
+def near_kernel(place_ref, z2_ref, z1_ref, z0_ref, q4_ref, bound_ref, *refs):
+    p_ref, st_ref = refs[-2:]
     me = place_ref[0]
     queries = q4_ref[...]
     row = lax.broadcasted_iota(jnp.int32, (ROWS, LANES), 0)
@@ -137,8 +138,6 @@
         put_row(st_ref, PEAK + 2 * i, peak)
     write_state(st_ref, state)
     put_row(st_ref, START, bound_ref[1:2, :])
-    for copy in copies:
-        copy.wait()
 
 
 def project_kernel(*refs):
@@ -292,35 +291,22 @@
     return (lax.rem(lax.div(place_ref[0], 2), 2) == 1).astype(jnp.float32)
 
 
-def settle_far(own_ref, back_ref, keep_ref, side_ref):
-    both = own_ref[...] + back_ref[...].astype(jnp.float32)
-    keep_ref[...] = both[:ROWS]
-    side_ref[...] = both[ROWS:].astype(jnp.bfloat16)
+def settle_kernel(own_ref, back_ref, low_ref, high_ref):
+    both = own_ref[...] + back_ref[: 2 * ROWS, :].astype(jnp.float32)
+    low_ref[...] = both[:ROWS].astype(low_ref.dtype)
+    high_ref[...] = both[ROWS:].astype(jnp.bfloat16)
 
 
 def relay_far(place_ref, keep_ref, side_ref, out_ref):
     out_ref[...] = (keep_ref[...] + side_ref[...].astype(jnp.float32) * is_upper(place_ref)).astype(jnp.bfloat16)
 
 
-def settle_near(own_ref, back_ref, keep_ref, side_ref):
-    both = own_ref[...] + back_ref[: 2 * ROWS, :].astype(jnp.float32)
-    keep_ref[...] = both[:ROWS]
-    side_ref[...] = both[ROWS:].astype(jnp.bfloat16)
-
-
-def relay_near(place_ref, keep_ref, near_ref, far_ref, *refs):
-    out_ref = refs[-1]
-    upper = is_upper(place_ref)
-    near, far = near_ref[...].astype(jnp.float32), far_ref[...].astype(jnp.float32)
-    out_ref[...] = (keep_ref[...] + near * upper + far * (1 - upper)).astype(jnp.bfloat16)
-
-
-def finish_kernel(place_ref, own_ref, back_ref, near_ref, one_ref, two_ref, k_ref, v_ref):
+def finish_kernel(place_ref, own_ref, back_ref, side_ref, two_ref, four_ref, eight_ref, k_ref, v_ref):
     def wide(x):
         return x.astype(jnp.float32)
 
-    total = own_ref[...] + wide(back_ref[2 * ROWS :, :]) + wide(near_ref[...]) * (1 - is_upper(place_ref))
-    total = (total + wide(one_ref[...]) + wide(two_ref[...])).astype(jnp.bfloat16)
+    total = own_ref[...] + wide(back_ref[2 * ROWS :, :]) + wide(side_ref[...]) * (1 - is_upper(place_ref))
+    total = (total + wide(two_ref[...]) + wide(four_ref[...]) + wide(eight_ref[...])).astype(jnp.bfloat16)
     k_ref[...] = total[:, :D]
     v_ref[...] = total[:, D:]
 
@@ -382,15 +368,15 @@
     kv = jnp.pad(keys, ((0, 0), (0, D))) + jnp.pad(values, ((0, 0), (D, 0)))
     z2 = turned(kv, "ctx", 2 * PLANE)
     z1 = turned(kv, "ctx", PLANE)
-    q4, bound = call(
+    q4, bound, weight = call(
         "load",
         load_kernel,
-        (shape(LANES, D, bf16), shape(8, LANES, f32)),
-        smem(1) + hbm(2),
-        (place, pinned(lengths), pinned(queries)),
-        [pltpu.SMEM((lengths.shape[0],), jnp.int32), dma((1 + HEADS,))],
-    )
-    other = first
+        (shape(LANES, D, bf16), shape(8, LANES, f32), shape(HEADS * D, 8 * BLOCK, bf16)),
+        smem(2) + hbm(3),
+        (place, head, pinned(lengths), pinned(queries), pinned(out_weight)),
+        [pltpu.SMEM((lengths.shape[0],), jnp.int32), dma((9 + HEADS,))],
+    )
+    other = call("stage", stage_kernel, shape(ROWS, BLOCK, bf16), vmem(1) + token(1), (first, q4))
     other_right = turned(other, "head", 2)
     other_left = turned(other, "head", -2)
     far = turned(right, "head", 2)
@@ -401,17 +387,12 @@
         "pick_side", pick_kernel, shape(2 * ROWS, 2 * D, bf16), smem(1) + vmem(3) + token(1), (place, z2, z1, kv, gate)
     )
     side = moved(picked, "ctx", lambda i: i ^ 2)
-    p_near, st, weight = call(
+    p_near, st = call(
         "near",
         near_kernel,
-        (
-            shape(3 * ROWS, LANES, bf16),
-            state,
-            shape(HEADS * D, 8 * BLOCK, bf16),
-        ),
-        smem(2) + vmem(5) + hbm(1) + token(3),
-        (place, head, z2, z1, kv, q4, bound, pinned(out_weight), picked, other_right, other_left),
-        [dma((8,))],
+        (shape(3 * ROWS, LANES, bf16), state),
+        smem(1) + vmem(5) + token(3),
+        (place, z2, z1, kv, q4, bound, picked, other_right, other_left),
     )
     own = call("join_slots", join_kernel, shape(SLOTS * ROWS, 2 * D, bf16), vmem(4) + token(1), (z2, z1, kv, side, st))
     par = moved(own, "ctx", lambda i: i ^ 1)
@@ -447,9 +428,10 @@
         flops=FL,
     )
     far_keep, far_side = call(
-        "settle_far", settle_far, (shape(ROWS, 2 * D, f32), shape(ROWS, 2 * D, bf16)), vmem(2), (far_own, far_back)
-    )
-    far_side = moved(far_side, "ctx", lambda i: i ^ 2)
+        "settle_far", settle_kernel, (shape(ROWS, 2 * D, f32), shape(ROWS, 2 * D, bf16)), vmem(2), (far_own, far_back)
+    )
+    count = lax.axis_size("ctx")
+    far_side = moved(far_side, "ctx", lambda i: (i + 2 if i // 2 % 2 == 0 else i - 6) % count)
     near_own, st = call(
         "own_near",
         functools.partial(own_kernel, (2, 3)),
@@ -458,33 +440,27 @@
         (q4, own, p_near, p_side, g4, st, far_keep),
         flops=FL,
     )
-    near_keep, near_side = call(
-        "settle_near", settle_near, (shape(ROWS, 2 * D, f32), shape(ROWS, 2 * D, bf16)), vmem(2), (near_own, near_back)
-    )
-    near_side = moved(near_side, "ctx", lambda i: i ^ 2)
+    by_four, by_two = call(
+        "settle_near", settle_kernel, (shape(ROWS, 2 * D, bf16), shape(ROWS, 2 * D, bf16)), vmem(2), (near_own, near_back)
+    )
+    by_four = turned(by_four, "ctx", -4)
+    by_two = turned(by_two, "ctx", -2)
+    to_eight = call("relay_far", relay_far, shape(ROWS, 2 * D, bf16), smem(1) + vmem(2), (place, far_keep, far_side))
+    by_eight = turned(to_eight, "ctx", -8)
     last_own, grad_queries = call(
         "own_last",
         functools.partial(own_kernel, (4,)),
         (shape(ROWS, 2 * D, f32), shape(ROWS, HEADS * D, bf16)),
-        vmem(6) + token(1),
-        (q4, own, p_near, p_side, g4, st, near_keep),
-    )
-    to_two = call("relay_far", relay_far, shape(ROWS, 2 * D, bf16), smem(1) + vmem(2), (place, far_keep, far_side))
-    got_two = turned(to_two, "ctx", -2 * PLANE)
-    to_one = call(
-        "relay_near",
-        relay_near,
-        shape(ROWS, 2 * D, bf16),
-        smem(1) + vmem(3) + token(2),
-        (place, near_keep, near_side, far_side, to_two, last_own),
-    )
-    got_one = turned(to_one, "ctx", -PLANE)
+        vmem(6) + token(3),
+        (q4, own, p_near, p_side, g4, st, to_eight, by_four, by_two),
+        flops=FL,
+    )
     grad_keys, grad_values = call(
         "finish",
         finish_kernel,
         (shape(ROWS, D, bf16), shape(ROWS, D, bf16)),
-        smem(1) + vmem(5),
-        (place, last_own, near_back, near_side, got_one, got_two),
+        smem(1) + vmem(6),
+        (place, last_own, near_back, far_side, by_two, by_four, by_eight),
     )
     return grad_queries, grad_keys, grad_values
 

time: 52.2 us -> 51.7 us (level)
  the two profiles are of different devices: /device:TPU:8 before, /device:TPU:102 now
where the time goes in v10:
time: 51.7 us; the launch traced here: 51.5 us
  starting transfers between devices  19.8 us (38%)
  waiting for transfers between devices  16.9 us (33%)
  Pallas kernels  13.1 us (25%)
  other arithmetic  0.83 us (2%)
  between operations  0.81 us (2%)
    ppermute x17, starting transfers between devices, moved(): lax.ppermute(x, axis, [(i, to(i)) for i in range(lax.axis_size(axis))])  19.8 us
    ppermute x17, waiting for transfers between devices, moved(): lax.ppermute(x, axis, [(i, to(i)) for i in range(lax.axis_size(axis))])  16.9 us
    pallas_call x18, Pallas kernels, call(): pl.pallas_call(kernel, out_shape=outs, in_specs=ins, out_specs=vmem(1)[0]...  13.1 us
  transfers between devices with their start and end apart: 17, of which 7 were waited for; matrix products, arithmetic and copies ran while one was open for 2% of the time, Pallas kernels for 19%

profile of v10, /device:TPU:102, one launch (start us, length us, event | category | flops | bytes accessed | tf_op | source)
XLA Modules:
  0.0 51.5 jit_solution(8512047687598671470)
XLA Ops:
  0.6 3.3 %collective-permute-start.2 = (bf16[192,512]{1,0:T(8,128)(2,1)}, bf16[192,512]{1,0:T(8,128)(2,1)S(1)}, u32[]{:S(2)}, u32[]{:S(2)}) collective-permute-start(bf16[192,512]{1,0:T(8,128)(2,1)} %refs_0_.1), channel_id=1, source_target_pairs={{0,1},{1,0},{2,3},{3,2},{4,5},{5,4},{6,7},{7,6},{8,9},{9,8},{10,11... | collective-permute-start | bytes 589832 | tf_op jit(solution)/shard_map/ppermute | solution.py:331
  4.4 1.5 %collective-permute-start.4 = (bf16[192,512]{1,0:T(8,128)(2,1)}, bf16[192,512]{1,0:T(8,128)(2,1)S(1)}, u32[]{:S(2)}, u32[]{:S(2)}) collective-permute-start(bf16[192,512]{1,0:T(8,128)(2,1)} %refs_0_.1), channel_id=1, source_target_pairs={{0,6},{1,7},{2,0},{3,1},{4,2},{5,3},{6,4},{7,5},{8,14},{9,15},{10,... | collective-permute-start | bytes 589832 | tf_op jit(solution)/shard_map/ppermute | solution.py:331
  5.9 0.8 %pad_add_fusion.z0_ref = bf16[192,256]{1,0:T(8,128)(2,1)S(1)} fusion(bf16[192,128]{1,0:T(8,128)(2,1)} %param.8, bf16[192,128]{1,0:T(8,128)(2,1)} %param.7), kind=kLoop, calls=%fused_computation | loop fusion | flops 196608 | bytes 196608 | tf_op jit(solution)/shard_map/add | solution.py:368
  6.8 3.2 %collective-permute-start.1 = (bf16[192,256]{1,0:T(8,128)(2,1)S(1)}, bf16[192,256]{1,0:T(8,128)(2,1)S(1)}, u32[]{:S(2)}, u32[]{:S(2)}) collective-permute-start(bf16[192,256]{1,0:T(8,128)(2,1)S(1)} %pad_add_fusion.z0_ref), channel_id=1, source_target_pairs={{0,32},{8,40},{16,48},{24,56},{32,64},{40,72},{48,80},{56,88},{64,... | collective-permute-start | bytes 294920 | tf_op jit(solution)/shard_map/ppermute | solution.py:331
  10.0 1.5 %collective-permute-start = (bf16[192,256]{1,0:T(8,128)(2,1)S(1)}, bf16[192,256]{1,0:T(8,128)(2,1)S(1)}, u32[]{:S(2)}, u32[]{:S(2)}) collective-permute-start(bf16[192,256]{1,0:T(8,128)(2,1)S(1)} %pad_add_fusion.z0_ref), channel_id=1, source_target_pairs={{0,64},{8,72},{16,80},{24,88},{32,96},{40,104},{48,112},{56,120},{... | collective-permute-start | bytes 294920 | tf_op jit(solution)/shard_map/ppermute | solution.py:331
  11.5 2.3 %load.1 = (bf16[768,128]{1,0:T(8,128)(2,1)S(1)}, f32[8,768]{1,0:T(8,128)S(1)}, bf16[512,4096]{1,0:T(8,128)(2,1)S(1)}) custom-call(s32[1]{0:T(128)} %bitcast.place_ref, s32[1]{0:T(128)} %bitcast.1.head_ref, s32[8]{0:T(128)} %len_hbm.1, bf16[192,512]{1,0:T(8,128)(2,1)} %q_hbm.1, bf16[512,4096]{1,0:T(8,128)(2,1)} %w_hbm.1), custom_call_target="tpu_custom_call" | custom-call | flops 1 | bytes 1 | tf_op jit(solution)/shard_map/load/pallas_call | solution.py:345
  13.8 0.9 %collective-permute-start.7 = (bf16[192,512]{1,0:T(8,128)(2,1)S(1)}, bf16[192,512]{1,0:T(8,128)(2,1)S(1)}, u32[]{:S(2)}, u32[]{:S(2)}) collective-permute-start(bf16[192,512]{1,0:T(8,128)(2,1)S(1)} %stage.1.refs_0_.refs_1_), channel_id=1, source_target_pairs={{0,6},{1,7},{2,0},{3,1},{4,2},{5,3},{6,4},{7,5},{8,14},{9,15},{10,... | collective-permute-start | bytes 589832 | tf_op jit(solution)/shard_map/ppermute | solution.py:331
  14.7 2.4 %collective-permute-start.6 = (bf16[192,512]{1,0:T(8,128)(2,1)S(1)}, bf16[192,512]{1,0:T(8,128)(2,1)S(1)}, u32[]{:S(2)}, u32[]{:S(2)}) collective-permute-start(bf16[192,512]{1,0:T(8,128)(2,1)S(1)} %stage.1.refs_0_.refs_1_), channel_id=1, source_target_pairs={{0,2},{1,3},{2,4},{3,5},{4,6},{5,7},{6,0},{7,1},{8,10},{9,11},{10,... | collective-permute-start | bytes 589832 | tf_op jit(solution)/shard_map/ppermute | solution.py:331
  17.2 0.8 %collective-permute-start.5 = (bf16[384,256]{1,0:T(8,128)(2,1)S(1)}, bf16[384,256]{1,0:T(8,128)(2,1)S(1)}, u32[]{:S(2)}, u32[]{:S(2)}) collective-permute-start(bf16[384,256]{1,0:T(8,128)(2,1)S(1)} %pick_side.1.refs_0_), channel_id=1, source_target_pairs={{0,16},{8,24},{16,0},{24,8},{32,48},{40,56},{48,32},{56,40},{64,80... | collective-permute-start | bytes 589832 | tf_op jit(solution)/shard_map/ppermute | solution.py:331
  18.0 0.5 collective-permute-start.8
  18.5 2.3 %collective-permute-done.7.refs_2_.refs_5_ = bf16[192,512]{1,0:T(8,128)(2,1)S(1)} collective-permute-done((bf16[192,512]{1,0:T(8,128)(2,1)S(1)}, bf16[192,512]{1,0:T(8,128)(2,1)S(1)}, u32[]{:S(2)}, u32[]{:S(2)}) %collective-permute-start.7) | collective-permute-done | bytes 196640 | tf_op jit(solution)/shard_map/ppermute | solution.py:331
  20.8 1.6 %collective-permute-done.6.refs_1_.refs_4_ = bf16[192,512]{1,0:T(8,128)(2,1)S(1)} collective-permute-done((bf16[192,512]{1,0:T(8,128)(2,1)S(1)}, bf16[192,512]{1,0:T(8,128)(2,1)S(1)}, u32[]{:S(2)}, u32[]{:S(2)}) %collective-permute-start.6) | collective-permute-done | bytes 196640 | tf_op jit(solution)/shard_map/ppermute | solution.py:331
  22.4 1.3 %near.1 = (bf16[576,768]{1,0:T(8,128)(2,1)S(1)}, f32[152,768]{1,0:T(8,128)S(1)}) custom-call(s32[1]{0:T(128)} %bitcast.place_ref, bf16[192,256]{1,0:T(8,128)(2,1)S(1)} %collective-permute-done.z2_ref, bf16[192,256]{1,0:T(8,128)(2,1)S(1)} %collective-permute-done.1.z1_ref, bf16[192,256]{1,0:T(8,128)(2,1)S(1)} %pad_add_fusion.z0_ref, ...), custom_call_target="tpu_custom_call" | custom-call | flops 1 | bytes 1 | tf_op jit(solution)/shard_map/near/pallas_call | solution.py:345
  24.0 0.5 collective-permute-done.8.refs_6_
  24.5 3.2 %collective-permute-done.9.refs_7_ = bf16[192,512]{1,0:T(8,128)(2,1)S(1)} collective-permute-done((bf16[192,512]{1,0:T(8,128)(2,1)S(1)}, bf16[192,512]{1,0:T(8,128)(2,1)S(1)}, u32[]{:S(2)}, u32[]{:S(2)}) %collective-permute-start.9) | collective-permute-done | bytes 196640 | tf_op jit(solution)/shard_map/ppermute | solution.py:331
  27.7 1.6 %project.1 = (bf16[768,128]{1,0:T(8,128)(2,1)S(1)}, f32[128,768]{1,0:T(8,128)S(1)}) custom-call(bf16[192,512]{1,0:T(8,128)(2,1)S(1)} %copy-done, bf16[192,512]{1,0:T(8,128)(2,1)S(1)} %stage.1.refs_0_.refs_1_, bf16[192,512]{1,0:T(8,128)(2,1)S(1)} %collective-permute-done.3.refs_1_.refs_2_, bf16[192,512]{1,0:T(8,128)(2,1)S(1)} %collective-permute-done.4.refs_2_.refs_3_, ...), custom_call_target="tpu_custom_call" | custom-call | flops 1 | bytes 1 | tf_op jit(solution)/shard_map/project/pallas_call | solution.py:345
  29.3 0.9 %middle.1 = (bf16[384,768]{1,0:T(8,128)(2,1)S(1)}, f32[152,768]{1,0:T(8,128)S(1)}) custom-call(s32[1]{0:T(128)} %bitcast.place_ref, bf16[960,256]{1,0:T(8,128)(2,1)S(1)} %join_slots.1.refs_9_.own_ref, bf16[768,128]{1,0:T(8,128)(2,1)S(1)} %get-tuple-element.30.after.refs_3_.q4_ref, f32[152,768]{1,0:T(8,128)S(1)} %get-tuple-element.32.refs_0_.st_in_ref, ...), custom_call_target="tpu_custom_call" | custom-call | flops 4000000000 | bytes 1 | tf_op jit(solution)/shard_map/middle/pallas_call | solution.py:345
  30.2 1.6 %across.1 = (bf16[768,768]{1,0:T(8,128)(2,1)S(1)}, f32[152,768]{1,0:T(8,128)S(1)}) custom-call(s32[1]{0:T(128)} %bitcast.place_ref, bf16[960,256]{1,0:T(8,128)(2,1)S(1)} %collective-permute-done.10.par_ref, bf16[768,128]{1,0:T(8,128)(2,1)S(1)} %get-tuple-element.30.after.refs_3_.q4_ref, f32[128,768]{1,0:T(8,128)S(1)} %get-tuple-element.35.after.gt_ref, ...), custom_call_target="tpu_custom_call" | custom-call | flops 1 | bytes 1 | tf_op jit(solution)/shard_map/across/pallas_call | solution.py:345
  31.8 0.9 %cross_far.1 = (bf16[384,256]{1,0:T(8,128)(2,1)S(1)}, f32[152,768]{1,0:T(8,128)S(1)}) custom-call(s32[1]{0:T(128)} %bitcast.place_ref, bf16[768,128]{1,0:T(8,128)(2,1)S(1)} %get-tuple-element.30.after.refs_3_.q4_ref, bf16[960,256]{1,0:T(8,128)(2,1)S(1)} %collective-permute-done.10.par_ref, bf16[768,768]{1,0:T(8,128)(2,1)S(1)} %get-tuple-element.39.p_ref, ...), custom_call_target="tpu_custom_call" | custom-call | flops 1 | bytes 1 | tf_op jit(solution)/shard_map/cross_far/pallas_call | solution.py:345
  32.8 0.8 %cross_near.1 = (bf16[576,256]{1,0:T(8,128)(2,1)S(1)}, f32[152,768]{1,0:T(8,128)S(1)}) custom-call(s32[1]{0:T(128)} %bitcast.place_ref, bf16[768,128]{1,0:T(8,128)(2,1)S(1)} %get-tuple-element.30.after.refs_3_.q4_ref, bf16[960,256]{1,0:T(8,128)(2,1)S(1)} %collective-permute-done.10.par_ref, bf16[768,768]{1,0:T(8,128)(2,1)S(1)} %get-tuple-element.39.p_ref, ...), custom_call_target="tpu_custom_call" | custom-call | flops 4000000000 | bytes 1 | tf_op jit(solution)/shard_map/cross_near/pallas_call | solution.py:345
  33.6 1.0 %collective-permute-start.13 = (bf16[576,256]{1,0:T(8,128)(2,1)S(1)}, bf16[576,256]{1,0:T(8,128)(2,1)S(1)}, u32[]{:S(2)}, u32[]{:S(2)}) collective-permute-start(bf16[576,256]{1,0:T(8,128)(2,1)S(1)} %get-tuple-element.50), channel_id=1, source_target_pairs={{0,8},{8,0},{16,24},{24,16},{32,40},{40,32},{48,56},{56,48},{64,72... | collective-permute-start | bytes 884744 | tf_op jit(solution)/shard_map/ppermute | solution.py:331
  34.7 0.8 %own_far.1 = (f32[384,256]{1,0:T(8,128)S(1)}, f32[152,768]{1,0:T(8,128)S(1)}) custom-call(bf16[768,128]{1,0:T(8,128)(2,1)S(1)} %get-tuple-element.30.after.refs_3_.q4_ref, bf16[960,256]{1,0:T(8,128)(2,1)S(1)} %join_slots.1.refs_9_.own_ref, bf16[576,768]{1,0:T(8,128)(2,1)S(1)} %get-tuple-element.33.near_ref, bf16[384,768]{1,0:T(8,128)(2,1)S(1)} %get-tuple-element.36.side_ref, ...), custom_call_target="tpu_custom_call" | custom-call | flops 4000000000 | bytes 1 | tf_op jit(solution)/shard_map/own_far/pallas_call | solution.py:345
  35.5 0.7 %collective-permute-start.12 = (bf16[192,256]{1,0:T(8,128)(2,1)S(1)}, bf16[192,256]{1,0:T(8,128)(2,1)S(1)}, u32[]{:S(2)}, u32[]{:S(2)}) collective-permute-start(bf16[192,256]{1,0:T(8,128)(2,1)S(1)} %get-tuple-element.48), channel_id=1, source_target_pairs={{0,16},{8,24},{16,224},{24,232},{32,48},{40,56},{48,0},{56,8},{64,... | collective-permute-start | bytes 294920 | tf_op jit(solution)/shard_map/ppermute | solution.py:331
  36.3 0.8 %own_near.1 = (f32[384,256]{1,0:T(8,128)S(1)}, f32[152,768]{1,0:T(8,128)S(1)}) custom-call(bf16[768,128]{1,0:T(8,128)(2,1)S(1)} %get-tuple-element.30.after.refs_3_.q4_ref, bf16[960,256]{1,0:T(8,128)(2,1)S(1)} %join_slots.1.refs_9_.own_ref, bf16[576,768]{1,0:T(8,128)(2,1)S(1)} %get-tuple-element.33.near_ref, ...), custom_call_target="tpu_custom_call" | custom-call | flops 4000000000 | bytes 1 | tf_op jit(solution)/shard_map/own_near/pallas_call | solution.py:345
  37.1 1.1 %collective-permute-start.14 = (bf16[192,256]{1,0:T(8,128)(2,1)S(1)}, bf16[192,256]{1,0:T(8,128)(2,1)S(1)}, u32[]{:S(2)}, u32[]{:S(2)}) collective-permute-start(bf16[192,256]{1,0:T(8,128)(2,1)S(1)} %get-tuple-element.51), channel_id=1, source_target_pairs={{0,224},{8,232},{16,240},{24,248},{32,0},{40,8},{48,16},{56,24},{6... | collective-permute-start | bytes 294920 | tf_op jit(solution)/shard_map/ppermute | solution.py:331
  38.2 1.3 %collective-permute-start.15 = (bf16[192,256]{1,0:T(8,128)(2,1)S(1)}, bf16[192,256]{1,0:T(8,128)(2,1)S(1)}, u32[]{:S(2)}, u32[]{:S(2)}) collective-permute-start(bf16[192,256]{1,0:T(8,128)(2,1)S(1)} %get-tuple-element.52), channel_id=1, source_target_pairs={{0,240},{8,248},{16,0},{24,8},{32,16},{40,24},{48,32},{56,40},{64,... | collective-permute-start | bytes 294920 | tf_op jit(solution)/shard_map/ppermute | solution.py:331
  39.5 3.4 %collective-permute-done.12.side_ref = bf16[192,256]{1,0:T(8,128)(2,1)S(1)} collective-permute-done((bf16[192,256]{1,0:T(8,128)(2,1)S(1)}, bf16[192,256]{1,0:T(8,128)(2,1)S(1)}, u32[]{:S(2)}, u32[]{:S(2)}) %collective-permute-start.12) | collective-permute-done | bytes 98336 | tf_op jit(solution)/shard_map/ppermute | solution.py:331
  42.9 0.8 %collective-permute-start.16 = (bf16[192,256]{1,0:T(8,128)(2,1)S(1)}, bf16[192,256]{1,0:T(8,128)(2,1)S(1)}, u32[]{:S(2)}, u32[]{:S(2)}) collective-permute-start(bf16[192,256]{1,0:T(8,128)(2,1)S(1)} %relay_far.1.refs_0_), channel_id=1, source_target_pairs={{0,192},{8,200},{16,208},{24,216},{32,224},{40,232},{48,240},{56,2... | collective-permute-start | bytes 294920 | tf_op jit(solution)/shard_map/ppermute | solution.py:331
  43.7 0.8 %collective-permute-done.15.refs_2_.two_ref = bf16[192,256]{1,0:T(8,128)(2,1)S(1)} collective-permute-done((bf16[192,256]{1,0:T(8,128)(2,1)S(1)}, bf16[192,256]{1,0:T(8,128)(2,1)S(1)}, u32[]{:S(2)}, u32[]{:S(2)}) %collective-permute-start.15) | collective-permute-done | bytes 98336 | tf_op jit(solution)/shard_map/ppermute | solution.py:331
  44.5 1.2 %own_last.1 = (f32[192,256]{1,0:T(8,128)S(1)}, bf16[192,512]{1,0:T(8,128)(2,1)}) custom-call(bf16[768,128]{1,0:T(8,128)(2,1)S(1)} %get-tuple-element.30.after.refs_3_.q4_ref, bf16[960,256]{1,0:T(8,128)(2,1)S(1)} %join_slots.1.refs_9_.own_ref, bf16[576,768]{1,0:T(8,128)(2,1)S(1)} %get-tuple-element.33.near_ref, ...), custom_call_target="tpu_custom_call" | custom-call | flops 4000000000 | bytes 1 | tf_op jit(solution)/shard_map/own_last/pallas_call | solution.py:345
  45.8 5.0 %collective-permute-done.16.eight_ref = bf16[192,256]{1,0:T(8,128)(2,1)S(1)} collective-permute-done((bf16[192,256]{1,0:T(8,128)(2,1)S(1)}, bf16[192,256]{1,0:T(8,128)(2,1)S(1)}, u32[]{:S(2)}, u32[]{:S(2)}) %collective-permute-start.16) | collective-permute-done | bytes 98336 | tf_op jit(solution)/shard_map/ppermute | solution.py:331
  50.8 0.7 %finish.1 = (bf16[192,128]{1,0:T(8,128)(2,1)}, bf16[192,128]{1,0:T(8,128)(2,1)}) custom-call(s32[1]{0:T(128)} %bitcast.place_ref, f32[192,256]{1,0:T(8,128)S(1)} %get-tuple-element.54.own_ref, bf16[576,256]{1,0:T(8,128)(2,1)S(1)} %collective-permute-done.13.back_ref, bf16[192,256]{1,0:T(8,128)(2,1)S(1)} %collective-permute-done.12.side_ref, ...), custom_call_target="tpu_custom_call" | custom-call | flops 1 | bytes 1 | tf_op jit(solution)/shard_map/finish/pallas_call | solution.py:345
  (23 shorter events, 1.1 us)
Async XLA Ops:
  0.6 13.2 %collective-permute-start.2 = (bf16[192,512]{1,0:T(8,128)(2,1)}, bf16[192,512]{1,0:T(8,128)(2,1)S(1)}, u32[]{:S(2)}, u32[]{:S(2)}) collective-permute-start(bf16[192,512]{1,0:T(8,128)(2,1)} %refs_0_.1), channel_id=1, source_target_pairs={{0,1},{1,0},{2,3},{3,2},{4,5},{5,4},{6,7},{7,6},{8,9},{9,8},{10,11... | collective-permute-start | bytes 589832 | tf_op jit(solution)/shard_map/ppermute | solution.py:331
  3.9 10.8 %collective-permute-start.3 = (bf16[192,512]{1,0:T(8,128)(2,1)}, bf16[192,512]{1,0:T(8,128)(2,1)S(1)}, u32[]{:S(2)}, u32[]{:S(2)}) collective-permute-start(bf16[192,512]{1,0:T(8,128)(2,1)} %refs_0_.1), channel_id=1, source_target_pairs={{0,2},{1,3},{2,4},{3,5},{4,6},{5,7},{6,0},{7,1},{8,10},{9,11},{10,... | collective-permute-start | bytes 589832 | tf_op jit(solution)/shard_map/ppermute | solution.py:331
  4.4 12.8 %collective-permute-start.4 = (bf16[192,512]{1,0:T(8,128)(2,1)}, bf16[192,512]{1,0:T(8,128)(2,1)S(1)}, u32[]{:S(2)}, u32[]{:S(2)}) collective-permute-start(bf16[192,512]{1,0:T(8,128)(2,1)} %refs_0_.1), channel_id=1, source_target_pairs={{0,6},{1,7},{2,0},{3,1},{4,2},{5,3},{6,4},{7,5},{8,14},{9,15},{10,... | collective-permute-start | bytes 589832 | tf_op jit(solution)/shard_map/ppermute | solution.py:331
  6.8 10.4 %collective-permute-start.1 = (bf16[192,256]{1,0:T(8,128)(2,1)S(1)}, bf16[192,256]{1,0:T(8,128)(2,1)S(1)}, u32[]{:S(2)}, u32[]{:S(2)}) collective-permute-start(bf16[192,256]{1,0:T(8,128)(2,1)S(1)} %pad_add_fusion.z0_ref), channel_id=1, source_target_pairs={{0,32},{8,40},{16,48},{24,56},{32,64},{40,72},{48,80},{56,88},{64,... | collective-permute-start | bytes 294920 | tf_op jit(solution)/shard_map/ppermute | solution.py:331
  10.0 7.2 %collective-permute-start = (bf16[192,256]{1,0:T(8,128)(2,1)S(1)}, bf16[192,256]{1,0:T(8,128)(2,1)S(1)}, u32[]{:S(2)}, u32[]{:S(2)}) collective-permute-start(bf16[192,256]{1,0:T(8,128)(2,1)S(1)} %pad_add_fusion.z0_ref), channel_id=1, source_target_pairs={{0,64},{8,72},{16,80},{24,88},{32,96},{40,104},{48,112},{56,120},{... | collective-permute-start | bytes 294920 | tf_op jit(solution)/shard_map/ppermute | solution.py:331
  11.5 16.2 %copy-start = (bf16[192,512]{1,0:T(8,128)(2,1)S(1)}, bf16[192,512]{1,0:T(8,128)(2,1)}, u32[]{:S(2)}) copy-start(bf16[192,512]{1,0:T(8,128)(2,1)} %refs_0_.1) | copy-start | bytes 589828
  13.8 7.0 %collective-permute-start.7 = (bf16[192,512]{1,0:T(8,128)(2,1)S(1)}, bf16[192,512]{1,0:T(8,128)(2,1)S(1)}, u32[]{:S(2)}, u32[]{:S(2)}) collective-permute-start(bf16[192,512]{1,0:T(8,128)(2,1)S(1)} %stage.1.refs_0_.refs_1_), channel_id=1, source_target_pairs={{0,6},{1,7},{2,0},{3,1},{4,2},{5,3},{6,4},{7,5},{8,14},{9,15},{10,... | collective-permute-start | bytes 589832 | tf_op jit(solution)/shard_map/ppermute | solution.py:331
  14.7 7.6 %collective-permute-start.6 = (bf16[192,512]{1,0:T(8,128)(2,1)S(1)}, bf16[192,512]{1,0:T(8,128)(2,1)S(1)}, u32[]{:S(2)}, u32[]{:S(2)}) collective-permute-start(bf16[192,512]{1,0:T(8,128)(2,1)S(1)} %stage.1.refs_0_.refs_1_), channel_id=1, source_target_pairs={{0,2},{1,3},{2,4},{3,5},{4,6},{5,7},{6,0},{7,1},{8,10},{9,11},{10,... | collective-permute-start | bytes 589832 | tf_op jit(solution)/shard_map/ppermute | solution.py:331
  17.2 6.4 %collective-permute-start.5 = (bf16[384,256]{1,0:T(8,128)(2,1)S(1)}, bf16[384,256]{1,0:T(8,128)(2,1)S(1)}, u32[]{:S(2)}, u32[]{:S(2)}) collective-permute-start(bf16[384,256]{1,0:T(8,128)(2,1)S(1)} %pick_side.1.refs_0_), channel_id=1, source_target_pairs={{0,16},{8,24},{16,0},{24,8},{32,48},{40,56},{48,32},{56,40},{64,80... | collective-permute-start | bytes 589832 | tf_op jit(solution)/shard_map/ppermute | solution.py:331
  18.0 6.5 %collective-permute-start.8 = (bf16[192,512]{1,0:T(8,128)(2,1)S(1)}, bf16[192,512]{1,0:T(8,128)(2,1)S(1)}, u32[]{:S(2)}, u32[]{:S(2)}) collective-permute-start(bf16[192,512]{1,0:T(8,128)(2,1)S(1)} %collective-permute-done.3.refs_1_.refs_2_), channel_id=1, source_target_pairs={{0,2},{1,3},{2,4},{3,5},{4,6},{5,7},{6,0},{7,1},{8,10},{9,11},{10,... | collective-permute-start | bytes 589832 | tf_op jit(solution)/shard_map/ppermute | solution.py:331
  20.8 6.9 %collective-permute-start.9 = (bf16[192,512]{1,0:T(8,128)(2,1)S(1)}, bf16[192,512]{1,0:T(8,128)(2,1)S(1)}, u32[]{:S(2)}, u32[]{:S(2)}) collective-permute-start(bf16[192,512]{1,0:T(8,128)(2,1)S(1)} %collective-permute-done.7.refs_2_.refs_5_), channel_id=1, source_target_pairs={{0,6},{1,7},{2,0},{3,1},{4,2},{5,3},{6,4},{7,5},{8,14},{9,15},{10,... | collective-permute-start | bytes 589832 | tf_op jit(solution)/shard_map/ppermute | solution.py:331
  23.7 6.5 %collective-permute-start.10 = (bf16[960,256]{1,0:T(8,128)(2,1)S(1)}, bf16[960,256]{1,0:T(8,128)(2,1)S(1)}, u32[]{:S(2)}, u32[]{:S(2)}) collective-permute-start(bf16[960,256]{1,0:T(8,128)(2,1)S(1)} %join_slots.1.refs_9_.own_ref), channel_id=1, source_target_pairs={{0,8},{8,0},{16,24},{24,16},{32,40},{40,32},{48,56},{56,48},{64,72... | collective-permute-start | bytes 1474568 | tf_op jit(solution)/shard_map/ppermute | solution.py:331
  32.7 2.7 %collective-permute-start.11 = (bf16[384,256]{1,0:T(8,128)(2,1)S(1)}, bf16[384,256]{1,0:T(8,128)(2,1)S(1)}, u32[]{:S(2)}, u32[]{:S(2)}) collective-permute-start(bf16[384,256]{1,0:T(8,128)(2,1)S(1)} %get-tuple-element.45), channel_id=1, source_target_pairs={{0,8},{8,0},{16,24},{24,16},{32,40},{40,32},{48,56},{56,48},{64,72... | collective-permute-start | bytes 589832 | tf_op jit(solution)/shard_map/ppermute | solution.py:331
  33.6 3.4 %collective-permute-start.13 = (bf16[576,256]{1,0:T(8,128)(2,1)S(1)}, bf16[576,256]{1,0:T(8,128)(2,1)S(1)}, u32[]{:S(2)}, u32[]{:S(2)}) collective-permute-start(bf16[576,256]{1,0:T(8,128)(2,1)S(1)} %get-tuple-element.50), channel_id=1, source_target_pairs={{0,8},{8,0},{16,24},{24,16},{32,40},{40,32},{48,56},{56,48},{64,72... | collective-permute-start | bytes 884744 | tf_op jit(solution)/shard_map/ppermute | solution.py:331
  35.5 7.4 %collective-permute-start.12 = (bf16[192,256]{1,0:T(8,128)(2,1)S(1)}, bf16[192,256]{1,0:T(8,128)(2,1)S(1)}, u32[]{:S(2)}, u32[]{:S(2)}) collective-permute-start(bf16[192,256]{1,0:T(8,128)(2,1)S(1)} %get-tuple-element.48), channel_id=1, source_target_pairs={{0,16},{8,24},{16,224},{24,232},{32,48},{40,56},{48,0},{56,8},{64,... | collective-permute-start | bytes 294920 | tf_op jit(solution)/shard_map/ppermute | solution.py:331
  37.1 6.6 %collective-permute-start.14 = (bf16[192,256]{1,0:T(8,128)(2,1)S(1)}, bf16[192,256]{1,0:T(8,128)(2,1)S(1)}, u32[]{:S(2)}, u32[]{:S(2)}) collective-permute-start(bf16[192,256]{1,0:T(8,128)(2,1)S(1)} %get-tuple-element.51), channel_id=1, source_target_pairs={{0,224},{8,232},{16,240},{24,248},{32,0},{40,8},{48,16},{56,24},{6... | collective-permute-start | bytes 294920 | tf_op jit(solution)/shard_map/ppermute | solution.py:331
  38.2 6.3 %collective-permute-start.15 = (bf16[192,256]{1,0:T(8,128)(2,1)S(1)}, bf16[192,256]{1,0:T(8,128)(2,1)S(1)}, u32[]{:S(2)}, u32[]{:S(2)}) collective-permute-start(bf16[192,256]{1,0:T(8,128)(2,1)S(1)} %get-tuple-element.52), channel_id=1, source_target_pairs={{0,240},{8,248},{16,0},{24,8},{32,16},{40,24},{48,32},{56,40},{64,... | collective-permute-start | bytes 294920 | tf_op jit(solution)/shard_map/ppermute | solution.py:331
  42.9 7.9 %collective-permute-start.16 = (bf16[192,256]{1,0:T(8,128)(2,1)S(1)}, bf16[192,256]{1,0:T(8,128)(2,1)S(1)}, u32[]{:S(2)}, u32[]{:S(2)}) collective-permute-start(bf16[192,256]{1,0:T(8,128)(2,1)S(1)} %relay_far.1.refs_0_), channel_id=1, source_target_pairs={{0,192},{8,200},{16,208},{24,216},{32,224},{40,232},{48,240},{56,2... | collective-permute-start | bytes 294920 | tf_op jit(solution)/shard_map/ppermute | solution.py:331

commit v11 on v10

--- a/solution.py
+++ b/solution.py
@@ -24,6 +24,7 @@
 LOG2E = 1.4426950408889634
 MIB = 1 << 20
 FL = 4 * 10**9
+COSTLY = 4 * 10**9
 
 
 def dot(a, b, ca, cb):
@@ -141,12 +142,16 @@
 
 
 def project_kernel(*refs):
-    pieces, (w_ref, after, g4_ref, gt_ref) = refs[:8], refs[8:]
+    pieces, (w_ref, after, acc_ref) = refs[:7], refs[7:]
     acc = None
     for i, piece in enumerate(pieces):
         part = dot(piece[...], w_ref[:, i * BLOCK : (i + 1) * BLOCK], 1, 1)
         acc = part if acc is None else acc + part
-    acc = acc.astype(jnp.bfloat16)
+    acc_ref[...] = acc
+
+
+def last_projection(piece_ref, w_ref, acc_ref, after, g4_ref, gt_ref):
+    acc = (acc_ref[...] + dot(piece_ref[...], w_ref[:, 7 * BLOCK :], 1, 1)).astype(jnp.bfloat16)
     for h in range(HEADS):
         g4_ref[h * ROWS : (h + 1) * ROWS, :] = acc[:, h * D : (h + 1) * D]
     gt_ref[...] = jnp.transpose(g4_ref[...].astype(jnp.float32))
@@ -397,15 +402,27 @@
     own = call("join_slots", join_kernel, shape(SLOTS * ROWS, 2 * D, bf16), vmem(4) + token(1), (z2, z1, kv, side, st))
     par = moved(own, "ctx", lambda i: i ^ 1)
 
-    g4, gt = call(
+    early = call(
         "project",
         project_kernel,
+        shape(ROWS, HEADS * D, f32),
+        vmem(8) + token(1),
+        (grad_out, other, right, left, other_right, other_left, far, weight, own),
+    )
+    p_side, st = call(
+        "middle",
+        middle_kernel,
+        (shape(2 * ROWS, LANES, bf16), state),
+        smem(1) + vmem(3) + token(1),
+        (place, own, q4, st, early),
+    )
+    g4, gt = call(
+        "last_projection",
+        last_projection,
         (shape(LANES, D, bf16), shape(D, LANES, f32)),
-        vmem(9) + token(1),
-        (grad_out, other, right, left, other_right, other_left, far, other_far, weight, own),
-    )
-    p_side, st = call(
-        "middle", middle_kernel, (shape(2 * ROWS, LANES, bf16), state), smem(1) + vmem(3) + token(1), (place, own, q4, st, gt), flops=4 * 10**9
+        vmem(3) + token(1),
+        (other_far, weight, early, st),
+        flops=COSTLY,
     )
     p_par, st = call(
         "across", across_kernel, (shape(REACH * ROWS, LANES, bf16), state), smem(1) + vmem(4), (place, par, q4, gt, st)

time: 51.7 us -> 51.4 us (level)
  the two profiles are of different devices: /device:TPU:102 before, /device:TPU:64 now
where the time goes in v11:
time: 51.4 us; the launch traced here: 51 us
  starting transfers between devices  22.3 us (43%)
  waiting for transfers between devices  13.7 us (27%)
  Pallas kernels  13.3 us (26%)
  other arithmetic  0.83 us (2%)
  between operations  0.82 us (2%)
    ppermute x17, starting transfers between devices, moved(): lax.ppermute(x, axis, [(i, to(i)) for i in range(lax.axis_size(axis))])  22.3 us
    ppermute x17, waiting for transfers between devices, moved(): lax.ppermute(x, axis, [(i, to(i)) for i in range(lax.axis_size(axis))])  13.7 us
    pallas_call x19, Pallas kernels, call(): pl.pallas_call(kernel, out_shape=outs, in_specs=ins, out_specs=vmem(1)[0]...  13.3 us
  transfers between devices with their start and end apart: 17, of which 7 were waited for; matrix products, arithmetic and copies ran while one was open for 2% of the time, Pallas kernels for 20%

profile of v11, /device:TPU:64, one launch (start us, length us, event | category | flops | bytes accessed | tf_op | source)
XLA Modules:
  0.0 51.0 jit_solution(11017044390705484959)
XLA Ops:
  0.6 3.3 %collective-permute-start.2 = (bf16[192,512]{1,0:T(8,128)(2,1)}, bf16[192,512]{1,0:T(8,128)(2,1)S(1)}, u32[]{:S(2)}, u32[]{:S(2)}) collective-permute-start(bf16[192,512]{1,0:T(8,128)(2,1)} %refs_0_.1), channel_id=1, source_target_pairs={{0,1},{1,0},{2,3},{3,2},{4,5},{5,4},{6,7},{7,6},{8,9},{9,8},{10,11... | collective-permute-start | bytes 589832 | tf_op jit(solution)/shard_map/ppermute | solution.py:336
  3.9 1.5 %collective-permute-start.3 = (bf16[192,512]{1,0:T(8,128)(2,1)}, bf16[192,512]{1,0:T(8,128)(2,1)S(1)}, u32[]{:S(2)}, u32[]{:S(2)}) collective-permute-start(bf16[192,512]{1,0:T(8,128)(2,1)} %refs_0_.1), channel_id=1, source_target_pairs={{0,2},{1,3},{2,4},{3,5},{4,6},{5,7},{6,0},{7,1},{8,10},{9,11},{10,... | collective-permute-start | bytes 589832 | tf_op jit(solution)/shard_map/ppermute | solution.py:336
  5.4 1.7 %collective-permute-start.4 = (bf16[192,512]{1,0:T(8,128)(2,1)}, bf16[192,512]{1,0:T(8,128)(2,1)S(1)}, u32[]{:S(2)}, u32[]{:S(2)}) collective-permute-start(bf16[192,512]{1,0:T(8,128)(2,1)} %refs_0_.1), channel_id=1, source_target_pairs={{0,6},{1,7},{2,0},{3,1},{4,2},{5,3},{6,4},{7,5},{8,14},{9,15},{10,... | collective-permute-start | bytes 589832 | tf_op jit(solution)/shard_map/ppermute | solution.py:336
  7.1 0.8 %pad_add_fusion.z0_ref = bf16[192,256]{1,0:T(8,128)(2,1)S(1)} fusion(bf16[192,128]{1,0:T(8,128)(2,1)} %param.8, bf16[192,128]{1,0:T(8,128)(2,1)} %param.7), kind=kLoop, calls=%fused_computation | loop fusion | flops 196608 | bytes 196608 | tf_op jit(solution)/shard_map/add | solution.py:373
  8.0 4.6 %collective-permute-start = (bf16[192,256]{1,0:T(8,128)(2,1)S(1)}, bf16[192,256]{1,0:T(8,128)(2,1)S(1)}, u32[]{:S(2)}, u32[]{:S(2)}) collective-permute-start(bf16[192,256]{1,0:T(8,128)(2,1)S(1)} %pad_add_fusion.z0_ref), channel_id=1, source_target_pairs={{0,64},{8,72},{16,80},{24,88},{32,96},{40,104},{48,112},{56,120},{... | collective-permute-start | bytes 294920 | tf_op jit(solution)/shard_map/ppermute | solution.py:336
  12.5 1.0 %collective-permute-start.1 = (bf16[192,256]{1,0:T(8,128)(2,1)S(1)}, bf16[192,256]{1,0:T(8,128)(2,1)S(1)}, u32[]{:S(2)}, u32[]{:S(2)}) collective-permute-start(bf16[192,256]{1,0:T(8,128)(2,1)S(1)} %pad_add_fusion.z0_ref), channel_id=1, source_target_pairs={{0,32},{8,40},{16,48},{24,56},{32,64},{40,72},{48,80},{56,88},{64,... | collective-permute-start | bytes 294920 | tf_op jit(solution)/shard_map/ppermute | solution.py:336
  13.6 2.3 %load.1 = (bf16[768,128]{1,0:T(8,128)(2,1)S(1)}, f32[8,768]{1,0:T(8,128)S(1)}, bf16[512,4096]{1,0:T(8,128)(2,1)S(1)}) custom-call(s32[1]{0:T(128)} %bitcast.place_ref, s32[1]{0:T(128)} %bitcast.1.head_ref, s32[8]{0:T(128)} %len_hbm.1, bf16[192,512]{1,0:T(8,128)(2,1)} %q_hbm.1, bf16[512,4096]{1,0:T(8,128)(2,1)} %w_hbm.1), custom_call_target="tpu_custom_call" | custom-call | flops 1 | bytes 1 | tf_op jit(solution)/shard_map/load/pallas_call | solution.py:350
  15.9 1.6 %collective-permute-start.7 = (bf16[192,512]{1,0:T(8,128)(2,1)S(1)}, bf16[192,512]{1,0:T(8,128)(2,1)S(1)}, u32[]{:S(2)}, u32[]{:S(2)}) collective-permute-start(bf16[192,512]{1,0:T(8,128)(2,1)S(1)} %stage.1.refs_0_.refs_1_), channel_id=1, source_target_pairs={{0,6},{1,7},{2,0},{3,1},{4,2},{5,3},{6,4},{7,5},{8,14},{9,15},{10,... | collective-permute-start | bytes 589832 | tf_op jit(solution)/shard_map/ppermute | solution.py:336
  17.6 0.5 collective-permute-start.6
  18.1 0.8 %collective-permute-start.5 = (bf16[384,256]{1,0:T(8,128)(2,1)S(1)}, bf16[384,256]{1,0:T(8,128)(2,1)S(1)}, u32[]{:S(2)}, u32[]{:S(2)}) collective-permute-start(bf16[384,256]{1,0:T(8,128)(2,1)S(1)} %pick_side.1.refs_0_), channel_id=1, source_target_pairs={{0,16},{8,24},{16,0},{24,8},{32,48},{40,56},{48,32},{56,40},{64,80... | collective-permute-start | bytes 589832 | tf_op jit(solution)/shard_map/ppermute | solution.py:336
  19.2 2.6 %collective-permute-done.7.refs_2_.refs_5_ = bf16[192,512]{1,0:T(8,128)(2,1)S(1)} collective-permute-done((bf16[192,512]{1,0:T(8,128)(2,1)S(1)}, bf16[192,512]{1,0:T(8,128)(2,1)S(1)}, u32[]{:S(2)}, u32[]{:S(2)}) %collective-permute-start.7) | collective-permute-done | bytes 196640 | tf_op jit(solution)/shard_map/ppermute | solution.py:336
  21.7 2.7 %collective-permute-start.9 = (bf16[192,512]{1,0:T(8,128)(2,1)S(1)}, bf16[192,512]{1,0:T(8,128)(2,1)S(1)}, u32[]{:S(2)}, u32[]{:S(2)}) collective-permute-start(bf16[192,512]{1,0:T(8,128)(2,1)S(1)} %collective-permute-done.7.refs_2_.refs_5_), channel_id=1, source_target_pairs={{0,6},{1,7},{2,0},{3,1},{4,2},{5,3},{6,4},{7,5},{8,14},{9,15},{10,... | collective-permute-start | bytes 589832 | tf_op jit(solution)/shard_map/ppermute | solution.py:336
  24.5 1.4 %collective-permute-done.6.refs_1_.refs_4_ = bf16[192,512]{1,0:T(8,128)(2,1)S(1)} collective-permute-done((bf16[192,512]{1,0:T(8,128)(2,1)S(1)}, bf16[192,512]{1,0:T(8,128)(2,1)S(1)}, u32[]{:S(2)}, u32[]{:S(2)}) %collective-permute-start.6) | collective-permute-done | bytes 196640 | tf_op jit(solution)/shard_map/ppermute | solution.py:336
  25.9 1.3 %near.1 = (bf16[576,768]{1,0:T(8,128)(2,1)S(1)}, f32[152,768]{1,0:T(8,128)S(1)}) custom-call(s32[1]{0:T(128)} %bitcast.place_ref, bf16[192,256]{1,0:T(8,128)(2,1)S(1)} %collective-permute-done.z2_ref, bf16[192,256]{1,0:T(8,128)(2,1)S(1)} %collective-permute-done.1.z1_ref, bf16[192,256]{1,0:T(8,128)(2,1)S(1)} %pad_add_fusion.z0_ref, ...), custom_call_target="tpu_custom_call" | custom-call | flops 1 | bytes 1 | tf_op jit(solution)/shard_map/near/pallas_call | solution.py:350
  27.5 0.5 collective-permute-done.8.refs_6_
  28.0 1.4 %project.1.after.acc_ref = f32[192,512]{1,0:T(8,128)S(1)} custom-call(bf16[192,512]{1,0:T(8,128)(2,1)S(1)} %copy-done, bf16[192,512]{1,0:T(8,128)(2,1)S(1)} %stage.1.refs_0_.refs_1_, bf16[192,512]{1,0:T(8,128)(2,1)S(1)} %collective-permute-done.3.refs_1_.refs_2_, bf16[192,512]{1,0:T(8,128)(2,1)S(1)} %collective-permute-done.4.refs_2_.refs_3_, ...), custom_call_target="tpu_custom_call" | custom-call | flops 1 | bytes 1 | tf_op jit(solution)/shard_map/project/pallas_call | solution.py:350
  29.3 0.9 %middle.1 = (bf16[384,768]{1,0:T(8,128)(2,1)S(1)}, f32[152,768]{1,0:T(8,128)S(1)}) custom-call(s32[1]{0:T(128)} %bitcast.place_ref, bf16[960,256]{1,0:T(8,128)(2,1)S(1)} %join_slots.1.refs_8_.own_ref, bf16[768,128]{1,0:T(8,128)(2,1)S(1)} %get-tuple-element.30.after.refs_3_.q4_ref, f32[152,768]{1,0:T(8,128)S(1)} %get-tuple-element.32.refs_0_.st_in_ref, ...), custom_call_target="tpu_custom_call" | custom-call | flops 1 | bytes 1 | tf_op jit(solution)/shard_map/middle/pallas_call | solution.py:350
  30.7 1.6 %across.1 = (bf16[768,768]{1,0:T(8,128)(2,1)S(1)}, f32[152,768]{1,0:T(8,128)S(1)}) custom-call(s32[1]{0:T(128)} %bitcast.place_ref, bf16[960,256]{1,0:T(8,128)(2,1)S(1)} %collective-permute-done.10.par_ref, bf16[768,128]{1,0:T(8,128)(2,1)S(1)} %get-tuple-element.30.after.refs_3_.q4_ref, f32[128,768]{1,0:T(8,128)S(1)} %get-tuple-element.38.gt_ref, ...), custom_call_target="tpu_custom_call" | custom-call | flops 1 | bytes 1 | tf_op jit(solution)/shard_map/across/pallas_call | solution.py:350
  32.3 0.9 %cross_far.1 = (bf16[384,256]{1,0:T(8,128)(2,1)S(1)}, f32[152,768]{1,0:T(8,128)S(1)}) custom-call(s32[1]{0:T(128)} %bitcast.place_ref, bf16[768,128]{1,0:T(8,128)(2,1)S(1)} %get-tuple-element.30.after.refs_3_.q4_ref, bf16[960,256]{1,0:T(8,128)(2,1)S(1)} %collective-permute-done.10.par_ref, bf16[768,768]{1,0:T(8,128)(2,1)S(1)} %get-tuple-element.39.p_ref, ...), custom_call_target="tpu_custom_call" | custom-call | flops 1 | bytes 1 | tf_op jit(solution)/shard_map/cross_far/pallas_call | solution.py:350
  33.3 0.8 %cross_near.1 = (bf16[576,256]{1,0:T(8,128)(2,1)S(1)}, f32[152,768]{1,0:T(8,128)S(1)}) custom-call(s32[1]{0:T(128)} %bitcast.place_ref, bf16[768,128]{1,0:T(8,128)(2,1)S(1)} %get-tuple-element.30.after.refs_3_.q4_ref, bf16[960,256]{1,0:T(8,128)(2,1)S(1)} %collective-permute-done.10.par_ref, bf16[768,768]{1,0:T(8,128)(2,1)S(1)} %get-tuple-element.39.p_ref, ...), custom_call_target="tpu_custom_call" | custom-call | flops 4000000000 | bytes 1 | tf_op jit(solution)/shard_map/cross_near/pallas_call | solution.py:350
  34.1 1.0 %collective-permute-start.13 = (bf16[576,256]{1,0:T(8,128)(2,1)S(1)}, bf16[576,256]{1,0:T(8,128)(2,1)S(1)}, u32[]{:S(2)}, u32[]{:S(2)}) collective-permute-start(bf16[576,256]{1,0:T(8,128)(2,1)S(1)} %get-tuple-element.50), channel_id=1, source_target_pairs={{0,8},{8,0},{16,24},{24,16},{32,40},{40,32},{48,56},{56,48},{64,72... | collective-permute-start | bytes 884744 | tf_op jit(solution)/shard_map/ppermute | solution.py:336
  35.2 0.8 %own_far.1 = (f32[384,256]{1,0:T(8,128)S(1)}, f32[152,768]{1,0:T(8,128)S(1)}) custom-call(bf16[768,128]{1,0:T(8,128)(2,1)S(1)} %get-tuple-element.30.after.refs_3_.q4_ref, bf16[960,256]{1,0:T(8,128)(2,1)S(1)} %join_slots.1.refs_8_.own_ref, bf16[576,768]{1,0:T(8,128)(2,1)S(1)} %get-tuple-element.33.near_ref, bf16[384,768]{1,0:T(8,128)(2,1)S(1)} %get-tuple-element.35.side_ref, ...), custom_call_target="tpu_custom_call" | custom-call | flops 4000000000 | bytes 1 | tf_op jit(solution)/shard_map/own_far/pallas_call | solution.py:350
  36.0 0.8 %collective-permute-start.12 = (bf16[192,256]{1,0:T(8,128)(2,1)S(1)}, bf16[192,256]{1,0:T(8,128)(2,1)S(1)}, u32[]{:S(2)}, u32[]{:S(2)}) collective-permute-start(bf16[192,256]{1,0:T(8,128)(2,1)S(1)} %get-tuple-element.48), channel_id=1, source_target_pairs={{0,16},{8,24},{16,224},{24,232},{32,48},{40,56},{48,0},{56,8},{64,... | collective-permute-start | bytes 294920 | tf_op jit(solution)/shard_map/ppermute | solution.py:336
  36.8 0.8 %own_near.1 = (f32[384,256]{1,0:T(8,128)S(1)}, f32[152,768]{1,0:T(8,128)S(1)}) custom-call(bf16[768,128]{1,0:T(8,128)(2,1)S(1)} %get-tuple-element.30.after.refs_3_.q4_ref, bf16[960,256]{1,0:T(8,128)(2,1)S(1)} %join_slots.1.refs_8_.own_ref, bf16[576,768]{1,0:T(8,128)(2,1)S(1)} %get-tuple-element.33.near_ref, ...), custom_call_target="tpu_custom_call" | custom-call | flops 4000000000 | bytes 1 | tf_op jit(solution)/shard_map/own_near/pallas_call | solution.py:350
  37.7 1.1 %collective-permute-start.14 = (bf16[192,256]{1,0:T(8,128)(2,1)S(1)}, bf16[192,256]{1,0:T(8,128)(2,1)S(1)}, u32[]{:S(2)}, u32[]{:S(2)}) collective-permute-start(bf16[192,256]{1,0:T(8,128)(2,1)S(1)} %get-tuple-element.51), channel_id=1, source_target_pairs={{0,224},{8,232},{16,240},{24,248},{32,0},{40,8},{48,16},{56,24},{6... | collective-permute-start | bytes 294920 | tf_op jit(solution)/shard_map/ppermute | solution.py:336
  38.7 1.0 %collective-permute-start.15 = (bf16[192,256]{1,0:T(8,128)(2,1)S(1)}, bf16[192,256]{1,0:T(8,128)(2,1)S(1)}, u32[]{:S(2)}, u32[]{:S(2)}) collective-permute-start(bf16[192,256]{1,0:T(8,128)(2,1)S(1)} %get-tuple-element.52), channel_id=1, source_target_pairs={{0,240},{8,248},{16,0},{24,8},{32,16},{40,24},{48,32},{56,40},{64,... | collective-permute-start | bytes 294920 | tf_op jit(solution)/shard_map/ppermute | solution.py:336
  39.7 2.5 %collective-permute-done.12.side_ref = bf16[192,256]{1,0:T(8,128)(2,1)S(1)} collective-permute-done((bf16[192,256]{1,0:T(8,128)(2,1)S(1)}, bf16[192,256]{1,0:T(8,128)(2,1)S(1)}, u32[]{:S(2)}, u32[]{:S(2)}) %collective-permute-start.12) | collective-permute-done | bytes 98336 | tf_op jit(solution)/shard_map/ppermute | solution.py:336
  42.3 1.0 %collective-permute-done.14.refs_1_.four_ref = bf16[192,256]{1,0:T(8,128)(2,1)S(1)} collective-permute-done((bf16[192,256]{1,0:T(8,128)(2,1)S(1)}, bf16[192,256]{1,0:T(8,128)(2,1)S(1)}, u32[]{:S(2)}, u32[]{:S(2)}) %collective-permute-start.14) | collective-permute-done | bytes 98336 | tf_op jit(solution)/shard_map/ppermute | solution.py:336
  43.3 1.5 %collective-permute-done.15.refs_2_.two_ref = bf16[192,256]{1,0:T(8,128)(2,1)S(1)} collective-permute-done((bf16[192,256]{1,0:T(8,128)(2,1)S(1)}, bf16[192,256]{1,0:T(8,128)(2,1)S(1)}, u32[]{:S(2)}, u32[]{:S(2)}) %collective-permute-start.15) | collective-permute-done | bytes 98336 | tf_op jit(solution)/shard_map/ppermute | solution.py:336
  44.8 1.2 %own_last.1 = (f32[192,256]{1,0:T(8,128)S(1)}, bf16[192,512]{1,0:T(8,128)(2,1)}) custom-call(bf16[768,128]{1,0:T(8,128)(2,1)S(1)} %get-tuple-element.30.after.refs_3_.q4_ref, bf16[960,256]{1,0:T(8,128)(2,1)S(1)} %join_slots.1.refs_8_.own_ref, bf16[576,768]{1,0:T(8,128)(2,1)S(1)} %get-tuple-element.33.near_ref, ...), custom_call_target="tpu_custom_call" | custom-call | flops 4000000000 | bytes 1 | tf_op jit(solution)/shard_map/own_last/pallas_call | solution.py:350
  46.0 4.2 %collective-permute-done.16.eight_ref = bf16[192,256]{1,0:T(8,128)(2,1)S(1)} collective-permute-done((bf16[192,256]{1,0:T(8,128)(2,1)S(1)}, bf16[192,256]{1,0:T(8,128)(2,1)S(1)}, u32[]{:S(2)}, u32[]{:S(2)}) %collective-permute-start.16) | collective-permute-done | bytes 98336 | tf_op jit(solution)/shard_map/ppermute | solution.py:336
  50.2 0.7 %finish.1 = (bf16[192,128]{1,0:T(8,128)(2,1)}, bf16[192,128]{1,0:T(8,128)(2,1)}) custom-call(s32[1]{0:T(128)} %bitcast.place_ref, f32[192,256]{1,0:T(8,128)S(1)} %get-tuple-element.54.own_ref, bf16[576,256]{1,0:T(8,128)(2,1)S(1)} %collective-permute-done.13.back_ref, bf16[192,256]{1,0:T(8,128)(2,1)S(1)} %collective-permute-done.12.side_ref, ...), custom_call_target="tpu_custom_call" | custom-call | flops 1 | bytes 1 | tf_op jit(solution)/shard_map/finish/pallas_call | solution.py:350
  (24 shorter events, 1.5 us)
Async XLA Ops:
  0.6 15.3 %collective-permute-start.2 = (bf16[192,512]{1,0:T(8,128)(2,1)}, bf16[192,512]{1,0:T(8,128)(2,1)S(1)}, u32[]{:S(2)}, u32[]{:S(2)}) collective-permute-start(bf16[192,512]{1,0:T(8,128)(2,1)} %refs_0_.1), channel_id=1, source_target_pairs={{0,1},{1,0},{2,3},{3,2},{4,5},{5,4},{6,7},{7,6},{8,9},{9,8},{10,11... | collective-permute-start | bytes 589832 | tf_op jit(solution)/shard_map/ppermute | solution.py:336
  3.9 13.7 %collective-permute-start.3 = (bf16[192,512]{1,0:T(8,128)(2,1)}, bf16[192,512]{1,0:T(8,128)(2,1)S(1)}, u32[]{:S(2)}, u32[]{:S(2)}) collective-permute-start(bf16[192,512]{1,0:T(8,128)(2,1)} %refs_0_.1), channel_id=1, source_target_pairs={{0,2},{1,3},{2,4},{3,5},{4,6},{5,7},{6,0},{7,1},{8,10},{9,11},{10,... | collective-permute-start | bytes 589832 | tf_op jit(solution)/shard_map/ppermute | solution.py:336
  5.4 12.7 %collective-permute-start.4 = (bf16[192,512]{1,0:T(8,128)(2,1)}, bf16[192,512]{1,0:T(8,128)(2,1)S(1)}, u32[]{:S(2)}, u32[]{:S(2)}) collective-permute-start(bf16[192,512]{1,0:T(8,128)(2,1)} %refs_0_.1), channel_id=1, source_target_pairs={{0,6},{1,7},{2,0},{3,1},{4,2},{5,3},{6,4},{7,5},{8,14},{9,15},{10,... | collective-permute-start | bytes 589832 | tf_op jit(solution)/shard_map/ppermute | solution.py:336
  8.0 10.1 %collective-permute-start = (bf16[192,256]{1,0:T(8,128)(2,1)S(1)}, bf16[192,256]{1,0:T(8,128)(2,1)S(1)}, u32[]{:S(2)}, u32[]{:S(2)}) collective-permute-start(bf16[192,256]{1,0:T(8,128)(2,1)S(1)} %pad_add_fusion.z0_ref), channel_id=1, source_target_pairs={{0,64},{8,72},{16,80},{24,88},{32,96},{40,104},{48,112},{56,120},{... | collective-permute-start | bytes 294920 | tf_op jit(solution)/shard_map/ppermute | solution.py:336
  12.5 5.5 %collective-permute-start.1 = (bf16[192,256]{1,0:T(8,128)(2,1)S(1)}, bf16[192,256]{1,0:T(8,128)(2,1)S(1)}, u32[]{:S(2)}, u32[]{:S(2)}) collective-permute-start(bf16[192,256]{1,0:T(8,128)(2,1)S(1)} %pad_add_fusion.z0_ref), channel_id=1, source_target_pairs={{0,32},{8,40},{16,48},{24,56},{32,64},{40,72},{48,80},{56,88},{64,... | collective-permute-start | bytes 294920 | tf_op jit(solution)/shard_map/ppermute | solution.py:336
  13.6 14.4 %copy-start = (bf16[192,512]{1,0:T(8,128)(2,1)S(1)}, bf16[192,512]{1,0:T(8,128)(2,1)}, u32[]{:S(2)}) copy-start(bf16[192,512]{1,0:T(8,128)(2,1)} %refs_0_.1) | copy-start | bytes 589828
  15.9 5.8 %collective-permute-start.7 = (bf16[192,512]{1,0:T(8,128)(2,1)S(1)}, bf16[192,512]{1,0:T(8,128)(2,1)S(1)}, u32[]{:S(2)}, u32[]{:S(2)}) collective-permute-start(bf16[192,512]{1,0:T(8,128)(2,1)S(1)} %stage.1.refs_0_.refs_1_), channel_id=1, source_target_pairs={{0,6},{1,7},{2,0},{3,1},{4,2},{5,3},{6,4},{7,5},{8,14},{9,15},{10,... | collective-permute-start | bytes 589832 | tf_op jit(solution)/shard_map/ppermute | solution.py:336
  17.6 8.3 %collective-permute-start.6 = (bf16[192,512]{1,0:T(8,128)(2,1)S(1)}, bf16[192,512]{1,0:T(8,128)(2,1)S(1)}, u32[]{:S(2)}, u32[]{:S(2)}) collective-permute-start(bf16[192,512]{1,0:T(8,128)(2,1)S(1)} %stage.1.refs_0_.refs_1_), channel_id=1, source_target_pairs={{0,2},{1,3},{2,4},{3,5},{4,6},{5,7},{6,0},{7,1},{8,10},{9,11},{10,... | collective-permute-start | bytes 589832 | tf_op jit(solution)/shard_map/ppermute | solution.py:336
  18.1 9.0 %collective-permute-start.5 = (bf16[384,256]{1,0:T(8,128)(2,1)S(1)}, bf16[384,256]{1,0:T(8,128)(2,1)S(1)}, u32[]{:S(2)}, u32[]{:S(2)}) collective-permute-start(bf16[384,256]{1,0:T(8,128)(2,1)S(1)} %pick_side.1.refs_0_), channel_id=1, source_target_pairs={{0,16},{8,24},{16,0},{24,8},{32,48},{40,56},{48,32},{56,40},{64,80... | collective-permute-start | bytes 589832 | tf_op jit(solution)/shard_map/ppermute | solution.py:336
  18.9 9.1 %collective-permute-start.8 = (bf16[192,512]{1,0:T(8,128)(2,1)S(1)}, bf16[192,512]{1,0:T(8,128)(2,1)S(1)}, u32[]{:S(2)}, u32[]{:S(2)}) collective-permute-start(bf16[192,512]{1,0:T(8,128)(2,1)S(1)} %collective-permute-done.3.refs_1_.refs_2_), channel_id=1, source_target_pairs={{0,2},{1,3},{2,4},{3,5},{4,6},{5,7},{6,0},{7,1},{8,10},{9,11},{10,... | collective-permute-start | bytes 589832 | tf_op jit(solution)/shard_map/ppermute | solution.py:336
  21.7 8.4 %collective-permute-start.9 = (bf16[192,512]{1,0:T(8,128)(2,1)S(1)}, bf16[192,512]{1,0:T(8,128)(2,1)S(1)}, u32[]{:S(2)}, u32[]{:S(2)}) collective-permute-start(bf16[192,512]{1,0:T(8,128)(2,1)S(1)} %collective-permute-done.7.refs_2_.refs_5_), channel_id=1, source_target_pairs={{0,6},{1,7},{2,0},{3,1},{4,2},{5,3},{6,4},{7,5},{8,14},{9,15},{10,... | collective-permute-start | bytes 589832 | tf_op jit(solution)/shard_map/ppermute | solution.py:336
  27.2 3.5 %collective-permute-start.10 = (bf16[960,256]{1,0:T(8,128)(2,1)S(1)}, bf16[960,256]{1,0:T(8,128)(2,1)S(1)}, u32[]{:S(2)}, u32[]{:S(2)}) collective-permute-start(bf16[960,256]{1,0:T(8,128)(2,1)S(1)} %join_slots.1.refs_8_.own_ref), channel_id=1, source_target_pairs={{0,8},{8,0},{16,24},{24,16},{32,40},{40,32},{48,56},{56,48},{64,72... | collective-permute-start | bytes 1474568 | tf_op jit(solution)/shard_map/ppermute | solution.py:336
  33.2 2.8 %collective-permute-start.11 = (bf16[384,256]{1,0:T(8,128)(2,1)S(1)}, bf16[384,256]{1,0:T(8,128)(2,1)S(1)}, u32[]{:S(2)}, u32[]{:S(2)}) collective-permute-start(bf16[384,256]{1,0:T(8,128)(2,1)S(1)} %get-tuple-element.45), channel_id=1, source_target_pairs={{0,8},{8,0},{16,24},{24,16},{32,40},{40,32},{48,56},{56,48},{64,72... | collective-permute-start | bytes 589832 | tf_op jit(solution)/shard_map/ppermute | solution.py:336
  34.1 3.5 %collective-permute-start.13 = (bf16[576,256]{1,0:T(8,128)(2,1)S(1)}, bf16[576,256]{1,0:T(8,128)(2,1)S(1)}, u32[]{:S(2)}, u32[]{:S(2)}) collective-permute-start(bf16[576,256]{1,0:T(8,128)(2,1)S(1)} %get-tuple-element.50), channel_id=1, source_target_pairs={{0,8},{8,0},{16,24},{24,16},{32,40},{40,32},{48,56},{56,48},{64,72... | collective-permute-start | bytes 884744 | tf_op jit(solution)/shard_map/ppermute | solution.py:336
  36.0 6.2 %collective-permute-start.12 = (bf16[192,256]{1,0:T(8,128)(2,1)S(1)}, bf16[192,256]{1,0:T(8,128)(2,1)S(1)}, u32[]{:S(2)}, u32[]{:S(2)}) collective-permute-start(bf16[192,256]{1,0:T(8,128)(2,1)S(1)} %get-tuple-element.48), channel_id=1, source_target_pairs={{0,16},{8,24},{16,224},{24,232},{32,48},{40,56},{48,0},{56,8},{64,... | collective-permute-start | bytes 294920 | tf_op jit(solution)/shard_map/ppermute | solution.py:336
  37.7 5.7 %collective-permute-start.14 = (bf16[192,256]{1,0:T(8,128)(2,1)S(1)}, bf16[192,256]{1,0:T(8,128)(2,1)S(1)}, u32[]{:S(2)}, u32[]{:S(2)}) collective-permute-start(bf16[192,256]{1,0:T(8,128)(2,1)S(1)} %get-tuple-element.51), channel_id=1, source_target_pairs={{0,224},{8,232},{16,240},{24,248},{32,0},{40,8},{48,16},{56,24},{6... | collective-permute-start | bytes 294920 | tf_op jit(solution)/shard_map/ppermute | solution.py:336
  38.7 6.1 %collective-permute-start.15 = (bf16[192,256]{1,0:T(8,128)(2,1)S(1)}, bf16[192,256]{1,0:T(8,128)(2,1)S(1)}, u32[]{:S(2)}, u32[]{:S(2)}) collective-permute-start(bf16[192,256]{1,0:T(8,128)(2,1)S(1)} %get-tuple-element.52), channel_id=1, source_target_pairs={{0,240},{8,248},{16,0},{24,8},{32,16},{40,24},{48,32},{56,40},{64,... | collective-permute-start | bytes 294920 | tf_op jit(solution)/shard_map/ppermute | solution.py:336
  42.2 8.0 %collective-permute-start.16 = (bf16[192,256]{1,0:T(8,128)(2,1)S(1)}, bf16[192,256]{1,0:T(8,128)(2,1)S(1)}, u32[]{:S(2)}, u32[]{:S(2)}) collective-permute-start(bf16[192,256]{1,0:T(8,128)(2,1)S(1)} %relay_far.1.refs_0_), channel_id=1, source_target_pairs={{0,192},{8,200},{16,208},{24,216},{32,224},{40,232},{48,240},{56,2... | collective-permute-start | bytes 294920 | tf_op jit(solution)/shard_map/ppermute | solution.py:336

commit v12 on v11

--- a/solution.py
+++ b/solution.py
@@ -292,26 +292,23 @@
             st_ref[:, h * D : (h + 1) * D] = dq[h * ROWS : (h + 1) * ROWS, :].astype(jnp.bfloat16)
 
 
-def is_upper(place_ref):
-    return (lax.rem(lax.div(place_ref[0], 2), 2) == 1).astype(jnp.float32)
-
-
 def settle_kernel(own_ref, back_ref, low_ref, high_ref):
     both = own_ref[...] + back_ref[: 2 * ROWS, :].astype(jnp.float32)
     low_ref[...] = both[:ROWS].astype(low_ref.dtype)
     high_ref[...] = both[ROWS:].astype(jnp.bfloat16)
 
 
-def relay_far(place_ref, keep_ref, side_ref, out_ref):
-    out_ref[...] = (keep_ref[...] + side_ref[...].astype(jnp.float32) * is_upper(place_ref)).astype(jnp.bfloat16)
-
-
-def finish_kernel(place_ref, own_ref, back_ref, side_ref, two_ref, four_ref, eight_ref, k_ref, v_ref):
-    def wide(x):
-        return x.astype(jnp.float32)
-
-    total = own_ref[...] + wide(back_ref[2 * ROWS :, :]) + wide(side_ref[...]) * (1 - is_upper(place_ref))
-    total = (total + wide(two_ref[...]) + wide(four_ref[...]) + wide(eight_ref[...])).astype(jnp.bfloat16)
+def relay_far(keep_ref, side_ref, out_ref):
+    out_ref[...] = (keep_ref[...] + side_ref[...].astype(jnp.float32)).astype(jnp.bfloat16)
+
+
+def gather_kernel(own_ref, back_ref, side_ref, two_ref, four_ref, out_ref):
+    total = own_ref[...] + back_ref[2 * ROWS :, :].astype(jnp.float32) + side_ref[...].astype(jnp.float32)
+    out_ref[...] = total + two_ref[...].astype(jnp.float32) + four_ref[...].astype(jnp.float32)
+
+
+def finish_kernel(sum_ref, eight_ref, k_ref, v_ref):
+    total = (sum_ref[...] + eight_ref[...].astype(jnp.float32)).astype(jnp.bfloat16)
     k_ref[...] = total[:, :D]
     v_ref[...] = total[:, D:]
 
@@ -448,7 +445,10 @@
         "settle_far", settle_kernel, (shape(ROWS, 2 * D, f32), shape(ROWS, 2 * D, bf16)), vmem(2), (far_own, far_back)
     )
     count = lax.axis_size("ctx")
-    far_side = moved(far_side, "ctx", lambda i: (i + 2 if i // 2 % 2 == 0 else i - 6) % count)
+    lower = [i for i in range(count) if i // 2 % 2 == 0]
+    upper = [i for i in range(count) if i // 2 % 2 == 1]
+    far_up = lax.ppermute(far_side, "ctx", [(i, i + 2) for i in lower])
+    far_down = lax.ppermute(far_side, "ctx", [(i, (i - 6) % count) for i in upper])
     near_own, st = call(
         "own_near",
         functools.partial(own_kernel, (2, 3)),
@@ -462,22 +462,25 @@
     )
     by_four = turned(by_four, "ctx", -4)
     by_two = turned(by_two, "ctx", -2)
-    to_eight = call("relay_far", relay_far, shape(ROWS, 2 * D, bf16), smem(1) + vmem(2), (place, far_keep, far_side))
+    to_eight = call("relay_far", relay_far, shape(ROWS, 2 * D, bf16), vmem(2), (far_keep, far_up))
     by_eight = turned(to_eight, "ctx", -8)
     last_own, grad_queries = call(
         "own_last",
         functools.partial(own_kernel, (4,)),
         (shape(ROWS, 2 * D, f32), shape(ROWS, HEADS * D, bf16)),
-        vmem(6) + token(3),
-        (q4, own, p_near, p_side, g4, st, to_eight, by_four, by_two),
-        flops=FL,
+        vmem(6) + token(1),
+        (q4, own, p_near, p_side, g4, st, to_eight),
+    )
+    partial_sum = call(
+        "gather_near",
+        gather_kernel,
+        shape(ROWS, 2 * D, f32),
+        vmem(5),
+        (last_own, near_back, far_down, by_two, by_four),
+        flops=COSTLY,
     )
     grad_keys, grad_values = call(
-        "finish",
-        finish_kernel,
-        (shape(ROWS, D, bf16), shape(ROWS, D, bf16)),
-        smem(1) + vmem(6),
-        (place, last_own, near_back, far_side, by_two, by_four, by_eight),
+        "finish", finish_kernel, (shape(ROWS, D, bf16), shape(ROWS, D, bf16)), vmem(2), (partial_sum, by_eight)
     )
     return grad_queries, grad_keys, grad_values
 

time: 51.4 us -> 56.4 us (1.097)
  starting transfers between devices: 22.3 us -> 29.8 us
  waiting for transfers between devices: 13.7 us -> 11.3 us
    ppermute x0 -> x2, starting transfers between devices: none -> 3.89 us  [the longest x1 2.59 us: local(): far_up = lax.ppermute(far_side, 'ctx', [(i, i + 2) for i in lower])]
    ppermute x17 -> x16, starting transfers between devices: 22.3 us -> 25.9 us  [moved(): lax.ppermute(x, axis, [(i, to(i)) for i in range(lax.axis_size(axis))])]
    ppermute x17 -> x16, waiting for transfers between devices: 13.7 us -> 11.3 us  [moved(): lax.ppermute(x, axis, [(i, to(i)) for i in range(lax.axis_size(axis))])]
    pallas_call x19 -> x20, Pallas kernels: 13.3 us -> 13.3 us  [call(): pl.pallas_call(kernel, out_shape=outs, in_specs=ins, out_specs=vmem(1)[0]...]
  transfers between devices with their start and end apart: 17 -> 18, of which waited for: 7 -> 5; matrix products, arithmetic and copies ran while one was open for 2% -> 1% of each run, Pallas kernels for 20% -> 18%
where the time goes in v12:
time: 56.4 us; the launch traced here: 56.2 us
  starting transfers between devices  29.8 us (53%)
  Pallas kernels  13.3 us (24%)
  waiting for transfers between devices  11.3 us (20%)
  between operations  0.85 us (2%)
  other arithmetic  0.83 us (1%)
    ppermute x16, starting transfers between devices, moved(): lax.ppermute(x, axis, [(i, to(i)) for i in range(lax.axis_size(axis))])  25.9 us
    pallas_call x20, Pallas kernels, call(): pl.pallas_call(kernel, out_shape=outs, in_specs=ins, out_specs=vmem(1)[0]...  13.3 us
    ppermute x16, waiting for transfers between devices, moved(): lax.ppermute(x, axis, [(i, to(i)) for i in range(lax.axis_size(axis))])  11.3 us
    ppermute x1, starting transfers between devices, local(): far_up = lax.ppermute(far_side, 'ctx', [(i, i + 2) for i in lower])  2.59 us
    ppermute x1, starting transfers between devices, local(): lax.ppermute(far_side, 'ctx', [(i, (i - 6) % count) for i in upper])  1.29 us
  transfers between devices with their start and end apart: 18, of which 5 were waited for; matrix products, arithmetic and copies ran while one was open for 1% of the time, Pallas kernels for 18%

profile of v12, /device:TPU:64, one launch (start us, length us, event | category | flops | bytes accessed | tf_op | source)
XLA Modules:
  0.0 56.2 jit_solution(4156545395693672552)
XLA Ops:
  0.6 3.3 %collective-permute-start.2 = (bf16[192,512]{1,0:T(8,128)(2,1)}, bf16[192,512]{1,0:T(8,128)(2,1)S(1)}, u32[]{:S(2)}, u32[]{:S(2)}) collective-permute-start(bf16[192,512]{1,0:T(8,128)(2,1)} %refs_0_.1), channel_id=1, source_target_pairs={{0,1},{1,0},{2,3},{3,2},{4,5},{5,4},{6,7},{7,6},{8,9},{9,8},{10,11... | collective-permute-start | bytes 589832 | tf_op jit(solution)/shard_map/ppermute | solution.py:333
  3.9 1.5 %collective-permute-start.3 = (bf16[192,512]{1,0:T(8,128)(2,1)}, bf16[192,512]{1,0:T(8,128)(2,1)S(1)}, u32[]{:S(2)}, u32[]{:S(2)}) collective-permute-start(bf16[192,512]{1,0:T(8,128)(2,1)} %refs_0_.1), channel_id=1, source_target_pairs={{0,2},{1,3},{2,4},{3,5},{4,6},{5,7},{6,0},{7,1},{8,10},{9,11},{10,... | collective-permute-start | bytes 589832 | tf_op jit(solution)/shard_map/ppermute | solution.py:333
  5.4 1.7 %collective-permute-start.4 = (bf16[192,512]{1,0:T(8,128)(2,1)}, bf16[192,512]{1,0:T(8,128)(2,1)S(1)}, u32[]{:S(2)}, u32[]{:S(2)}) collective-permute-start(bf16[192,512]{1,0:T(8,128)(2,1)} %refs_0_.1), channel_id=1, source_target_pairs={{0,6},{1,7},{2,0},{3,1},{4,2},{5,3},{6,4},{7,5},{8,14},{9,15},{10,... | collective-permute-start | bytes 589832 | tf_op jit(solution)/shard_map/ppermute | solution.py:333
  7.1 0.8 %pad_add_fusion.z0_ref = bf16[192,256]{1,0:T(8,128)(2,1)S(1)} fusion(bf16[192,128]{1,0:T(8,128)(2,1)} %param.8, bf16[192,128]{1,0:T(8,128)(2,1)} %param.7), kind=kLoop, calls=%fused_computation | loop fusion | flops 196608 | bytes 196608 | tf_op jit(solution)/shard_map/add | solution.py:370
  8.0 4.6 %collective-permute-start = (bf16[192,256]{1,0:T(8,128)(2,1)S(1)}, bf16[192,256]{1,0:T(8,128)(2,1)S(1)}, u32[]{:S(2)}, u32[]{:S(2)}) collective-permute-start(bf16[192,256]{1,0:T(8,128)(2,1)S(1)} %pad_add_fusion.z0_ref), channel_id=1, source_target_pairs={{0,64},{8,72},{16,80},{24,88},{32,96},{40,104},{48,112},{56,120},{... | collective-permute-start | bytes 294920 | tf_op jit(solution)/shard_map/ppermute | solution.py:333
  12.5 1.0 %collective-permute-start.1 = (bf16[192,256]{1,0:T(8,128)(2,1)S(1)}, bf16[192,256]{1,0:T(8,128)(2,1)S(1)}, u32[]{:S(2)}, u32[]{:S(2)}) collective-permute-start(bf16[192,256]{1,0:T(8,128)(2,1)S(1)} %pad_add_fusion.z0_ref), channel_id=1, source_target_pairs={{0,32},{8,40},{16,48},{24,56},{32,64},{40,72},{48,80},{56,88},{64,... | collective-permute-start | bytes 294920 | tf_op jit(solution)/shard_map/ppermute | solution.py:333
  13.6 2.3 %load.1 = (bf16[768,128]{1,0:T(8,128)(2,1)S(1)}, f32[8,768]{1,0:T(8,128)S(1)}, bf16[512,4096]{1,0:T(8,128)(2,1)S(1)}) custom-call(s32[1]{0:T(128)} %bitcast.place_ref, s32[1]{0:T(128)} %bitcast.1.head_ref, s32[8]{0:T(128)} %len_hbm.1, bf16[192,512]{1,0:T(8,128)(2,1)} %q_hbm.1, bf16[512,4096]{1,0:T(8,128)(2,1)} %w_hbm.1), custom_call_target="tpu_custom_call" | custom-call | flops 1 | bytes 1 | tf_op jit(solution)/shard_map/load/pallas_call | solution.py:347
  15.9 1.6 %collective-permute-start.7 = (bf16[192,512]{1,0:T(8,128)(2,1)S(1)}, bf16[192,512]{1,0:T(8,128)(2,1)S(1)}, u32[]{:S(2)}, u32[]{:S(2)}) collective-permute-start(bf16[192,512]{1,0:T(8,128)(2,1)S(1)} %stage.1.refs_0_.refs_1_), channel_id=1, source_target_pairs={{0,6},{1,7},{2,0},{3,1},{4,2},{5,3},{6,4},{7,5},{8,14},{9,15},{10,... | collective-permute-start | bytes 589832 | tf_op jit(solution)/shard_map/ppermute | solution.py:333
  17.6 0.5 collective-permute-start.6
  18.1 0.8 %collective-permute-start.5 = (bf16[384,256]{1,0:T(8,128)(2,1)S(1)}, bf16[384,256]{1,0:T(8,128)(2,1)S(1)}, u32[]{:S(2)}, u32[]{:S(2)}) collective-permute-start(bf16[384,256]{1,0:T(8,128)(2,1)S(1)} %pick_side.1.refs_0_), channel_id=1, source_target_pairs={{0,16},{8,24},{16,0},{24,8},{32,48},{40,56},{48,32},{56,40},{64,80... | collective-permute-start | bytes 589832 | tf_op jit(solution)/shard_map/ppermute | solution.py:333
  19.2 2.6 %collective-permute-done.7.refs_2_.refs_5_ = bf16[192,512]{1,0:T(8,128)(2,1)S(1)} collective-permute-done((bf16[192,512]{1,0:T(8,128)(2,1)S(1)}, bf16[192,512]{1,0:T(8,128)(2,1)S(1)}, u32[]{:S(2)}, u32[]{:S(2)}) %collective-permute-start.7) | collective-permute-done | bytes 196640 | tf_op jit(solution)/shard_map/ppermute | solution.py:333
  21.7 2.7 %collective-permute-start.9 = (bf16[192,512]{1,0:T(8,128)(2,1)S(1)}, bf16[192,512]{1,0:T(8,128)(2,1)S(1)}, u32[]{:S(2)}, u32[]{:S(2)}) collective-permute-start(bf16[192,512]{1,0:T(8,128)(2,1)S(1)} %collective-permute-done.7.refs_2_.refs_5_), channel_id=1, source_target_pairs={{0,6},{1,7},{2,0},{3,1},{4,2},{5,3},{6,4},{7,5},{8,14},{9,15},{10,... | collective-permute-start | bytes 589832 | tf_op jit(solution)/shard_map/ppermute | solution.py:333
  24.5 1.4 %collective-permute-done.6.refs_1_.refs_4_ = bf16[192,512]{1,0:T(8,128)(2,1)S(1)} collective-permute-done((bf16[192,512]{1,0:T(8,128)(2,1)S(1)}, bf16[192,512]{1,0:T(8,128)(2,1)S(1)}, u32[]{:S(2)}, u32[]{:S(2)}) %collective-permute-start.6) | collective-permute-done | bytes 196640 | tf_op jit(solution)/shard_map/ppermute | solution.py:333
  25.9 1.3 %near.1 = (bf16[576,768]{1,0:T(8,128)(2,1)S(1)}, f32[152,768]{1,0:T(8,128)S(1)}) custom-call(s32[1]{0:T(128)} %bitcast.place_ref, bf16[192,256]{1,0:T(8,128)(2,1)S(1)} %collective-permute-done.z2_ref, bf16[192,256]{1,0:T(8,128)(2,1)S(1)} %collective-permute-done.1.z1_ref, bf16[192,256]{1,0:T(8,128)(2,1)S(1)} %pad_add_fusion.z0_ref, ...), custom_call_target="tpu_custom_call" | custom-call | flops 1 | bytes 1 | tf_op jit(solution)/shard_map/near/pallas_call | solution.py:347
  27.5 0.5 collective-permute-done.8.refs_6_
  28.0 1.4 %project.1.after.acc_ref = f32[192,512]{1,0:T(8,128)S(1)} custom-call(bf16[192,512]{1,0:T(8,128)(2,1)S(1)} %copy-done, bf16[192,512]{1,0:T(8,128)(2,1)S(1)} %stage.1.refs_0_.refs_1_, bf16[192,512]{1,0:T(8,128)(2,1)S(1)} %collective-permute-done.3.refs_1_.refs_2_, bf16[192,512]{1,0:T(8,128)(2,1)S(1)} %collective-permute-done.4.refs_2_.refs_3_, ...), custom_call_target="tpu_custom_call" | custom-call | flops 1 | bytes 1 | tf_op jit(solution)/shard_map/project/pallas_call | solution.py:347
  29.3 0.9 %middle.1 = (bf16[384,768]{1,0:T(8,128)(2,1)S(1)}, f32[152,768]{1,0:T(8,128)S(1)}) custom-call(s32[1]{0:T(128)} %bitcast.place_ref, bf16[960,256]{1,0:T(8,128)(2,1)S(1)} %join_slots.1.refs_8_.own_ref, bf16[768,128]{1,0:T(8,128)(2,1)S(1)} %get-tuple-element.30.after.refs_3_.q4_ref, f32[152,768]{1,0:T(8,128)S(1)} %get-tuple-element.32.refs_0_.st_in_ref, ...), custom_call_target="tpu_custom_call" | custom-call | flops 1 | bytes 1 | tf_op jit(solution)/shard_map/middle/pallas_call | solution.py:347
  30.7 1.6 %across.1 = (bf16[768,768]{1,0:T(8,128)(2,1)S(1)}, f32[152,768]{1,0:T(8,128)S(1)}) custom-call(s32[1]{0:T(128)} %bitcast.place_ref, bf16[960,256]{1,0:T(8,128)(2,1)S(1)} %collective-permute-done.10.par_ref, bf16[768,128]{1,0:T(8,128)(2,1)S(1)} %get-tuple-element.30.after.refs_3_.q4_ref, f32[128,768]{1,0:T(8,128)S(1)} %get-tuple-element.38.gt_ref, ...), custom_call_target="tpu_custom_call" | custom-call | flops 1 | bytes 1 | tf_op jit(solution)/shard_map/across/pallas_call | solution.py:347
  32.3 0.9 %cross_far.1 = (bf16[384,256]{1,0:T(8,128)(2,1)S(1)}, f32[152,768]{1,0:T(8,128)S(1)}) custom-call(s32[1]{0:T(128)} %bitcast.place_ref, bf16[768,128]{1,0:T(8,128)(2,1)S(1)} %get-tuple-element.30.after.refs_3_.q4_ref, bf16[960,256]{1,0:T(8,128)(2,1)S(1)} %collective-permute-done.10.par_ref, bf16[768,768]{1,0:T(8,128)(2,1)S(1)} %get-tuple-element.39.p_ref, ...), custom_call_target="tpu_custom_call" | custom-call | flops 1 | bytes 1 | tf_op jit(solution)/shard_map/cross_far/pallas_call | solution.py:347
  33.3 0.8 %cross_near.1 = (bf16[576,256]{1,0:T(8,128)(2,1)S(1)}, f32[152,768]{1,0:T(8,128)S(1)}) custom-call(s32[1]{0:T(128)} %bitcast.place_ref, bf16[768,128]{1,0:T(8,128)(2,1)S(1)} %get-tuple-element.30.after.refs_3_.q4_ref, bf16[960,256]{1,0:T(8,128)(2,1)S(1)} %collective-permute-done.10.par_ref, bf16[768,768]{1,0:T(8,128)(2,1)S(1)} %get-tuple-element.39.p_ref, ...), custom_call_target="tpu_custom_call" | custom-call | flops 4000000000 | bytes 1 | tf_op jit(solution)/shard_map/cross_near/pallas_call | solution.py:347
  34.1 1.0 %collective-permute-start.13 = (bf16[576,256]{1,0:T(8,128)(2,1)S(1)}, bf16[576,256]{1,0:T(8,128)(2,1)S(1)}, u32[]{:S(2)}, u32[]{:S(2)}) collective-permute-start(bf16[576,256]{1,0:T(8,128)(2,1)S(1)} %get-tuple-element.51), channel_id=1, source_target_pairs={{0,8},{8,0},{16,24},{24,16},{32,40},{40,32},{48,56},{56,48},{64,72... | collective-permute-start | bytes 884744 | tf_op jit(solution)/shard_map/ppermute | solution.py:333
  35.2 0.8 %own_far.1 = (f32[384,256]{1,0:T(8,128)S(1)}, f32[152,768]{1,0:T(8,128)S(1)}) custom-call(bf16[768,128]{1,0:T(8,128)(2,1)S(1)} %get-tuple-element.30.after.refs_3_.q4_ref, bf16[960,256]{1,0:T(8,128)(2,1)S(1)} %join_slots.1.refs_8_.own_ref, bf16[576,768]{1,0:T(8,128)(2,1)S(1)} %get-tuple-element.33.near_ref, bf16[384,768]{1,0:T(8,128)(2,1)S(1)} %get-tuple-element.35.side_ref, ...), custom_call_target="tpu_custom_call" | custom-call | flops 4000000000 | bytes 1 | tf_op jit(solution)/shard_map/own_far/pallas_call | solution.py:347
  36.0 2.6 %collective-permute-start.12 = (bf16[192,256]{1,0:T(8,128)(2,1)S(1)}, bf16[192,256]{1,0:T(8,128)(2,1)S(1)}, u32[]{:S(2)}, u32[]{:S(2)}) collective-permute-start(bf16[192,256]{1,0:T(8,128)(2,1)S(1)} %get-tuple-element.48), channel_id=1, source_target_pairs={{0,16},{8,24},{32,48},{40,56},{64,80},{72,88},{96,112},{104,120},{... | collective-permute-start | bytes 294920 | tf_op jit(solution)/shard_map/ppermute | solution.py:450
  38.6 1.3 %collective-permute-start.14 = (bf16[192,256]{1,0:T(8,128)(2,1)S(1)}, bf16[192,256]{1,0:T(8,128)(2,1)S(1)}, u32[]{:S(2)}, u32[]{:S(2)}) collective-permute-start(bf16[192,256]{1,0:T(8,128)(2,1)S(1)} %get-tuple-element.48), channel_id=1, source_target_pairs={{16,224},{24,232},{48,0},{56,8},{80,32},{88,40},{112,64},{120,72},... | collective-permute-start | bytes 294920 | tf_op jit(solution)/shard_map/ppermute | solution.py:451
  39.9 0.8 %own_near.1 = (f32[384,256]{1,0:T(8,128)S(1)}, f32[152,768]{1,0:T(8,128)S(1)}) custom-call(bf16[768,128]{1,0:T(8,128)(2,1)S(1)} %get-tuple-element.30.after.refs_3_.q4_ref, bf16[960,256]{1,0:T(8,128)(2,1)S(1)} %join_slots.1.refs_8_.own_ref, bf16[576,768]{1,0:T(8,128)(2,1)S(1)} %get-tuple-element.33.near_ref, ...), custom_call_target="tpu_custom_call" | custom-call | flops 4000000000 | bytes 1 | tf_op jit(solution)/shard_map/own_near/pallas_call | solution.py:347
  40.8 2.5 %collective-permute-start.15 = (bf16[192,256]{1,0:T(8,128)(2,1)S(1)}, bf16[192,256]{1,0:T(8,128)(2,1)S(1)}, u32[]{:S(2)}, u32[]{:S(2)}) collective-permute-start(bf16[192,256]{1,0:T(8,128)(2,1)S(1)} %get-tuple-element.53), channel_id=1, source_target_pairs={{0,240},{8,248},{16,0},{24,8},{32,16},{40,24},{48,32},{56,40},{64,... | collective-permute-start | bytes 294920 | tf_op jit(solution)/shard_map/ppermute | solution.py:333
  43.3 1.3 %collective-permute-start.16 = (bf16[192,256]{1,0:T(8,128)(2,1)S(1)}, bf16[192,256]{1,0:T(8,128)(2,1)S(1)}, u32[]{:S(2)}, u32[]{:S(2)}) collective-permute-start(bf16[192,256]{1,0:T(8,128)(2,1)S(1)} %get-tuple-element.54), channel_id=1, source_target_pairs={{0,224},{8,232},{16,240},{24,248},{32,0},{40,8},{48,16},{56,24},{6... | collective-permute-start | bytes 294920 | tf_op jit(solution)/shard_map/ppermute | solution.py:333
  44.6 2.8 %collective-permute-start.17 = (bf16[192,256]{1,0:T(8,128)(2,1)S(1)}, bf16[192,256]{1,0:T(8,128)(2,1)S(1)}, u32[]{:S(2)}, u32[]{:S(2)}) collective-permute-start(bf16[192,256]{1,0:T(8,128)(2,1)S(1)} %relay_far.1.refs_0_), channel_id=1, source_target_pairs={{0,192},{8,200},{16,208},{24,216},{32,224},{40,232},{48,240},{56,2... | collective-permute-start | bytes 294920 | tf_op jit(solution)/shard_map/ppermute | solution.py:333
  47.4 1.2 %own_last.1 = (f32[192,256]{1,0:T(8,128)S(1)}, bf16[192,512]{1,0:T(8,128)(2,1)}) custom-call(bf16[768,128]{1,0:T(8,128)(2,1)S(1)} %get-tuple-element.30.after.refs_3_.q4_ref, bf16[960,256]{1,0:T(8,128)(2,1)S(1)} %join_slots.1.refs_8_.own_ref, bf16[576,768]{1,0:T(8,128)(2,1)S(1)} %get-tuple-element.33.near_ref, ...), custom_call_target="tpu_custom_call" | custom-call | flops 1 | bytes 1 | tf_op jit(solution)/shard_map/own_last/pallas_call | solution.py:347
  48.6 2.7 %collective-permute-done.16.four_ref = bf16[192,256]{1,0:T(8,128)(2,1)S(1)} collective-permute-done((bf16[192,256]{1,0:T(8,128)(2,1)S(1)}, bf16[192,256]{1,0:T(8,128)(2,1)S(1)}, u32[]{:S(2)}, u32[]{:S(2)}) %collective-permute-start.16) | collective-permute-done | bytes 98336 | tf_op jit(solution)/shard_map/ppermute | solution.py:333
  51.4 4.1 %collective-permute-done.17.eight_ref = bf16[192,256]{1,0:T(8,128)(2,1)S(1)} collective-permute-done((bf16[192,256]{1,0:T(8,128)(2,1)S(1)}, bf16[192,256]{1,0:T(8,128)(2,1)S(1)}, u32[]{:S(2)}, u32[]{:S(2)}) %collective-permute-start.17) | collective-permute-done | bytes 98336 | tf_op jit(solution)/shard_map/ppermute | solution.py:333
  55.5 0.6 %finish.1 = (bf16[192,128]{1,0:T(8,128)(2,1)}, bf16[192,128]{1,0:T(8,128)(2,1)}) custom-call(f32[192,256]{1,0:T(8,128)S(1)} %gather_near.1.sum_ref, bf16[192,256]{1,0:T(8,128)(2,1)S(1)} %collective-permute-done.17.eight_ref), custom_call_target="tpu_custom_call" | custom-call | flops 1 | bytes 1 | tf_op jit(solution)/shard_map/finish/pallas_call | solution.py:347
  (27 shorter events, 1.4 us)
Async XLA Ops:
  0.6 15.3 %collective-permute-start.2 = (bf16[192,512]{1,0:T(8,128)(2,1)}, bf16[192,512]{1,0:T(8,128)(2,1)S(1)}, u32[]{:S(2)}, u32[]{:S(2)}) collective-permute-start(bf16[192,512]{1,0:T(8,128)(2,1)} %refs_0_.1), channel_id=1, source_target_pairs={{0,1},{1,0},{2,3},{3,2},{4,5},{5,4},{6,7},{7,6},{8,9},{9,8},{10,11... | collective-permute-start | bytes 589832 | tf_op jit(solution)/shard_map/ppermute | solution.py:333
  3.9 13.7 %collective-permute-start.3 = (bf16[192,512]{1,0:T(8,128)(2,1)}, bf16[192,512]{1,0:T(8,128)(2,1)S(1)}, u32[]{:S(2)}, u32[]{:S(2)}) collective-permute-start(bf16[192,512]{1,0:T(8,128)(2,1)} %refs_0_.1), channel_id=1, source_target_pairs={{0,2},{1,3},{2,4},{3,5},{4,6},{5,7},{6,0},{7,1},{8,10},{9,11},{10,... | collective-permute-start | bytes 589832 | tf_op jit(solution)/shard_map/ppermute | solution.py:333
  5.4 12.7 %collective-permute-start.4 = (bf16[192,512]{1,0:T(8,128)(2,1)}, bf16[192,512]{1,0:T(8,128)(2,1)S(1)}, u32[]{:S(2)}, u32[]{:S(2)}) collective-permute-start(bf16[192,512]{1,0:T(8,128)(2,1)} %refs_0_.1), channel_id=1, source_target_pairs={{0,6},{1,7},{2,0},{3,1},{4,2},{5,3},{6,4},{7,5},{8,14},{9,15},{10,... | collective-permute-start | bytes 589832 | tf_op jit(solution)/shard_map/ppermute | solution.py:333
  8.0 10.1 %collective-permute-start = (bf16[192,256]{1,0:T(8,128)(2,1)S(1)}, bf16[192,256]{1,0:T(8,128)(2,1)S(1)}, u32[]{:S(2)}, u32[]{:S(2)}) collective-permute-start(bf16[192,256]{1,0:T(8,128)(2,1)S(1)} %pad_add_fusion.z0_ref), channel_id=1, source_target_pairs={{0,64},{8,72},{16,80},{24,88},{32,96},{40,104},{48,112},{56,120},{... | collective-permute-start | bytes 294920 | tf_op jit(solution)/shard_map/ppermute | solution.py:333
  12.5 5.5 %collective-permute-start.1 = (bf16[192,256]{1,0:T(8,128)(2,1)S(1)}, bf16[192,256]{1,0:T(8,128)(2,1)S(1)}, u32[]{:S(2)}, u32[]{:S(2)}) collective-permute-start(bf16[192,256]{1,0:T(8,128)(2,1)S(1)} %pad_add_fusion.z0_ref), channel_id=1, source_target_pairs={{0,32},{8,40},{16,48},{24,56},{32,64},{40,72},{48,80},{56,88},{64,... | collective-permute-start | bytes 294920 | tf_op jit(solution)/shard_map/ppermute | solution.py:333
  13.6 14.4 %copy-start = (bf16[192,512]{1,0:T(8,128)(2,1)S(1)}, bf16[192,512]{1,0:T(8,128)(2,1)}, u32[]{:S(2)}) copy-start(bf16[192,512]{1,0:T(8,128)(2,1)} %refs_0_.1) | copy-start | bytes 589828
  15.9 5.8 %collective-permute-start.7 = (bf16[192,512]{1,0:T(8,128)(2,1)S(1)}, bf16[192,512]{1,0:T(8,128)(2,1)S(1)}, u32[]{:S(2)}, u32[]{:S(2)}) collective-permute-start(bf16[192,512]{1,0:T(8,128)(2,1)S(1)} %stage.1.refs_0_.refs_1_), channel_id=1, source_target_pairs={{0,6},{1,7},{2,0},{3,1},{4,2},{5,3},{6,4},{7,5},{8,14},{9,15},{10,... | collective-permute-start | bytes 589832 | tf_op jit(solution)/shard_map/ppermute | solution.py:333
  17.6 8.3 %collective-permute-start.6 = (bf16[192,512]{1,0:T(8,128)(2,1)S(1)}, bf16[192,512]{1,0:T(8,128)(2,1)S(1)}, u32[]{:S(2)}, u32[]{:S(2)}) collective-permute-start(bf16[192,512]{1,0:T(8,128)(2,1)S(1)} %stage.1.refs_0_.refs_1_), channel_id=1, source_target_pairs={{0,2},{1,3},{2,4},{3,5},{4,6},{5,7},{6,0},{7,1},{8,10},{9,11},{10,... | collective-permute-start | bytes 589832 | tf_op jit(solution)/shard_map/ppermute | solution.py:333
  18.1 9.0 %collective-permute-start.5 = (bf16[384,256]{1,0:T(8,128)(2,1)S(1)}, bf16[384,256]{1,0:T(8,128)(2,1)S(1)}, u32[]{:S(2)}, u32[]{:S(2)}) collective-permute-start(bf16[384,256]{1,0:T(8,128)(2,1)S(1)} %pick_side.1.refs_0_), channel_id=1, source_target_pairs={{0,16},{8,24},{16,0},{24,8},{32,48},{40,56},{48,32},{56,40},{64,80... | collective-permute-start | bytes 589832 | tf_op jit(solution)/shard_map/ppermute | solution.py:333
  18.9 9.1 %collective-permute-start.8 = (bf16[192,512]{1,0:T(8,128)(2,1)S(1)}, bf16[192,512]{1,0:T(8,128)(2,1)S(1)}, u32[]{:S(2)}, u32[]{:S(2)}) collective-permute-start(bf16[192,512]{1,0:T(8,128)(2,1)S(1)} %collective-permute-done.3.refs_1_.refs_2_), channel_id=1, source_target_pairs={{0,2},{1,3},{2,4},{3,5},{4,6},{5,7},{6,0},{7,1},{8,10},{9,11},{10,... | collective-permute-start | bytes 589832 | tf_op jit(solution)/shard_map/ppermute | solution.py:333
  21.7 8.4 %collective-permute-start.9 = (bf16[192,512]{1,0:T(8,128)(2,1)S(1)}, bf16[192,512]{1,0:T(8,128)(2,1)S(1)}, u32[]{:S(2)}, u32[]{:S(2)}) collective-permute-start(bf16[192,512]{1,0:T(8,128)(2,1)S(1)} %collective-permute-done.7.refs_2_.refs_5_), channel_id=1, source_target_pairs={{0,6},{1,7},{2,0},{3,1},{4,2},{5,3},{6,4},{7,5},{8,14},{9,15},{10,... | collective-permute-start | bytes 589832 | tf_op jit(solution)/shard_map/ppermute | solution.py:333
  27.2 3.5 %collective-permute-start.10 = (bf16[960,256]{1,0:T(8,128)(2,1)S(1)}, bf16[960,256]{1,0:T(8,128)(2,1)S(1)}, u32[]{:S(2)}, u32[]{:S(2)}) collective-permute-start(bf16[960,256]{1,0:T(8,128)(2,1)S(1)} %join_slots.1.refs_8_.own_ref), channel_id=1, source_target_pairs={{0,8},{8,0},{16,24},{24,16},{32,40},{40,32},{48,56},{56,48},{64,72... | collective-permute-start | bytes 1474568 | tf_op jit(solution)/shard_map/ppermute | solution.py:333
  33.2 2.8 %collective-permute-start.11 = (bf16[384,256]{1,0:T(8,128)(2,1)S(1)}, bf16[384,256]{1,0:T(8,128)(2,1)S(1)}, u32[]{:S(2)}, u32[]{:S(2)}) collective-permute-start(bf16[384,256]{1,0:T(8,128)(2,1)S(1)} %get-tuple-element.45), channel_id=1, source_target_pairs={{0,8},{8,0},{16,24},{24,16},{32,40},{40,32},{48,56},{56,48},{64,72... | collective-permute-start | bytes 589832 | tf_op jit(solution)/shard_map/ppermute | solution.py:333
  34.1 6.6 %collective-permute-start.13 = (bf16[576,256]{1,0:T(8,128)(2,1)S(1)}, bf16[576,256]{1,0:T(8,128)(2,1)S(1)}, u32[]{:S(2)}, u32[]{:S(2)}) collective-permute-start(bf16[576,256]{1,0:T(8,128)(2,1)S(1)} %get-tuple-element.51), channel_id=1, source_target_pairs={{0,8},{8,0},{16,24},{24,16},{32,40},{40,32},{48,56},{56,48},{64,72... | collective-permute-start | bytes 884744 | tf_op jit(solution)/shard_map/ppermute | solution.py:333
  36.0 8.6 %collective-permute-start.12 = (bf16[192,256]{1,0:T(8,128)(2,1)S(1)}, bf16[192,256]{1,0:T(8,128)(2,1)S(1)}, u32[]{:S(2)}, u32[]{:S(2)}) collective-permute-start(bf16[192,256]{1,0:T(8,128)(2,1)S(1)} %get-tuple-element.48), channel_id=1, source_target_pairs={{0,16},{8,24},{32,48},{40,56},{64,80},{72,88},{96,112},{104,120},{... | collective-permute-start | bytes 294920 | tf_op jit(solution)/shard_map/ppermute | solution.py:450
  38.6 10.0 %collective-permute-start.14 = (bf16[192,256]{1,0:T(8,128)(2,1)S(1)}, bf16[192,256]{1,0:T(8,128)(2,1)S(1)}, u32[]{:S(2)}, u32[]{:S(2)}) collective-permute-start(bf16[192,256]{1,0:T(8,128)(2,1)S(1)} %get-tuple-element.48), channel_id=1, source_target_pairs={{16,224},{24,232},{48,0},{56,8},{80,32},{88,40},{112,64},{120,72},... | collective-permute-start | bytes 294920 | tf_op jit(solution)/shard_map/ppermute | solution.py:451
  40.8 7.9 %collective-permute-start.15 = (bf16[192,256]{1,0:T(8,128)(2,1)S(1)}, bf16[192,256]{1,0:T(8,128)(2,1)S(1)}, u32[]{:S(2)}, u32[]{:S(2)}) collective-permute-start(bf16[192,256]{1,0:T(8,128)(2,1)S(1)} %get-tuple-element.53), channel_id=1, source_target_pairs={{0,240},{8,248},{16,0},{24,8},{32,16},{40,24},{48,32},{56,40},{64,... | collective-permute-start | bytes 294920 | tf_op jit(solution)/shard_map/ppermute | solution.py:333
  43.3 8.0 %collective-permute-start.16 = (bf16[192,256]{1,0:T(8,128)(2,1)S(1)}, bf16[192,256]{1,0:T(8,128)(2,1)S(1)}, u32[]{:S(2)}, u32[]{:S(2)}) collective-permute-start(bf16[192,256]{1,0:T(8,128)(2,1)S(1)} %get-tuple-element.54), channel_id=1, source_target_pairs={{0,224},{8,232},{16,240},{24,248},{32,0},{40,8},{48,16},{56,24},{6... | collective-permute-start | bytes 294920 | tf_op jit(solution)/shard_map/ppermute | solution.py:333
  44.6 10.9 %collective-permute-start.17 = (bf16[192,256]{1,0:T(8,128)(2,1)S(1)}, bf16[192,256]{1,0:T(8,128)(2,1)S(1)}, u32[]{:S(2)}, u32[]{:S(2)}) collective-permute-start(bf16[192,256]{1,0:T(8,128)(2,1)S(1)} %relay_far.1.refs_0_), channel_id=1, source_target_pairs={{0,192},{8,200},{16,208},{24,216},{32,224},{40,232},{48,240},{56,2... | collective-permute-start | bytes 294920 | tf_op jit(solution)/shard_map/ppermute | solution.py:333

commit v13 on v11

--- a/solution.py
+++ b/solution.py
@@ -23,7 +23,6 @@
 SCALE = D**-0.5
 LOG2E = 1.4426950408889634
 MIB = 1 << 20
-FL = 4 * 10**9
 COSTLY = 4 * 10**9
 
 
@@ -213,60 +212,31 @@
     return dk, dv, dq
 
 
-def put(out_ref, slot, dk, dv):
-    at = pl.ds(pl.multiple_of(slot * ROWS, ROWS), ROWS)
-    out_ref[at, :D] = dk.astype(out_ref.dtype)
-    out_ref[at, D:] = dv.astype(out_ref.dtype)
-
-
-def cross_step(slot, core, par_ref, p_ref, st_ref, g4, q4_ref, rd):
-    share = st_ref[pl.ds(PEAK + SLOTS + slot - core, 1), :]
-    return back_block(par_ref[rows(slot), :], p_ref[rows(slot - core), :], share, g4, q4_ref[...], rd)
-
-
-def cross_far(place_ref, q4_ref, par_ref, p_ref, g_ref, st_in_ref, out_ref, st_ref):
+def cross_kernel(place_ref, q4_ref, par_ref, p_ref, g_ref, st_in_ref, out_ref, st_ref):
     core = lax.rem(place_ref[0], 2)
     g4 = g_ref[...]
     rd = st_in_ref[DOT : DOT + 1, :]
     st_ref[DOT : DOT + 1, :] = rd
     st_ref[PEAK:, :] = st_in_ref[PEAK:, :]
-    dk, dv, dq = cross_step(1, core, par_ref, p_ref, st_ref, g4, q4_ref, rd)
-    put(out_ref, 1, dk, dv)
-    st_ref[:D, :] = dq
-
-    @pl.when(core == 1)
-    def _():
-        out_ref[:ROWS, :] = jnp.zeros((ROWS, 2 * D), out_ref.dtype)
-
-    @pl.when(core == 0)
-    def _():
-        dk, dv, dq = cross_step(0, core, par_ref, p_ref, st_ref, g4, q4_ref, rd)
-        put(out_ref, 0, dk, dv)
-        st_ref[:D, :] += dq
-
-
-def cross_near(place_ref, q4_ref, par_ref, p_ref, g_ref, st_in_ref, out_ref, st_ref):
-    core = lax.rem(place_ref[0], 2)
-    g4 = g_ref[...]
-    rd = st_in_ref[DOT : DOT + 1, :]
-    st_ref[DOT : DOT + 1, :] = rd
-    st_ref[PEAK:, :] = st_in_ref[PEAK:, :]
-    total = st_in_ref[:D, :]
-    for slot in (2, 3):
-        dk, dv, dq = cross_step(slot, core, par_ref, p_ref, st_ref, g4, q4_ref, rd)
-        put(out_ref, slot - 2, dk, dv)
-        total = total + dq
+    total = None
+    for i in range(REACH):
+        share = st_in_ref[PEAK + SLOTS + i : PEAK + SLOTS + i + 1, :]
+        prob = p_ref[i * ROWS : (i + 1) * ROWS, :]
+        dk, dv, dq = back_block(par_ref[rows(i + core), :], prob, share, g4, q4_ref[...], rd)
+        out_ref[i * ROWS : (i + 1) * ROWS, :D] = dk.astype(out_ref.dtype)
+        out_ref[i * ROWS : (i + 1) * ROWS, D:] = dv.astype(out_ref.dtype)
+        total = dq if total is None else total + dq
     st_ref[:D, :] = total
 
-    @pl.when(core == 0)
-    def _():
-        out_ref[2 * ROWS :, :] = jnp.zeros((ROWS, 2 * D), out_ref.dtype)
-
-    @pl.when(core == 1)
-    def _():
-        dk, dv, dq = cross_step(4, core, par_ref, p_ref, st_ref, g4, q4_ref, rd)
-        put(out_ref, 2, dk, dv)
-        st_ref[:D, :] += dq
+
+def returned(back_ref, place_ref, slot):
+    odd = lax.rem(place_ref[0], 2).astype(jnp.float32)
+    value = None
+    for i, share in ((slot, odd), (slot - 1, 1 - odd)):
+        if 0 <= i < REACH:
+            part = back_ref[i * ROWS : (i + 1) * ROWS, :].astype(jnp.float32) * share
+            value = part if value is None else value + part
+    return value
 
 
 def own_kernel(slots, q4_ref, own_ref, near_ref, side_ref, g_ref, st_in_ref, *refs):
@@ -292,26 +262,30 @@
             st_ref[:, h * D : (h + 1) * D] = dq[h * ROWS : (h + 1) * ROWS, :].astype(jnp.bfloat16)
 
 
-def is_upper(place_ref):
-    return (lax.rem(lax.div(place_ref[0], 2), 2) == 1).astype(jnp.float32)
-
-
-def settle_kernel(own_ref, back_ref, low_ref, high_ref):
-    both = own_ref[...] + back_ref[: 2 * ROWS, :].astype(jnp.float32)
-    low_ref[...] = both[:ROWS].astype(low_ref.dtype)
-    high_ref[...] = both[ROWS:].astype(jnp.bfloat16)
-
-
-def relay_far(place_ref, keep_ref, side_ref, out_ref):
-    out_ref[...] = (keep_ref[...] + side_ref[...].astype(jnp.float32) * is_upper(place_ref)).astype(jnp.bfloat16)
-
-
-def finish_kernel(place_ref, own_ref, back_ref, side_ref, two_ref, four_ref, eight_ref, k_ref, v_ref):
+def settle_kernel(place_ref, own_ref, back_ref, keep_ref, side_ref):
+    for slot in range(REACH):
+        both = own_ref[slot * ROWS : (slot + 1) * ROWS, :] + returned(back_ref, place_ref, slot)
+        target = pl.ds(slot // 2 * ROWS, ROWS)
+        if slot % 2:
+            side_ref[target, :] = both.astype(jnp.bfloat16)
+        else:
+            keep_ref[target, :] = both
+
+
+def relay_kernel(place_ref, keep_ref, side_ref, after, two_ref, one_ref):
+    upper = (lax.rem(lax.div(place_ref[0], 2), 2) == 1).astype(jnp.float32)
+    first, second = side_ref[:ROWS, :].astype(jnp.float32), side_ref[ROWS:, :].astype(jnp.float32)
+    two_ref[...] = (keep_ref[:ROWS, :] + first * upper).astype(jnp.bfloat16)
+    one_ref[...] = (keep_ref[ROWS:, :] + second * upper + first * (1 - upper)).astype(jnp.bfloat16)
+
+
+def finish_kernel(place_ref, own_ref, back_ref, side_ref, two_ref, one_ref, k_ref, v_ref):
     def wide(x):
         return x.astype(jnp.float32)
 
-    total = own_ref[...] + wide(back_ref[2 * ROWS :, :]) + wide(side_ref[...]) * (1 - is_upper(place_ref))
-    total = (total + wide(two_ref[...]) + wide(four_ref[...]) + wide(eight_ref[...])).astype(jnp.bfloat16)
+    upper = (lax.rem(lax.div(place_ref[0], 2), 2) == 1).astype(jnp.float32)
+    total = own_ref[...] + returned(back_ref, place_ref, REACH) + wide(side_ref[ROWS:, :]) * (1 - upper)
+    total = (total + wide(one_ref[...]) + wide(two_ref[...])).astype(jnp.bfloat16)
     k_ref[...] = total[:, :D]
     v_ref[...] = total[:, D:]
 
@@ -428,56 +402,43 @@
         "across", across_kernel, (shape(REACH * ROWS, LANES, bf16), state), smem(1) + vmem(4), (place, par, q4, gt, st)
     )
 
-    far_cross, st = call(
-        "cross_far", cross_far, (shape(2 * ROWS, 2 * D, bf16), state), smem(1) + vmem(5), (place, q4, par, p_par, g4, st)
-    )
-    far_back = moved(far_cross, "ctx", lambda i: i ^ 1)
-    near_cross, st = call(
-        "cross_near", cross_near, (shape(3 * ROWS, 2 * D, bf16), state), smem(1) + vmem(5), (place, q4, par, p_par, g4, st), flops=FL
-    )
-    near_back = moved(near_cross, "ctx", lambda i: i ^ 1)
-    far_own, st = call(
-        "own_far",
-        functools.partial(own_kernel, (0, 1)),
-        (shape(2 * ROWS, 2 * D, f32), state),
+    cross, st = call(
+        "cross", cross_kernel, (shape(REACH * ROWS, 2 * D, bf16), state), smem(1) + vmem(5), (place, q4, par, p_par, g4, st)
+    )
+    back = moved(cross, "ctx", lambda i: i ^ 1)
+    mine, st = call(
+        "own_earlier",
+        functools.partial(own_kernel, (0, 1, 2, 3)),
+        (shape(REACH * ROWS, 2 * D, f32), state),
         vmem(6),
         (q4, own, p_near, p_side, g4, st),
-        flops=FL,
-    )
-    far_keep, far_side = call(
-        "settle_far", settle_kernel, (shape(ROWS, 2 * D, f32), shape(ROWS, 2 * D, bf16)), vmem(2), (far_own, far_back)
-    )
-    count = lax.axis_size("ctx")
-    far_side = moved(far_side, "ctx", lambda i: (i + 2 if i // 2 % 2 == 0 else i - 6) % count)
-    near_own, st = call(
-        "own_near",
-        functools.partial(own_kernel, (2, 3)),
-        (shape(2 * ROWS, 2 * D, f32), state),
-        vmem(6) + token(1),
-        (q4, own, p_near, p_side, g4, st, far_keep),
-        flops=FL,
-    )
-    by_four, by_two = call(
-        "settle_near", settle_kernel, (shape(ROWS, 2 * D, bf16), shape(ROWS, 2 * D, bf16)), vmem(2), (near_own, near_back)
-    )
-    by_four = turned(by_four, "ctx", -4)
-    by_two = turned(by_two, "ctx", -2)
-    to_eight = call("relay_far", relay_far, shape(ROWS, 2 * D, bf16), smem(1) + vmem(2), (place, far_keep, far_side))
-    by_eight = turned(to_eight, "ctx", -8)
-    last_own, grad_queries = call(
+    )
+    keep, side_out = call(
+        "settle", settle_kernel, (shape(2 * ROWS, 2 * D, f32), shape(2 * ROWS, 2 * D, bf16)), smem(1) + vmem(2), (place, mine, back)
+    )
+    crossed = moved(side_out, "ctx", lambda i: i ^ 2)
+    last, grad_queries = call(
         "own_last",
         functools.partial(own_kernel, (4,)),
         (shape(ROWS, 2 * D, f32), shape(ROWS, HEADS * D, bf16)),
-        vmem(6) + token(3),
-        (q4, own, p_near, p_side, g4, st, to_eight, by_four, by_two),
-        flops=FL,
-    )
+        vmem(6) + token(1),
+        (q4, own, p_near, p_side, g4, st, keep),
+    )
+    to_two, to_one = call(
+        "relay",
+        relay_kernel,
+        (shape(ROWS, 2 * D, bf16), shape(ROWS, 2 * D, bf16)),
+        smem(1) + vmem(2) + token(1),
+        (place, keep, crossed, last),
+    )
+    got_two = turned(to_two, "ctx", -2 * PLANE)
+    got_one = turned(to_one, "ctx", -PLANE)
     grad_keys, grad_values = call(
         "finish",
         finish_kernel,
         (shape(ROWS, D, bf16), shape(ROWS, D, bf16)),
-        smem(1) + vmem(6),
-        (place, last_own, near_back, far_side, by_two, by_four, by_eight),
+        smem(1) + vmem(5),
+        (place, last, back, crossed, got_two, got_one),
     )
     return grad_queries, grad_keys, grad_values
 

time: 51.4 us -> 53.4 us (1.039)
  waiting for transfers between devices: 13.7 us -> 17.9 us
  starting transfers between devices: 22.3 us -> 20.4 us
  Pallas kernels: 13.3 us -> 12.7 us
    ppermute x17 -> x15, waiting for transfers between devices: 13.7 us -> 17.9 us  [moved(): lax.ppermute(x, axis, [(i, to(i)) for i in range(lax.axis_size(axis))])]
    ppermute x17 -> x15, starting transfers between devices: 22.3 us -> 20.4 us  [moved(): lax.ppermute(x, axis, [(i, to(i)) for i in range(lax.axis_size(axis))])]
    pallas_call x19 -> x16, Pallas kernels: 13.3 us -> 12.7 us  [call(): pl.pallas_call(kernel, out_shape=outs, in_specs=ins, out_specs=vmem(1)[0]...]
  transfers between devices with their start and end apart: 17 -> 15, of which waited for: 7 -> 6; matrix products, arithmetic and copies ran while one was open for 2% -> 2% of each run, Pallas kernels for 20% -> 17%
where the time goes in v13:
time: 53.4 us; the launch traced here: 52.6 us
  starting transfers between devices  20.4 us (38%)
  waiting for transfers between devices  17.9 us (34%)
  Pallas kernels  12.7 us (24%)
  other arithmetic  0.83 us (2%)
  between operations  0.78 us (1%)
    ppermute x15, starting transfers between devices, moved(): lax.ppermute(x, axis, [(i, to(i)) for i in range(lax.axis_size(axis))])  20.4 us
    ppermute x15, waiting for transfers between devices, moved(): lax.ppermute(x, axis, [(i, to(i)) for i in range(lax.axis_size(axis))])  17.9 us
    pallas_call x16, Pallas kernels, call(): pl.pallas_call(kernel, out_shape=outs, in_specs=ins, out_specs=vmem(1)[0]...  12.7 us
  transfers between devices with their start and end apart: 15, of which 6 were waited for; matrix products, arithmetic and copies ran while one was open for 2% of the time, Pallas kernels for 17%

profile of v13, /device:TPU:64, one launch (start us, length us, event | category | flops | bytes accessed | tf_op | source)
XLA Modules:
  0.0 52.6 jit_solution(5910656650517383271)
XLA Ops:
  0.6 3.3 %collective-permute-start.2 = (bf16[192,512]{1,0:T(8,128)(2,1)}, bf16[192,512]{1,0:T(8,128)(2,1)S(1)}, u32[]{:S(2)}, u32[]{:S(2)}) collective-permute-start(bf16[192,512]{1,0:T(8,128)(2,1)} %refs_0_.1), channel_id=1, source_target_pairs={{0,1},{1,0},{2,3},{3,2},{4,5},{5,4},{6,7},{7,6},{8,9},{9,8},{10,11... | collective-permute-start | bytes 589832 | tf_op jit(solution)/shard_map/ppermute | solution.py:310
  3.9 1.5 %collective-permute-start.3 = (bf16[192,512]{1,0:T(8,128)(2,1)}, bf16[192,512]{1,0:T(8,128)(2,1)S(1)}, u32[]{:S(2)}, u32[]{:S(2)}) collective-permute-start(bf16[192,512]{1,0:T(8,128)(2,1)} %refs_0_.1), channel_id=1, source_target_pairs={{0,2},{1,3},{2,4},{3,5},{4,6},{5,7},{6,0},{7,1},{8,10},{9,11},{10,... | collective-permute-start | bytes 589832 | tf_op jit(solution)/shard_map/ppermute | solution.py:310
  5.4 1.7 %collective-permute-start.4 = (bf16[192,512]{1,0:T(8,128)(2,1)}, bf16[192,512]{1,0:T(8,128)(2,1)S(1)}, u32[]{:S(2)}, u32[]{:S(2)}) collective-permute-start(bf16[192,512]{1,0:T(8,128)(2,1)} %refs_0_.1), channel_id=1, source_target_pairs={{0,6},{1,7},{2,0},{3,1},{4,2},{5,3},{6,4},{7,5},{8,14},{9,15},{10,... | collective-permute-start | bytes 589832 | tf_op jit(solution)/shard_map/ppermute | solution.py:310
  7.1 0.8 %pad_add_fusion.z0_ref = bf16[192,256]{1,0:T(8,128)(2,1)S(1)} fusion(bf16[192,128]{1,0:T(8,128)(2,1)} %param.8, bf16[192,128]{1,0:T(8,128)(2,1)} %param.7), kind=kLoop, calls=%fused_computation | loop fusion | flops 196608 | bytes 196608 | tf_op jit(solution)/shard_map/add | solution.py:347
  8.0 4.6 %collective-permute-start = (bf16[192,256]{1,0:T(8,128)(2,1)S(1)}, bf16[192,256]{1,0:T(8,128)(2,1)S(1)}, u32[]{:S(2)}, u32[]{:S(2)}) collective-permute-start(bf16[192,256]{1,0:T(8,128)(2,1)S(1)} %pad_add_fusion.z0_ref), channel_id=1, source_target_pairs={{0,64},{8,72},{16,80},{24,88},{32,96},{40,104},{48,112},{56,120},{... | collective-permute-start | bytes 294920 | tf_op jit(solution)/shard_map/ppermute | solution.py:310
  12.5 1.0 %collective-permute-start.1 = (bf16[192,256]{1,0:T(8,128)(2,1)S(1)}, bf16[192,256]{1,0:T(8,128)(2,1)S(1)}, u32[]{:S(2)}, u32[]{:S(2)}) collective-permute-start(bf16[192,256]{1,0:T(8,128)(2,1)S(1)} %pad_add_fusion.z0_ref), channel_id=1, source_target_pairs={{0,32},{8,40},{16,48},{24,56},{32,64},{40,72},{48,80},{56,88},{64,... | collective-permute-start | bytes 294920 | tf_op jit(solution)/shard_map/ppermute | solution.py:310
  13.6 2.3 %load.1 = (bf16[768,128]{1,0:T(8,128)(2,1)S(1)}, f32[8,768]{1,0:T(8,128)S(1)}, bf16[512,4096]{1,0:T(8,128)(2,1)S(1)}) custom-call(s32[1]{0:T(128)} %bitcast.place_ref, s32[1]{0:T(128)} %bitcast.1.head_ref, s32[8]{0:T(128)} %len_hbm.1, bf16[192,512]{1,0:T(8,128)(2,1)} %q_hbm.1, bf16[512,4096]{1,0:T(8,128)(2,1)} %w_hbm.1), custom_call_target="tpu_custom_call" | custom-call | flops 1 | bytes 1 | tf_op jit(solution)/shard_map/load/pallas_call | solution.py:324
  15.9 1.6 %collective-permute-start.7 = (bf16[192,512]{1,0:T(8,128)(2,1)S(1)}, bf16[192,512]{1,0:T(8,128)(2,1)S(1)}, u32[]{:S(2)}, u32[]{:S(2)}) collective-permute-start(bf16[192,512]{1,0:T(8,128)(2,1)S(1)} %stage.1.refs_0_.refs_1_), channel_id=1, source_target_pairs={{0,6},{1,7},{2,0},{3,1},{4,2},{5,3},{6,4},{7,5},{8,14},{9,15},{10,... | collective-permute-start | bytes 589832 | tf_op jit(solution)/shard_map/ppermute | solution.py:310
  17.6 0.5 collective-permute-start.6
  18.1 0.8 %collective-permute-start.5 = (bf16[384,256]{1,0:T(8,128)(2,1)S(1)}, bf16[384,256]{1,0:T(8,128)(2,1)S(1)}, u32[]{:S(2)}, u32[]{:S(2)}) collective-permute-start(bf16[384,256]{1,0:T(8,128)(2,1)S(1)} %pick_side.1.refs_0_), channel_id=1, source_target_pairs={{0,16},{8,24},{16,0},{24,8},{32,48},{40,56},{48,32},{56,40},{64,80... | collective-permute-start | bytes 589832 | tf_op jit(solution)/shard_map/ppermute | solution.py:310
  18.9 0.3 collective-permute-start.8
  19.2 2.6 %collective-permute-done.7.refs_2_.refs_5_ = bf16[192,512]{1,0:T(8,128)(2,1)S(1)} collective-permute-done((bf16[192,512]{1,0:T(8,128)(2,1)S(1)}, bf16[192,512]{1,0:T(8,128)(2,1)S(1)}, u32[]{:S(2)}, u32[]{:S(2)}) %collective-permute-start.7) | collective-permute-done | bytes 196640 | tf_op jit(solution)/shard_map/ppermute | solution.py:310
  21.7 2.7 %collective-permute-start.9 = (bf16[192,512]{1,0:T(8,128)(2,1)S(1)}, bf16[192,512]{1,0:T(8,128)(2,1)S(1)}, u32[]{:S(2)}, u32[]{:S(2)}) collective-permute-start(bf16[192,512]{1,0:T(8,128)(2,1)S(1)} %collective-permute-done.7.refs_2_.refs_5_), channel_id=1, source_target_pairs={{0,6},{1,7},{2,0},{3,1},{4,2},{5,3},{6,4},{7,5},{8,14},{9,15},{10,... | collective-permute-start | bytes 589832 | tf_op jit(solution)/shard_map/ppermute | solution.py:310
  24.5 1.4 %collective-permute-done.6.refs_1_.refs_4_ = bf16[192,512]{1,0:T(8,128)(2,1)S(1)} collective-permute-done((bf16[192,512]{1,0:T(8,128)(2,1)S(1)}, bf16[192,512]{1,0:T(8,128)(2,1)S(1)}, u32[]{:S(2)}, u32[]{:S(2)}) %collective-permute-start.6) | collective-permute-done | bytes 196640 | tf_op jit(solution)/shard_map/ppermute | solution.py:310
  25.9 1.3 %near.1 = (bf16[576,768]{1,0:T(8,128)(2,1)S(1)}, f32[152,768]{1,0:T(8,128)S(1)}) custom-call(s32[1]{0:T(128)} %bitcast.place_ref, bf16[192,256]{1,0:T(8,128)(2,1)S(1)} %collective-permute-done.z2_ref, bf16[192,256]{1,0:T(8,128)(2,1)S(1)} %collective-permute-done.1.z1_ref, bf16[192,256]{1,0:T(8,128)(2,1)S(1)} %pad_add_fusion.z0_ref, ...), custom_call_target="tpu_custom_call" | custom-call | flops 1 | bytes 1 | tf_op jit(solution)/shard_map/near/pallas_call | solution.py:324
  27.2 0.3 collective-permute-start.10
  27.5 0.5 collective-permute-done.8.refs_6_
  28.0 1.4 %project.1.after.acc_ref = f32[192,512]{1,0:T(8,128)S(1)} custom-call(bf16[192,512]{1,0:T(8,128)(2,1)S(1)} %copy-done, bf16[192,512]{1,0:T(8,128)(2,1)S(1)} %stage.1.refs_0_.refs_1_, bf16[192,512]{1,0:T(8,128)(2,1)S(1)} %collective-permute-done.3.refs_1_.refs_2_, bf16[192,512]{1,0:T(8,128)(2,1)S(1)} %collective-permute-done.4.refs_2_.refs_3_, ...), custom_call_target="tpu_custom_call" | custom-call | flops 1 | bytes 1 | tf_op jit(solution)/shard_map/project/pallas_call | solution.py:324
  29.3 0.9 %middle.1 = (bf16[384,768]{1,0:T(8,128)(2,1)S(1)}, f32[152,768]{1,0:T(8,128)S(1)}) custom-call(s32[1]{0:T(128)} %bitcast.place_ref, bf16[960,256]{1,0:T(8,128)(2,1)S(1)} %join_slots.1.refs_8_.own_ref, bf16[768,128]{1,0:T(8,128)(2,1)S(1)} %get-tuple-element.26.after.refs_3_.q4_ref, f32[152,768]{1,0:T(8,128)S(1)} %get-tuple-element.28.refs_0_.st_in_ref, ...), custom_call_target="tpu_custom_call" | custom-call | flops 1 | bytes 1 | tf_op jit(solution)/shard_map/middle/pallas_call | solution.py:324
  30.2 0.5 last_projection.1
  30.7 1.6 %across.1 = (bf16[768,768]{1,0:T(8,128)(2,1)S(1)}, f32[152,768]{1,0:T(8,128)S(1)}) custom-call(s32[1]{0:T(128)} %bitcast.place_ref, bf16[960,256]{1,0:T(8,128)(2,1)S(1)} %collective-permute-done.10.par_ref, bf16[768,128]{1,0:T(8,128)(2,1)S(1)} %get-tuple-element.26.after.refs_3_.q4_ref, f32[128,768]{1,0:T(8,128)S(1)} %get-tuple-element.34.gt_ref, ...), custom_call_target="tpu_custom_call" | custom-call | flops 1 | bytes 1 | tf_op jit(solution)/shard_map/across/pallas_call | solution.py:324
  32.3 1.3 %cross.1 = (bf16[768,256]{1,0:T(8,128)(2,1)S(1)}, f32[152,768]{1,0:T(8,128)S(1)}) custom-call(s32[1]{0:T(128)} %bitcast.place_ref, bf16[768,128]{1,0:T(8,128)(2,1)S(1)} %get-tuple-element.26.after.refs_3_.q4_ref, bf16[960,256]{1,0:T(8,128)(2,1)S(1)} %collective-permute-done.10.par_ref, bf16[768,768]{1,0:T(8,128)(2,1)S(1)} %get-tuple-element.35.p_ref, ...), custom_call_target="tpu_custom_call" | custom-call | flops 1 | bytes 1 | tf_op jit(solution)/shard_map/cross/pallas_call | solution.py:324
  33.7 1.3 %own_earlier.1 = (f32[768,256]{1,0:T(8,128)S(1)}, f32[152,768]{1,0:T(8,128)S(1)}) custom-call(bf16[768,128]{1,0:T(8,128)(2,1)S(1)} %get-tuple-element.26.after.refs_3_.q4_ref, bf16[960,256]{1,0:T(8,128)(2,1)S(1)} %join_slots.1.refs_8_.own_ref, bf16[576,768]{1,0:T(8,128)(2,1)S(1)} %get-tuple-element.29.near_ref, ...), custom_call_target="tpu_custom_call" | custom-call | flops 1 | bytes 1 | tf_op jit(solution)/shard_map/own_earlier/pallas_call | solution.py:324
  35.0 0.4 collective-permute-done.11.back_ref
  35.4 0.1 settle.1
  35.6 0.8 %collective-permute-start.12 = (bf16[384,256]{1,0:T(8,128)(2,1)S(1)}, bf16[384,256]{1,0:T(8,128)(2,1)S(1)}, u32[]{:S(2)}, u32[]{:S(2)}) collective-permute-start(bf16[384,256]{1,0:T(8,128)(2,1)S(1)} %get-tuple-element.44), channel_id=1, source_target_pairs={{0,16},{8,24},{16,0},{24,8},{32,48},{40,56},{48,32},{56,40},{64,80... | collective-permute-start | bytes 589832 | tf_op jit(solution)/shard_map/ppermute | solution.py:310
  36.3 1.2 %own_last.1 = (f32[192,256]{1,0:T(8,128)S(1)}, bf16[192,512]{1,0:T(8,128)(2,1)}) custom-call(bf16[768,128]{1,0:T(8,128)(2,1)S(1)} %get-tuple-element.26.after.refs_3_.q4_ref, bf16[960,256]{1,0:T(8,128)(2,1)S(1)} %join_slots.1.refs_8_.own_ref, bf16[576,768]{1,0:T(8,128)(2,1)S(1)} %get-tuple-element.29.near_ref, ...), custom_call_target="tpu_custom_call" | custom-call | flops 1 | bytes 1 | tf_op jit(solution)/shard_map/own_last/pallas_call | solution.py:324
  37.5 5.0 %collective-permute-done.12.side_ref = bf16[384,256]{1,0:T(8,128)(2,1)S(1)} collective-permute-done((bf16[384,256]{1,0:T(8,128)(2,1)S(1)}, bf16[384,256]{1,0:T(8,128)(2,1)S(1)}, u32[]{:S(2)}, u32[]{:S(2)}) %collective-permute-start.12) | collective-permute-done | bytes 196640 | tf_op jit(solution)/shard_map/ppermute | solution.py:310
  42.7 0.1 collective-permute-start.13
  42.8 1.2 %collective-permute-start.14 = (bf16[192,256]{1,0:T(8,128)(2,1)S(1)}, bf16[192,256]{1,0:T(8,128)(2,1)S(1)}, u32[]{:S(2)}, u32[]{:S(2)}) collective-permute-start(bf16[192,256]{1,0:T(8,128)(2,1)S(1)} %get-tuple-element.46), channel_id=1, source_target_pairs={{0,224},{8,232},{16,240},{24,248},{32,0},{40,8},{48,16},{56,24},{6... | collective-permute-start | bytes 294920 | tf_op jit(solution)/shard_map/ppermute | solution.py:310
  44.0 8.0 %collective-permute-done.13.two_ref = bf16[192,256]{1,0:T(8,128)(2,1)S(1)} collective-permute-done((bf16[192,256]{1,0:T(8,128)(2,1)S(1)}, bf16[192,256]{1,0:T(8,128)(2,1)S(1)}, u32[]{:S(2)}, u32[]{:S(2)}) %collective-permute-start.13) | collective-permute-done | bytes 98336 | tf_op jit(solution)/shard_map/ppermute | solution.py:310
  51.9 0.7 %finish.1 = (bf16[192,128]{1,0:T(8,128)(2,1)}, bf16[192,128]{1,0:T(8,128)(2,1)}) custom-call(s32[1]{0:T(128)} %bitcast.place_ref, f32[192,256]{1,0:T(8,128)S(1)} %get-tuple-element.43.after.own_ref, bf16[768,256]{1,0:T(8,128)(2,1)S(1)} %collective-permute-done.11.back_ref, bf16[384,256]{1,0:T(8,128)(2,1)S(1)} %collective-permute-done.12.side_ref, ...), custom_call_target="tpu_custom_call" | custom-call | flops 1 | bytes 1 | tf_op jit(solution)/shard_map/finish/pallas_call | solution.py:324
  (17 shorter events, 0.3 us)
Async XLA Ops:
  0.6 15.3 %collective-permute-start.2 = (bf16[192,512]{1,0:T(8,128)(2,1)}, bf16[192,512]{1,0:T(8,128)(2,1)S(1)}, u32[]{:S(2)}, u32[]{:S(2)}) collective-permute-start(bf16[192,512]{1,0:T(8,128)(2,1)} %refs_0_.1), channel_id=1, source_target_pairs={{0,1},{1,0},{2,3},{3,2},{4,5},{5,4},{6,7},{7,6},{8,9},{9,8},{10,11... | collective-permute-start | bytes 589832 | tf_op jit(solution)/shard_map/ppermute | solution.py:310
  3.9 13.7 %collective-permute-start.3 = (bf16[192,512]{1,0:T(8,128)(2,1)}, bf16[192,512]{1,0:T(8,128)(2,1)S(1)}, u32[]{:S(2)}, u32[]{:S(2)}) collective-permute-start(bf16[192,512]{1,0:T(8,128)(2,1)} %refs_0_.1), channel_id=1, source_target_pairs={{0,2},{1,3},{2,4},{3,5},{4,6},{5,7},{6,0},{7,1},{8,10},{9,11},{10,... | collective-permute-start | bytes 589832 | tf_op jit(solution)/shard_map/ppermute | solution.py:310
  5.4 12.7 %collective-permute-start.4 = (bf16[192,512]{1,0:T(8,128)(2,1)}, bf16[192,512]{1,0:T(8,128)(2,1)S(1)}, u32[]{:S(2)}, u32[]{:S(2)}) collective-permute-start(bf16[192,512]{1,0:T(8,128)(2,1)} %refs_0_.1), channel_id=1, source_target_pairs={{0,6},{1,7},{2,0},{3,1},{4,2},{5,3},{6,4},{7,5},{8,14},{9,15},{10,... | collective-permute-start | bytes 589832 | tf_op jit(solution)/shard_map/ppermute | solution.py:310
  8.0 10.1 %collective-permute-start = (bf16[192,256]{1,0:T(8,128)(2,1)S(1)}, bf16[192,256]{1,0:T(8,128)(2,1)S(1)}, u32[]{:S(2)}, u32[]{:S(2)}) collective-permute-start(bf16[192,256]{1,0:T(8,128)(2,1)S(1)} %pad_add_fusion.z0_ref), channel_id=1, source_target_pairs={{0,64},{8,72},{16,80},{24,88},{32,96},{40,104},{48,112},{56,120},{... | collective-permute-start | bytes 294920 | tf_op jit(solution)/shard_map/ppermute | solution.py:310
  12.5 5.5 %collective-permute-start.1 = (bf16[192,256]{1,0:T(8,128)(2,1)S(1)}, bf16[192,256]{1,0:T(8,128)(2,1)S(1)}, u32[]{:S(2)}, u32[]{:S(2)}) collective-permute-start(bf16[192,256]{1,0:T(8,128)(2,1)S(1)} %pad_add_fusion.z0_ref), channel_id=1, source_target_pairs={{0,32},{8,40},{16,48},{24,56},{32,64},{40,72},{48,80},{56,88},{64,... | collective-permute-start | bytes 294920 | tf_op jit(solution)/shard_map/ppermute | solution.py:310
  13.6 14.4 %copy-start = (bf16[192,512]{1,0:T(8,128)(2,1)S(1)}, bf16[192,512]{1,0:T(8,128)(2,1)}, u32[]{:S(2)}) copy-start(bf16[192,512]{1,0:T(8,128)(2,1)} %refs_0_.1) | copy-start | bytes 589828
  15.9 5.8 %collective-permute-start.7 = (bf16[192,512]{1,0:T(8,128)(2,1)S(1)}, bf16[192,512]{1,0:T(8,128)(2,1)S(1)}, u32[]{:S(2)}, u32[]{:S(2)}) collective-permute-start(bf16[192,512]{1,0:T(8,128)(2,1)S(1)} %stage.1.refs_0_.refs_1_), channel_id=1, source_target_pairs={{0,6},{1,7},{2,0},{3,1},{4,2},{5,3},{6,4},{7,5},{8,14},{9,15},{10,... | collective-permute-start | bytes 589832 | tf_op jit(solution)/shard_map/ppermute | solution.py:310
  17.6 8.3 %collective-permute-start.6 = (bf16[192,512]{1,0:T(8,128)(2,1)S(1)}, bf16[192,512]{1,0:T(8,128)(2,1)S(1)}, u32[]{:S(2)}, u32[]{:S(2)}) collective-permute-start(bf16[192,512]{1,0:T(8,128)(2,1)S(1)} %stage.1.refs_0_.refs_1_), channel_id=1, source_target_pairs={{0,2},{1,3},{2,4},{3,5},{4,6},{5,7},{6,0},{7,1},{8,10},{9,11},{10,... | collective-permute-start | bytes 589832 | tf_op jit(solution)/shard_map/ppermute | solution.py:310
  18.1 9.0 %collective-permute-start.5 = (bf16[384,256]{1,0:T(8,128)(2,1)S(1)}, bf16[384,256]{1,0:T(8,128)(2,1)S(1)}, u32[]{:S(2)}, u32[]{:S(2)}) collective-permute-start(bf16[384,256]{1,0:T(8,128)(2,1)S(1)} %pick_side.1.refs_0_), channel_id=1, source_target_pairs={{0,16},{8,24},{16,0},{24,8},{32,48},{40,56},{48,32},{56,40},{64,80... | collective-permute-start | bytes 589832 | tf_op jit(solution)/shard_map/ppermute | solution.py:310
  18.9 9.1 %collective-permute-start.8 = (bf16[192,512]{1,0:T(8,128)(2,1)S(1)}, bf16[192,512]{1,0:T(8,128)(2,1)S(1)}, u32[]{:S(2)}, u32[]{:S(2)}) collective-permute-start(bf16[192,512]{1,0:T(8,128)(2,1)S(1)} %collective-permute-done.3.refs_1_.refs_2_), channel_id=1, source_target_pairs={{0,2},{1,3},{2,4},{3,5},{4,6},{5,7},{6,0},{7,1},{8,10},{9,11},{10,... | collective-permute-start | bytes 589832 | tf_op jit(solution)/shard_map/ppermute | solution.py:310
  21.7 8.4 %collective-permute-start.9 = (bf16[192,512]{1,0:T(8,128)(2,1)S(1)}, bf16[192,512]{1,0:T(8,128)(2,1)S(1)}, u32[]{:S(2)}, u32[]{:S(2)}) collective-permute-start(bf16[192,512]{1,0:T(8,128)(2,1)S(1)} %collective-permute-done.7.refs_2_.refs_5_), channel_id=1, source_target_pairs={{0,6},{1,7},{2,0},{3,1},{4,2},{5,3},{6,4},{7,5},{8,14},{9,15},{10,... | collective-permute-start | bytes 589832 | tf_op jit(solution)/shard_map/ppermute | solution.py:310
  27.2 3.5 %collective-permute-start.10 = (bf16[960,256]{1,0:T(8,128)(2,1)S(1)}, bf16[960,256]{1,0:T(8,128)(2,1)S(1)}, u32[]{:S(2)}, u32[]{:S(2)}) collective-permute-start(bf16[960,256]{1,0:T(8,128)(2,1)S(1)} %join_slots.1.refs_8_.own_ref), channel_id=1, source_target_pairs={{0,8},{8,0},{16,24},{24,16},{32,40},{40,32},{48,56},{56,48},{64,72... | collective-permute-start | bytes 1474568 | tf_op jit(solution)/shard_map/ppermute | solution.py:310
  33.6 1.8 %collective-permute-start.11 = (bf16[768,256]{1,0:T(8,128)(2,1)S(1)}, bf16[768,256]{1,0:T(8,128)(2,1)S(1)}, u32[]{:S(2)}, u32[]{:S(2)}) collective-permute-start(bf16[768,256]{1,0:T(8,128)(2,1)S(1)} %get-tuple-element.40), channel_id=1, source_target_pairs={{0,8},{8,0},{16,24},{24,16},{32,40},{40,32},{48,56},{56,48},{64,72... | collective-permute-start | bytes 1179656 | tf_op jit(solution)/shard_map/ppermute | solution.py:310
  35.6 7.0 %collective-permute-start.12 = (bf16[384,256]{1,0:T(8,128)(2,1)S(1)}, bf16[384,256]{1,0:T(8,128)(2,1)S(1)}, u32[]{:S(2)}, u32[]{:S(2)}) collective-permute-start(bf16[384,256]{1,0:T(8,128)(2,1)S(1)} %get-tuple-element.44), channel_id=1, source_target_pairs={{0,16},{8,24},{16,0},{24,8},{32,48},{40,56},{48,32},{56,40},{64,80... | collective-permute-start | bytes 589832 | tf_op jit(solution)/shard_map/ppermute | solution.py:310
  42.7 9.3 %collective-permute-start.13 = (bf16[192,256]{1,0:T(8,128)(2,1)S(1)}, bf16[192,256]{1,0:T(8,128)(2,1)S(1)}, u32[]{:S(2)}, u32[]{:S(2)}) collective-permute-start(bf16[192,256]{1,0:T(8,128)(2,1)S(1)} %get-tuple-element.45), channel_id=1, source_target_pairs={{0,192},{8,200},{16,208},{24,216},{32,224},{40,232},{48,240},{56,2... | collective-permute-start | bytes 294920 | tf_op jit(solution)/shard_map/ppermute | solution.py:310
  42.8 9.1 %collective-permute-start.14 = (bf16[192,256]{1,0:T(8,128)(2,1)S(1)}, bf16[192,256]{1,0:T(8,128)(2,1)S(1)}, u32[]{:S(2)}, u32[]{:S(2)}) collective-permute-start(bf16[192,256]{1,0:T(8,128)(2,1)S(1)} %get-tuple-element.46), channel_id=1, source_target_pairs={{0,224},{8,232},{16,240},{24,248},{32,0},{40,8},{48,16},{56,24},{6... | collective-permute-start | bytes 294920 | tf_op jit(solution)/shard_map/ppermute | solution.py:310

commit v14 on v12

--- a/solution.py
+++ b/solution.py
@@ -150,7 +150,7 @@
     acc_ref[...] = acc
 
 
-def last_projection(piece_ref, w_ref, acc_ref, after, g4_ref, gt_ref):
+def last_projection(piece_ref, w_ref, acc_ref, g4_ref, gt_ref):
     acc = (acc_ref[...] + dot(piece_ref[...], w_ref[:, 7 * BLOCK :], 1, 1)).astype(jnp.bfloat16)
     for h in range(HEADS):
         g4_ref[h * ROWS : (h + 1) * ROWS, :] = acc[:, h * D : (h + 1) * D]
@@ -166,7 +166,7 @@
     return at + 1 - 2 * lax.rem(at, 2) if flip else at
 
 
-def middle_kernel(place_ref, own_ref, q4_ref, st_in_ref, after, p_ref, st_ref):
+def middle_kernel(place_ref, own_ref, q4_ref, st_in_ref, p_ref, st_ref):
     queries = q4_ref[...]
     row = lax.broadcasted_iota(jnp.int32, (ROWS, LANES), 0)
     start = st_in_ref[START : START + 1, :].astype(jnp.int32)
@@ -292,18 +292,23 @@
             st_ref[:, h * D : (h + 1) * D] = dq[h * ROWS : (h + 1) * ROWS, :].astype(jnp.bfloat16)
 
 
+def is_upper(place_ref):
+    return (lax.rem(lax.div(place_ref[0], 2), 2) == 1).astype(jnp.float32)
+
+
 def settle_kernel(own_ref, back_ref, low_ref, high_ref):
     both = own_ref[...] + back_ref[: 2 * ROWS, :].astype(jnp.float32)
     low_ref[...] = both[:ROWS].astype(low_ref.dtype)
     high_ref[...] = both[ROWS:].astype(jnp.bfloat16)
 
 
-def relay_far(keep_ref, side_ref, out_ref):
-    out_ref[...] = (keep_ref[...] + side_ref[...].astype(jnp.float32)).astype(jnp.bfloat16)
-
-
-def gather_kernel(own_ref, back_ref, side_ref, two_ref, four_ref, out_ref):
-    total = own_ref[...] + back_ref[2 * ROWS :, :].astype(jnp.float32) + side_ref[...].astype(jnp.float32)
+def relay_far(place_ref, keep_ref, side_ref, out_ref):
+    out_ref[...] = (keep_ref[...] + side_ref[...].astype(jnp.float32) * is_upper(place_ref)).astype(jnp.bfloat16)
+
+
+def gather_kernel(place_ref, own_ref, back_ref, side_ref, two_ref, four_ref, out_ref):
+    total = own_ref[...] + back_ref[2 * ROWS :, :].astype(jnp.float32)
+    total = total + side_ref[...].astype(jnp.float32) * (1 - is_upper(place_ref))
     out_ref[...] = total + two_ref[...].astype(jnp.float32) + four_ref[...].astype(jnp.float32)
 
 
@@ -399,26 +404,26 @@
     own = call("join_slots", join_kernel, shape(SLOTS * ROWS, 2 * D, bf16), vmem(4) + token(1), (z2, z1, kv, side, st))
     par = moved(own, "ctx", lambda i: i ^ 1)
 
+    p_side, st = call(
+        "middle",
+        middle_kernel,
+        (shape(2 * ROWS, LANES, bf16), state),
+        smem(1) + vmem(3),
+        (place, own, q4, st),
+    )
     early = call(
         "project",
         project_kernel,
         shape(ROWS, HEADS * D, f32),
         vmem(8) + token(1),
-        (grad_out, other, right, left, other_right, other_left, far, weight, own),
-    )
-    p_side, st = call(
-        "middle",
-        middle_kernel,
-        (shape(2 * ROWS, LANES, bf16), state),
-        smem(1) + vmem(3) + token(1),
-        (place, own, q4, st, early),
+        (grad_out, other, right, left, other_right, other_left, far, weight, st),
     )
     g4, gt = call(
         "last_projection",
         last_projection,
         (shape(LANES, D, bf16), shape(D, LANES, f32)),
-        vmem(3) + token(1),
-        (other_far, weight, early, st),
+        vmem(3),
+        (other_far, weight, early),
         flops=COSTLY,
     )
     p_par, st = call(
@@ -445,10 +450,7 @@
         "settle_far", settle_kernel, (shape(ROWS, 2 * D, f32), shape(ROWS, 2 * D, bf16)), vmem(2), (far_own, far_back)
     )
     count = lax.axis_size("ctx")
-    lower = [i for i in range(count) if i // 2 % 2 == 0]
-    upper = [i for i in range(count) if i // 2 % 2 == 1]
-    far_up = lax.ppermute(far_side, "ctx", [(i, i + 2) for i in lower])
-    far_down = lax.ppermute(far_side, "ctx", [(i, (i - 6) % count) for i in upper])
+    far_side = moved(far_side, "ctx", lambda i: (i + 2 if i // 2 % 2 == 0 else i - 6) % count)
     near_own, st = call(
         "own_near",
         functools.partial(own_kernel, (2, 3)),
@@ -462,7 +464,7 @@
     )
     by_four = turned(by_four, "ctx", -4)
     by_two = turned(by_two, "ctx", -2)
-    to_eight = call("relay_far", relay_far, shape(ROWS, 2 * D, bf16), vmem(2), (far_keep, far_up))
+    to_eight = call("relay_far", relay_far, shape(ROWS, 2 * D, bf16), smem(1) + vmem(2), (place, far_keep, far_side))
     by_eight = turned(to_eight, "ctx", -8)
     last_own, grad_queries = call(
         "own_last",
@@ -475,8 +477,8 @@
         "gather_near",
         gather_kernel,
         shape(ROWS, 2 * D, f32),
-        vmem(5),
-        (last_own, near_back, far_down, by_two, by_four),
+        smem(1) + vmem(5),
+        (place, last_own, near_back, far_side, by_two, by_four),
         flops=COSTLY,
     )
     grad_keys, grad_values = call(

time: 56.4 us -> 51.5 us (0.913)
  starting transfers between devices: 29.8 us -> 22.3 us
  waiting for transfers between devices: 11.3 us -> 14 us
    ppermute x2 -> x0, starting transfers between devices: 3.89 us -> none  [the longest x1 2.59 us: local(): far_up = lax.ppermute(far_side, 'ctx', [(i, i + 2) for i in lower])]
    ppermute x16 -> x17, starting transfers between devices: 25.9 us -> 22.3 us  [moved(): lax.ppermute(x, axis, [(i, to(i)) for i in range(lax.axis_size(axis))])]
    ppermute x16 -> x17, waiting for transfers between devices: 11.3 us -> 14 us  [moved(): lax.ppermute(x, axis, [(i, to(i)) for i in range(lax.axis_size(axis))])]
  transfers between devices with their start and end apart: 18 -> 17, of which waited for: 5 -> 6; matrix products, arithmetic and copies ran while one was open for 1% -> 2% of each run, Pallas kernels for 18% -> 20%
where the time goes in v14:
time: 51.5 us; the launch traced here: 51.4 us
  starting transfers between devices  22.3 us (43%)
  waiting for transfers between devices  14 us (27%)
  Pallas kernels  13.3 us (26%)
  between operations  0.85 us (2%)
  other arithmetic  0.83 us (2%)
    ppermute x17, starting transfers between devices, moved(): lax.ppermute(x, axis, [(i, to(i)) for i in range(lax.axis_size(axis))])  22.3 us
    ppermute x17, waiting for transfers between devices, moved(): lax.ppermute(x, axis, [(i, to(i)) for i in range(lax.axis_size(axis))])  14 us
    pallas_call x20, Pallas kernels, call(): pl.pallas_call(kernel, out_shape=outs, in_specs=ins, out_specs=vmem(1)[0]...  13.3 us
  transfers between devices with their start and end apart: 17, of which 6 were waited for; matrix products, arithmetic and copies ran while one was open for 2% of the time, Pallas kernels for 20%

profile of v14, /device:TPU:64, one launch (start us, length us, event | category | flops | bytes accessed | tf_op | source)
XLA Modules:
  0.0 51.4 jit_solution(3976147119759217478)
XLA Ops:
  0.6 3.3 %collective-permute-start.2 = (bf16[192,512]{1,0:T(8,128)(2,1)}, bf16[192,512]{1,0:T(8,128)(2,1)S(1)}, u32[]{:S(2)}, u32[]{:S(2)}) collective-permute-start(bf16[192,512]{1,0:T(8,128)(2,1)} %refs_0_.1), channel_id=1, source_target_pairs={{0,1},{1,0},{2,3},{3,2},{4,5},{5,4},{6,7},{7,6},{8,9},{9,8},{10,11... | collective-permute-start | bytes 589832 | tf_op jit(solution)/shard_map/ppermute | solution.py:338
  3.9 1.5 %collective-permute-start.3 = (bf16[192,512]{1,0:T(8,128)(2,1)}, bf16[192,512]{1,0:T(8,128)(2,1)S(1)}, u32[]{:S(2)}, u32[]{:S(2)}) collective-permute-start(bf16[192,512]{1,0:T(8,128)(2,1)} %refs_0_.1), channel_id=1, source_target_pairs={{0,2},{1,3},{2,4},{3,5},{4,6},{5,7},{6,0},{7,1},{8,10},{9,11},{10,... | collective-permute-start | bytes 589832 | tf_op jit(solution)/shard_map/ppermute | solution.py:338
  5.4 1.7 %collective-permute-start.4 = (bf16[192,512]{1,0:T(8,128)(2,1)}, bf16[192,512]{1,0:T(8,128)(2,1)S(1)}, u32[]{:S(2)}, u32[]{:S(2)}) collective-permute-start(bf16[192,512]{1,0:T(8,128)(2,1)} %refs_0_.1), channel_id=1, source_target_pairs={{0,6},{1,7},{2,0},{3,1},{4,2},{5,3},{6,4},{7,5},{8,14},{9,15},{10,... | collective-permute-start | bytes 589832 | tf_op jit(solution)/shard_map/ppermute | solution.py:338
  7.1 0.8 %pad_add_fusion.z0_ref = bf16[192,256]{1,0:T(8,128)(2,1)S(1)} fusion(bf16[192,128]{1,0:T(8,128)(2,1)} %param.8, bf16[192,128]{1,0:T(8,128)(2,1)} %param.7), kind=kLoop, calls=%fused_computation | loop fusion | flops 196608 | bytes 196608 | tf_op jit(solution)/shard_map/add | solution.py:375
  8.0 4.6 %collective-permute-start = (bf16[192,256]{1,0:T(8,128)(2,1)S(1)}, bf16[192,256]{1,0:T(8,128)(2,1)S(1)}, u32[]{:S(2)}, u32[]{:S(2)}) collective-permute-start(bf16[192,256]{1,0:T(8,128)(2,1)S(1)} %pad_add_fusion.z0_ref), channel_id=1, source_target_pairs={{0,64},{8,72},{16,80},{24,88},{32,96},{40,104},{48,112},{56,120},{... | collective-permute-start | bytes 294920 | tf_op jit(solution)/shard_map/ppermute | solution.py:338
  12.5 1.0 %collective-permute-start.1 = (bf16[192,256]{1,0:T(8,128)(2,1)S(1)}, bf16[192,256]{1,0:T(8,128)(2,1)S(1)}, u32[]{:S(2)}, u32[]{:S(2)}) collective-permute-start(bf16[192,256]{1,0:T(8,128)(2,1)S(1)} %pad_add_fusion.z0_ref), channel_id=1, source_target_pairs={{0,32},{8,40},{16,48},{24,56},{32,64},{40,72},{48,80},{56,88},{64,... | collective-permute-start | bytes 294920 | tf_op jit(solution)/shard_map/ppermute | solution.py:338
  13.6 2.3 %load.1 = (bf16[768,128]{1,0:T(8,128)(2,1)S(1)}, f32[8,768]{1,0:T(8,128)S(1)}, bf16[512,4096]{1,0:T(8,128)(2,1)S(1)}) custom-call(s32[1]{0:T(128)} %bitcast.place_ref, s32[1]{0:T(128)} %bitcast.1.head_ref, s32[8]{0:T(128)} %len_hbm.1, bf16[192,512]{1,0:T(8,128)(2,1)} %q_hbm.1, bf16[512,4096]{1,0:T(8,128)(2,1)} %w_hbm.1), custom_call_target="tpu_custom_call" | custom-call | flops 1 | bytes 1 | tf_op jit(solution)/shard_map/load/pallas_call | solution.py:352
  15.9 1.6 %collective-permute-start.7 = (bf16[192,512]{1,0:T(8,128)(2,1)S(1)}, bf16[192,512]{1,0:T(8,128)(2,1)S(1)}, u32[]{:S(2)}, u32[]{:S(2)}) collective-permute-start(bf16[192,512]{1,0:T(8,128)(2,1)S(1)} %stage.1.refs_0_.refs_1_), channel_id=1, source_target_pairs={{0,6},{1,7},{2,0},{3,1},{4,2},{5,3},{6,4},{7,5},{8,14},{9,15},{10,... | collective-permute-start | bytes 589832 | tf_op jit(solution)/shard_map/ppermute | solution.py:338
  17.6 0.5 collective-permute-start.6
  18.1 0.8 %collective-permute-start.5 = (bf16[384,256]{1,0:T(8,128)(2,1)S(1)}, bf16[384,256]{1,0:T(8,128)(2,1)S(1)}, u32[]{:S(2)}, u32[]{:S(2)}) collective-permute-start(bf16[384,256]{1,0:T(8,128)(2,1)S(1)} %pick_side.1.refs_0_), channel_id=1, source_target_pairs={{0,16},{8,24},{16,0},{24,8},{32,48},{40,56},{48,32},{56,40},{64,80... | collective-permute-start | bytes 589832 | tf_op jit(solution)/shard_map/ppermute | solution.py:338
  19.2 2.6 %collective-permute-done.7.refs_2_.refs_5_ = bf16[192,512]{1,0:T(8,128)(2,1)S(1)} collective-permute-done((bf16[192,512]{1,0:T(8,128)(2,1)S(1)}, bf16[192,512]{1,0:T(8,128)(2,1)S(1)}, u32[]{:S(2)}, u32[]{:S(2)}) %collective-permute-start.7) | collective-permute-done | bytes 196640 | tf_op jit(solution)/shard_map/ppermute | solution.py:338
  21.7 2.7 %collective-permute-start.8 = (bf16[192,512]{1,0:T(8,128)(2,1)S(1)}, bf16[192,512]{1,0:T(8,128)(2,1)S(1)}, u32[]{:S(2)}, u32[]{:S(2)}) collective-permute-start(bf16[192,512]{1,0:T(8,128)(2,1)S(1)} %collective-permute-done.7.refs_2_.refs_5_), channel_id=1, source_target_pairs={{0,6},{1,7},{2,0},{3,1},{4,2},{5,3},{6,4},{7,5},{8,14},{9,15},{10,... | collective-permute-start | bytes 589832 | tf_op jit(solution)/shard_map/ppermute | solution.py:338
  24.5 1.4 %collective-permute-done.6.refs_1_.refs_4_ = bf16[192,512]{1,0:T(8,128)(2,1)S(1)} collective-permute-done((bf16[192,512]{1,0:T(8,128)(2,1)S(1)}, bf16[192,512]{1,0:T(8,128)(2,1)S(1)}, u32[]{:S(2)}, u32[]{:S(2)}) %collective-permute-start.6) | collective-permute-done | bytes 196640 | tf_op jit(solution)/shard_map/ppermute | solution.py:338
  25.9 1.3 %near.1 = (bf16[576,768]{1,0:T(8,128)(2,1)S(1)}, f32[152,768]{1,0:T(8,128)S(1)}) custom-call(s32[1]{0:T(128)} %bitcast.place_ref, bf16[192,256]{1,0:T(8,128)(2,1)S(1)} %collective-permute-done.z2_ref, bf16[192,256]{1,0:T(8,128)(2,1)S(1)} %collective-permute-done.1.z1_ref, bf16[192,256]{1,0:T(8,128)(2,1)S(1)} %pad_add_fusion.z0_ref, ...), custom_call_target="tpu_custom_call" | custom-call | flops 1 | bytes 1 | tf_op jit(solution)/shard_map/near/pallas_call | solution.py:352
  27.5 0.9 %middle.1 = (bf16[384,768]{1,0:T(8,128)(2,1)S(1)}, f32[152,768]{1,0:T(8,128)S(1)}) custom-call(s32[1]{0:T(128)} %bitcast.place_ref, bf16[960,256]{1,0:T(8,128)(2,1)S(1)} %join_slots.1.own_ref, bf16[768,128]{1,0:T(8,128)(2,1)S(1)} %get-tuple-element.30.after.refs_3_.q4_ref, f32[152,768]{1,0:T(8,128)S(1)} %get-tuple-element.32.refs_0_.st_in_ref), custom_call_target="tpu_custom_call" | custom-call | flops 1 | bytes 1 | tf_op jit(solution)/shard_map/middle/pallas_call | solution.py:352
  28.4 1.4 %project.1.acc_ref = f32[192,512]{1,0:T(8,128)S(1)} custom-call(bf16[192,512]{1,0:T(8,128)(2,1)S(1)} %copy-done, bf16[192,512]{1,0:T(8,128)(2,1)S(1)} %stage.1.refs_0_.refs_1_, bf16[192,512]{1,0:T(8,128)(2,1)S(1)} %collective-permute-done.3.refs_1_.refs_2_, bf16[192,512]{1,0:T(8,128)(2,1)S(1)} %collective-permute-done.4.refs_2_.refs_3_, ...), custom_call_target="tpu_custom_call" | custom-call | flops 1 | bytes 1 | tf_op jit(solution)/shard_map/project/pallas_call | solution.py:352
  29.7 0.5 last_projection.1
  30.2 1.6 %across.1 = (bf16[768,768]{1,0:T(8,128)(2,1)S(1)}, f32[152,768]{1,0:T(8,128)S(1)}) custom-call(s32[1]{0:T(128)} %bitcast.place_ref, bf16[960,256]{1,0:T(8,128)(2,1)S(1)} %collective-permute-done.10.par_ref, bf16[768,128]{1,0:T(8,128)(2,1)S(1)} %get-tuple-element.30.after.refs_3_.q4_ref, f32[128,768]{1,0:T(8,128)S(1)} %get-tuple-element.38.gt_ref, ...), custom_call_target="tpu_custom_call" | custom-call | flops 1 | bytes 1 | tf_op jit(solution)/shard_map/across/pallas_call | solution.py:352
  31.8 0.9 %cross_far.1 = (bf16[384,256]{1,0:T(8,128)(2,1)S(1)}, f32[152,768]{1,0:T(8,128)S(1)}) custom-call(s32[1]{0:T(128)} %bitcast.place_ref, bf16[768,128]{1,0:T(8,128)(2,1)S(1)} %get-tuple-element.30.after.refs_3_.q4_ref, bf16[960,256]{1,0:T(8,128)(2,1)S(1)} %collective-permute-done.10.par_ref, bf16[768,768]{1,0:T(8,128)(2,1)S(1)} %get-tuple-element.39.p_ref, ...), custom_call_target="tpu_custom_call" | custom-call | flops 1 | bytes 1 | tf_op jit(solution)/shard_map/cross_far/pallas_call | solution.py:352
  32.9 0.8 %cross_near.1 = (bf16[576,256]{1,0:T(8,128)(2,1)S(1)}, f32[152,768]{1,0:T(8,128)S(1)}) custom-call(s32[1]{0:T(128)} %bitcast.place_ref, bf16[768,128]{1,0:T(8,128)(2,1)S(1)} %get-tuple-element.30.after.refs_3_.q4_ref, bf16[960,256]{1,0:T(8,128)(2,1)S(1)} %collective-permute-done.10.par_ref, bf16[768,768]{1,0:T(8,128)(2,1)S(1)} %get-tuple-element.39.p_ref, ...), custom_call_target="tpu_custom_call" | custom-call | flops 4000000000 | bytes 1 | tf_op jit(solution)/shard_map/cross_near/pallas_call | solution.py:352
  33.7 1.0 %collective-permute-start.13 = (bf16[576,256]{1,0:T(8,128)(2,1)S(1)}, bf16[576,256]{1,0:T(8,128)(2,1)S(1)}, u32[]{:S(2)}, u32[]{:S(2)}) collective-permute-start(bf16[576,256]{1,0:T(8,128)(2,1)S(1)} %get-tuple-element.51), channel_id=1, source_target_pairs={{0,8},{8,0},{16,24},{24,16},{32,40},{40,32},{48,56},{56,48},{64,72... | collective-permute-start | bytes 884744 | tf_op jit(solution)/shard_map/ppermute | solution.py:338
  34.7 0.8 %own_far.1 = (f32[384,256]{1,0:T(8,128)S(1)}, f32[152,768]{1,0:T(8,128)S(1)}) custom-call(bf16[768,128]{1,0:T(8,128)(2,1)S(1)} %get-tuple-element.30.after.refs_3_.q4_ref, bf16[960,256]{1,0:T(8,128)(2,1)S(1)} %join_slots.1.own_ref, bf16[576,768]{1,0:T(8,128)(2,1)S(1)} %get-tuple-element.33.near_ref, bf16[384,768]{1,0:T(8,128)(2,1)S(1)} %get-tuple-element.34.side_ref, ...), custom_call_target="tpu_custom_call" | custom-call | flops 4000000000 | bytes 1 | tf_op jit(solution)/shard_map/own_far/pallas_call | solution.py:352
  35.6 0.8 %collective-permute-start.12 = (bf16[192,256]{1,0:T(8,128)(2,1)S(1)}, bf16[192,256]{1,0:T(8,128)(2,1)S(1)}, u32[]{:S(2)}, u32[]{:S(2)}) collective-permute-start(bf16[192,256]{1,0:T(8,128)(2,1)S(1)} %get-tuple-element.48), channel_id=1, source_target_pairs={{0,16},{8,24},{16,224},{24,232},{32,48},{40,56},{48,0},{56,8},{64,... | collective-permute-start | bytes 294920 | tf_op jit(solution)/shard_map/ppermute | solution.py:338
  36.3 0.8 %own_near.1 = (f32[384,256]{1,0:T(8,128)S(1)}, f32[152,768]{1,0:T(8,128)S(1)}) custom-call(bf16[768,128]{1,0:T(8,128)(2,1)S(1)} %get-tuple-element.30.after.refs_3_.q4_ref, bf16[960,256]{1,0:T(8,128)(2,1)S(1)} %join_slots.1.own_ref, bf16[576,768]{1,0:T(8,128)(2,1)S(1)} %get-tuple-element.33.near_ref, bf16[384,768]{1,0:T(8,128)(2,1)S(1)} %get-tuple-element.34.side_ref, ...), custom_call_target="tpu_custom_call" | custom-call | flops 4000000000 | bytes 1 | tf_op jit(solution)/shard_map/own_near/pallas_call | solution.py:352
  37.2 0.5 %collective-permute-start.14 = (bf16[192,256]{1,0:T(8,128)(2,1)S(1)}, bf16[192,256]{1,0:T(8,128)(2,1)S(1)}, u32[]{:S(2)}, u32[]{:S(2)}) collective-permute-start(bf16[192,256]{1,0:T(8,128)(2,1)S(1)} %get-tuple-element.53), channel_id=1, source_target_pairs={{0,240},{8,248},{16,0},{24,8},{32,16},{40,24},{48,32},{56,40},{64,... | collective-permute-start | bytes 294920 | tf_op jit(solution)/shard_map/ppermute | solution.py:338
  37.7 1.5 %collective-permute-start.15 = (bf16[192,256]{1,0:T(8,128)(2,1)S(1)}, bf16[192,256]{1,0:T(8,128)(2,1)S(1)}, u32[]{:S(2)}, u32[]{:S(2)}) collective-permute-start(bf16[192,256]{1,0:T(8,128)(2,1)S(1)} %get-tuple-element.54), channel_id=1, source_target_pairs={{0,224},{8,232},{16,240},{24,248},{32,0},{40,8},{48,16},{56,24},{6... | collective-permute-start | bytes 294920 | tf_op jit(solution)/shard_map/ppermute | solution.py:338
  39.3 2.4 %collective-permute-done.12.side_ref = bf16[192,256]{1,0:T(8,128)(2,1)S(1)} collective-permute-done((bf16[192,256]{1,0:T(8,128)(2,1)S(1)}, bf16[192,256]{1,0:T(8,128)(2,1)S(1)}, u32[]{:S(2)}, u32[]{:S(2)}) %collective-permute-start.12) | collective-permute-done | bytes 98336 | tf_op jit(solution)/shard_map/ppermute | solution.py:338
  41.7 1.2 %own_last.1 = (f32[192,256]{1,0:T(8,128)S(1)}, bf16[192,512]{1,0:T(8,128)(2,1)}) custom-call(bf16[768,128]{1,0:T(8,128)(2,1)S(1)} %get-tuple-element.30.after.refs_3_.q4_ref, bf16[960,256]{1,0:T(8,128)(2,1)S(1)} %join_slots.1.own_ref, bf16[576,768]{1,0:T(8,128)(2,1)S(1)} %get-tuple-element.33.near_ref, bf16[384,768]{1,0:T(8,128)(2,1)S(1)} %get-tuple-element.34.side_ref, ...), custom_call_target="tpu_custom_call" | custom-call | flops 1 | bytes 1 | tf_op jit(solution)/shard_map/own_last/pallas_call | solution.py:352
  43.0 0.4 collective-permute-done.14.two_ref
  43.4 3.4 %collective-permute-done.15.four_ref = bf16[192,256]{1,0:T(8,128)(2,1)S(1)} collective-permute-done((bf16[192,256]{1,0:T(8,128)(2,1)S(1)}, bf16[192,256]{1,0:T(8,128)(2,1)S(1)}, u32[]{:S(2)}, u32[]{:S(2)}) %collective-permute-start.15) | collective-permute-done | bytes 98336 | tf_op jit(solution)/shard_map/ppermute | solution.py:338
  46.8 3.9 %collective-permute-done.16.eight_ref = bf16[192,256]{1,0:T(8,128)(2,1)S(1)} collective-permute-done((bf16[192,256]{1,0:T(8,128)(2,1)S(1)}, bf16[192,256]{1,0:T(8,128)(2,1)S(1)}, u32[]{:S(2)}, u32[]{:S(2)}) %collective-permute-start.16) | collective-permute-done | bytes 98336 | tf_op jit(solution)/shard_map/ppermute | solution.py:338
  50.7 0.6 %finish.1 = (bf16[192,128]{1,0:T(8,128)(2,1)}, bf16[192,128]{1,0:T(8,128)(2,1)}) custom-call(f32[192,256]{1,0:T(8,128)S(1)} %gather_near.1.sum_ref, bf16[192,256]{1,0:T(8,128)(2,1)S(1)} %collective-permute-done.16.eight_ref), custom_call_target="tpu_custom_call" | custom-call | flops 1 | bytes 1 | tf_op jit(solution)/shard_map/finish/pallas_call | solution.py:352
  (25 shorter events, 1.0 us)
Async XLA Ops:
  0.6 15.3 %collective-permute-start.2 = (bf16[192,512]{1,0:T(8,128)(2,1)}, bf16[192,512]{1,0:T(8,128)(2,1)S(1)}, u32[]{:S(2)}, u32[]{:S(2)}) collective-permute-start(bf16[192,512]{1,0:T(8,128)(2,1)} %refs_0_.1), channel_id=1, source_target_pairs={{0,1},{1,0},{2,3},{3,2},{4,5},{5,4},{6,7},{7,6},{8,9},{9,8},{10,11... | collective-permute-start | bytes 589832 | tf_op jit(solution)/shard_map/ppermute | solution.py:338
  3.9 13.7 %collective-permute-start.3 = (bf16[192,512]{1,0:T(8,128)(2,1)}, bf16[192,512]{1,0:T(8,128)(2,1)S(1)}, u32[]{:S(2)}, u32[]{:S(2)}) collective-permute-start(bf16[192,512]{1,0:T(8,128)(2,1)} %refs_0_.1), channel_id=1, source_target_pairs={{0,2},{1,3},{2,4},{3,5},{4,6},{5,7},{6,0},{7,1},{8,10},{9,11},{10,... | collective-permute-start | bytes 589832 | tf_op jit(solution)/shard_map/ppermute | solution.py:338
  5.4 12.7 %collective-permute-start.4 = (bf16[192,512]{1,0:T(8,128)(2,1)}, bf16[192,512]{1,0:T(8,128)(2,1)S(1)}, u32[]{:S(2)}, u32[]{:S(2)}) collective-permute-start(bf16[192,512]{1,0:T(8,128)(2,1)} %refs_0_.1), channel_id=1, source_target_pairs={{0,6},{1,7},{2,0},{3,1},{4,2},{5,3},{6,4},{7,5},{8,14},{9,15},{10,... | collective-permute-start | bytes 589832 | tf_op jit(solution)/shard_map/ppermute | solution.py:338
  8.0 10.1 %collective-permute-start = (bf16[192,256]{1,0:T(8,128)(2,1)S(1)}, bf16[192,256]{1,0:T(8,128)(2,1)S(1)}, u32[]{:S(2)}, u32[]{:S(2)}) collective-permute-start(bf16[192,256]{1,0:T(8,128)(2,1)S(1)} %pad_add_fusion.z0_ref), channel_id=1, source_target_pairs={{0,64},{8,72},{16,80},{24,88},{32,96},{40,104},{48,112},{56,120},{... | collective-permute-start | bytes 294920 | tf_op jit(solution)/shard_map/ppermute | solution.py:338
  12.5 5.5 %collective-permute-start.1 = (bf16[192,256]{1,0:T(8,128)(2,1)S(1)}, bf16[192,256]{1,0:T(8,128)(2,1)S(1)}, u32[]{:S(2)}, u32[]{:S(2)}) collective-permute-start(bf16[192,256]{1,0:T(8,128)(2,1)S(1)} %pad_add_fusion.z0_ref), channel_id=1, source_target_pairs={{0,32},{8,40},{16,48},{24,56},{32,64},{40,72},{48,80},{56,88},{64,... | collective-permute-start | bytes 294920 | tf_op jit(solution)/shard_map/ppermute | solution.py:338
  13.6 14.8 %copy-start = (bf16[192,512]{1,0:T(8,128)(2,1)S(1)}, bf16[192,512]{1,0:T(8,128)(2,1)}, u32[]{:S(2)}) copy-start(bf16[192,512]{1,0:T(8,128)(2,1)} %refs_0_.1) | copy-start | bytes 589828
  15.9 5.8 %collective-permute-start.7 = (bf16[192,512]{1,0:T(8,128)(2,1)S(1)}, bf16[192,512]{1,0:T(8,128)(2,1)S(1)}, u32[]{:S(2)}, u32[]{:S(2)}) collective-permute-start(bf16[192,512]{1,0:T(8,128)(2,1)S(1)} %stage.1.refs_0_.refs_1_), channel_id=1, source_target_pairs={{0,6},{1,7},{2,0},{3,1},{4,2},{5,3},{6,4},{7,5},{8,14},{9,15},{10,... | collective-permute-start | bytes 589832 | tf_op jit(solution)/shard_map/ppermute | solution.py:338
  17.6 8.3 %collective-permute-start.6 = (bf16[192,512]{1,0:T(8,128)(2,1)S(1)}, bf16[192,512]{1,0:T(8,128)(2,1)S(1)}, u32[]{:S(2)}, u32[]{:S(2)}) collective-permute-start(bf16[192,512]{1,0:T(8,128)(2,1)S(1)} %stage.1.refs_0_.refs_1_), channel_id=1, source_target_pairs={{0,2},{1,3},{2,4},{3,5},{4,6},{5,7},{6,0},{7,1},{8,10},{9,11},{10,... | collective-permute-start | bytes 589832 | tf_op jit(solution)/shard_map/ppermute | solution.py:338
  18.1 9.0 %collective-permute-start.5 = (bf16[384,256]{1,0:T(8,128)(2,1)S(1)}, bf16[384,256]{1,0:T(8,128)(2,1)S(1)}, u32[]{:S(2)}, u32[]{:S(2)}) collective-permute-start(bf16[384,256]{1,0:T(8,128)(2,1)S(1)} %pick_side.1.refs_0_), channel_id=1, source_target_pairs={{0,16},{8,24},{16,0},{24,8},{32,48},{40,56},{48,32},{56,40},{64,80... | collective-permute-start | bytes 589832 | tf_op jit(solution)/shard_map/ppermute | solution.py:338
  18.9 9.5 %collective-permute-start.9 = (bf16[192,512]{1,0:T(8,128)(2,1)S(1)}, bf16[192,512]{1,0:T(8,128)(2,1)S(1)}, u32[]{:S(2)}, u32[]{:S(2)}) collective-permute-start(bf16[192,512]{1,0:T(8,128)(2,1)S(1)} %collective-permute-done.3.refs_1_.refs_2_), channel_id=1, source_target_pairs={{0,2},{1,3},{2,4},{3,5},{4,6},{5,7},{6,0},{7,1},{8,10},{9,11},{10,... | collective-permute-start | bytes 589832 | tf_op jit(solution)/shard_map/ppermute | solution.py:338
  21.7 8.0 %collective-permute-start.8 = (bf16[192,512]{1,0:T(8,128)(2,1)S(1)}, bf16[192,512]{1,0:T(8,128)(2,1)S(1)}, u32[]{:S(2)}, u32[]{:S(2)}) collective-permute-start(bf16[192,512]{1,0:T(8,128)(2,1)S(1)} %collective-permute-done.7.refs_2_.refs_5_), channel_id=1, source_target_pairs={{0,6},{1,7},{2,0},{3,1},{4,2},{5,3},{6,4},{7,5},{8,14},{9,15},{10,... | collective-permute-start | bytes 589832 | tf_op jit(solution)/shard_map/ppermute | solution.py:338
  27.2 3.0 %collective-permute-start.10 = (bf16[960,256]{1,0:T(8,128)(2,1)S(1)}, bf16[960,256]{1,0:T(8,128)(2,1)S(1)}, u32[]{:S(2)}, u32[]{:S(2)}) collective-permute-start(bf16[960,256]{1,0:T(8,128)(2,1)S(1)} %join_slots.1.own_ref), channel_id=1, source_target_pairs={{0,8},{8,0},{16,24},{24,16},{32,40},{40,32},{48,56},{56,48},{64,72... | collective-permute-start | bytes 1474568 | tf_op jit(solution)/shard_map/ppermute | solution.py:338
  32.7 2.8 %collective-permute-start.11 = (bf16[384,256]{1,0:T(8,128)(2,1)S(1)}, bf16[384,256]{1,0:T(8,128)(2,1)S(1)}, u32[]{:S(2)}, u32[]{:S(2)}) collective-permute-start(bf16[384,256]{1,0:T(8,128)(2,1)S(1)} %get-tuple-element.45), channel_id=1, source_target_pairs={{0,8},{8,0},{16,24},{24,16},{32,40},{40,32},{48,56},{56,48},{64,72... | collective-permute-start | bytes 589832 | tf_op jit(solution)/shard_map/ppermute | solution.py:338
  33.7 3.4 %collective-permute-start.13 = (bf16[576,256]{1,0:T(8,128)(2,1)S(1)}, bf16[576,256]{1,0:T(8,128)(2,1)S(1)}, u32[]{:S(2)}, u32[]{:S(2)}) collective-permute-start(bf16[576,256]{1,0:T(8,128)(2,1)S(1)} %get-tuple-element.51), channel_id=1, source_target_pairs={{0,8},{8,0},{16,24},{24,16},{32,40},{40,32},{48,56},{56,48},{64,72... | collective-permute-start | bytes 884744 | tf_op jit(solution)/shard_map/ppermute | solution.py:338
  35.6 6.1 %collective-permute-start.12 = (bf16[192,256]{1,0:T(8,128)(2,1)S(1)}, bf16[192,256]{1,0:T(8,128)(2,1)S(1)}, u32[]{:S(2)}, u32[]{:S(2)}) collective-permute-start(bf16[192,256]{1,0:T(8,128)(2,1)S(1)} %get-tuple-element.48), channel_id=1, source_target_pairs={{0,16},{8,24},{16,224},{24,232},{32,48},{40,56},{48,0},{56,8},{64,... | collective-permute-start | bytes 294920 | tf_op jit(solution)/shard_map/ppermute | solution.py:338
  37.2 6.2 %collective-permute-start.14 = (bf16[192,256]{1,0:T(8,128)(2,1)S(1)}, bf16[192,256]{1,0:T(8,128)(2,1)S(1)}, u32[]{:S(2)}, u32[]{:S(2)}) collective-permute-start(bf16[192,256]{1,0:T(8,128)(2,1)S(1)} %get-tuple-element.53), channel_id=1, source_target_pairs={{0,240},{8,248},{16,0},{24,8},{32,16},{40,24},{48,32},{56,40},{64,... | collective-permute-start | bytes 294920 | tf_op jit(solution)/shard_map/ppermute | solution.py:338
  37.7 9.0 %collective-permute-start.15 = (bf16[192,256]{1,0:T(8,128)(2,1)S(1)}, bf16[192,256]{1,0:T(8,128)(2,1)S(1)}, u32[]{:S(2)}, u32[]{:S(2)}) collective-permute-start(bf16[192,256]{1,0:T(8,128)(2,1)S(1)} %get-tuple-element.54), channel_id=1, source_target_pairs={{0,224},{8,232},{16,240},{24,248},{32,0},{40,8},{48,16},{56,24},{6... | collective-permute-start | bytes 294920 | tf_op jit(solution)/shard_map/ppermute | solution.py:338
  41.6 9.1 %collective-permute-start.16 = (bf16[192,256]{1,0:T(8,128)(2,1)S(1)}, bf16[192,256]{1,0:T(8,128)(2,1)S(1)}, u32[]{:S(2)}, u32[]{:S(2)}) collective-permute-start(bf16[192,256]{1,0:T(8,128)(2,1)S(1)} %relay_far.1.refs_0_), channel_id=1, source_target_pairs={{0,192},{8,200},{16,208},{24,216},{32,224},{40,232},{48,240},{56,2... | collective-permute-start | bytes 294920 | tf_op jit(solution)/shard_map/ppermute | solution.py:338

commit v15 on v14

--- a/solution.py
+++ b/solution.py
@@ -296,24 +296,27 @@
     return (lax.rem(lax.div(place_ref[0], 2), 2) == 1).astype(jnp.float32)
 
 
-def settle_kernel(own_ref, back_ref, low_ref, high_ref):
+def settle_kernel(own_ref, back_ref, keep_ref, send_ref):
     both = own_ref[...] + back_ref[: 2 * ROWS, :].astype(jnp.float32)
-    low_ref[...] = both[:ROWS].astype(low_ref.dtype)
-    high_ref[...] = both[ROWS:].astype(jnp.bfloat16)
-
-
-def relay_far(place_ref, keep_ref, side_ref, out_ref):
-    out_ref[...] = (keep_ref[...] + side_ref[...].astype(jnp.float32) * is_upper(place_ref)).astype(jnp.bfloat16)
-
-
-def gather_kernel(place_ref, own_ref, back_ref, side_ref, two_ref, four_ref, out_ref):
+    keep_ref[...] = both[:ROWS]
+    send_ref[...] = both[ROWS:].astype(jnp.bfloat16)
+
+
+def relay_kernel(place_ref, far_ref, near_ref, side_ref, eight_ref, four_ref):
+    side = side_ref[...].astype(jnp.float32)
+    upper = is_upper(place_ref)
+    eight_ref[...] = (far_ref[...] + side * upper).astype(jnp.bfloat16)
+    four_ref[...] = (near_ref[...] + side * (1 - upper)).astype(jnp.bfloat16)
+
+
+def gather_kernel(own_ref, back_ref, two_ref, out_ref):
     total = own_ref[...] + back_ref[2 * ROWS :, :].astype(jnp.float32)
-    total = total + side_ref[...].astype(jnp.float32) * (1 - is_upper(place_ref))
-    out_ref[...] = total + two_ref[...].astype(jnp.float32) + four_ref[...].astype(jnp.float32)
-
-
-def finish_kernel(sum_ref, eight_ref, k_ref, v_ref):
-    total = (sum_ref[...] + eight_ref[...].astype(jnp.float32)).astype(jnp.bfloat16)
+    out_ref[...] = total + two_ref[...].astype(jnp.float32)
+
+
+def finish_kernel(sum_ref, four_ref, eight_ref, k_ref, v_ref):
+    total = sum_ref[...] + four_ref[...].astype(jnp.float32) + eight_ref[...].astype(jnp.float32)
+    total = total.astype(jnp.bfloat16)
     k_ref[...] = total[:, :D]
     v_ref[...] = total[:, D:]
 
@@ -449,8 +452,7 @@
     far_keep, far_side = call(
         "settle_far", settle_kernel, (shape(ROWS, 2 * D, f32), shape(ROWS, 2 * D, bf16)), vmem(2), (far_own, far_back)
     )
-    count = lax.axis_size("ctx")
-    far_side = moved(far_side, "ctx", lambda i: (i + 2 if i // 2 % 2 == 0 else i - 6) % count)
+    far_side = moved(far_side, "ctx", lambda i: i ^ 2)
     near_own, st = call(
         "own_near",
         functools.partial(own_kernel, (2, 3)),
@@ -459,13 +461,19 @@
         (q4, own, p_near, p_side, g4, st, far_keep),
         flops=FL,
     )
-    by_four, by_two = call(
-        "settle_near", settle_kernel, (shape(ROWS, 2 * D, bf16), shape(ROWS, 2 * D, bf16)), vmem(2), (near_own, near_back)
-    )
-    by_four = turned(by_four, "ctx", -4)
+    near_keep, by_two = call(
+        "settle_near", settle_kernel, (shape(ROWS, 2 * D, f32), shape(ROWS, 2 * D, bf16)), vmem(2), (near_own, near_back)
+    )
     by_two = turned(by_two, "ctx", -2)
-    to_eight = call("relay_far", relay_far, shape(ROWS, 2 * D, bf16), smem(1) + vmem(2), (place, far_keep, far_side))
-    by_eight = turned(to_eight, "ctx", -8)
+    to_eight, to_four = call(
+        "relay",
+        relay_kernel,
+        (shape(ROWS, 2 * D, bf16), shape(ROWS, 2 * D, bf16)),
+        smem(1) + vmem(3),
+        (place, far_keep, near_keep, far_side),
+    )
+    by_eight = turned(to_eight, "ctx", -2 * PLANE)
+    by_four = turned(to_four, "ctx", -PLANE)
     last_own, grad_queries = call(
         "own_last",
         functools.partial(own_kernel, (4,)),
@@ -474,15 +482,10 @@
         (q4, own, p_near, p_side, g4, st, to_eight),
     )
     partial_sum = call(
-        "gather_near",
-        gather_kernel,
-        shape(ROWS, 2 * D, f32),
-        smem(1) + vmem(5),
-        (place, last_own, near_back, far_side, by_two, by_four),
-        flops=COSTLY,
+        "gather_near", gather_kernel, shape(ROWS, 2 * D, f32), vmem(3), (last_own, near_back, by_two), flops=COSTLY
     )
     grad_keys, grad_values = call(
-        "finish", finish_kernel, (shape(ROWS, D, bf16), shape(ROWS, D, bf16)), vmem(2), (partial_sum, by_eight)
+        "finish", finish_kernel, (shape(ROWS, D, bf16), shape(ROWS, D, bf16)), vmem(3), (partial_sum, by_four, by_eight)
     )
     return grad_queries, grad_keys, grad_values
 

time: 51.5 us -> 50.8 us (0.986)
  waiting for transfers between devices: 14 us -> 12.4 us
  starting transfers between devices: 22.3 us -> 23.3 us
    ppermute x17, waiting for transfers between devices: 14 us -> 12.4 us  [moved(): lax.ppermute(x, axis, [(i, to(i)) for i in range(lax.axis_size(axis))])]
    ppermute x17, starting transfers between devices: 22.3 us -> 23.3 us  [moved(): lax.ppermute(x, axis, [(i, to(i)) for i in range(lax.axis_size(axis))])]
  transfers between devices with their start and end apart: 17 -> 17, of which waited for: 6 -> 5; matrix products, arithmetic and copies ran while one was open for 2% -> 2% of each run, Pallas kernels for 20% -> 20%
where the time goes in v15:
time: 50.8 us; the launch traced here: 50.7 us
  starting transfers between devices  23.3 us (46%)
  Pallas kernels  13.3 us (26%)
  waiting for transfers between devices  12.4 us (24%)
  between operations  0.85 us (2%)
  other arithmetic  0.83 us (2%)
    ppermute x17, starting transfers between devices, moved(): lax.ppermute(x, axis, [(i, to(i)) for i in range(lax.axis_size(axis))])  23.3 us
    pallas_call x20, Pallas kernels, call(): pl.pallas_call(kernel, out_shape=outs, in_specs=ins, out_specs=vmem(1)[0]...  13.3 us
    ppermute x17, waiting for transfers between devices, moved(): lax.ppermute(x, axis, [(i, to(i)) for i in range(lax.axis_size(axis))])  12.4 us
  transfers between devices with their start and end apart: 17, of which 5 were waited for; matrix products, arithmetic and copies ran while one was open for 2% of the time, Pallas kernels for 20%

profile of v15, /device:TPU:64, one launch (start us, length us, event | category | flops | bytes accessed | tf_op | source)
XLA Modules:
  0.0 50.7 jit_solution(5557784769330878681)
XLA Ops:
  0.6 3.3 %collective-permute-start.2 = (bf16[192,512]{1,0:T(8,128)(2,1)}, bf16[192,512]{1,0:T(8,128)(2,1)S(1)}, u32[]{:S(2)}, u32[]{:S(2)}) collective-permute-start(bf16[192,512]{1,0:T(8,128)(2,1)} %refs_0_.1), channel_id=1, source_target_pairs={{0,1},{1,0},{2,3},{3,2},{4,5},{5,4},{6,7},{7,6},{8,9},{9,8},{10,11... | collective-permute-start | bytes 589832 | tf_op jit(solution)/shard_map/ppermute | solution.py:341
  3.9 1.5 %collective-permute-start.3 = (bf16[192,512]{1,0:T(8,128)(2,1)}, bf16[192,512]{1,0:T(8,128)(2,1)S(1)}, u32[]{:S(2)}, u32[]{:S(2)}) collective-permute-start(bf16[192,512]{1,0:T(8,128)(2,1)} %refs_0_.1), channel_id=1, source_target_pairs={{0,2},{1,3},{2,4},{3,5},{4,6},{5,7},{6,0},{7,1},{8,10},{9,11},{10,... | collective-permute-start | bytes 589832 | tf_op jit(solution)/shard_map/ppermute | solution.py:341
  5.4 1.7 %collective-permute-start.4 = (bf16[192,512]{1,0:T(8,128)(2,1)}, bf16[192,512]{1,0:T(8,128)(2,1)S(1)}, u32[]{:S(2)}, u32[]{:S(2)}) collective-permute-start(bf16[192,512]{1,0:T(8,128)(2,1)} %refs_0_.1), channel_id=1, source_target_pairs={{0,6},{1,7},{2,0},{3,1},{4,2},{5,3},{6,4},{7,5},{8,14},{9,15},{10,... | collective-permute-start | bytes 589832 | tf_op jit(solution)/shard_map/ppermute | solution.py:341
  7.1 0.8 %pad_add_fusion.z0_ref = bf16[192,256]{1,0:T(8,128)(2,1)S(1)} fusion(bf16[192,128]{1,0:T(8,128)(2,1)} %param.8, bf16[192,128]{1,0:T(8,128)(2,1)} %param.7), kind=kLoop, calls=%fused_computation | loop fusion | flops 196608 | bytes 196608 | tf_op jit(solution)/shard_map/add | solution.py:378
  8.0 4.6 %collective-permute-start = (bf16[192,256]{1,0:T(8,128)(2,1)S(1)}, bf16[192,256]{1,0:T(8,128)(2,1)S(1)}, u32[]{:S(2)}, u32[]{:S(2)}) collective-permute-start(bf16[192,256]{1,0:T(8,128)(2,1)S(1)} %pad_add_fusion.z0_ref), channel_id=1, source_target_pairs={{0,64},{8,72},{16,80},{24,88},{32,96},{40,104},{48,112},{56,120},{... | collective-permute-start | bytes 294920 | tf_op jit(solution)/shard_map/ppermute | solution.py:341
  12.5 1.0 %collective-permute-start.1 = (bf16[192,256]{1,0:T(8,128)(2,1)S(1)}, bf16[192,256]{1,0:T(8,128)(2,1)S(1)}, u32[]{:S(2)}, u32[]{:S(2)}) collective-permute-start(bf16[192,256]{1,0:T(8,128)(2,1)S(1)} %pad_add_fusion.z0_ref), channel_id=1, source_target_pairs={{0,32},{8,40},{16,48},{24,56},{32,64},{40,72},{48,80},{56,88},{64,... | collective-permute-start | bytes 294920 | tf_op jit(solution)/shard_map/ppermute | solution.py:341
  13.6 2.3 %load.1 = (bf16[768,128]{1,0:T(8,128)(2,1)S(1)}, f32[8,768]{1,0:T(8,128)S(1)}, bf16[512,4096]{1,0:T(8,128)(2,1)S(1)}) custom-call(s32[1]{0:T(128)} %bitcast.place_ref, s32[1]{0:T(128)} %bitcast.1.head_ref, s32[8]{0:T(128)} %len_hbm.1, bf16[192,512]{1,0:T(8,128)(2,1)} %q_hbm.1, bf16[512,4096]{1,0:T(8,128)(2,1)} %w_hbm.1), custom_call_target="tpu_custom_call" | custom-call | flops 1 | bytes 1 | tf_op jit(solution)/shard_map/load/pallas_call | solution.py:355
  15.9 1.6 %collective-permute-start.7 = (bf16[192,512]{1,0:T(8,128)(2,1)S(1)}, bf16[192,512]{1,0:T(8,128)(2,1)S(1)}, u32[]{:S(2)}, u32[]{:S(2)}) collective-permute-start(bf16[192,512]{1,0:T(8,128)(2,1)S(1)} %stage.1.refs_0_.refs_1_), channel_id=1, source_target_pairs={{0,6},{1,7},{2,0},{3,1},{4,2},{5,3},{6,4},{7,5},{8,14},{9,15},{10,... | collective-permute-start | bytes 589832 | tf_op jit(solution)/shard_map/ppermute | solution.py:341
  17.6 0.5 collective-permute-start.6
  18.1 0.8 %collective-permute-start.5 = (bf16[384,256]{1,0:T(8,128)(2,1)S(1)}, bf16[384,256]{1,0:T(8,128)(2,1)S(1)}, u32[]{:S(2)}, u32[]{:S(2)}) collective-permute-start(bf16[384,256]{1,0:T(8,128)(2,1)S(1)} %pick_side.1.refs_0_), channel_id=1, source_target_pairs={{0,16},{8,24},{16,0},{24,8},{32,48},{40,56},{48,32},{56,40},{64,80... | collective-permute-start | bytes 589832 | tf_op jit(solution)/shard_map/ppermute | solution.py:341
  18.9 0.3 collective-permute-start.9
  19.2 2.6 %collective-permute-done.7.refs_2_.refs_5_ = bf16[192,512]{1,0:T(8,128)(2,1)S(1)} collective-permute-done((bf16[192,512]{1,0:T(8,128)(2,1)S(1)}, bf16[192,512]{1,0:T(8,128)(2,1)S(1)}, u32[]{:S(2)}, u32[]{:S(2)}) %collective-permute-start.7) | collective-permute-done | bytes 196640 | tf_op jit(solution)/shard_map/ppermute | solution.py:341
  21.7 2.7 %collective-permute-start.8 = (bf16[192,512]{1,0:T(8,128)(2,1)S(1)}, bf16[192,512]{1,0:T(8,128)(2,1)S(1)}, u32[]{:S(2)}, u32[]{:S(2)}) collective-permute-start(bf16[192,512]{1,0:T(8,128)(2,1)S(1)} %collective-permute-done.7.refs_2_.refs_5_), channel_id=1, source_target_pairs={{0,6},{1,7},{2,0},{3,1},{4,2},{5,3},{6,4},{7,5},{8,14},{9,15},{10,... | collective-permute-start | bytes 589832 | tf_op jit(solution)/shard_map/ppermute | solution.py:341
  24.5 1.4 %collective-permute-done.6.refs_1_.refs_4_ = bf16[192,512]{1,0:T(8,128)(2,1)S(1)} collective-permute-done((bf16[192,512]{1,0:T(8,128)(2,1)S(1)}, bf16[192,512]{1,0:T(8,128)(2,1)S(1)}, u32[]{:S(2)}, u32[]{:S(2)}) %collective-permute-start.6) | collective-permute-done | bytes 196640 | tf_op jit(solution)/shard_map/ppermute | solution.py:341
  25.9 1.3 %near.1 = (bf16[576,768]{1,0:T(8,128)(2,1)S(1)}, f32[152,768]{1,0:T(8,128)S(1)}) custom-call(s32[1]{0:T(128)} %bitcast.place_ref, bf16[192,256]{1,0:T(8,128)(2,1)S(1)} %collective-permute-done.z2_ref, bf16[192,256]{1,0:T(8,128)(2,1)S(1)} %collective-permute-done.1.z1_ref, bf16[192,256]{1,0:T(8,128)(2,1)S(1)} %pad_add_fusion.z0_ref, ...), custom_call_target="tpu_custom_call" | custom-call | flops 1 | bytes 1 | tf_op jit(solution)/shard_map/near/pallas_call | solution.py:355
  27.5 0.9 %middle.1 = (bf16[384,768]{1,0:T(8,128)(2,1)S(1)}, f32[152,768]{1,0:T(8,128)S(1)}) custom-call(s32[1]{0:T(128)} %bitcast.place_ref, bf16[960,256]{1,0:T(8,128)(2,1)S(1)} %join_slots.1.own_ref, bf16[768,128]{1,0:T(8,128)(2,1)S(1)} %get-tuple-element.32.after.refs_3_.q4_ref, f32[152,768]{1,0:T(8,128)S(1)} %get-tuple-element.34.refs_0_.st_in_ref), custom_call_target="tpu_custom_call" | custom-call | flops 1 | bytes 1 | tf_op jit(solution)/shard_map/middle/pallas_call | solution.py:355
  28.4 1.4 %project.1.acc_ref = f32[192,512]{1,0:T(8,128)S(1)} custom-call(bf16[192,512]{1,0:T(8,128)(2,1)S(1)} %copy-done, bf16[192,512]{1,0:T(8,128)(2,1)S(1)} %stage.1.refs_0_.refs_1_, bf16[192,512]{1,0:T(8,128)(2,1)S(1)} %collective-permute-done.3.refs_1_.refs_2_, bf16[192,512]{1,0:T(8,128)(2,1)S(1)} %collective-permute-done.4.refs_2_.refs_3_, ...), custom_call_target="tpu_custom_call" | custom-call | flops 1 | bytes 1 | tf_op jit(solution)/shard_map/project/pallas_call | solution.py:355
  29.7 0.5 last_projection.1
  30.2 1.6 %across.1 = (bf16[768,768]{1,0:T(8,128)(2,1)S(1)}, f32[152,768]{1,0:T(8,128)S(1)}) custom-call(s32[1]{0:T(128)} %bitcast.place_ref, bf16[960,256]{1,0:T(8,128)(2,1)S(1)} %collective-permute-done.10.par_ref, bf16[768,128]{1,0:T(8,128)(2,1)S(1)} %get-tuple-element.32.after.refs_3_.q4_ref, f32[128,768]{1,0:T(8,128)S(1)} %get-tuple-element.40.gt_ref, ...), custom_call_target="tpu_custom_call" | custom-call | flops 1 | bytes 1 | tf_op jit(solution)/shard_map/across/pallas_call | solution.py:355
  31.8 0.9 %cross_far.1 = (bf16[384,256]{1,0:T(8,128)(2,1)S(1)}, f32[152,768]{1,0:T(8,128)S(1)}) custom-call(s32[1]{0:T(128)} %bitcast.place_ref, bf16[768,128]{1,0:T(8,128)(2,1)S(1)} %get-tuple-element.32.after.refs_3_.q4_ref, bf16[960,256]{1,0:T(8,128)(2,1)S(1)} %collective-permute-done.10.par_ref, bf16[768,768]{1,0:T(8,128)(2,1)S(1)} %get-tuple-element.41.p_ref, ...), custom_call_target="tpu_custom_call" | custom-call | flops 1 | bytes 1 | tf_op jit(solution)/shard_map/cross_far/pallas_call | solution.py:355
  32.9 0.8 %cross_near.1 = (bf16[576,256]{1,0:T(8,128)(2,1)S(1)}, f32[152,768]{1,0:T(8,128)S(1)}) custom-call(s32[1]{0:T(128)} %bitcast.place_ref, bf16[768,128]{1,0:T(8,128)(2,1)S(1)} %get-tuple-element.32.after.refs_3_.q4_ref, bf16[960,256]{1,0:T(8,128)(2,1)S(1)} %collective-permute-done.10.par_ref, bf16[768,768]{1,0:T(8,128)(2,1)S(1)} %get-tuple-element.41.p_ref, ...), custom_call_target="tpu_custom_call" | custom-call | flops 4000000000 | bytes 1 | tf_op jit(solution)/shard_map/cross_near/pallas_call | solution.py:355
  33.7 1.0 %collective-permute-start.12 = (bf16[576,256]{1,0:T(8,128)(2,1)S(1)}, bf16[576,256]{1,0:T(8,128)(2,1)S(1)}, u32[]{:S(2)}, u32[]{:S(2)}) collective-permute-start(bf16[576,256]{1,0:T(8,128)(2,1)S(1)} %get-tuple-element.51), channel_id=1, source_target_pairs={{0,8},{8,0},{16,24},{24,16},{32,40},{40,32},{48,56},{56,48},{64,72... | collective-permute-start | bytes 884744 | tf_op jit(solution)/shard_map/ppermute | solution.py:341
  34.7 0.8 %own_far.1 = (f32[384,256]{1,0:T(8,128)S(1)}, f32[152,768]{1,0:T(8,128)S(1)}) custom-call(bf16[768,128]{1,0:T(8,128)(2,1)S(1)} %get-tuple-element.32.after.refs_3_.q4_ref, bf16[960,256]{1,0:T(8,128)(2,1)S(1)} %join_slots.1.own_ref, bf16[576,768]{1,0:T(8,128)(2,1)S(1)} %get-tuple-element.35.near_ref, bf16[384,768]{1,0:T(8,128)(2,1)S(1)} %get-tuple-element.36.side_ref, ...), custom_call_target="tpu_custom_call" | custom-call | flops 4000000000 | bytes 1 | tf_op jit(solution)/shard_map/own_far/pallas_call | solution.py:355
  35.6 0.8 %collective-permute-start.13 = (bf16[192,256]{1,0:T(8,128)(2,1)S(1)}, bf16[192,256]{1,0:T(8,128)(2,1)S(1)}, u32[]{:S(2)}, u32[]{:S(2)}) collective-permute-start(bf16[192,256]{1,0:T(8,128)(2,1)S(1)} %get-tuple-element.53), channel_id=1, source_target_pairs={{0,16},{8,24},{16,0},{24,8},{32,48},{40,56},{48,32},{56,40},{64,80... | collective-permute-start | bytes 294920 | tf_op jit(solution)/shard_map/ppermute | solution.py:341
  36.3 0.8 %own_near.1 = (f32[384,256]{1,0:T(8,128)S(1)}, f32[152,768]{1,0:T(8,128)S(1)}) custom-call(bf16[768,128]{1,0:T(8,128)(2,1)S(1)} %get-tuple-element.32.after.refs_3_.q4_ref, bf16[960,256]{1,0:T(8,128)(2,1)S(1)} %join_slots.1.own_ref, bf16[576,768]{1,0:T(8,128)(2,1)S(1)} %get-tuple-element.35.near_ref, bf16[384,768]{1,0:T(8,128)(2,1)S(1)} %get-tuple-element.36.side_ref, ...), custom_call_target="tpu_custom_call" | custom-call | flops 4000000000 | bytes 1 | tf_op jit(solution)/shard_map/own_near/pallas_call | solution.py:355
  37.2 1.9 %collective-permute-start.14 = (bf16[192,256]{1,0:T(8,128)(2,1)S(1)}, bf16[192,256]{1,0:T(8,128)(2,1)S(1)}, u32[]{:S(2)}, u32[]{:S(2)}) collective-permute-start(bf16[192,256]{1,0:T(8,128)(2,1)S(1)} %get-tuple-element.57), channel_id=1, source_target_pairs={{0,240},{8,248},{16,0},{24,8},{32,16},{40,24},{48,32},{56,40},{64,... | collective-permute-start | bytes 294920 | tf_op jit(solution)/shard_map/ppermute | solution.py:341
  39.0 2.1 %collective-permute-done.13.side_ref = bf16[192,256]{1,0:T(8,128)(2,1)S(1)} collective-permute-done((bf16[192,256]{1,0:T(8,128)(2,1)S(1)}, bf16[192,256]{1,0:T(8,128)(2,1)S(1)}, u32[]{:S(2)}, u32[]{:S(2)}) %collective-permute-start.13) | collective-permute-done | bytes 98336 | tf_op jit(solution)/shard_map/ppermute | solution.py:341
  41.3 1.2 %own_last.1 = (f32[192,256]{1,0:T(8,128)S(1)}, bf16[192,512]{1,0:T(8,128)(2,1)}) custom-call(bf16[768,128]{1,0:T(8,128)(2,1)S(1)} %get-tuple-element.32.after.refs_3_.q4_ref, bf16[960,256]{1,0:T(8,128)(2,1)S(1)} %join_slots.1.own_ref, bf16[576,768]{1,0:T(8,128)(2,1)S(1)} %get-tuple-element.35.near_ref, bf16[384,768]{1,0:T(8,128)(2,1)S(1)} %get-tuple-element.36.side_ref, ...), custom_call_target="tpu_custom_call" | custom-call | flops 1 | bytes 1 | tf_op jit(solution)/shard_map/own_last/pallas_call | solution.py:355
  42.5 1.2 %collective-permute-start.15 = (bf16[192,256]{1,0:T(8,128)(2,1)S(1)}, bf16[192,256]{1,0:T(8,128)(2,1)S(1)}, u32[]{:S(2)}, u32[]{:S(2)}) collective-permute-start(bf16[192,256]{1,0:T(8,128)(2,1)S(1)} %get-tuple-element.58), channel_id=1, source_target_pairs={{0,224},{8,232},{16,240},{24,248},{32,0},{40,8},{48,16},{56,24},{6... | collective-permute-start | bytes 294920 | tf_op jit(solution)/shard_map/ppermute | solution.py:341
  43.7 5.0 %collective-permute-done.15.four_ref = bf16[192,256]{1,0:T(8,128)(2,1)S(1)} collective-permute-done((bf16[192,256]{1,0:T(8,128)(2,1)S(1)}, bf16[192,256]{1,0:T(8,128)(2,1)S(1)}, u32[]{:S(2)}, u32[]{:S(2)}) %collective-permute-start.15) | collective-permute-done | bytes 98336 | tf_op jit(solution)/shard_map/ppermute | solution.py:341
  48.7 1.3 %collective-permute-done.16.eight_ref = bf16[192,256]{1,0:T(8,128)(2,1)S(1)} collective-permute-done((bf16[192,256]{1,0:T(8,128)(2,1)S(1)}, bf16[192,256]{1,0:T(8,128)(2,1)S(1)}, u32[]{:S(2)}, u32[]{:S(2)}) %collective-permute-start.16) | collective-permute-done | bytes 98336 | tf_op jit(solution)/shard_map/ppermute | solution.py:341
  50.0 0.7 %finish.1 = (bf16[192,128]{1,0:T(8,128)(2,1)}, bf16[192,128]{1,0:T(8,128)(2,1)}) custom-call(f32[192,256]{1,0:T(8,128)S(1)} %gather_near.1.sum_ref, bf16[192,256]{1,0:T(8,128)(2,1)S(1)} %collective-permute-done.15.four_ref, bf16[192,256]{1,0:T(8,128)(2,1)S(1)} %collective-permute-done.16.eight_ref), custom_call_target="tpu_custom_call" | custom-call | flops 1 | bytes 1 | tf_op jit(solution)/shard_map/finish/pallas_call | solution.py:355
  (25 shorter events, 0.7 us)
Async XLA Ops:
  0.6 15.3 %collective-permute-start.2 = (bf16[192,512]{1,0:T(8,128)(2,1)}, bf16[192,512]{1,0:T(8,128)(2,1)S(1)}, u32[]{:S(2)}, u32[]{:S(2)}) collective-permute-start(bf16[192,512]{1,0:T(8,128)(2,1)} %refs_0_.1), channel_id=1, source_target_pairs={{0,1},{1,0},{2,3},{3,2},{4,5},{5,4},{6,7},{7,6},{8,9},{9,8},{10,11... | collective-permute-start | bytes 589832 | tf_op jit(solution)/shard_map/ppermute | solution.py:341
  3.9 13.7 %collective-permute-start.3 = (bf16[192,512]{1,0:T(8,128)(2,1)}, bf16[192,512]{1,0:T(8,128)(2,1)S(1)}, u32[]{:S(2)}, u32[]{:S(2)}) collective-permute-start(bf16[192,512]{1,0:T(8,128)(2,1)} %refs_0_.1), channel_id=1, source_target_pairs={{0,2},{1,3},{2,4},{3,5},{4,6},{5,7},{6,0},{7,1},{8,10},{9,11},{10,... | collective-permute-start | bytes 589832 | tf_op jit(solution)/shard_map/ppermute | solution.py:341
  5.4 12.7 %collective-permute-start.4 = (bf16[192,512]{1,0:T(8,128)(2,1)}, bf16[192,512]{1,0:T(8,128)(2,1)S(1)}, u32[]{:S(2)}, u32[]{:S(2)}) collective-permute-start(bf16[192,512]{1,0:T(8,128)(2,1)} %refs_0_.1), channel_id=1, source_target_pairs={{0,6},{1,7},{2,0},{3,1},{4,2},{5,3},{6,4},{7,5},{8,14},{9,15},{10,... | collective-permute-start | bytes 589832 | tf_op jit(solution)/shard_map/ppermute | solution.py:341
  8.0 10.1 %collective-permute-start = (bf16[192,256]{1,0:T(8,128)(2,1)S(1)}, bf16[192,256]{1,0:T(8,128)(2,1)S(1)}, u32[]{:S(2)}, u32[]{:S(2)}) collective-permute-start(bf16[192,256]{1,0:T(8,128)(2,1)S(1)} %pad_add_fusion.z0_ref), channel_id=1, source_target_pairs={{0,64},{8,72},{16,80},{24,88},{32,96},{40,104},{48,112},{56,120},{... | collective-permute-start | bytes 294920 | tf_op jit(solution)/shard_map/ppermute | solution.py:341
  12.5 5.5 %collective-permute-start.1 = (bf16[192,256]{1,0:T(8,128)(2,1)S(1)}, bf16[192,256]{1,0:T(8,128)(2,1)S(1)}, u32[]{:S(2)}, u32[]{:S(2)}) collective-permute-start(bf16[192,256]{1,0:T(8,128)(2,1)S(1)} %pad_add_fusion.z0_ref), channel_id=1, source_target_pairs={{0,32},{8,40},{16,48},{24,56},{32,64},{40,72},{48,80},{56,88},{64,... | collective-permute-start | bytes 294920 | tf_op jit(solution)/shard_map/ppermute | solution.py:341
  13.6 14.8 %copy-start = (bf16[192,512]{1,0:T(8,128)(2,1)S(1)}, bf16[192,512]{1,0:T(8,128)(2,1)}, u32[]{:S(2)}) copy-start(bf16[192,512]{1,0:T(8,128)(2,1)} %refs_0_.1) | copy-start | bytes 589828
  15.9 5.8 %collective-permute-start.7 = (bf16[192,512]{1,0:T(8,128)(2,1)S(1)}, bf16[192,512]{1,0:T(8,128)(2,1)S(1)}, u32[]{:S(2)}, u32[]{:S(2)}) collective-permute-start(bf16[192,512]{1,0:T(8,128)(2,1)S(1)} %stage.1.refs_0_.refs_1_), channel_id=1, source_target_pairs={{0,6},{1,7},{2,0},{3,1},{4,2},{5,3},{6,4},{7,5},{8,14},{9,15},{10,... | collective-permute-start | bytes 589832 | tf_op jit(solution)/shard_map/ppermute | solution.py:341
  17.6 8.3 %collective-permute-start.6 = (bf16[192,512]{1,0:T(8,128)(2,1)S(1)}, bf16[192,512]{1,0:T(8,128)(2,1)S(1)}, u32[]{:S(2)}, u32[]{:S(2)}) collective-permute-start(bf16[192,512]{1,0:T(8,128)(2,1)S(1)} %stage.1.refs_0_.refs_1_), channel_id=1, source_target_pairs={{0,2},{1,3},{2,4},{3,5},{4,6},{5,7},{6,0},{7,1},{8,10},{9,11},{10,... | collective-permute-start | bytes 589832 | tf_op jit(solution)/shard_map/ppermute | solution.py:341
  18.1 9.0 %collective-permute-start.5 = (bf16[384,256]{1,0:T(8,128)(2,1)S(1)}, bf16[384,256]{1,0:T(8,128)(2,1)S(1)}, u32[]{:S(2)}, u32[]{:S(2)}) collective-permute-start(bf16[384,256]{1,0:T(8,128)(2,1)S(1)} %pick_side.1.refs_0_), channel_id=1, source_target_pairs={{0,16},{8,24},{16,0},{24,8},{32,48},{40,56},{48,32},{56,40},{64,80... | collective-permute-start | bytes 589832 | tf_op jit(solution)/shard_map/ppermute | solution.py:341
  18.9 9.5 %collective-permute-start.9 = (bf16[192,512]{1,0:T(8,128)(2,1)S(1)}, bf16[192,512]{1,0:T(8,128)(2,1)S(1)}, u32[]{:S(2)}, u32[]{:S(2)}) collective-permute-start(bf16[192,512]{1,0:T(8,128)(2,1)S(1)} %collective-permute-done.3.refs_1_.refs_2_), channel_id=1, source_target_pairs={{0,2},{1,3},{2,4},{3,5},{4,6},{5,7},{6,0},{7,1},{8,10},{9,11},{10,... | collective-permute-start | bytes 589832 | tf_op jit(solution)/shard_map/ppermute | solution.py:341
  21.7 8.0 %collective-permute-start.8 = (bf16[192,512]{1,0:T(8,128)(2,1)S(1)}, bf16[192,512]{1,0:T(8,128)(2,1)S(1)}, u32[]{:S(2)}, u32[]{:S(2)}) collective-permute-start(bf16[192,512]{1,0:T(8,128)(2,1)S(1)} %collective-permute-done.7.refs_2_.refs_5_), channel_id=1, source_target_pairs={{0,6},{1,7},{2,0},{3,1},{4,2},{5,3},{6,4},{7,5},{8,14},{9,15},{10,... | collective-permute-start | bytes 589832 | tf_op jit(solution)/shard_map/ppermute | solution.py:341
  27.2 3.0 %collective-permute-start.10 = (bf16[960,256]{1,0:T(8,128)(2,1)S(1)}, bf16[960,256]{1,0:T(8,128)(2,1)S(1)}, u32[]{:S(2)}, u32[]{:S(2)}) collective-permute-start(bf16[960,256]{1,0:T(8,128)(2,1)S(1)} %join_slots.1.own_ref), channel_id=1, source_target_pairs={{0,8},{8,0},{16,24},{24,16},{32,40},{40,32},{48,56},{56,48},{64,72... | collective-permute-start | bytes 1474568 | tf_op jit(solution)/shard_map/ppermute | solution.py:341
  32.7 2.8 %collective-permute-start.11 = (bf16[384,256]{1,0:T(8,128)(2,1)S(1)}, bf16[384,256]{1,0:T(8,128)(2,1)S(1)}, u32[]{:S(2)}, u32[]{:S(2)}) collective-permute-start(bf16[384,256]{1,0:T(8,128)(2,1)S(1)} %get-tuple-element.47), channel_id=1, source_target_pairs={{0,8},{8,0},{16,24},{24,16},{32,40},{40,32},{48,56},{56,48},{64,72... | collective-permute-start | bytes 589832 | tf_op jit(solution)/shard_map/ppermute | solution.py:341
  33.7 3.5 %collective-permute-start.12 = (bf16[576,256]{1,0:T(8,128)(2,1)S(1)}, bf16[576,256]{1,0:T(8,128)(2,1)S(1)}, u32[]{:S(2)}, u32[]{:S(2)}) collective-permute-start(bf16[576,256]{1,0:T(8,128)(2,1)S(1)} %get-tuple-element.51), channel_id=1, source_target_pairs={{0,8},{8,0},{16,24},{24,16},{32,40},{40,32},{48,56},{56,48},{64,72... | collective-permute-start | bytes 884744 | tf_op jit(solution)/shard_map/ppermute | solution.py:341
  35.6 5.6 %collective-permute-start.13 = (bf16[192,256]{1,0:T(8,128)(2,1)S(1)}, bf16[192,256]{1,0:T(8,128)(2,1)S(1)}, u32[]{:S(2)}, u32[]{:S(2)}) collective-permute-start(bf16[192,256]{1,0:T(8,128)(2,1)S(1)} %get-tuple-element.53), channel_id=1, source_target_pairs={{0,16},{8,24},{16,0},{24,8},{32,48},{40,56},{48,32},{56,40},{64,80... | collective-permute-start | bytes 294920 | tf_op jit(solution)/shard_map/ppermute | solution.py:341
  37.2 6.5 %collective-permute-start.14 = (bf16[192,256]{1,0:T(8,128)(2,1)S(1)}, bf16[192,256]{1,0:T(8,128)(2,1)S(1)}, u32[]{:S(2)}, u32[]{:S(2)}) collective-permute-start(bf16[192,256]{1,0:T(8,128)(2,1)S(1)} %get-tuple-element.57), channel_id=1, source_target_pairs={{0,240},{8,248},{16,0},{24,8},{32,16},{40,24},{48,32},{56,40},{64,... | collective-permute-start | bytes 294920 | tf_op jit(solution)/shard_map/ppermute | solution.py:341
  41.2 8.8 %collective-permute-start.16 = (bf16[192,256]{1,0:T(8,128)(2,1)S(1)}, bf16[192,256]{1,0:T(8,128)(2,1)S(1)}, u32[]{:S(2)}, u32[]{:S(2)}) collective-permute-start(bf16[192,256]{1,0:T(8,128)(2,1)S(1)} %get-tuple-element.54.refs_0_), channel_id=1, source_target_pairs={{0,192},{8,200},{16,208},{24,216},{32,224},{40,232},{48,240},{56,2... | collective-permute-start | bytes 294920 | tf_op jit(solution)/shard_map/ppermute | solution.py:341
  42.5 6.2 %collective-permute-start.15 = (bf16[192,256]{1,0:T(8,128)(2,1)S(1)}, bf16[192,256]{1,0:T(8,128)(2,1)S(1)}, u32[]{:S(2)}, u32[]{:S(2)}) collective-permute-start(bf16[192,256]{1,0:T(8,128)(2,1)S(1)} %get-tuple-element.58), channel_id=1, source_target_pairs={{0,224},{8,232},{16,240},{24,248},{32,0},{40,8},{48,16},{56,24},{6... | collective-permute-start | bytes 294920 | tf_op jit(solution)/shard_map/ppermute | solution.py:341

commit v16 on v15

--- a/solution.py
+++ b/solution.py
@@ -314,7 +314,7 @@
     out_ref[...] = total + two_ref[...].astype(jnp.float32)
 
 
-def finish_kernel(sum_ref, four_ref, eight_ref, k_ref, v_ref):
+def finish_kernel(sum_ref, eight_ref, four_ref, k_ref, v_ref):
     total = sum_ref[...] + four_ref[...].astype(jnp.float32) + eight_ref[...].astype(jnp.float32)
     total = total.astype(jnp.bfloat16)
     k_ref[...] = total[:, :D]
@@ -478,14 +478,15 @@
         "own_last",
         functools.partial(own_kernel, (4,)),
         (shape(ROWS, 2 * D, f32), shape(ROWS, HEADS * D, bf16)),
-        vmem(6) + token(1),
-        (q4, own, p_near, p_side, g4, st, to_eight),
+        vmem(6) + token(2),
+        (q4, own, p_near, p_side, g4, st, to_eight, by_two),
+        flops=COSTLY,
     )
     partial_sum = call(
-        "gather_near", gather_kernel, shape(ROWS, 2 * D, f32), vmem(3), (last_own, near_back, by_two), flops=COSTLY
+        "gather_near", gather_kernel, shape(ROWS, 2 * D, f32), vmem(3), (last_own, near_back, by_two)
     )
     grad_keys, grad_values = call(
-        "finish", finish_kernel, (shape(ROWS, D, bf16), shape(ROWS, D, bf16)), vmem(3), (partial_sum, by_four, by_eight)
+        "finish", finish_kernel, (shape(ROWS, D, bf16), shape(ROWS, D, bf16)), vmem(3), (partial_sum, by_eight, by_four)
     )
     return grad_queries, grad_keys, grad_values
 

time: 50.8 us -> 50.6 us (level)
  waiting for transfers between devices: 12.4 us -> 11.7 us
    ppermute x17, waiting for transfers between devices: 12.4 us -> 11.7 us  [moved(): lax.ppermute(x, axis, [(i, to(i)) for i in range(lax.axis_size(axis))])]
where the time goes in v16:
time: 50.6 us; the launch traced here: 50 us
  starting transfers between devices  23.3 us (46%)
  Pallas kernels  13.4 us (26%)
  waiting for transfers between devices  11.7 us (23%)
  between operations  0.84 us (2%)
  other arithmetic  0.83 us (2%)
    ppermute x17, starting transfers between devices, moved(): lax.ppermute(x, axis, [(i, to(i)) for i in range(lax.axis_size(axis))])  23.3 us
    pallas_call x20, Pallas kernels, call(): pl.pallas_call(kernel, out_shape=outs, in_specs=ins, out_specs=vmem(1)[0]...  13.4 us
    ppermute x17, waiting for transfers between devices, moved(): lax.ppermute(x, axis, [(i, to(i)) for i in range(lax.axis_size(axis))])  11.7 us
  transfers between devices with their start and end apart: 17, of which 5 were waited for; matrix products, arithmetic and copies ran while one was open for 2% of the time, Pallas kernels for 20%

profile of v16, /device:TPU:64, one launch (start us, length us, event | category | flops | bytes accessed | tf_op | source)
XLA Modules:
  0.0 50.0 jit_solution(4796910524359169388)
XLA Ops:
  0.6 3.3 %collective-permute-start.2 = (bf16[192,512]{1,0:T(8,128)(2,1)}, bf16[192,512]{1,0:T(8,128)(2,1)S(1)}, u32[]{:S(2)}, u32[]{:S(2)}) collective-permute-start(bf16[192,512]{1,0:T(8,128)(2,1)} %refs_0_.1), channel_id=1, source_target_pairs={{0,1},{1,0},{2,3},{3,2},{4,5},{5,4},{6,7},{7,6},{8,9},{9,8},{10,11... | collective-permute-start | bytes 589832 | tf_op jit(solution)/shard_map/ppermute | solution.py:341
  3.9 1.5 %collective-permute-start.3 = (bf16[192,512]{1,0:T(8,128)(2,1)}, bf16[192,512]{1,0:T(8,128)(2,1)S(1)}, u32[]{:S(2)}, u32[]{:S(2)}) collective-permute-start(bf16[192,512]{1,0:T(8,128)(2,1)} %refs_0_.1), channel_id=1, source_target_pairs={{0,2},{1,3},{2,4},{3,5},{4,6},{5,7},{6,0},{7,1},{8,10},{9,11},{10,... | collective-permute-start | bytes 589832 | tf_op jit(solution)/shard_map/ppermute | solution.py:341
  5.4 1.7 %collective-permute-start.4 = (bf16[192,512]{1,0:T(8,128)(2,1)}, bf16[192,512]{1,0:T(8,128)(2,1)S(1)}, u32[]{:S(2)}, u32[]{:S(2)}) collective-permute-start(bf16[192,512]{1,0:T(8,128)(2,1)} %refs_0_.1), channel_id=1, source_target_pairs={{0,6},{1,7},{2,0},{3,1},{4,2},{5,3},{6,4},{7,5},{8,14},{9,15},{10,... | collective-permute-start | bytes 589832 | tf_op jit(solution)/shard_map/ppermute | solution.py:341
  7.1 0.8 %pad_add_fusion.z0_ref = bf16[192,256]{1,0:T(8,128)(2,1)S(1)} fusion(bf16[192,128]{1,0:T(8,128)(2,1)} %param.8, bf16[192,128]{1,0:T(8,128)(2,1)} %param.7), kind=kLoop, calls=%fused_computation | loop fusion | flops 196608 | bytes 196608 | tf_op jit(solution)/shard_map/add | solution.py:378
  8.0 4.6 %collective-permute-start = (bf16[192,256]{1,0:T(8,128)(2,1)S(1)}, bf16[192,256]{1,0:T(8,128)(2,1)S(1)}, u32[]{:S(2)}, u32[]{:S(2)}) collective-permute-start(bf16[192,256]{1,0:T(8,128)(2,1)S(1)} %pad_add_fusion.z0_ref), channel_id=1, source_target_pairs={{0,64},{8,72},{16,80},{24,88},{32,96},{40,104},{48,112},{56,120},{... | collective-permute-start | bytes 294920 | tf_op jit(solution)/shard_map/ppermute | solution.py:341
  12.5 1.0 %collective-permute-start.1 = (bf16[192,256]{1,0:T(8,128)(2,1)S(1)}, bf16[192,256]{1,0:T(8,128)(2,1)S(1)}, u32[]{:S(2)}, u32[]{:S(2)}) collective-permute-start(bf16[192,256]{1,0:T(8,128)(2,1)S(1)} %pad_add_fusion.z0_ref), channel_id=1, source_target_pairs={{0,32},{8,40},{16,48},{24,56},{32,64},{40,72},{48,80},{56,88},{64,... | collective-permute-start | bytes 294920 | tf_op jit(solution)/shard_map/ppermute | solution.py:341
  13.6 2.3 %load.1 = (bf16[768,128]{1,0:T(8,128)(2,1)S(1)}, f32[8,768]{1,0:T(8,128)S(1)}, bf16[512,4096]{1,0:T(8,128)(2,1)S(1)}) custom-call(s32[1]{0:T(128)} %bitcast.place_ref, s32[1]{0:T(128)} %bitcast.1.head_ref, s32[8]{0:T(128)} %len_hbm.1, bf16[192,512]{1,0:T(8,128)(2,1)} %q_hbm.1, bf16[512,4096]{1,0:T(8,128)(2,1)} %w_hbm.1), custom_call_target="tpu_custom_call" | custom-call | flops 1 | bytes 1 | tf_op jit(solution)/shard_map/load/pallas_call | solution.py:355
  15.9 1.6 %collective-permute-start.7 = (bf16[192,512]{1,0:T(8,128)(2,1)S(1)}, bf16[192,512]{1,0:T(8,128)(2,1)S(1)}, u32[]{:S(2)}, u32[]{:S(2)}) collective-permute-start(bf16[192,512]{1,0:T(8,128)(2,1)S(1)} %stage.1.refs_0_.refs_1_), channel_id=1, source_target_pairs={{0,6},{1,7},{2,0},{3,1},{4,2},{5,3},{6,4},{7,5},{8,14},{9,15},{10,... | collective-permute-start | bytes 589832 | tf_op jit(solution)/shard_map/ppermute | solution.py:341
  17.6 0.5 collective-permute-start.6
  18.1 0.8 %collective-permute-start.5 = (bf16[384,256]{1,0:T(8,128)(2,1)S(1)}, bf16[384,256]{1,0:T(8,128)(2,1)S(1)}, u32[]{:S(2)}, u32[]{:S(2)}) collective-permute-start(bf16[384,256]{1,0:T(8,128)(2,1)S(1)} %pick_side.1.refs_0_), channel_id=1, source_target_pairs={{0,16},{8,24},{16,0},{24,8},{32,48},{40,56},{48,32},{56,40},{64,80... | collective-permute-start | bytes 589832 | tf_op jit(solution)/shard_map/ppermute | solution.py:341
  18.9 0.3 collective-permute-start.9
  19.2 2.6 %collective-permute-done.7.refs_2_.refs_5_ = bf16[192,512]{1,0:T(8,128)(2,1)S(1)} collective-permute-done((bf16[192,512]{1,0:T(8,128)(2,1)S(1)}, bf16[192,512]{1,0:T(8,128)(2,1)S(1)}, u32[]{:S(2)}, u32[]{:S(2)}) %collective-permute-start.7) | collective-permute-done | bytes 196640 | tf_op jit(solution)/shard_map/ppermute | solution.py:341
  21.7 2.7 %collective-permute-start.8 = (bf16[192,512]{1,0:T(8,128)(2,1)S(1)}, bf16[192,512]{1,0:T(8,128)(2,1)S(1)}, u32[]{:S(2)}, u32[]{:S(2)}) collective-permute-start(bf16[192,512]{1,0:T(8,128)(2,1)S(1)} %collective-permute-done.7.refs_2_.refs_5_), channel_id=1, source_target_pairs={{0,6},{1,7},{2,0},{3,1},{4,2},{5,3},{6,4},{7,5},{8,14},{9,15},{10,... | collective-permute-start | bytes 589832 | tf_op jit(solution)/shard_map/ppermute | solution.py:341
  24.5 1.4 %collective-permute-done.6.refs_1_.refs_4_ = bf16[192,512]{1,0:T(8,128)(2,1)S(1)} collective-permute-done((bf16[192,512]{1,0:T(8,128)(2,1)S(1)}, bf16[192,512]{1,0:T(8,128)(2,1)S(1)}, u32[]{:S(2)}, u32[]{:S(2)}) %collective-permute-start.6) | collective-permute-done | bytes 196640 | tf_op jit(solution)/shard_map/ppermute | solution.py:341
  25.9 1.3 %near.1 = (bf16[576,768]{1,0:T(8,128)(2,1)S(1)}, f32[152,768]{1,0:T(8,128)S(1)}) custom-call(s32[1]{0:T(128)} %bitcast.place_ref, bf16[192,256]{1,0:T(8,128)(2,1)S(1)} %collective-permute-done.z2_ref, bf16[192,256]{1,0:T(8,128)(2,1)S(1)} %collective-permute-done.1.z1_ref, bf16[192,256]{1,0:T(8,128)(2,1)S(1)} %pad_add_fusion.z0_ref, ...), custom_call_target="tpu_custom_call" | custom-call | flops 1 | bytes 1 | tf_op jit(solution)/shard_map/near/pallas_call | solution.py:355
  27.5 0.9 %middle.1 = (bf16[384,768]{1,0:T(8,128)(2,1)S(1)}, f32[152,768]{1,0:T(8,128)S(1)}) custom-call(s32[1]{0:T(128)} %bitcast.place_ref, bf16[960,256]{1,0:T(8,128)(2,1)S(1)} %join_slots.1.own_ref, bf16[768,128]{1,0:T(8,128)(2,1)S(1)} %get-tuple-element.32.after.refs_3_.q4_ref, f32[152,768]{1,0:T(8,128)S(1)} %get-tuple-element.34.refs_0_.st_in_ref), custom_call_target="tpu_custom_call" | custom-call | flops 1 | bytes 1 | tf_op jit(solution)/shard_map/middle/pallas_call | solution.py:355
  28.4 1.4 %project.1.acc_ref = f32[192,512]{1,0:T(8,128)S(1)} custom-call(bf16[192,512]{1,0:T(8,128)(2,1)S(1)} %copy-done, bf16[192,512]{1,0:T(8,128)(2,1)S(1)} %stage.1.refs_0_.refs_1_, bf16[192,512]{1,0:T(8,128)(2,1)S(1)} %collective-permute-done.3.refs_1_.refs_2_, bf16[192,512]{1,0:T(8,128)(2,1)S(1)} %collective-permute-done.4.refs_2_.refs_3_, ...), custom_call_target="tpu_custom_call" | custom-call | flops 1 | bytes 1 | tf_op jit(solution)/shard_map/project/pallas_call | solution.py:355
  29.7 0.5 last_projection.1
  30.2 1.6 %across.1 = (bf16[768,768]{1,0:T(8,128)(2,1)S(1)}, f32[152,768]{1,0:T(8,128)S(1)}) custom-call(s32[1]{0:T(128)} %bitcast.place_ref, bf16[960,256]{1,0:T(8,128)(2,1)S(1)} %collective-permute-done.10.par_ref, bf16[768,128]{1,0:T(8,128)(2,1)S(1)} %get-tuple-element.32.after.refs_3_.q4_ref, f32[128,768]{1,0:T(8,128)S(1)} %get-tuple-element.40.gt_ref, ...), custom_call_target="tpu_custom_call" | custom-call | flops 1 | bytes 1 | tf_op jit(solution)/shard_map/across/pallas_call | solution.py:355
  31.8 0.9 %cross_far.1 = (bf16[384,256]{1,0:T(8,128)(2,1)S(1)}, f32[152,768]{1,0:T(8,128)S(1)}) custom-call(s32[1]{0:T(128)} %bitcast.place_ref, bf16[768,128]{1,0:T(8,128)(2,1)S(1)} %get-tuple-element.32.after.refs_3_.q4_ref, bf16[960,256]{1,0:T(8,128)(2,1)S(1)} %collective-permute-done.10.par_ref, bf16[768,768]{1,0:T(8,128)(2,1)S(1)} %get-tuple-element.41.p_ref, ...), custom_call_target="tpu_custom_call" | custom-call | flops 1 | bytes 1 | tf_op jit(solution)/shard_map/cross_far/pallas_call | solution.py:355
  32.9 0.8 %cross_near.1 = (bf16[576,256]{1,0:T(8,128)(2,1)S(1)}, f32[152,768]{1,0:T(8,128)S(1)}) custom-call(s32[1]{0:T(128)} %bitcast.place_ref, bf16[768,128]{1,0:T(8,128)(2,1)S(1)} %get-tuple-element.32.after.refs_3_.q4_ref, bf16[960,256]{1,0:T(8,128)(2,1)S(1)} %collective-permute-done.10.par_ref, bf16[768,768]{1,0:T(8,128)(2,1)S(1)} %get-tuple-element.41.p_ref, ...), custom_call_target="tpu_custom_call" | custom-call | flops 4000000000 | bytes 1 | tf_op jit(solution)/shard_map/cross_near/pallas_call | solution.py:355
  33.7 1.0 %collective-permute-start.12 = (bf16[576,256]{1,0:T(8,128)(2,1)S(1)}, bf16[576,256]{1,0:T(8,128)(2,1)S(1)}, u32[]{:S(2)}, u32[]{:S(2)}) collective-permute-start(bf16[576,256]{1,0:T(8,128)(2,1)S(1)} %get-tuple-element.51), channel_id=1, source_target_pairs={{0,8},{8,0},{16,24},{24,16},{32,40},{40,32},{48,56},{56,48},{64,72... | collective-permute-start | bytes 884744 | tf_op jit(solution)/shard_map/ppermute | solution.py:341
  34.7 0.8 %own_far.1 = (f32[384,256]{1,0:T(8,128)S(1)}, f32[152,768]{1,0:T(8,128)S(1)}) custom-call(bf16[768,128]{1,0:T(8,128)(2,1)S(1)} %get-tuple-element.32.after.refs_3_.q4_ref, bf16[960,256]{1,0:T(8,128)(2,1)S(1)} %join_slots.1.own_ref, bf16[576,768]{1,0:T(8,128)(2,1)S(1)} %get-tuple-element.35.near_ref, bf16[384,768]{1,0:T(8,128)(2,1)S(1)} %get-tuple-element.36.side_ref, ...), custom_call_target="tpu_custom_call" | custom-call | flops 4000000000 | bytes 1 | tf_op jit(solution)/shard_map/own_far/pallas_call | solution.py:355
  35.6 0.8 %collective-permute-start.13 = (bf16[192,256]{1,0:T(8,128)(2,1)S(1)}, bf16[192,256]{1,0:T(8,128)(2,1)S(1)}, u32[]{:S(2)}, u32[]{:S(2)}) collective-permute-start(bf16[192,256]{1,0:T(8,128)(2,1)S(1)} %get-tuple-element.53), channel_id=1, source_target_pairs={{0,16},{8,24},{16,0},{24,8},{32,48},{40,56},{48,32},{56,40},{64,80... | collective-permute-start | bytes 294920 | tf_op jit(solution)/shard_map/ppermute | solution.py:341
  36.3 0.8 %own_near.1 = (f32[384,256]{1,0:T(8,128)S(1)}, f32[152,768]{1,0:T(8,128)S(1)}) custom-call(bf16[768,128]{1,0:T(8,128)(2,1)S(1)} %get-tuple-element.32.after.refs_3_.q4_ref, bf16[960,256]{1,0:T(8,128)(2,1)S(1)} %join_slots.1.own_ref, bf16[576,768]{1,0:T(8,128)(2,1)S(1)} %get-tuple-element.35.near_ref, bf16[384,768]{1,0:T(8,128)(2,1)S(1)} %get-tuple-element.36.side_ref, ...), custom_call_target="tpu_custom_call" | custom-call | flops 4000000000 | bytes 1 | tf_op jit(solution)/shard_map/own_near/pallas_call | solution.py:355
  37.2 1.9 %collective-permute-start.14 = (bf16[192,256]{1,0:T(8,128)(2,1)S(1)}, bf16[192,256]{1,0:T(8,128)(2,1)S(1)}, u32[]{:S(2)}, u32[]{:S(2)}) collective-permute-start(bf16[192,256]{1,0:T(8,128)(2,1)S(1)} %get-tuple-element.55), channel_id=1, source_target_pairs={{0,240},{8,248},{16,0},{24,8},{32,16},{40,24},{48,32},{56,40},{64,... | collective-permute-start | bytes 294920 | tf_op jit(solution)/shard_map/ppermute | solution.py:341
  39.1 2.1 %collective-permute-done.13.side_ref = bf16[192,256]{1,0:T(8,128)(2,1)S(1)} collective-permute-done((bf16[192,256]{1,0:T(8,128)(2,1)S(1)}, bf16[192,256]{1,0:T(8,128)(2,1)S(1)}, u32[]{:S(2)}, u32[]{:S(2)}) %collective-permute-start.13) | collective-permute-done | bytes 98336 | tf_op jit(solution)/shard_map/ppermute | solution.py:341
  41.3 1.2 %collective-permute-start.16 = (bf16[192,256]{1,0:T(8,128)(2,1)S(1)}, bf16[192,256]{1,0:T(8,128)(2,1)S(1)}, u32[]{:S(2)}, u32[]{:S(2)}) collective-permute-start(bf16[192,256]{1,0:T(8,128)(2,1)S(1)} %get-tuple-element.58), channel_id=1, source_target_pairs={{0,224},{8,232},{16,240},{24,248},{32,0},{40,8},{48,16},{56,24},{6... | collective-permute-start | bytes 294920 | tf_op jit(solution)/shard_map/ppermute | solution.py:341
  42.5 0.8 %collective-permute-done.14.refs_1_.two_ref = bf16[192,256]{1,0:T(8,128)(2,1)S(1)} collective-permute-done((bf16[192,256]{1,0:T(8,128)(2,1)S(1)}, bf16[192,256]{1,0:T(8,128)(2,1)S(1)}, u32[]{:S(2)}, u32[]{:S(2)}) %collective-permute-start.14) | collective-permute-done | bytes 98336 | tf_op jit(solution)/shard_map/ppermute | solution.py:341
  43.3 1.2 %own_last.1 = (f32[192,256]{1,0:T(8,128)S(1)}, bf16[192,512]{1,0:T(8,128)(2,1)}) custom-call(bf16[768,128]{1,0:T(8,128)(2,1)S(1)} %get-tuple-element.32.after.refs_3_.q4_ref, bf16[960,256]{1,0:T(8,128)(2,1)S(1)} %join_slots.1.own_ref, bf16[576,768]{1,0:T(8,128)(2,1)S(1)} %get-tuple-element.35.near_ref, bf16[384,768]{1,0:T(8,128)(2,1)S(1)} %get-tuple-element.36.side_ref, ...), custom_call_target="tpu_custom_call" | custom-call | flops 4000000000 | bytes 1 | tf_op jit(solution)/shard_map/own_last/pallas_call | solution.py:355
  44.5 4.8 %collective-permute-done.15.eight_ref = bf16[192,256]{1,0:T(8,128)(2,1)S(1)} collective-permute-done((bf16[192,256]{1,0:T(8,128)(2,1)S(1)}, bf16[192,256]{1,0:T(8,128)(2,1)S(1)}, u32[]{:S(2)}, u32[]{:S(2)}) %collective-permute-start.15) | collective-permute-done | bytes 98336 | tf_op jit(solution)/shard_map/ppermute | solution.py:341
  49.3 0.7 %finish.1 = (bf16[192,128]{1,0:T(8,128)(2,1)}, bf16[192,128]{1,0:T(8,128)(2,1)}) custom-call(f32[192,256]{1,0:T(8,128)S(1)} %gather_near.1.sum_ref, bf16[192,256]{1,0:T(8,128)(2,1)S(1)} %collective-permute-done.15.eight_ref, bf16[192,256]{1,0:T(8,128)(2,1)S(1)} %collective-permute-done.16.four_ref), custom_call_target="tpu_custom_call" | custom-call | flops 1 | bytes 1 | tf_op jit(solution)/shard_map/finish/pallas_call | solution.py:355
  (25 shorter events, 0.8 us)
Async XLA Ops:
  0.6 15.3 %collective-permute-start.2 = (bf16[192,512]{1,0:T(8,128)(2,1)}, bf16[192,512]{1,0:T(8,128)(2,1)S(1)}, u32[]{:S(2)}, u32[]{:S(2)}) collective-permute-start(bf16[192,512]{1,0:T(8,128)(2,1)} %refs_0_.1), channel_id=1, source_target_pairs={{0,1},{1,0},{2,3},{3,2},{4,5},{5,4},{6,7},{7,6},{8,9},{9,8},{10,11... | collective-permute-start | bytes 589832 | tf_op jit(solution)/shard_map/ppermute | solution.py:341
  3.9 13.7 %collective-permute-start.3 = (bf16[192,512]{1,0:T(8,128)(2,1)}, bf16[192,512]{1,0:T(8,128)(2,1)S(1)}, u32[]{:S(2)}, u32[]{:S(2)}) collective-permute-start(bf16[192,512]{1,0:T(8,128)(2,1)} %refs_0_.1), channel_id=1, source_target_pairs={{0,2},{1,3},{2,4},{3,5},{4,6},{5,7},{6,0},{7,1},{8,10},{9,11},{10,... | collective-permute-start | bytes 589832 | tf_op jit(solution)/shard_map/ppermute | solution.py:341
  5.4 12.7 %collective-permute-start.4 = (bf16[192,512]{1,0:T(8,128)(2,1)}, bf16[192,512]{1,0:T(8,128)(2,1)S(1)}, u32[]{:S(2)}, u32[]{:S(2)}) collective-permute-start(bf16[192,512]{1,0:T(8,128)(2,1)} %refs_0_.1), channel_id=1, source_target_pairs={{0,6},{1,7},{2,0},{3,1},{4,2},{5,3},{6,4},{7,5},{8,14},{9,15},{10,... | collective-permute-start | bytes 589832 | tf_op jit(solution)/shard_map/ppermute | solution.py:341
  8.0 10.1 %collective-permute-start = (bf16[192,256]{1,0:T(8,128)(2,1)S(1)}, bf16[192,256]{1,0:T(8,128)(2,1)S(1)}, u32[]{:S(2)}, u32[]{:S(2)}) collective-permute-start(bf16[192,256]{1,0:T(8,128)(2,1)S(1)} %pad_add_fusion.z0_ref), channel_id=1, source_target_pairs={{0,64},{8,72},{16,80},{24,88},{32,96},{40,104},{48,112},{56,120},{... | collective-permute-start | bytes 294920 | tf_op jit(solution)/shard_map/ppermute | solution.py:341
  12.5 5.5 %collective-permute-start.1 = (bf16[192,256]{1,0:T(8,128)(2,1)S(1)}, bf16[192,256]{1,0:T(8,128)(2,1)S(1)}, u32[]{:S(2)}, u32[]{:S(2)}) collective-permute-start(bf16[192,256]{1,0:T(8,128)(2,1)S(1)} %pad_add_fusion.z0_ref), channel_id=1, source_target_pairs={{0,32},{8,40},{16,48},{24,56},{32,64},{40,72},{48,80},{56,88},{64,... | collective-permute-start | bytes 294920 | tf_op jit(solution)/shard_map/ppermute | solution.py:341
  13.6 14.8 %copy-start = (bf16[192,512]{1,0:T(8,128)(2,1)S(1)}, bf16[192,512]{1,0:T(8,128)(2,1)}, u32[]{:S(2)}) copy-start(bf16[192,512]{1,0:T(8,128)(2,1)} %refs_0_.1) | copy-start | bytes 589828
  15.9 5.8 %collective-permute-start.7 = (bf16[192,512]{1,0:T(8,128)(2,1)S(1)}, bf16[192,512]{1,0:T(8,128)(2,1)S(1)}, u32[]{:S(2)}, u32[]{:S(2)}) collective-permute-start(bf16[192,512]{1,0:T(8,128)(2,1)S(1)} %stage.1.refs_0_.refs_1_), channel_id=1, source_target_pairs={{0,6},{1,7},{2,0},{3,1},{4,2},{5,3},{6,4},{7,5},{8,14},{9,15},{10,... | collective-permute-start | bytes 589832 | tf_op jit(solution)/shard_map/ppermute | solution.py:341
  17.6 8.3 %collective-permute-start.6 = (bf16[192,512]{1,0:T(8,128)(2,1)S(1)}, bf16[192,512]{1,0:T(8,128)(2,1)S(1)}, u32[]{:S(2)}, u32[]{:S(2)}) collective-permute-start(bf16[192,512]{1,0:T(8,128)(2,1)S(1)} %stage.1.refs_0_.refs_1_), channel_id=1, source_target_pairs={{0,2},{1,3},{2,4},{3,5},{4,6},{5,7},{6,0},{7,1},{8,10},{9,11},{10,... | collective-permute-start | bytes 589832 | tf_op jit(solution)/shard_map/ppermute | solution.py:341
  18.1 9.0 %collective-permute-start.5 = (bf16[384,256]{1,0:T(8,128)(2,1)S(1)}, bf16[384,256]{1,0:T(8,128)(2,1)S(1)}, u32[]{:S(2)}, u32[]{:S(2)}) collective-permute-start(bf16[384,256]{1,0:T(8,128)(2,1)S(1)} %pick_side.1.refs_0_), channel_id=1, source_target_pairs={{0,16},{8,24},{16,0},{24,8},{32,48},{40,56},{48,32},{56,40},{64,80... | collective-permute-start | bytes 589832 | tf_op jit(solution)/shard_map/ppermute | solution.py:341
  18.9 9.5 %collective-permute-start.9 = (bf16[192,512]{1,0:T(8,128)(2,1)S(1)}, bf16[192,512]{1,0:T(8,128)(2,1)S(1)}, u32[]{:S(2)}, u32[]{:S(2)}) collective-permute-start(bf16[192,512]{1,0:T(8,128)(2,1)S(1)} %collective-permute-done.3.refs_1_.refs_2_), channel_id=1, source_target_pairs={{0,2},{1,3},{2,4},{3,5},{4,6},{5,7},{6,0},{7,1},{8,10},{9,11},{10,... | collective-permute-start | bytes 589832 | tf_op jit(solution)/shard_map/ppermute | solution.py:341
  21.7 8.0 %collective-permute-start.8 = (bf16[192,512]{1,0:T(8,128)(2,1)S(1)}, bf16[192,512]{1,0:T(8,128)(2,1)S(1)}, u32[]{:S(2)}, u32[]{:S(2)}) collective-permute-start(bf16[192,512]{1,0:T(8,128)(2,1)S(1)} %collective-permute-done.7.refs_2_.refs_5_), channel_id=1, source_target_pairs={{0,6},{1,7},{2,0},{3,1},{4,2},{5,3},{6,4},{7,5},{8,14},{9,15},{10,... | collective-permute-start | bytes 589832 | tf_op jit(solution)/shard_map/ppermute | solution.py:341
  27.2 3.0 %collective-permute-start.10 = (bf16[960,256]{1,0:T(8,128)(2,1)S(1)}, bf16[960,256]{1,0:T(8,128)(2,1)S(1)}, u32[]{:S(2)}, u32[]{:S(2)}) collective-permute-start(bf16[960,256]{1,0:T(8,128)(2,1)S(1)} %join_slots.1.own_ref), channel_id=1, source_target_pairs={{0,8},{8,0},{16,24},{24,16},{32,40},{40,32},{48,56},{56,48},{64,72... | collective-permute-start | bytes 1474568 | tf_op jit(solution)/shard_map/ppermute | solution.py:341
  32.7 2.8 %collective-permute-start.11 = (bf16[384,256]{1,0:T(8,128)(2,1)S(1)}, bf16[384,256]{1,0:T(8,128)(2,1)S(1)}, u32[]{:S(2)}, u32[]{:S(2)}) collective-permute-start(bf16[384,256]{1,0:T(8,128)(2,1)S(1)} %get-tuple-element.47), channel_id=1, source_target_pairs={{0,8},{8,0},{16,24},{24,16},{32,40},{40,32},{48,56},{56,48},{64,72... | collective-permute-start | bytes 589832 | tf_op jit(solution)/shard_map/ppermute | solution.py:341
  33.7 3.5 %collective-permute-start.12 = (bf16[576,256]{1,0:T(8,128)(2,1)S(1)}, bf16[576,256]{1,0:T(8,128)(2,1)S(1)}, u32[]{:S(2)}, u32[]{:S(2)}) collective-permute-start(bf16[576,256]{1,0:T(8,128)(2,1)S(1)} %get-tuple-element.51), channel_id=1, source_target_pairs={{0,8},{8,0},{16,24},{24,16},{32,40},{40,32},{48,56},{56,48},{64,72... | collective-permute-start | bytes 884744 | tf_op jit(solution)/shard_map/ppermute | solution.py:341
  35.6 5.6 %collective-permute-start.13 = (bf16[192,256]{1,0:T(8,128)(2,1)S(1)}, bf16[192,256]{1,0:T(8,128)(2,1)S(1)}, u32[]{:S(2)}, u32[]{:S(2)}) collective-permute-start(bf16[192,256]{1,0:T(8,128)(2,1)S(1)} %get-tuple-element.53), channel_id=1, source_target_pairs={{0,16},{8,24},{16,0},{24,8},{32,48},{40,56},{48,32},{56,40},{64,80... | collective-permute-start | bytes 294920 | tf_op jit(solution)/shard_map/ppermute | solution.py:341
  37.2 6.1 %collective-permute-start.14 = (bf16[192,256]{1,0:T(8,128)(2,1)S(1)}, bf16[192,256]{1,0:T(8,128)(2,1)S(1)}, u32[]{:S(2)}, u32[]{:S(2)}) collective-permute-start(bf16[192,256]{1,0:T(8,128)(2,1)S(1)} %get-tuple-element.55), channel_id=1, source_target_pairs={{0,240},{8,248},{16,0},{24,8},{32,16},{40,24},{48,32},{56,40},{64,... | collective-permute-start | bytes 294920 | tf_op jit(solution)/shard_map/ppermute | solution.py:341
  41.2 8.1 %collective-permute-start.15 = (bf16[192,256]{1,0:T(8,128)(2,1)S(1)}, bf16[192,256]{1,0:T(8,128)(2,1)S(1)}, u32[]{:S(2)}, u32[]{:S(2)}) collective-permute-start(bf16[192,256]{1,0:T(8,128)(2,1)S(1)} %get-tuple-element.54.refs_0_), channel_id=1, source_target_pairs={{0,192},{8,200},{16,208},{24,216},{32,224},{40,232},{48,240},{56,2... | collective-permute-start | bytes 294920 | tf_op jit(solution)/shard_map/ppermute | solution.py:341
  41.3 8.1 %collective-permute-start.16 = (bf16[192,256]{1,0:T(8,128)(2,1)S(1)}, bf16[192,256]{1,0:T(8,128)(2,1)S(1)}, u32[]{:S(2)}, u32[]{:S(2)}) collective-permute-start(bf16[192,256]{1,0:T(8,128)(2,1)S(1)} %get-tuple-element.58), channel_id=1, source_target_pairs={{0,224},{8,232},{16,240},{24,248},{32,0},{40,8},{48,16},{56,24},{6... | collective-permute-start | bytes 294920 | tf_op jit(solution)/shard_map/ppermute | solution.py:341

commit v17 on v16

--- a/solution.py
+++ b/solution.py
@@ -142,7 +142,7 @@
 
 
 def project_kernel(*refs):
-    pieces, (w_ref, after, acc_ref) = refs[:7], refs[7:]
+    pieces, (w_ref, after, acc_ref) = refs[:6], refs[6:]
     acc = None
     for i, piece in enumerate(pieces):
         part = dot(piece[...], w_ref[:, i * BLOCK : (i + 1) * BLOCK], 1, 1)
@@ -150,8 +150,9 @@
     acc_ref[...] = acc
 
 
-def last_projection(piece_ref, w_ref, acc_ref, g4_ref, gt_ref):
-    acc = (acc_ref[...] + dot(piece_ref[...], w_ref[:, 7 * BLOCK :], 1, 1)).astype(jnp.bfloat16)
+def last_projection(far_ref, piece_ref, w_ref, acc_ref, g4_ref, gt_ref):
+    acc = acc_ref[...] + dot(far_ref[...], w_ref[:, 6 * BLOCK : 7 * BLOCK], 1, 1)
+    acc = (acc + dot(piece_ref[...], w_ref[:, 7 * BLOCK :], 1, 1)).astype(jnp.bfloat16)
     for h in range(HEADS):
         g4_ref[h * ROWS : (h + 1) * ROWS, :] = acc[:, h * D : (h + 1) * D]
     gt_ref[...] = jnp.transpose(g4_ref[...].astype(jnp.float32))
@@ -418,15 +419,15 @@
         "project",
         project_kernel,
         shape(ROWS, HEADS * D, f32),
-        vmem(8) + token(1),
-        (grad_out, other, right, left, other_right, other_left, far, weight, st),
+        vmem(7) + token(1),
+        (grad_out, other, right, left, other_right, other_left, weight, st),
     )
     g4, gt = call(
         "last_projection",
         last_projection,
         (shape(LANES, D, bf16), shape(D, LANES, f32)),
-        vmem(3),
-        (other_far, weight, early),
+        vmem(4),
+        (far, other_far, weight, early),
         flops=COSTLY,
     )
     p_par, st = call(

time: 50.6 us -> 50.6 us (level)
  no operation moved by 1% of the time
where the time goes in v17:
time: 50.6 us; the launch traced here: 50.1 us
  starting transfers between devices  23.4 us (46%)
  Pallas kernels  13.4 us (26%)
  waiting for transfers between devices  11.7 us (23%)
  between operations  0.84 us (2%)
  other arithmetic  0.83 us (2%)
    ppermute x17, starting transfers between devices, moved(): lax.ppermute(x, axis, [(i, to(i)) for i in range(lax.axis_size(axis))])  23.4 us
    pallas_call x20, Pallas kernels, call(): pl.pallas_call(kernel, out_shape=outs, in_specs=ins, out_specs=vmem(1)[0]...  13.4 us
    ppermute x17, waiting for transfers between devices, moved(): lax.ppermute(x, axis, [(i, to(i)) for i in range(lax.axis_size(axis))])  11.7 us
  transfers between devices with their start and end apart: 17, of which 5 were waited for; matrix products, arithmetic and copies ran while one was open for 2% of the time, Pallas kernels for 20%

profile of v17, /device:TPU:64, one launch (start us, length us, event | category | flops | bytes accessed | tf_op | source)
XLA Modules:
  0.0 50.1 jit_solution(13319587195487722473)
XLA Ops:
  0.6 3.3 %collective-permute-start.2 = (bf16[192,512]{1,0:T(8,128)(2,1)}, bf16[192,512]{1,0:T(8,128)(2,1)S(1)}, u32[]{:S(2)}, u32[]{:S(2)}) collective-permute-start(bf16[192,512]{1,0:T(8,128)(2,1)} %refs_0_.1), channel_id=1, source_target_pairs={{0,1},{1,0},{2,3},{3,2},{4,5},{5,4},{6,7},{7,6},{8,9},{9,8},{10,11... | collective-permute-start | bytes 589832 | tf_op jit(solution)/shard_map/ppermute | solution.py:342
  3.9 1.5 %collective-permute-start.3 = (bf16[192,512]{1,0:T(8,128)(2,1)}, bf16[192,512]{1,0:T(8,128)(2,1)S(1)}, u32[]{:S(2)}, u32[]{:S(2)}) collective-permute-start(bf16[192,512]{1,0:T(8,128)(2,1)} %refs_0_.1), channel_id=1, source_target_pairs={{0,2},{1,3},{2,4},{3,5},{4,6},{5,7},{6,0},{7,1},{8,10},{9,11},{10,... | collective-permute-start | bytes 589832 | tf_op jit(solution)/shard_map/ppermute | solution.py:342
  5.4 1.7 %collective-permute-start.4 = (bf16[192,512]{1,0:T(8,128)(2,1)}, bf16[192,512]{1,0:T(8,128)(2,1)S(1)}, u32[]{:S(2)}, u32[]{:S(2)}) collective-permute-start(bf16[192,512]{1,0:T(8,128)(2,1)} %refs_0_.1), channel_id=1, source_target_pairs={{0,6},{1,7},{2,0},{3,1},{4,2},{5,3},{6,4},{7,5},{8,14},{9,15},{10,... | collective-permute-start | bytes 589832 | tf_op jit(solution)/shard_map/ppermute | solution.py:342
  7.1 0.8 %pad_add_fusion.z0_ref = bf16[192,256]{1,0:T(8,128)(2,1)S(1)} fusion(bf16[192,128]{1,0:T(8,128)(2,1)} %param.8, bf16[192,128]{1,0:T(8,128)(2,1)} %param.7), kind=kLoop, calls=%fused_computation | loop fusion | flops 196608 | bytes 196608 | tf_op jit(solution)/shard_map/add | solution.py:379
  8.0 4.6 %collective-permute-start = (bf16[192,256]{1,0:T(8,128)(2,1)S(1)}, bf16[192,256]{1,0:T(8,128)(2,1)S(1)}, u32[]{:S(2)}, u32[]{:S(2)}) collective-permute-start(bf16[192,256]{1,0:T(8,128)(2,1)S(1)} %pad_add_fusion.z0_ref), channel_id=1, source_target_pairs={{0,64},{8,72},{16,80},{24,88},{32,96},{40,104},{48,112},{56,120},{... | collective-permute-start | bytes 294920 | tf_op jit(solution)/shard_map/ppermute | solution.py:342
  12.5 1.0 %collective-permute-start.1 = (bf16[192,256]{1,0:T(8,128)(2,1)S(1)}, bf16[192,256]{1,0:T(8,128)(2,1)S(1)}, u32[]{:S(2)}, u32[]{:S(2)}) collective-permute-start(bf16[192,256]{1,0:T(8,128)(2,1)S(1)} %pad_add_fusion.z0_ref), channel_id=1, source_target_pairs={{0,32},{8,40},{16,48},{24,56},{32,64},{40,72},{48,80},{56,88},{64,... | collective-permute-start | bytes 294920 | tf_op jit(solution)/shard_map/ppermute | solution.py:342
  13.6 2.3 %load.1 = (bf16[768,128]{1,0:T(8,128)(2,1)S(1)}, f32[8,768]{1,0:T(8,128)S(1)}, bf16[512,4096]{1,0:T(8,128)(2,1)S(1)}) custom-call(s32[1]{0:T(128)} %bitcast.place_ref, s32[1]{0:T(128)} %bitcast.1.head_ref, s32[8]{0:T(128)} %len_hbm.1, bf16[192,512]{1,0:T(8,128)(2,1)} %q_hbm.1, bf16[512,4096]{1,0:T(8,128)(2,1)} %w_hbm.1), custom_call_target="tpu_custom_call" | custom-call | flops 1 | bytes 1 | tf_op jit(solution)/shard_map/load/pallas_call | solution.py:356
  15.9 1.6 %collective-permute-start.7 = (bf16[192,512]{1,0:T(8,128)(2,1)S(1)}, bf16[192,512]{1,0:T(8,128)(2,1)S(1)}, u32[]{:S(2)}, u32[]{:S(2)}) collective-permute-start(bf16[192,512]{1,0:T(8,128)(2,1)S(1)} %stage.1.refs_0_.refs_1_), channel_id=1, source_target_pairs={{0,6},{1,7},{2,0},{3,1},{4,2},{5,3},{6,4},{7,5},{8,14},{9,15},{10,... | collective-permute-start | bytes 589832 | tf_op jit(solution)/shard_map/ppermute | solution.py:342
  17.6 0.5 collective-permute-start.6
  18.1 0.8 %collective-permute-start.5 = (bf16[384,256]{1,0:T(8,128)(2,1)S(1)}, bf16[384,256]{1,0:T(8,128)(2,1)S(1)}, u32[]{:S(2)}, u32[]{:S(2)}) collective-permute-start(bf16[384,256]{1,0:T(8,128)(2,1)S(1)} %pick_side.1.refs_0_), channel_id=1, source_target_pairs={{0,16},{8,24},{16,0},{24,8},{32,48},{40,56},{48,32},{56,40},{64,80... | collective-permute-start | bytes 589832 | tf_op jit(solution)/shard_map/ppermute | solution.py:342
  18.9 0.3 collective-permute-start.8
  19.2 2.6 %collective-permute-done.7.refs_2_.refs_5_ = bf16[192,512]{1,0:T(8,128)(2,1)S(1)} collective-permute-done((bf16[192,512]{1,0:T(8,128)(2,1)S(1)}, bf16[192,512]{1,0:T(8,128)(2,1)S(1)}, u32[]{:S(2)}, u32[]{:S(2)}) %collective-permute-start.7) | collective-permute-done | bytes 196640 | tf_op jit(solution)/shard_map/ppermute | solution.py:342
  21.7 2.7 %collective-permute-start.9 = (bf16[192,512]{1,0:T(8,128)(2,1)S(1)}, bf16[192,512]{1,0:T(8,128)(2,1)S(1)}, u32[]{:S(2)}, u32[]{:S(2)}) collective-permute-start(bf16[192,512]{1,0:T(8,128)(2,1)S(1)} %collective-permute-done.7.refs_2_.refs_5_), channel_id=1, source_target_pairs={{0,6},{1,7},{2,0},{3,1},{4,2},{5,3},{6,4},{7,5},{8,14},{9,15},{10,... | collective-permute-start | bytes 589832 | tf_op jit(solution)/shard_map/ppermute | solution.py:342
  24.5 1.4 %collective-permute-done.6.refs_1_.refs_4_ = bf16[192,512]{1,0:T(8,128)(2,1)S(1)} collective-permute-done((bf16[192,512]{1,0:T(8,128)(2,1)S(1)}, bf16[192,512]{1,0:T(8,128)(2,1)S(1)}, u32[]{:S(2)}, u32[]{:S(2)}) %collective-permute-start.6) | collective-permute-done | bytes 196640 | tf_op jit(solution)/shard_map/ppermute | solution.py:342
  25.9 1.3 %near.1 = (bf16[576,768]{1,0:T(8,128)(2,1)S(1)}, f32[152,768]{1,0:T(8,128)S(1)}) custom-call(s32[1]{0:T(128)} %bitcast.place_ref, bf16[192,256]{1,0:T(8,128)(2,1)S(1)} %collective-permute-done.z2_ref, bf16[192,256]{1,0:T(8,128)(2,1)S(1)} %collective-permute-done.1.z1_ref, bf16[192,256]{1,0:T(8,128)(2,1)S(1)} %pad_add_fusion.z0_ref, ...), custom_call_target="tpu_custom_call" | custom-call | flops 1 | bytes 1 | tf_op jit(solution)/shard_map/near/pallas_call | solution.py:356
  27.5 0.9 %middle.1 = (bf16[384,768]{1,0:T(8,128)(2,1)S(1)}, f32[152,768]{1,0:T(8,128)S(1)}) custom-call(s32[1]{0:T(128)} %bitcast.place_ref, bf16[960,256]{1,0:T(8,128)(2,1)S(1)} %join_slots.1.own_ref, bf16[768,128]{1,0:T(8,128)(2,1)S(1)} %get-tuple-element.32.after.refs_3_.q4_ref, f32[152,768]{1,0:T(8,128)S(1)} %get-tuple-element.34.refs_0_.st_in_ref), custom_call_target="tpu_custom_call" | custom-call | flops 1 | bytes 1 | tf_op jit(solution)/shard_map/middle/pallas_call | solution.py:356
  28.4 1.2 %project.1.acc_ref = f32[192,512]{1,0:T(8,128)S(1)} custom-call(bf16[192,512]{1,0:T(8,128)(2,1)S(1)} %copy-done, bf16[192,512]{1,0:T(8,128)(2,1)S(1)} %stage.1.refs_0_.refs_1_, bf16[192,512]{1,0:T(8,128)(2,1)S(1)} %collective-permute-done.3.refs_1_.refs_2_, bf16[192,512]{1,0:T(8,128)(2,1)S(1)} %collective-permute-done.4.refs_2_.refs_3_, ...), custom_call_target="tpu_custom_call" | custom-call | flops 1 | bytes 1 | tf_op jit(solution)/shard_map/project/pallas_call | solution.py:356
  29.6 0.6 %last_projection.1 = (bf16[768,128]{1,0:T(8,128)(2,1)S(1)}, f32[128,768]{1,0:T(8,128)S(1)}) custom-call(bf16[192,512]{1,0:T(8,128)(2,1)S(1)} %collective-permute-done.8.far_ref, bf16[192,512]{1,0:T(8,128)(2,1)S(1)} %collective-permute-done.9.piece_ref, bf16[512,4096]{1,0:T(8,128)(2,1)S(1)} %get-tuple-element.37.refs_6_.w_ref, f32[192,512]{1,0:T(8,128)S(1)} %project.1.acc_ref), custom_call_target="tpu_custom_call" | custom-call | flops 4000000000 | bytes 1 | tf_op jit(solution)/shard_map/last_projection/pallas_call | solution.py:356
  30.2 1.6 %across.1 = (bf16[768,768]{1,0:T(8,128)(2,1)S(1)}, f32[152,768]{1,0:T(8,128)S(1)}) custom-call(s32[1]{0:T(128)} %bitcast.place_ref, bf16[960,256]{1,0:T(8,128)(2,1)S(1)} %collective-permute-done.10.par_ref, bf16[768,128]{1,0:T(8,128)(2,1)S(1)} %get-tuple-element.32.after.refs_3_.q4_ref, f32[128,768]{1,0:T(8,128)S(1)} %get-tuple-element.40.gt_ref, ...), custom_call_target="tpu_custom_call" | custom-call | flops 1 | bytes 1 | tf_op jit(solution)/shard_map/across/pallas_call | solution.py:356
  31.8 0.9 %cross_far.1 = (bf16[384,256]{1,0:T(8,128)(2,1)S(1)}, f32[152,768]{1,0:T(8,128)S(1)}) custom-call(s32[1]{0:T(128)} %bitcast.place_ref, bf16[768,128]{1,0:T(8,128)(2,1)S(1)} %get-tuple-element.32.after.refs_3_.q4_ref, bf16[960,256]{1,0:T(8,128)(2,1)S(1)} %collective-permute-done.10.par_ref, bf16[768,768]{1,0:T(8,128)(2,1)S(1)} %get-tuple-element.41.p_ref, ...), custom_call_target="tpu_custom_call" | custom-call | flops 1 | bytes 1 | tf_op jit(solution)/shard_map/cross_far/pallas_call | solution.py:356
  32.9 0.8 %cross_near.1 = (bf16[576,256]{1,0:T(8,128)(2,1)S(1)}, f32[152,768]{1,0:T(8,128)S(1)}) custom-call(s32[1]{0:T(128)} %bitcast.place_ref, bf16[768,128]{1,0:T(8,128)(2,1)S(1)} %get-tuple-element.32.after.refs_3_.q4_ref, bf16[960,256]{1,0:T(8,128)(2,1)S(1)} %collective-permute-done.10.par_ref, bf16[768,768]{1,0:T(8,128)(2,1)S(1)} %get-tuple-element.41.p_ref, ...), custom_call_target="tpu_custom_call" | custom-call | flops 4000000000 | bytes 1 | tf_op jit(solution)/shard_map/cross_near/pallas_call | solution.py:356
  33.7 1.0 %collective-permute-start.12 = (bf16[576,256]{1,0:T(8,128)(2,1)S(1)}, bf16[576,256]{1,0:T(8,128)(2,1)S(1)}, u32[]{:S(2)}, u32[]{:S(2)}) collective-permute-start(bf16[576,256]{1,0:T(8,128)(2,1)S(1)} %get-tuple-element.51), channel_id=1, source_target_pairs={{0,8},{8,0},{16,24},{24,16},{32,40},{40,32},{48,56},{56,48},{64,72... | collective-permute-start | bytes 884744 | tf_op jit(solution)/shard_map/ppermute | solution.py:342
  34.7 0.8 %own_far.1 = (f32[384,256]{1,0:T(8,128)S(1)}, f32[152,768]{1,0:T(8,128)S(1)}) custom-call(bf16[768,128]{1,0:T(8,128)(2,1)S(1)} %get-tuple-element.32.after.refs_3_.q4_ref, bf16[960,256]{1,0:T(8,128)(2,1)S(1)} %join_slots.1.own_ref, bf16[576,768]{1,0:T(8,128)(2,1)S(1)} %get-tuple-element.35.near_ref, bf16[384,768]{1,0:T(8,128)(2,1)S(1)} %get-tuple-element.36.side_ref, ...), custom_call_target="tpu_custom_call" | custom-call | flops 4000000000 | bytes 1 | tf_op jit(solution)/shard_map/own_far/pallas_call | solution.py:356
  35.6 0.8 %collective-permute-start.13 = (bf16[192,256]{1,0:T(8,128)(2,1)S(1)}, bf16[192,256]{1,0:T(8,128)(2,1)S(1)}, u32[]{:S(2)}, u32[]{:S(2)}) collective-permute-start(bf16[192,256]{1,0:T(8,128)(2,1)S(1)} %get-tuple-element.53), channel_id=1, source_target_pairs={{0,16},{8,24},{16,0},{24,8},{32,48},{40,56},{48,32},{56,40},{64,80... | collective-permute-start | bytes 294920 | tf_op jit(solution)/shard_map/ppermute | solution.py:342
  36.3 0.8 %own_near.1 = (f32[384,256]{1,0:T(8,128)S(1)}, f32[152,768]{1,0:T(8,128)S(1)}) custom-call(bf16[768,128]{1,0:T(8,128)(2,1)S(1)} %get-tuple-element.32.after.refs_3_.q4_ref, bf16[960,256]{1,0:T(8,128)(2,1)S(1)} %join_slots.1.own_ref, bf16[576,768]{1,0:T(8,128)(2,1)S(1)} %get-tuple-element.35.near_ref, bf16[384,768]{1,0:T(8,128)(2,1)S(1)} %get-tuple-element.36.side_ref, ...), custom_call_target="tpu_custom_call" | custom-call | flops 4000000000 | bytes 1 | tf_op jit(solution)/shard_map/own_near/pallas_call | solution.py:356
  37.2 1.9 %collective-permute-start.14 = (bf16[192,256]{1,0:T(8,128)(2,1)S(1)}, bf16[192,256]{1,0:T(8,128)(2,1)S(1)}, u32[]{:S(2)}, u32[]{:S(2)}) collective-permute-start(bf16[192,256]{1,0:T(8,128)(2,1)S(1)} %get-tuple-element.55), channel_id=1, source_target_pairs={{0,240},{8,248},{16,0},{24,8},{32,16},{40,24},{48,32},{56,40},{64,... | collective-permute-start | bytes 294920 | tf_op jit(solution)/shard_map/ppermute | solution.py:342
  39.1 2.1 %collective-permute-done.13.side_ref = bf16[192,256]{1,0:T(8,128)(2,1)S(1)} collective-permute-done((bf16[192,256]{1,0:T(8,128)(2,1)S(1)}, bf16[192,256]{1,0:T(8,128)(2,1)S(1)}, u32[]{:S(2)}, u32[]{:S(2)}) %collective-permute-start.13) | collective-permute-done | bytes 98336 | tf_op jit(solution)/shard_map/ppermute | solution.py:342
  41.3 1.3 %collective-permute-start.16 = (bf16[192,256]{1,0:T(8,128)(2,1)S(1)}, bf16[192,256]{1,0:T(8,128)(2,1)S(1)}, u32[]{:S(2)}, u32[]{:S(2)}) collective-permute-start(bf16[192,256]{1,0:T(8,128)(2,1)S(1)} %get-tuple-element.58), channel_id=1, source_target_pairs={{0,224},{8,232},{16,240},{24,248},{32,0},{40,8},{48,16},{56,24},{6... | collective-permute-start | bytes 294920 | tf_op jit(solution)/shard_map/ppermute | solution.py:342
  42.5 0.7 %collective-permute-done.14.refs_1_.two_ref = bf16[192,256]{1,0:T(8,128)(2,1)S(1)} collective-permute-done((bf16[192,256]{1,0:T(8,128)(2,1)S(1)}, bf16[192,256]{1,0:T(8,128)(2,1)S(1)}, u32[]{:S(2)}, u32[]{:S(2)}) %collective-permute-start.14) | collective-permute-done | bytes 98336 | tf_op jit(solution)/shard_map/ppermute | solution.py:342
  43.3 1.2 %own_last.1 = (f32[192,256]{1,0:T(8,128)S(1)}, bf16[192,512]{1,0:T(8,128)(2,1)}) custom-call(bf16[768,128]{1,0:T(8,128)(2,1)S(1)} %get-tuple-element.32.after.refs_3_.q4_ref, bf16[960,256]{1,0:T(8,128)(2,1)S(1)} %join_slots.1.own_ref, bf16[576,768]{1,0:T(8,128)(2,1)S(1)} %get-tuple-element.35.near_ref, bf16[384,768]{1,0:T(8,128)(2,1)S(1)} %get-tuple-element.36.side_ref, ...), custom_call_target="tpu_custom_call" | custom-call | flops 4000000000 | bytes 1 | tf_op jit(solution)/shard_map/own_last/pallas_call | solution.py:356
  44.5 4.9 %collective-permute-done.15.eight_ref = bf16[192,256]{1,0:T(8,128)(2,1)S(1)} collective-permute-done((bf16[192,256]{1,0:T(8,128)(2,1)S(1)}, bf16[192,256]{1,0:T(8,128)(2,1)S(1)}, u32[]{:S(2)}, u32[]{:S(2)}) %collective-permute-start.15) | collective-permute-done | bytes 98336 | tf_op jit(solution)/shard_map/ppermute | solution.py:342
  49.4 0.7 %finish.1 = (bf16[192,128]{1,0:T(8,128)(2,1)}, bf16[192,128]{1,0:T(8,128)(2,1)}) custom-call(f32[192,256]{1,0:T(8,128)S(1)} %gather_near.1.sum_ref, bf16[192,256]{1,0:T(8,128)(2,1)S(1)} %collective-permute-done.15.eight_ref, bf16[192,256]{1,0:T(8,128)(2,1)S(1)} %collective-permute-done.16.four_ref), custom_call_target="tpu_custom_call" | custom-call | flops 1 | bytes 1 | tf_op jit(solution)/shard_map/finish/pallas_call | solution.py:356
  (25 shorter events, 0.8 us)
Async XLA Ops:
  0.6 15.3 %collective-permute-start.2 = (bf16[192,512]{1,0:T(8,128)(2,1)}, bf16[192,512]{1,0:T(8,128)(2,1)S(1)}, u32[]{:S(2)}, u32[]{:S(2)}) collective-permute-start(bf16[192,512]{1,0:T(8,128)(2,1)} %refs_0_.1), channel_id=1, source_target_pairs={{0,1},{1,0},{2,3},{3,2},{4,5},{5,4},{6,7},{7,6},{8,9},{9,8},{10,11... | collective-permute-start | bytes 589832 | tf_op jit(solution)/shard_map/ppermute | solution.py:342
  3.9 13.7 %collective-permute-start.3 = (bf16[192,512]{1,0:T(8,128)(2,1)}, bf16[192,512]{1,0:T(8,128)(2,1)S(1)}, u32[]{:S(2)}, u32[]{:S(2)}) collective-permute-start(bf16[192,512]{1,0:T(8,128)(2,1)} %refs_0_.1), channel_id=1, source_target_pairs={{0,2},{1,3},{2,4},{3,5},{4,6},{5,7},{6,0},{7,1},{8,10},{9,11},{10,... | collective-permute-start | bytes 589832 | tf_op jit(solution)/shard_map/ppermute | solution.py:342
  5.4 12.7 %collective-permute-start.4 = (bf16[192,512]{1,0:T(8,128)(2,1)}, bf16[192,512]{1,0:T(8,128)(2,1)S(1)}, u32[]{:S(2)}, u32[]{:S(2)}) collective-permute-start(bf16[192,512]{1,0:T(8,128)(2,1)} %refs_0_.1), channel_id=1, source_target_pairs={{0,6},{1,7},{2,0},{3,1},{4,2},{5,3},{6,4},{7,5},{8,14},{9,15},{10,... | collective-permute-start | bytes 589832 | tf_op jit(solution)/shard_map/ppermute | solution.py:342
  8.0 10.1 %collective-permute-start = (bf16[192,256]{1,0:T(8,128)(2,1)S(1)}, bf16[192,256]{1,0:T(8,128)(2,1)S(1)}, u32[]{:S(2)}, u32[]{:S(2)}) collective-permute-start(bf16[192,256]{1,0:T(8,128)(2,1)S(1)} %pad_add_fusion.z0_ref), channel_id=1, source_target_pairs={{0,64},{8,72},{16,80},{24,88},{32,96},{40,104},{48,112},{56,120},{... | collective-permute-start | bytes 294920 | tf_op jit(solution)/shard_map/ppermute | solution.py:342
  12.5 5.5 %collective-permute-start.1 = (bf16[192,256]{1,0:T(8,128)(2,1)S(1)}, bf16[192,256]{1,0:T(8,128)(2,1)S(1)}, u32[]{:S(2)}, u32[]{:S(2)}) collective-permute-start(bf16[192,256]{1,0:T(8,128)(2,1)S(1)} %pad_add_fusion.z0_ref), channel_id=1, source_target_pairs={{0,32},{8,40},{16,48},{24,56},{32,64},{40,72},{48,80},{56,88},{64,... | collective-permute-start | bytes 294920 | tf_op jit(solution)/shard_map/ppermute | solution.py:342
  13.6 14.8 %copy-start = (bf16[192,512]{1,0:T(8,128)(2,1)S(1)}, bf16[192,512]{1,0:T(8,128)(2,1)}, u32[]{:S(2)}) copy-start(bf16[192,512]{1,0:T(8,128)(2,1)} %refs_0_.1) | copy-start | bytes 589828
  15.9 5.8 %collective-permute-start.7 = (bf16[192,512]{1,0:T(8,128)(2,1)S(1)}, bf16[192,512]{1,0:T(8,128)(2,1)S(1)}, u32[]{:S(2)}, u32[]{:S(2)}) collective-permute-start(bf16[192,512]{1,0:T(8,128)(2,1)S(1)} %stage.1.refs_0_.refs_1_), channel_id=1, source_target_pairs={{0,6},{1,7},{2,0},{3,1},{4,2},{5,3},{6,4},{7,5},{8,14},{9,15},{10,... | collective-permute-start | bytes 589832 | tf_op jit(solution)/shard_map/ppermute | solution.py:342
  17.6 8.3 %collective-permute-start.6 = (bf16[192,512]{1,0:T(8,128)(2,1)S(1)}, bf16[192,512]{1,0:T(8,128)(2,1)S(1)}, u32[]{:S(2)}, u32[]{:S(2)}) collective-permute-start(bf16[192,512]{1,0:T(8,128)(2,1)S(1)} %stage.1.refs_0_.refs_1_), channel_id=1, source_target_pairs={{0,2},{1,3},{2,4},{3,5},{4,6},{5,7},{6,0},{7,1},{8,10},{9,11},{10,... | collective-permute-start | bytes 589832 | tf_op jit(solution)/shard_map/ppermute | solution.py:342
  18.1 9.0 %collective-permute-start.5 = (bf16[384,256]{1,0:T(8,128)(2,1)S(1)}, bf16[384,256]{1,0:T(8,128)(2,1)S(1)}, u32[]{:S(2)}, u32[]{:S(2)}) collective-permute-start(bf16[384,256]{1,0:T(8,128)(2,1)S(1)} %pick_side.1.refs_0_), channel_id=1, source_target_pairs={{0,16},{8,24},{16,0},{24,8},{32,48},{40,56},{48,32},{56,40},{64,80... | collective-permute-start | bytes 589832 | tf_op jit(solution)/shard_map/ppermute | solution.py:342
  18.9 10.7 %collective-permute-start.8 = (bf16[192,512]{1,0:T(8,128)(2,1)S(1)}, bf16[192,512]{1,0:T(8,128)(2,1)S(1)}, u32[]{:S(2)}, u32[]{:S(2)}) collective-permute-start(bf16[192,512]{1,0:T(8,128)(2,1)S(1)} %collective-permute-done.3.refs_1_.refs_2_), channel_id=1, source_target_pairs={{0,2},{1,3},{2,4},{3,5},{4,6},{5,7},{6,0},{7,1},{8,10},{9,11},{10,... | collective-permute-start | bytes 589832 | tf_op jit(solution)/shard_map/ppermute | solution.py:342
  21.7 7.8 %collective-permute-start.9 = (bf16[192,512]{1,0:T(8,128)(2,1)S(1)}, bf16[192,512]{1,0:T(8,128)(2,1)S(1)}, u32[]{:S(2)}, u32[]{:S(2)}) collective-permute-start(bf16[192,512]{1,0:T(8,128)(2,1)S(1)} %collective-permute-done.7.refs_2_.refs_5_), channel_id=1, source_target_pairs={{0,6},{1,7},{2,0},{3,1},{4,2},{5,3},{6,4},{7,5},{8,14},{9,15},{10,... | collective-permute-start | bytes 589832 | tf_op jit(solution)/shard_map/ppermute | solution.py:342
  27.2 3.0 %collective-permute-start.10 = (bf16[960,256]{1,0:T(8,128)(2,1)S(1)}, bf16[960,256]{1,0:T(8,128)(2,1)S(1)}, u32[]{:S(2)}, u32[]{:S(2)}) collective-permute-start(bf16[960,256]{1,0:T(8,128)(2,1)S(1)} %join_slots.1.own_ref), channel_id=1, source_target_pairs={{0,8},{8,0},{16,24},{24,16},{32,40},{40,32},{48,56},{56,48},{64,72... | collective-permute-start | bytes 1474568 | tf_op jit(solution)/shard_map/ppermute | solution.py:342
  32.8 2.8 %collective-permute-start.11 = (bf16[384,256]{1,0:T(8,128)(2,1)S(1)}, bf16[384,256]{1,0:T(8,128)(2,1)S(1)}, u32[]{:S(2)}, u32[]{:S(2)}) collective-permute-start(bf16[384,256]{1,0:T(8,128)(2,1)S(1)} %get-tuple-element.47), channel_id=1, source_target_pairs={{0,8},{8,0},{16,24},{24,16},{32,40},{40,32},{48,56},{56,48},{64,72... | collective-permute-start | bytes 589832 | tf_op jit(solution)/shard_map/ppermute | solution.py:342
  33.7 3.5 %collective-permute-start.12 = (bf16[576,256]{1,0:T(8,128)(2,1)S(1)}, bf16[576,256]{1,0:T(8,128)(2,1)S(1)}, u32[]{:S(2)}, u32[]{:S(2)}) collective-permute-start(bf16[576,256]{1,0:T(8,128)(2,1)S(1)} %get-tuple-element.51), channel_id=1, source_target_pairs={{0,8},{8,0},{16,24},{24,16},{32,40},{40,32},{48,56},{56,48},{64,72... | collective-permute-start | bytes 884744 | tf_op jit(solution)/shard_map/ppermute | solution.py:342
  35.6 5.6 %collective-permute-start.13 = (bf16[192,256]{1,0:T(8,128)(2,1)S(1)}, bf16[192,256]{1,0:T(8,128)(2,1)S(1)}, u32[]{:S(2)}, u32[]{:S(2)}) collective-permute-start(bf16[192,256]{1,0:T(8,128)(2,1)S(1)} %get-tuple-element.53), channel_id=1, source_target_pairs={{0,16},{8,24},{16,0},{24,8},{32,48},{40,56},{48,32},{56,40},{64,80... | collective-permute-start | bytes 294920 | tf_op jit(solution)/shard_map/ppermute | solution.py:342
  37.2 6.1 %collective-permute-start.14 = (bf16[192,256]{1,0:T(8,128)(2,1)S(1)}, bf16[192,256]{1,0:T(8,128)(2,1)S(1)}, u32[]{:S(2)}, u32[]{:S(2)}) collective-permute-start(bf16[192,256]{1,0:T(8,128)(2,1)S(1)} %get-tuple-element.55), channel_id=1, source_target_pairs={{0,240},{8,248},{16,0},{24,8},{32,16},{40,24},{48,32},{56,40},{64,... | collective-permute-start | bytes 294920 | tf_op jit(solution)/shard_map/ppermute | solution.py:342
  41.2 8.3 %collective-permute-start.15 = (bf16[192,256]{1,0:T(8,128)(2,1)S(1)}, bf16[192,256]{1,0:T(8,128)(2,1)S(1)}, u32[]{:S(2)}, u32[]{:S(2)}) collective-permute-start(bf16[192,256]{1,0:T(8,128)(2,1)S(1)} %get-tuple-element.54.refs_0_), channel_id=1, source_target_pairs={{0,192},{8,200},{16,208},{24,216},{32,224},{40,232},{48,240},{56,2... | collective-permute-start | bytes 294920 | tf_op jit(solution)/shard_map/ppermute | solution.py:342
  41.3 8.2 %collective-permute-start.16 = (bf16[192,256]{1,0:T(8,128)(2,1)S(1)}, bf16[192,256]{1,0:T(8,128)(2,1)S(1)}, u32[]{:S(2)}, u32[]{:S(2)}) collective-permute-start(bf16[192,256]{1,0:T(8,128)(2,1)S(1)} %get-tuple-element.58), channel_id=1, source_target_pairs={{0,224},{8,232},{16,240},{24,248},{32,0},{40,8},{48,16},{56,24},{6... | collective-permute-start | bytes 294920 | tf_op jit(solution)/shard_map/ppermute | solution.py:342

commit v18 on v16

--- a/solution.py
+++ b/solution.py
@@ -314,7 +314,7 @@
     out_ref[...] = total + two_ref[...].astype(jnp.float32)
 
 
-def finish_kernel(sum_ref, eight_ref, four_ref, k_ref, v_ref):
+def finish_kernel(sum_ref, four_ref, eight_ref, k_ref, v_ref):
     total = sum_ref[...] + four_ref[...].astype(jnp.float32) + eight_ref[...].astype(jnp.float32)
     total = total.astype(jnp.bfloat16)
     k_ref[...] = total[:, :D]
@@ -486,7 +486,7 @@
         "gather_near", gather_kernel, shape(ROWS, 2 * D, f32), vmem(3), (last_own, near_back, by_two)
     )
     grad_keys, grad_values = call(
-        "finish", finish_kernel, (shape(ROWS, D, bf16), shape(ROWS, D, bf16)), vmem(3), (partial_sum, by_eight, by_four)
+        "finish", finish_kernel, (shape(ROWS, D, bf16), shape(ROWS, D, bf16)), vmem(3), (partial_sum, by_four, by_eight)
     )
     return grad_queries, grad_keys, grad_values
 

time: 50.6 us -> 51.4 us (1.016)
  waiting for transfers between devices: 11.7 us -> 12.9 us
    ppermute x17, waiting for transfers between devices: 11.7 us -> 12.9 us  [moved(): lax.ppermute(x, axis, [(i, to(i)) for i in range(lax.axis_size(axis))])]
where the time goes in v18:
time: 51.4 us; the launch traced here: 51.2 us
  starting transfers between devices  23.3 us (45%)
  Pallas kernels  13.4 us (26%)
  waiting for transfers between devices  12.9 us (25%)
  other arithmetic  0.83 us (2%)
  between operations  0.83 us (2%)
    ppermute x17, starting transfers between devices, moved(): lax.ppermute(x, axis, [(i, to(i)) for i in range(lax.axis_size(axis))])  23.3 us
    pallas_call x20, Pallas kernels, call(): pl.pallas_call(kernel, out_shape=outs, in_specs=ins, out_specs=vmem(1)[0]...  13.4 us
    ppermute x17, waiting for transfers between devices, moved(): lax.ppermute(x, axis, [(i, to(i)) for i in range(lax.axis_size(axis))])  12.9 us
  transfers between devices with their start and end apart: 17, of which 5 were waited for; matrix products, arithmetic and copies ran while one was open for 2% of the time, Pallas kernels for 20%

profile of v18, /device:TPU:64, one launch (start us, length us, event | category | flops | bytes accessed | tf_op | source)
XLA Modules:
  0.0 51.2 jit_solution(16609905923698284860)
XLA Ops:
  0.6 3.3 %collective-permute-start.2 = (bf16[192,512]{1,0:T(8,128)(2,1)}, bf16[192,512]{1,0:T(8,128)(2,1)S(1)}, u32[]{:S(2)}, u32[]{:S(2)}) collective-permute-start(bf16[192,512]{1,0:T(8,128)(2,1)} %refs_0_.1), channel_id=1, source_target_pairs={{0,1},{1,0},{2,3},{3,2},{4,5},{5,4},{6,7},{7,6},{8,9},{9,8},{10,11... | collective-permute-start | bytes 589832 | tf_op jit(solution)/shard_map/ppermute | solution.py:341
  3.9 1.5 %collective-permute-start.3 = (bf16[192,512]{1,0:T(8,128)(2,1)}, bf16[192,512]{1,0:T(8,128)(2,1)S(1)}, u32[]{:S(2)}, u32[]{:S(2)}) collective-permute-start(bf16[192,512]{1,0:T(8,128)(2,1)} %refs_0_.1), channel_id=1, source_target_pairs={{0,2},{1,3},{2,4},{3,5},{4,6},{5,7},{6,0},{7,1},{8,10},{9,11},{10,... | collective-permute-start | bytes 589832 | tf_op jit(solution)/shard_map/ppermute | solution.py:341
  5.4 1.7 %collective-permute-start.4 = (bf16[192,512]{1,0:T(8,128)(2,1)}, bf16[192,512]{1,0:T(8,128)(2,1)S(1)}, u32[]{:S(2)}, u32[]{:S(2)}) collective-permute-start(bf16[192,512]{1,0:T(8,128)(2,1)} %refs_0_.1), channel_id=1, source_target_pairs={{0,6},{1,7},{2,0},{3,1},{4,2},{5,3},{6,4},{7,5},{8,14},{9,15},{10,... | collective-permute-start | bytes 589832 | tf_op jit(solution)/shard_map/ppermute | solution.py:341
  7.1 0.8 %pad_add_fusion.z0_ref = bf16[192,256]{1,0:T(8,128)(2,1)S(1)} fusion(bf16[192,128]{1,0:T(8,128)(2,1)} %param.8, bf16[192,128]{1,0:T(8,128)(2,1)} %param.7), kind=kLoop, calls=%fused_computation | loop fusion | flops 196608 | bytes 196608 | tf_op jit(solution)/shard_map/add | solution.py:378
  8.0 4.6 %collective-permute-start = (bf16[192,256]{1,0:T(8,128)(2,1)S(1)}, bf16[192,256]{1,0:T(8,128)(2,1)S(1)}, u32[]{:S(2)}, u32[]{:S(2)}) collective-permute-start(bf16[192,256]{1,0:T(8,128)(2,1)S(1)} %pad_add_fusion.z0_ref), channel_id=1, source_target_pairs={{0,64},{8,72},{16,80},{24,88},{32,96},{40,104},{48,112},{56,120},{... | collective-permute-start | bytes 294920 | tf_op jit(solution)/shard_map/ppermute | solution.py:341
  12.5 1.0 %collective-permute-start.1 = (bf16[192,256]{1,0:T(8,128)(2,1)S(1)}, bf16[192,256]{1,0:T(8,128)(2,1)S(1)}, u32[]{:S(2)}, u32[]{:S(2)}) collective-permute-start(bf16[192,256]{1,0:T(8,128)(2,1)S(1)} %pad_add_fusion.z0_ref), channel_id=1, source_target_pairs={{0,32},{8,40},{16,48},{24,56},{32,64},{40,72},{48,80},{56,88},{64,... | collective-permute-start | bytes 294920 | tf_op jit(solution)/shard_map/ppermute | solution.py:341
  13.6 2.3 %load.1 = (bf16[768,128]{1,0:T(8,128)(2,1)S(1)}, f32[8,768]{1,0:T(8,128)S(1)}, bf16[512,4096]{1,0:T(8,128)(2,1)S(1)}) custom-call(s32[1]{0:T(128)} %bitcast.place_ref, s32[1]{0:T(128)} %bitcast.1.head_ref, s32[8]{0:T(128)} %len_hbm.1, bf16[192,512]{1,0:T(8,128)(2,1)} %q_hbm.1, bf16[512,4096]{1,0:T(8,128)(2,1)} %w_hbm.1), custom_call_target="tpu_custom_call" | custom-call | flops 1 | bytes 1 | tf_op jit(solution)/shard_map/load/pallas_call | solution.py:355
  15.9 1.6 %collective-permute-start.7 = (bf16[192,512]{1,0:T(8,128)(2,1)S(1)}, bf16[192,512]{1,0:T(8,128)(2,1)S(1)}, u32[]{:S(2)}, u32[]{:S(2)}) collective-permute-start(bf16[192,512]{1,0:T(8,128)(2,1)S(1)} %stage.1.refs_0_.refs_1_), channel_id=1, source_target_pairs={{0,6},{1,7},{2,0},{3,1},{4,2},{5,3},{6,4},{7,5},{8,14},{9,15},{10,... | collective-permute-start | bytes 589832 | tf_op jit(solution)/shard_map/ppermute | solution.py:341
  17.6 0.5 collective-permute-start.6
  18.1 0.8 %collective-permute-start.5 = (bf16[384,256]{1,0:T(8,128)(2,1)S(1)}, bf16[384,256]{1,0:T(8,128)(2,1)S(1)}, u32[]{:S(2)}, u32[]{:S(2)}) collective-permute-start(bf16[384,256]{1,0:T(8,128)(2,1)S(1)} %pick_side.1.refs_0_), channel_id=1, source_target_pairs={{0,16},{8,24},{16,0},{24,8},{32,48},{40,56},{48,32},{56,40},{64,80... | collective-permute-start | bytes 589832 | tf_op jit(solution)/shard_map/ppermute | solution.py:341
  18.9 0.3 collective-permute-start.9
  19.2 2.6 %collective-permute-done.7.refs_2_.refs_5_ = bf16[192,512]{1,0:T(8,128)(2,1)S(1)} collective-permute-done((bf16[192,512]{1,0:T(8,128)(2,1)S(1)}, bf16[192,512]{1,0:T(8,128)(2,1)S(1)}, u32[]{:S(2)}, u32[]{:S(2)}) %collective-permute-start.7) | collective-permute-done | bytes 196640 | tf_op jit(solution)/shard_map/ppermute | solution.py:341
  21.7 2.7 %collective-permute-start.8 = (bf16[192,512]{1,0:T(8,128)(2,1)S(1)}, bf16[192,512]{1,0:T(8,128)(2,1)S(1)}, u32[]{:S(2)}, u32[]{:S(2)}) collective-permute-start(bf16[192,512]{1,0:T(8,128)(2,1)S(1)} %collective-permute-done.7.refs_2_.refs_5_), channel_id=1, source_target_pairs={{0,6},{1,7},{2,0},{3,1},{4,2},{5,3},{6,4},{7,5},{8,14},{9,15},{10,... | collective-permute-start | bytes 589832 | tf_op jit(solution)/shard_map/ppermute | solution.py:341
  24.5 1.4 %collective-permute-done.6.refs_1_.refs_4_ = bf16[192,512]{1,0:T(8,128)(2,1)S(1)} collective-permute-done((bf16[192,512]{1,0:T(8,128)(2,1)S(1)}, bf16[192,512]{1,0:T(8,128)(2,1)S(1)}, u32[]{:S(2)}, u32[]{:S(2)}) %collective-permute-start.6) | collective-permute-done | bytes 196640 | tf_op jit(solution)/shard_map/ppermute | solution.py:341
  25.9 1.3 %near.1 = (bf16[576,768]{1,0:T(8,128)(2,1)S(1)}, f32[152,768]{1,0:T(8,128)S(1)}) custom-call(s32[1]{0:T(128)} %bitcast.place_ref, bf16[192,256]{1,0:T(8,128)(2,1)S(1)} %collective-permute-done.z2_ref, bf16[192,256]{1,0:T(8,128)(2,1)S(1)} %collective-permute-done.1.z1_ref, bf16[192,256]{1,0:T(8,128)(2,1)S(1)} %pad_add_fusion.z0_ref, ...), custom_call_target="tpu_custom_call" | custom-call | flops 1 | bytes 1 | tf_op jit(solution)/shard_map/near/pallas_call | solution.py:355
  27.5 0.9 %middle.1 = (bf16[384,768]{1,0:T(8,128)(2,1)S(1)}, f32[152,768]{1,0:T(8,128)S(1)}) custom-call(s32[1]{0:T(128)} %bitcast.place_ref, bf16[960,256]{1,0:T(8,128)(2,1)S(1)} %join_slots.1.own_ref, bf16[768,128]{1,0:T(8,128)(2,1)S(1)} %get-tuple-element.32.after.refs_3_.q4_ref, f32[152,768]{1,0:T(8,128)S(1)} %get-tuple-element.34.refs_0_.st_in_ref), custom_call_target="tpu_custom_call" | custom-call | flops 1 | bytes 1 | tf_op jit(solution)/shard_map/middle/pallas_call | solution.py:355
  28.4 1.4 %project.1.acc_ref = f32[192,512]{1,0:T(8,128)S(1)} custom-call(bf16[192,512]{1,0:T(8,128)(2,1)S(1)} %copy-done, bf16[192,512]{1,0:T(8,128)(2,1)S(1)} %stage.1.refs_0_.refs_1_, bf16[192,512]{1,0:T(8,128)(2,1)S(1)} %collective-permute-done.3.refs_1_.refs_2_, bf16[192,512]{1,0:T(8,128)(2,1)S(1)} %collective-permute-done.4.refs_2_.refs_3_, ...), custom_call_target="tpu_custom_call" | custom-call | flops 1 | bytes 1 | tf_op jit(solution)/shard_map/project/pallas_call | solution.py:355
  29.7 0.5 last_projection.1
  30.2 1.6 %across.1 = (bf16[768,768]{1,0:T(8,128)(2,1)S(1)}, f32[152,768]{1,0:T(8,128)S(1)}) custom-call(s32[1]{0:T(128)} %bitcast.place_ref, bf16[960,256]{1,0:T(8,128)(2,1)S(1)} %collective-permute-done.10.par_ref, bf16[768,128]{1,0:T(8,128)(2,1)S(1)} %get-tuple-element.32.after.refs_3_.q4_ref, f32[128,768]{1,0:T(8,128)S(1)} %get-tuple-element.40.gt_ref, ...), custom_call_target="tpu_custom_call" | custom-call | flops 1 | bytes 1 | tf_op jit(solution)/shard_map/across/pallas_call | solution.py:355
  31.8 0.9 %cross_far.1 = (bf16[384,256]{1,0:T(8,128)(2,1)S(1)}, f32[152,768]{1,0:T(8,128)S(1)}) custom-call(s32[1]{0:T(128)} %bitcast.place_ref, bf16[768,128]{1,0:T(8,128)(2,1)S(1)} %get-tuple-element.32.after.refs_3_.q4_ref, bf16[960,256]{1,0:T(8,128)(2,1)S(1)} %collective-permute-done.10.par_ref, bf16[768,768]{1,0:T(8,128)(2,1)S(1)} %get-tuple-element.41.p_ref, ...), custom_call_target="tpu_custom_call" | custom-call | flops 1 | bytes 1 | tf_op jit(solution)/shard_map/cross_far/pallas_call | solution.py:355
  32.9 0.8 %cross_near.1 = (bf16[576,256]{1,0:T(8,128)(2,1)S(1)}, f32[152,768]{1,0:T(8,128)S(1)}) custom-call(s32[1]{0:T(128)} %bitcast.place_ref, bf16[768,128]{1,0:T(8,128)(2,1)S(1)} %get-tuple-element.32.after.refs_3_.q4_ref, bf16[960,256]{1,0:T(8,128)(2,1)S(1)} %collective-permute-done.10.par_ref, bf16[768,768]{1,0:T(8,128)(2,1)S(1)} %get-tuple-element.41.p_ref, ...), custom_call_target="tpu_custom_call" | custom-call | flops 4000000000 | bytes 1 | tf_op jit(solution)/shard_map/cross_near/pallas_call | solution.py:355
  33.7 1.0 %collective-permute-start.12 = (bf16[576,256]{1,0:T(8,128)(2,1)S(1)}, bf16[576,256]{1,0:T(8,128)(2,1)S(1)}, u32[]{:S(2)}, u32[]{:S(2)}) collective-permute-start(bf16[576,256]{1,0:T(8,128)(2,1)S(1)} %get-tuple-element.51), channel_id=1, source_target_pairs={{0,8},{8,0},{16,24},{24,16},{32,40},{40,32},{48,56},{56,48},{64,72... | collective-permute-start | bytes 884744 | tf_op jit(solution)/shard_map/ppermute | solution.py:341
  34.7 0.8 %own_far.1 = (f32[384,256]{1,0:T(8,128)S(1)}, f32[152,768]{1,0:T(8,128)S(1)}) custom-call(bf16[768,128]{1,0:T(8,128)(2,1)S(1)} %get-tuple-element.32.after.refs_3_.q4_ref, bf16[960,256]{1,0:T(8,128)(2,1)S(1)} %join_slots.1.own_ref, bf16[576,768]{1,0:T(8,128)(2,1)S(1)} %get-tuple-element.35.near_ref, bf16[384,768]{1,0:T(8,128)(2,1)S(1)} %get-tuple-element.36.side_ref, ...), custom_call_target="tpu_custom_call" | custom-call | flops 4000000000 | bytes 1 | tf_op jit(solution)/shard_map/own_far/pallas_call | solution.py:355
  35.6 0.8 %collective-permute-start.13 = (bf16[192,256]{1,0:T(8,128)(2,1)S(1)}, bf16[192,256]{1,0:T(8,128)(2,1)S(1)}, u32[]{:S(2)}, u32[]{:S(2)}) collective-permute-start(bf16[192,256]{1,0:T(8,128)(2,1)S(1)} %get-tuple-element.53), channel_id=1, source_target_pairs={{0,16},{8,24},{16,0},{24,8},{32,48},{40,56},{48,32},{56,40},{64,80... | collective-permute-start | bytes 294920 | tf_op jit(solution)/shard_map/ppermute | solution.py:341
  36.3 0.8 %own_near.1 = (f32[384,256]{1,0:T(8,128)S(1)}, f32[152,768]{1,0:T(8,128)S(1)}) custom-call(bf16[768,128]{1,0:T(8,128)(2,1)S(1)} %get-tuple-element.32.after.refs_3_.q4_ref, bf16[960,256]{1,0:T(8,128)(2,1)S(1)} %join_slots.1.own_ref, bf16[576,768]{1,0:T(8,128)(2,1)S(1)} %get-tuple-element.35.near_ref, bf16[384,768]{1,0:T(8,128)(2,1)S(1)} %get-tuple-element.36.side_ref, ...), custom_call_target="tpu_custom_call" | custom-call | flops 4000000000 | bytes 1 | tf_op jit(solution)/shard_map/own_near/pallas_call | solution.py:355
  37.2 1.9 %collective-permute-start.14 = (bf16[192,256]{1,0:T(8,128)(2,1)S(1)}, bf16[192,256]{1,0:T(8,128)(2,1)S(1)}, u32[]{:S(2)}, u32[]{:S(2)}) collective-permute-start(bf16[192,256]{1,0:T(8,128)(2,1)S(1)} %get-tuple-element.55), channel_id=1, source_target_pairs={{0,240},{8,248},{16,0},{24,8},{32,16},{40,24},{48,32},{56,40},{64,... | collective-permute-start | bytes 294920 | tf_op jit(solution)/shard_map/ppermute | solution.py:341
  39.1 2.1 %collective-permute-done.13.side_ref = bf16[192,256]{1,0:T(8,128)(2,1)S(1)} collective-permute-done((bf16[192,256]{1,0:T(8,128)(2,1)S(1)}, bf16[192,256]{1,0:T(8,128)(2,1)S(1)}, u32[]{:S(2)}, u32[]{:S(2)}) %collective-permute-start.13) | collective-permute-done | bytes 98336 | tf_op jit(solution)/shard_map/ppermute | solution.py:341
  41.2 1.1 %collective-permute-start.15 = (bf16[192,256]{1,0:T(8,128)(2,1)S(1)}, bf16[192,256]{1,0:T(8,128)(2,1)S(1)}, u32[]{:S(2)}, u32[]{:S(2)}) collective-permute-start(bf16[192,256]{1,0:T(8,128)(2,1)S(1)} %get-tuple-element.58), channel_id=1, source_target_pairs={{0,224},{8,232},{16,240},{24,248},{32,0},{40,8},{48,16},{56,24},{6... | collective-permute-start | bytes 294920 | tf_op jit(solution)/shard_map/ppermute | solution.py:341
  42.5 1.2 %own_last.1 = (f32[192,256]{1,0:T(8,128)S(1)}, bf16[192,512]{1,0:T(8,128)(2,1)}) custom-call(bf16[768,128]{1,0:T(8,128)(2,1)S(1)} %get-tuple-element.32.after.refs_3_.q4_ref, bf16[960,256]{1,0:T(8,128)(2,1)S(1)} %join_slots.1.own_ref, bf16[576,768]{1,0:T(8,128)(2,1)S(1)} %get-tuple-element.35.near_ref, bf16[384,768]{1,0:T(8,128)(2,1)S(1)} %get-tuple-element.36.side_ref, ...), custom_call_target="tpu_custom_call" | custom-call | flops 4000000000 | bytes 1 | tf_op jit(solution)/shard_map/own_last/pallas_call | solution.py:355
  43.7 2.6 %collective-permute-done.15.four_ref = bf16[192,256]{1,0:T(8,128)(2,1)S(1)} collective-permute-done((bf16[192,256]{1,0:T(8,128)(2,1)S(1)}, bf16[192,256]{1,0:T(8,128)(2,1)S(1)}, u32[]{:S(2)}, u32[]{:S(2)}) %collective-permute-start.15) | collective-permute-done | bytes 98336 | tf_op jit(solution)/shard_map/ppermute | solution.py:341
  46.3 4.2 %collective-permute-done.16.eight_ref = bf16[192,256]{1,0:T(8,128)(2,1)S(1)} collective-permute-done((bf16[192,256]{1,0:T(8,128)(2,1)S(1)}, bf16[192,256]{1,0:T(8,128)(2,1)S(1)}, u32[]{:S(2)}, u32[]{:S(2)}) %collective-permute-start.16) | collective-permute-done | bytes 98336 | tf_op jit(solution)/shard_map/ppermute | solution.py:341
  50.5 0.7 %finish.1 = (bf16[192,128]{1,0:T(8,128)(2,1)}, bf16[192,128]{1,0:T(8,128)(2,1)}) custom-call(f32[192,256]{1,0:T(8,128)S(1)} %gather_near.1.sum_ref, bf16[192,256]{1,0:T(8,128)(2,1)S(1)} %collective-permute-done.15.four_ref, bf16[192,256]{1,0:T(8,128)(2,1)S(1)} %collective-permute-done.16.eight_ref), custom_call_target="tpu_custom_call" | custom-call | flops 1 | bytes 1 | tf_op jit(solution)/shard_map/finish/pallas_call | solution.py:355
  (25 shorter events, 0.9 us)
Async XLA Ops:
  0.6 15.3 %collective-permute-start.2 = (bf16[192,512]{1,0:T(8,128)(2,1)}, bf16[192,512]{1,0:T(8,128)(2,1)S(1)}, u32[]{:S(2)}, u32[]{:S(2)}) collective-permute-start(bf16[192,512]{1,0:T(8,128)(2,1)} %refs_0_.1), channel_id=1, source_target_pairs={{0,1},{1,0},{2,3},{3,2},{4,5},{5,4},{6,7},{7,6},{8,9},{9,8},{10,11... | collective-permute-start | bytes 589832 | tf_op jit(solution)/shard_map/ppermute | solution.py:341
  3.9 13.7 %collective-permute-start.3 = (bf16[192,512]{1,0:T(8,128)(2,1)}, bf16[192,512]{1,0:T(8,128)(2,1)S(1)}, u32[]{:S(2)}, u32[]{:S(2)}) collective-permute-start(bf16[192,512]{1,0:T(8,128)(2,1)} %refs_0_.1), channel_id=1, source_target_pairs={{0,2},{1,3},{2,4},{3,5},{4,6},{5,7},{6,0},{7,1},{8,10},{9,11},{10,... | collective-permute-start | bytes 589832 | tf_op jit(solution)/shard_map/ppermute | solution.py:341
  5.4 12.7 %collective-permute-start.4 = (bf16[192,512]{1,0:T(8,128)(2,1)}, bf16[192,512]{1,0:T(8,128)(2,1)S(1)}, u32[]{:S(2)}, u32[]{:S(2)}) collective-permute-start(bf16[192,512]{1,0:T(8,128)(2,1)} %refs_0_.1), channel_id=1, source_target_pairs={{0,6},{1,7},{2,0},{3,1},{4,2},{5,3},{6,4},{7,5},{8,14},{9,15},{10,... | collective-permute-start | bytes 589832 | tf_op jit(solution)/shard_map/ppermute | solution.py:341
  8.0 10.1 %collective-permute-start = (bf16[192,256]{1,0:T(8,128)(2,1)S(1)}, bf16[192,256]{1,0:T(8,128)(2,1)S(1)}, u32[]{:S(2)}, u32[]{:S(2)}) collective-permute-start(bf16[192,256]{1,0:T(8,128)(2,1)S(1)} %pad_add_fusion.z0_ref), channel_id=1, source_target_pairs={{0,64},{8,72},{16,80},{24,88},{32,96},{40,104},{48,112},{56,120},{... | collective-permute-start | bytes 294920 | tf_op jit(solution)/shard_map/ppermute | solution.py:341
  12.5 5.5 %collective-permute-start.1 = (bf16[192,256]{1,0:T(8,128)(2,1)S(1)}, bf16[192,256]{1,0:T(8,128)(2,1)S(1)}, u32[]{:S(2)}, u32[]{:S(2)}) collective-permute-start(bf16[192,256]{1,0:T(8,128)(2,1)S(1)} %pad_add_fusion.z0_ref), channel_id=1, source_target_pairs={{0,32},{8,40},{16,48},{24,56},{32,64},{40,72},{48,80},{56,88},{64,... | collective-permute-start | bytes 294920 | tf_op jit(solution)/shard_map/ppermute | solution.py:341
  13.6 14.8 %copy-start = (bf16[192,512]{1,0:T(8,128)(2,1)S(1)}, bf16[192,512]{1,0:T(8,128)(2,1)}, u32[]{:S(2)}) copy-start(bf16[192,512]{1,0:T(8,128)(2,1)} %refs_0_.1) | copy-start | bytes 589828
  15.9 5.8 %collective-permute-start.7 = (bf16[192,512]{1,0:T(8,128)(2,1)S(1)}, bf16[192,512]{1,0:T(8,128)(2,1)S(1)}, u32[]{:S(2)}, u32[]{:S(2)}) collective-permute-start(bf16[192,512]{1,0:T(8,128)(2,1)S(1)} %stage.1.refs_0_.refs_1_), channel_id=1, source_target_pairs={{0,6},{1,7},{2,0},{3,1},{4,2},{5,3},{6,4},{7,5},{8,14},{9,15},{10,... | collective-permute-start | bytes 589832 | tf_op jit(solution)/shard_map/ppermute | solution.py:341
  17.6 8.3 %collective-permute-start.6 = (bf16[192,512]{1,0:T(8,128)(2,1)S(1)}, bf16[192,512]{1,0:T(8,128)(2,1)S(1)}, u32[]{:S(2)}, u32[]{:S(2)}) collective-permute-start(bf16[192,512]{1,0:T(8,128)(2,1)S(1)} %stage.1.refs_0_.refs_1_), channel_id=1, source_target_pairs={{0,2},{1,3},{2,4},{3,5},{4,6},{5,7},{6,0},{7,1},{8,10},{9,11},{10,... | collective-permute-start | bytes 589832 | tf_op jit(solution)/shard_map/ppermute | solution.py:341
  18.1 9.0 %collective-permute-start.5 = (bf16[384,256]{1,0:T(8,128)(2,1)S(1)}, bf16[384,256]{1,0:T(8,128)(2,1)S(1)}, u32[]{:S(2)}, u32[]{:S(2)}) collective-permute-start(bf16[384,256]{1,0:T(8,128)(2,1)S(1)} %pick_side.1.refs_0_), channel_id=1, source_target_pairs={{0,16},{8,24},{16,0},{24,8},{32,48},{40,56},{48,32},{56,40},{64,80... | collective-permute-start | bytes 589832 | tf_op jit(solution)/shard_map/ppermute | solution.py:341
  18.9 9.5 %collective-permute-start.9 = (bf16[192,512]{1,0:T(8,128)(2,1)S(1)}, bf16[192,512]{1,0:T(8,128)(2,1)S(1)}, u32[]{:S(2)}, u32[]{:S(2)}) collective-permute-start(bf16[192,512]{1,0:T(8,128)(2,1)S(1)} %collective-permute-done.3.refs_1_.refs_2_), channel_id=1, source_target_pairs={{0,2},{1,3},{2,4},{3,5},{4,6},{5,7},{6,0},{7,1},{8,10},{9,11},{10,... | collective-permute-start | bytes 589832 | tf_op jit(solution)/shard_map/ppermute | solution.py:341
  21.7 8.0 %collective-permute-start.8 = (bf16[192,512]{1,0:T(8,128)(2,1)S(1)}, bf16[192,512]{1,0:T(8,128)(2,1)S(1)}, u32[]{:S(2)}, u32[]{:S(2)}) collective-permute-start(bf16[192,512]{1,0:T(8,128)(2,1)S(1)} %collective-permute-done.7.refs_2_.refs_5_), channel_id=1, source_target_pairs={{0,6},{1,7},{2,0},{3,1},{4,2},{5,3},{6,4},{7,5},{8,14},{9,15},{10,... | collective-permute-start | bytes 589832 | tf_op jit(solution)/shard_map/ppermute | solution.py:341
  27.2 3.0 %collective-permute-start.10 = (bf16[960,256]{1,0:T(8,128)(2,1)S(1)}, bf16[960,256]{1,0:T(8,128)(2,1)S(1)}, u32[]{:S(2)}, u32[]{:S(2)}) collective-permute-start(bf16[960,256]{1,0:T(8,128)(2,1)S(1)} %join_slots.1.own_ref), channel_id=1, source_target_pairs={{0,8},{8,0},{16,24},{24,16},{32,40},{40,32},{48,56},{56,48},{64,72... | collective-permute-start | bytes 1474568 | tf_op jit(solution)/shard_map/ppermute | solution.py:341
  32.7 2.8 %collective-permute-start.11 = (bf16[384,256]{1,0:T(8,128)(2,1)S(1)}, bf16[384,256]{1,0:T(8,128)(2,1)S(1)}, u32[]{:S(2)}, u32[]{:S(2)}) collective-permute-start(bf16[384,256]{1,0:T(8,128)(2,1)S(1)} %get-tuple-element.47), channel_id=1, source_target_pairs={{0,8},{8,0},{16,24},{24,16},{32,40},{40,32},{48,56},{56,48},{64,72... | collective-permute-start | bytes 589832 | tf_op jit(solution)/shard_map/ppermute | solution.py:341
  33.7 3.5 %collective-permute-start.12 = (bf16[576,256]{1,0:T(8,128)(2,1)S(1)}, bf16[576,256]{1,0:T(8,128)(2,1)S(1)}, u32[]{:S(2)}, u32[]{:S(2)}) collective-permute-start(bf16[576,256]{1,0:T(8,128)(2,1)S(1)} %get-tuple-element.51), channel_id=1, source_target_pairs={{0,8},{8,0},{16,24},{24,16},{32,40},{40,32},{48,56},{56,48},{64,72... | collective-permute-start | bytes 884744 | tf_op jit(solution)/shard_map/ppermute | solution.py:341
  35.6 5.6 %collective-permute-start.13 = (bf16[192,256]{1,0:T(8,128)(2,1)S(1)}, bf16[192,256]{1,0:T(8,128)(2,1)S(1)}, u32[]{:S(2)}, u32[]{:S(2)}) collective-permute-start(bf16[192,256]{1,0:T(8,128)(2,1)S(1)} %get-tuple-element.53), channel_id=1, source_target_pairs={{0,16},{8,24},{16,0},{24,8},{32,48},{40,56},{48,32},{56,40},{64,80... | collective-permute-start | bytes 294920 | tf_op jit(solution)/shard_map/ppermute | solution.py:341
  37.2 5.3 %collective-permute-start.14 = (bf16[192,256]{1,0:T(8,128)(2,1)S(1)}, bf16[192,256]{1,0:T(8,128)(2,1)S(1)}, u32[]{:S(2)}, u32[]{:S(2)}) collective-permute-start(bf16[192,256]{1,0:T(8,128)(2,1)S(1)} %get-tuple-element.55), channel_id=1, source_target_pairs={{0,240},{8,248},{16,0},{24,8},{32,16},{40,24},{48,32},{56,40},{64,... | collective-permute-start | bytes 294920 | tf_op jit(solution)/shard_map/ppermute | solution.py:341
  41.2 5.1 %collective-permute-start.15 = (bf16[192,256]{1,0:T(8,128)(2,1)S(1)}, bf16[192,256]{1,0:T(8,128)(2,1)S(1)}, u32[]{:S(2)}, u32[]{:S(2)}) collective-permute-start(bf16[192,256]{1,0:T(8,128)(2,1)S(1)} %get-tuple-element.58), channel_id=1, source_target_pairs={{0,224},{8,232},{16,240},{24,248},{32,0},{40,8},{48,16},{56,24},{6... | collective-permute-start | bytes 294920 | tf_op jit(solution)/shard_map/ppermute | solution.py:341
  42.2 8.3 %collective-permute-start.16 = (bf16[192,256]{1,0:T(8,128)(2,1)S(1)}, bf16[192,256]{1,0:T(8,128)(2,1)S(1)}, u32[]{:S(2)}, u32[]{:S(2)}) collective-permute-start(bf16[192,256]{1,0:T(8,128)(2,1)S(1)} %get-tuple-element.54.refs_0_), channel_id=1, source_target_pairs={{0,192},{8,200},{16,208},{24,216},{32,224},{40,232},{48,240},{56,2... | collective-permute-start | bytes 294920 | tf_op jit(solution)/shard_map/ppermute | solution.py:341

commit v19 on v16

--- a/solution.py
+++ b/solution.py
@@ -65,6 +65,15 @@
         copy.wait()
 
 
+def pack_kernel(k_hbm, v_hbm, out_ref, sems):
+    first = pltpu.make_async_copy(k_hbm, out_ref.at[:, :D], sems.at[0])
+    second = pltpu.make_async_copy(v_hbm, out_ref.at[:, D:], sems.at[1])
+    first.start()
+    second.start()
+    first.wait()
+    second.wait()
+
+
 def stage_kernel(piece_ref, after, out_ref):
     out_ref[...] = piece_ref[...]
 
@@ -375,7 +384,7 @@
     first = moved(grad_out, "head", lambda i: i ^ 1)
     right = turned(grad_out, "head", 2)
     left = turned(grad_out, "head", -2)
-    kv = jnp.pad(keys, ((0, 0), (0, D))) + jnp.pad(values, ((0, 0), (D, 0)))
+    kv = call("pack", pack_kernel, shape(ROWS, 2 * D, bf16), hbm(2), (pinned(keys), pinned(values)), [dma((2,))])
     z2 = turned(kv, "ctx", 2 * PLANE)
     z1 = turned(kv, "ctx", PLANE)
     q4, bound, weight = call(

time: 50.6 us -> 50.6 us (level)
  other arithmetic: 0.83 us -> 0 us
  Pallas kernels: 13.4 us -> 14.2 us
    pallas_call x20 -> x21, Pallas kernels: 13.4 us -> 14.2 us  [call(): pl.pallas_call(kernel, out_shape=outs, in_specs=ins, out_specs=vmem(1)[0]...]
    add x1 -> x0, other arithmetic: 0.83 us -> none  [local(): kv = jnp.pad(keys, ((0, 0), (0, D))) + jnp.pad(values, ((0, 0), (D, 0)))]
  transfers between devices with their start and end apart: 17 -> 17, of which waited for: 5 -> 5; matrix products, arithmetic and copies ran while one was open for 2% -> 0% of each run, Pallas kernels for 20% -> 22%
where the time goes in v19:
time: 50.6 us; the launch traced here: 50 us
  starting transfers between devices  23.3 us (46%)
  Pallas kernels  14.2 us (28%)
  waiting for transfers between devices  11.7 us (23%)
  between operations  0.84 us (2%)
    ppermute x17, starting transfers between devices, moved(): lax.ppermute(x, axis, [(i, to(i)) for i in range(lax.axis_size(axis))])  23.3 us
    pallas_call x21, Pallas kernels, call(): pl.pallas_call(kernel, out_shape=outs, in_specs=ins, out_specs=vmem(1)[0]...  14.2 us
    ppermute x17, waiting for transfers between devices, moved(): lax.ppermute(x, axis, [(i, to(i)) for i in range(lax.axis_size(axis))])  11.7 us
  transfers between devices with their start and end apart: 17, of which 5 were waited for; matrix products, arithmetic and copies ran while one was open for 0% of the time, Pallas kernels for 22%

profile of v19, /device:TPU:64, one launch (start us, length us, event | category | flops | bytes accessed | tf_op | source)
XLA Modules:
  0.0 50.0 jit_solution(5906131829069212454)
XLA Ops:
  0.6 3.3 %collective-permute-start.2 = (bf16[192,512]{1,0:T(8,128)(2,1)}, bf16[192,512]{1,0:T(8,128)(2,1)S(1)}, u32[]{:S(2)}, u32[]{:S(2)}) collective-permute-start(bf16[192,512]{1,0:T(8,128)(2,1)} %refs_0_.1), channel_id=1, source_target_pairs={{0,1},{1,0},{2,3},{3,2},{4,5},{5,4},{6,7},{7,6},{8,9},{9,8},{10,11... | collective-permute-start | bytes 589832 | tf_op jit(solution)/shard_map/ppermute | solution.py:350
  3.9 1.5 %collective-permute-start.3 = (bf16[192,512]{1,0:T(8,128)(2,1)}, bf16[192,512]{1,0:T(8,128)(2,1)S(1)}, u32[]{:S(2)}, u32[]{:S(2)}) collective-permute-start(bf16[192,512]{1,0:T(8,128)(2,1)} %refs_0_.1), channel_id=1, source_target_pairs={{0,2},{1,3},{2,4},{3,5},{4,6},{5,7},{6,0},{7,1},{8,10},{9,11},{10,... | collective-permute-start | bytes 589832 | tf_op jit(solution)/shard_map/ppermute | solution.py:350
  5.4 1.7 %collective-permute-start.4 = (bf16[192,512]{1,0:T(8,128)(2,1)}, bf16[192,512]{1,0:T(8,128)(2,1)S(1)}, u32[]{:S(2)}, u32[]{:S(2)}) collective-permute-start(bf16[192,512]{1,0:T(8,128)(2,1)} %refs_0_.1), channel_id=1, source_target_pairs={{0,6},{1,7},{2,0},{3,1},{4,2},{5,3},{6,4},{7,5},{8,14},{9,15},{10,... | collective-permute-start | bytes 589832 | tf_op jit(solution)/shard_map/ppermute | solution.py:350
  7.1 0.8 %pack.1.z0_ref = bf16[192,256]{1,0:T(8,128)(2,1)S(1)} custom-call(bf16[192,128]{1,0:T(8,128)(2,1)} %k_hbm.1, bf16[192,128]{1,0:T(8,128)(2,1)} %v_hbm.1), custom_call_target="tpu_custom_call" | custom-call | flops 1 | bytes 1 | tf_op jit(solution)/shard_map/pack/pallas_call | solution.py:364
  8.0 4.6 %collective-permute-start = (bf16[192,256]{1,0:T(8,128)(2,1)S(1)}, bf16[192,256]{1,0:T(8,128)(2,1)S(1)}, u32[]{:S(2)}, u32[]{:S(2)}) collective-permute-start(bf16[192,256]{1,0:T(8,128)(2,1)S(1)} %pack.1.z0_ref), channel_id=1, source_target_pairs={{0,64},{8,72},{16,80},{24,88},{32,96},{40,104},{48,112},{56,120},{... | collective-permute-start | bytes 294920 | tf_op jit(solution)/shard_map/ppermute | solution.py:350
  12.6 1.0 %collective-permute-start.1 = (bf16[192,256]{1,0:T(8,128)(2,1)S(1)}, bf16[192,256]{1,0:T(8,128)(2,1)S(1)}, u32[]{:S(2)}, u32[]{:S(2)}) collective-permute-start(bf16[192,256]{1,0:T(8,128)(2,1)S(1)} %pack.1.z0_ref), channel_id=1, source_target_pairs={{0,32},{8,40},{16,48},{24,56},{32,64},{40,72},{48,80},{56,88},{64,... | collective-permute-start | bytes 294920 | tf_op jit(solution)/shard_map/ppermute | solution.py:350
  13.6 2.3 %load.1 = (bf16[768,128]{1,0:T(8,128)(2,1)S(1)}, f32[8,768]{1,0:T(8,128)S(1)}, bf16[512,4096]{1,0:T(8,128)(2,1)S(1)}) custom-call(s32[1]{0:T(128)} %bitcast.place_ref, s32[1]{0:T(128)} %bitcast.1.head_ref, s32[8]{0:T(128)} %len_hbm.1, bf16[192,512]{1,0:T(8,128)(2,1)} %q_hbm.1, bf16[512,4096]{1,0:T(8,128)(2,1)} %w_hbm.1), custom_call_target="tpu_custom_call" | custom-call | flops 1 | bytes 1 | tf_op jit(solution)/shard_map/load/pallas_call | solution.py:364
  16.0 1.6 %collective-permute-start.7 = (bf16[192,512]{1,0:T(8,128)(2,1)S(1)}, bf16[192,512]{1,0:T(8,128)(2,1)S(1)}, u32[]{:S(2)}, u32[]{:S(2)}) collective-permute-start(bf16[192,512]{1,0:T(8,128)(2,1)S(1)} %stage.1.refs_0_.refs_1_), channel_id=1, source_target_pairs={{0,6},{1,7},{2,0},{3,1},{4,2},{5,3},{6,4},{7,5},{8,14},{9,15},{10,... | collective-permute-start | bytes 589832 | tf_op jit(solution)/shard_map/ppermute | solution.py:350
  17.6 0.5 collective-permute-start.6
  18.1 0.8 %collective-permute-start.5 = (bf16[384,256]{1,0:T(8,128)(2,1)S(1)}, bf16[384,256]{1,0:T(8,128)(2,1)S(1)}, u32[]{:S(2)}, u32[]{:S(2)}) collective-permute-start(bf16[384,256]{1,0:T(8,128)(2,1)S(1)} %pick_side.1.refs_0_), channel_id=1, source_target_pairs={{0,16},{8,24},{16,0},{24,8},{32,48},{40,56},{48,32},{56,40},{64,80... | collective-permute-start | bytes 589832 | tf_op jit(solution)/shard_map/ppermute | solution.py:350
  18.9 0.3 collective-permute-start.9
  19.2 2.6 %collective-permute-done.7.refs_2_.refs_5_ = bf16[192,512]{1,0:T(8,128)(2,1)S(1)} collective-permute-done((bf16[192,512]{1,0:T(8,128)(2,1)S(1)}, bf16[192,512]{1,0:T(8,128)(2,1)S(1)}, u32[]{:S(2)}, u32[]{:S(2)}) %collective-permute-start.7) | collective-permute-done | bytes 196640 | tf_op jit(solution)/shard_map/ppermute | solution.py:350
  21.8 2.7 %collective-permute-start.8 = (bf16[192,512]{1,0:T(8,128)(2,1)S(1)}, bf16[192,512]{1,0:T(8,128)(2,1)S(1)}, u32[]{:S(2)}, u32[]{:S(2)}) collective-permute-start(bf16[192,512]{1,0:T(8,128)(2,1)S(1)} %collective-permute-done.7.refs_2_.refs_5_), channel_id=1, source_target_pairs={{0,6},{1,7},{2,0},{3,1},{4,2},{5,3},{6,4},{7,5},{8,14},{9,15},{10,... | collective-permute-start | bytes 589832 | tf_op jit(solution)/shard_map/ppermute | solution.py:350
  24.5 1.4 %collective-permute-done.6.refs_1_.refs_4_ = bf16[192,512]{1,0:T(8,128)(2,1)S(1)} collective-permute-done((bf16[192,512]{1,0:T(8,128)(2,1)S(1)}, bf16[192,512]{1,0:T(8,128)(2,1)S(1)}, u32[]{:S(2)}, u32[]{:S(2)}) %collective-permute-start.6) | collective-permute-done | bytes 196640 | tf_op jit(solution)/shard_map/ppermute | solution.py:350
  25.9 1.3 %near.1 = (bf16[576,768]{1,0:T(8,128)(2,1)S(1)}, f32[152,768]{1,0:T(8,128)S(1)}) custom-call(s32[1]{0:T(128)} %bitcast.place_ref, bf16[192,256]{1,0:T(8,128)(2,1)S(1)} %collective-permute-done.z2_ref, bf16[192,256]{1,0:T(8,128)(2,1)S(1)} %collective-permute-done.1.z1_ref, bf16[192,256]{1,0:T(8,128)(2,1)S(1)} %pack.1.z0_ref, ...), custom_call_target="tpu_custom_call" | custom-call | flops 1 | bytes 1 | tf_op jit(solution)/shard_map/near/pallas_call | solution.py:364
  27.5 0.9 %middle.1 = (bf16[384,768]{1,0:T(8,128)(2,1)S(1)}, f32[152,768]{1,0:T(8,128)S(1)}) custom-call(s32[1]{0:T(128)} %bitcast.place_ref, bf16[960,256]{1,0:T(8,128)(2,1)S(1)} %join_slots.1.own_ref, bf16[768,128]{1,0:T(8,128)(2,1)S(1)} %get-tuple-element.32.after.refs_3_.q4_ref, f32[152,768]{1,0:T(8,128)S(1)} %get-tuple-element.34.refs_0_.st_in_ref), custom_call_target="tpu_custom_call" | custom-call | flops 1 | bytes 1 | tf_op jit(solution)/shard_map/middle/pallas_call | solution.py:364
  28.4 1.4 %project.1.acc_ref = f32[192,512]{1,0:T(8,128)S(1)} custom-call(bf16[192,512]{1,0:T(8,128)(2,1)S(1)} %copy-done, bf16[192,512]{1,0:T(8,128)(2,1)S(1)} %stage.1.refs_0_.refs_1_, bf16[192,512]{1,0:T(8,128)(2,1)S(1)} %collective-permute-done.3.refs_1_.refs_2_, bf16[192,512]{1,0:T(8,128)(2,1)S(1)} %collective-permute-done.4.refs_2_.refs_3_, ...), custom_call_target="tpu_custom_call" | custom-call | flops 1 | bytes 1 | tf_op jit(solution)/shard_map/project/pallas_call | solution.py:364
  29.7 0.5 last_projection.1
  30.2 1.6 %across.1 = (bf16[768,768]{1,0:T(8,128)(2,1)S(1)}, f32[152,768]{1,0:T(8,128)S(1)}) custom-call(s32[1]{0:T(128)} %bitcast.place_ref, bf16[960,256]{1,0:T(8,128)(2,1)S(1)} %collective-permute-done.10.par_ref, bf16[768,128]{1,0:T(8,128)(2,1)S(1)} %get-tuple-element.32.after.refs_3_.q4_ref, f32[128,768]{1,0:T(8,128)S(1)} %get-tuple-element.40.gt_ref, ...), custom_call_target="tpu_custom_call" | custom-call | flops 1 | bytes 1 | tf_op jit(solution)/shard_map/across/pallas_call | solution.py:364
  31.8 0.9 %cross_far.1 = (bf16[384,256]{1,0:T(8,128)(2,1)S(1)}, f32[152,768]{1,0:T(8,128)S(1)}) custom-call(s32[1]{0:T(128)} %bitcast.place_ref, bf16[768,128]{1,0:T(8,128)(2,1)S(1)} %get-tuple-element.32.after.refs_3_.q4_ref, bf16[960,256]{1,0:T(8,128)(2,1)S(1)} %collective-permute-done.10.par_ref, bf16[768,768]{1,0:T(8,128)(2,1)S(1)} %get-tuple-element.41.p_ref, ...), custom_call_target="tpu_custom_call" | custom-call | flops 1 | bytes 1 | tf_op jit(solution)/shard_map/cross_far/pallas_call | solution.py:364
  32.9 0.8 %cross_near.1 = (bf16[576,256]{1,0:T(8,128)(2,1)S(1)}, f32[152,768]{1,0:T(8,128)S(1)}) custom-call(s32[1]{0:T(128)} %bitcast.place_ref, bf16[768,128]{1,0:T(8,128)(2,1)S(1)} %get-tuple-element.32.after.refs_3_.q4_ref, bf16[960,256]{1,0:T(8,128)(2,1)S(1)} %collective-permute-done.10.par_ref, bf16[768,768]{1,0:T(8,128)(2,1)S(1)} %get-tuple-element.41.p_ref, ...), custom_call_target="tpu_custom_call" | custom-call | flops 4000000000 | bytes 1 | tf_op jit(solution)/shard_map/cross_near/pallas_call | solution.py:364
  33.7 1.0 %collective-permute-start.12 = (bf16[576,256]{1,0:T(8,128)(2,1)S(1)}, bf16[576,256]{1,0:T(8,128)(2,1)S(1)}, u32[]{:S(2)}, u32[]{:S(2)}) collective-permute-start(bf16[576,256]{1,0:T(8,128)(2,1)S(1)} %get-tuple-element.51), channel_id=1, source_target_pairs={{0,8},{8,0},{16,24},{24,16},{32,40},{40,32},{48,56},{56,48},{64,72... | collective-permute-start | bytes 884744 | tf_op jit(solution)/shard_map/ppermute | solution.py:350
  34.7 0.8 %own_far.1 = (f32[384,256]{1,0:T(8,128)S(1)}, f32[152,768]{1,0:T(8,128)S(1)}) custom-call(bf16[768,128]{1,0:T(8,128)(2,1)S(1)} %get-tuple-element.32.after.refs_3_.q4_ref, bf16[960,256]{1,0:T(8,128)(2,1)S(1)} %join_slots.1.own_ref, bf16[576,768]{1,0:T(8,128)(2,1)S(1)} %get-tuple-element.35.near_ref, bf16[384,768]{1,0:T(8,128)(2,1)S(1)} %get-tuple-element.36.side_ref, ...), custom_call_target="tpu_custom_call" | custom-call | flops 4000000000 | bytes 1 | tf_op jit(solution)/shard_map/own_far/pallas_call | solution.py:364
  35.6 0.8 %collective-permute-start.13 = (bf16[192,256]{1,0:T(8,128)(2,1)S(1)}, bf16[192,256]{1,0:T(8,128)(2,1)S(1)}, u32[]{:S(2)}, u32[]{:S(2)}) collective-permute-start(bf16[192,256]{1,0:T(8,128)(2,1)S(1)} %get-tuple-element.53), channel_id=1, source_target_pairs={{0,16},{8,24},{16,0},{24,8},{32,48},{40,56},{48,32},{56,40},{64,80... | collective-permute-start | bytes 294920 | tf_op jit(solution)/shard_map/ppermute | solution.py:350
  36.3 0.8 %own_near.1 = (f32[384,256]{1,0:T(8,128)S(1)}, f32[152,768]{1,0:T(8,128)S(1)}) custom-call(bf16[768,128]{1,0:T(8,128)(2,1)S(1)} %get-tuple-element.32.after.refs_3_.q4_ref, bf16[960,256]{1,0:T(8,128)(2,1)S(1)} %join_slots.1.own_ref, bf16[576,768]{1,0:T(8,128)(2,1)S(1)} %get-tuple-element.35.near_ref, bf16[384,768]{1,0:T(8,128)(2,1)S(1)} %get-tuple-element.36.side_ref, ...), custom_call_target="tpu_custom_call" | custom-call | flops 4000000000 | bytes 1 | tf_op jit(solution)/shard_map/own_near/pallas_call | solution.py:364
  37.2 1.9 %collective-permute-start.14 = (bf16[192,256]{1,0:T(8,128)(2,1)S(1)}, bf16[192,256]{1,0:T(8,128)(2,1)S(1)}, u32[]{:S(2)}, u32[]{:S(2)}) collective-permute-start(bf16[192,256]{1,0:T(8,128)(2,1)S(1)} %get-tuple-element.55), channel_id=1, source_target_pairs={{0,240},{8,248},{16,0},{24,8},{32,16},{40,24},{48,32},{56,40},{64,... | collective-permute-start | bytes 294920 | tf_op jit(solution)/shard_map/ppermute | solution.py:350
  39.1 2.1 %collective-permute-done.13.side_ref = bf16[192,256]{1,0:T(8,128)(2,1)S(1)} collective-permute-done((bf16[192,256]{1,0:T(8,128)(2,1)S(1)}, bf16[192,256]{1,0:T(8,128)(2,1)S(1)}, u32[]{:S(2)}, u32[]{:S(2)}) %collective-permute-start.13) | collective-permute-done | bytes 98336 | tf_op jit(solution)/shard_map/ppermute | solution.py:350
  41.3 1.2 %collective-permute-start.16 = (bf16[192,256]{1,0:T(8,128)(2,1)S(1)}, bf16[192,256]{1,0:T(8,128)(2,1)S(1)}, u32[]{:S(2)}, u32[]{:S(2)}) collective-permute-start(bf16[192,256]{1,0:T(8,128)(2,1)S(1)} %get-tuple-element.58), channel_id=1, source_target_pairs={{0,224},{8,232},{16,240},{24,248},{32,0},{40,8},{48,16},{56,24},{6... | collective-permute-start | bytes 294920 | tf_op jit(solution)/shard_map/ppermute | solution.py:350
  42.5 0.8 %collective-permute-done.14.refs_1_.two_ref = bf16[192,256]{1,0:T(8,128)(2,1)S(1)} collective-permute-done((bf16[192,256]{1,0:T(8,128)(2,1)S(1)}, bf16[192,256]{1,0:T(8,128)(2,1)S(1)}, u32[]{:S(2)}, u32[]{:S(2)}) %collective-permute-start.14) | collective-permute-done | bytes 98336 | tf_op jit(solution)/shard_map/ppermute | solution.py:350
  43.3 1.2 %own_last.1 = (f32[192,256]{1,0:T(8,128)S(1)}, bf16[192,512]{1,0:T(8,128)(2,1)}) custom-call(bf16[768,128]{1,0:T(8,128)(2,1)S(1)} %get-tuple-element.32.after.refs_3_.q4_ref, bf16[960,256]{1,0:T(8,128)(2,1)S(1)} %join_slots.1.own_ref, bf16[576,768]{1,0:T(8,128)(2,1)S(1)} %get-tuple-element.35.near_ref, bf16[384,768]{1,0:T(8,128)(2,1)S(1)} %get-tuple-element.36.side_ref, ...), custom_call_target="tpu_custom_call" | custom-call | flops 4000000000 | bytes 1 | tf_op jit(solution)/shard_map/own_last/pallas_call | solution.py:364
  44.5 4.8 %collective-permute-done.15.eight_ref = bf16[192,256]{1,0:T(8,128)(2,1)S(1)} collective-permute-done((bf16[192,256]{1,0:T(8,128)(2,1)S(1)}, bf16[192,256]{1,0:T(8,128)(2,1)S(1)}, u32[]{:S(2)}, u32[]{:S(2)}) %collective-permute-start.15) | collective-permute-done | bytes 98336 | tf_op jit(solution)/shard_map/ppermute | solution.py:350
  49.3 0.7 %finish.1 = (bf16[192,128]{1,0:T(8,128)(2,1)}, bf16[192,128]{1,0:T(8,128)(2,1)}) custom-call(f32[192,256]{1,0:T(8,128)S(1)} %gather_near.1.sum_ref, bf16[192,256]{1,0:T(8,128)(2,1)S(1)} %collective-permute-done.15.eight_ref, bf16[192,256]{1,0:T(8,128)(2,1)S(1)} %collective-permute-done.16.four_ref), custom_call_target="tpu_custom_call" | custom-call | flops 1 | bytes 1 | tf_op jit(solution)/shard_map/finish/pallas_call | solution.py:364
  (25 shorter events, 0.8 us)
Async XLA Ops:
  0.6 15.3 %collective-permute-start.2 = (bf16[192,512]{1,0:T(8,128)(2,1)}, bf16[192,512]{1,0:T(8,128)(2,1)S(1)}, u32[]{:S(2)}, u32[]{:S(2)}) collective-permute-start(bf16[192,512]{1,0:T(8,128)(2,1)} %refs_0_.1), channel_id=1, source_target_pairs={{0,1},{1,0},{2,3},{3,2},{4,5},{5,4},{6,7},{7,6},{8,9},{9,8},{10,11... | collective-permute-start | bytes 589832 | tf_op jit(solution)/shard_map/ppermute | solution.py:350
  3.9 13.7 %collective-permute-start.3 = (bf16[192,512]{1,0:T(8,128)(2,1)}, bf16[192,512]{1,0:T(8,128)(2,1)S(1)}, u32[]{:S(2)}, u32[]{:S(2)}) collective-permute-start(bf16[192,512]{1,0:T(8,128)(2,1)} %refs_0_.1), channel_id=1, source_target_pairs={{0,2},{1,3},{2,4},{3,5},{4,6},{5,7},{6,0},{7,1},{8,10},{9,11},{10,... | collective-permute-start | bytes 589832 | tf_op jit(solution)/shard_map/ppermute | solution.py:350
  5.4 12.7 %collective-permute-start.4 = (bf16[192,512]{1,0:T(8,128)(2,1)}, bf16[192,512]{1,0:T(8,128)(2,1)S(1)}, u32[]{:S(2)}, u32[]{:S(2)}) collective-permute-start(bf16[192,512]{1,0:T(8,128)(2,1)} %refs_0_.1), channel_id=1, source_target_pairs={{0,6},{1,7},{2,0},{3,1},{4,2},{5,3},{6,4},{7,5},{8,14},{9,15},{10,... | collective-permute-start | bytes 589832 | tf_op jit(solution)/shard_map/ppermute | solution.py:350
  8.0 10.1 %collective-permute-start = (bf16[192,256]{1,0:T(8,128)(2,1)S(1)}, bf16[192,256]{1,0:T(8,128)(2,1)S(1)}, u32[]{:S(2)}, u32[]{:S(2)}) collective-permute-start(bf16[192,256]{1,0:T(8,128)(2,1)S(1)} %pack.1.z0_ref), channel_id=1, source_target_pairs={{0,64},{8,72},{16,80},{24,88},{32,96},{40,104},{48,112},{56,120},{... | collective-permute-start | bytes 294920 | tf_op jit(solution)/shard_map/ppermute | solution.py:350
  12.6 5.5 %collective-permute-start.1 = (bf16[192,256]{1,0:T(8,128)(2,1)S(1)}, bf16[192,256]{1,0:T(8,128)(2,1)S(1)}, u32[]{:S(2)}, u32[]{:S(2)}) collective-permute-start(bf16[192,256]{1,0:T(8,128)(2,1)S(1)} %pack.1.z0_ref), channel_id=1, source_target_pairs={{0,32},{8,40},{16,48},{24,56},{32,64},{40,72},{48,80},{56,88},{64,... | collective-permute-start | bytes 294920 | tf_op jit(solution)/shard_map/ppermute | solution.py:350
  13.6 14.8 %copy-start = (bf16[192,512]{1,0:T(8,128)(2,1)S(1)}, bf16[192,512]{1,0:T(8,128)(2,1)}, u32[]{:S(2)}) copy-start(bf16[192,512]{1,0:T(8,128)(2,1)} %refs_0_.1) | copy-start | bytes 589828
  16.0 5.8 %collective-permute-start.7 = (bf16[192,512]{1,0:T(8,128)(2,1)S(1)}, bf16[192,512]{1,0:T(8,128)(2,1)S(1)}, u32[]{:S(2)}, u32[]{:S(2)}) collective-permute-start(bf16[192,512]{1,0:T(8,128)(2,1)S(1)} %stage.1.refs_0_.refs_1_), channel_id=1, source_target_pairs={{0,6},{1,7},{2,0},{3,1},{4,2},{5,3},{6,4},{7,5},{8,14},{9,15},{10,... | collective-permute-start | bytes 589832 | tf_op jit(solution)/shard_map/ppermute | solution.py:350
  17.6 8.3 %collective-permute-start.6 = (bf16[192,512]{1,0:T(8,128)(2,1)S(1)}, bf16[192,512]{1,0:T(8,128)(2,1)S(1)}, u32[]{:S(2)}, u32[]{:S(2)}) collective-permute-start(bf16[192,512]{1,0:T(8,128)(2,1)S(1)} %stage.1.refs_0_.refs_1_), channel_id=1, source_target_pairs={{0,2},{1,3},{2,4},{3,5},{4,6},{5,7},{6,0},{7,1},{8,10},{9,11},{10,... | collective-permute-start | bytes 589832 | tf_op jit(solution)/shard_map/ppermute | solution.py:350
  18.1 9.0 %collective-permute-start.5 = (bf16[384,256]{1,0:T(8,128)(2,1)S(1)}, bf16[384,256]{1,0:T(8,128)(2,1)S(1)}, u32[]{:S(2)}, u32[]{:S(2)}) collective-permute-start(bf16[384,256]{1,0:T(8,128)(2,1)S(1)} %pick_side.1.refs_0_), channel_id=1, source_target_pairs={{0,16},{8,24},{16,0},{24,8},{32,48},{40,56},{48,32},{56,40},{64,80... | collective-permute-start | bytes 589832 | tf_op jit(solution)/shard_map/ppermute | solution.py:350
  18.9 9.5 %collective-permute-start.9 = (bf16[192,512]{1,0:T(8,128)(2,1)S(1)}, bf16[192,512]{1,0:T(8,128)(2,1)S(1)}, u32[]{:S(2)}, u32[]{:S(2)}) collective-permute-start(bf16[192,512]{1,0:T(8,128)(2,1)S(1)} %collective-permute-done.3.refs_1_.refs_2_), channel_id=1, source_target_pairs={{0,2},{1,3},{2,4},{3,5},{4,6},{5,7},{6,0},{7,1},{8,10},{9,11},{10,... | collective-permute-start | bytes 589832 | tf_op jit(solution)/shard_map/ppermute | solution.py:350
  21.8 8.0 %collective-permute-start.8 = (bf16[192,512]{1,0:T(8,128)(2,1)S(1)}, bf16[192,512]{1,0:T(8,128)(2,1)S(1)}, u32[]{:S(2)}, u32[]{:S(2)}) collective-permute-start(bf16[192,512]{1,0:T(8,128)(2,1)S(1)} %collective-permute-done.7.refs_2_.refs_5_), channel_id=1, source_target_pairs={{0,6},{1,7},{2,0},{3,1},{4,2},{5,3},{6,4},{7,5},{8,14},{9,15},{10,... | collective-permute-start | bytes 589832 | tf_op jit(solution)/shard_map/ppermute | solution.py:350
  27.2 3.0 %collective-permute-start.10 = (bf16[960,256]{1,0:T(8,128)(2,1)S(1)}, bf16[960,256]{1,0:T(8,128)(2,1)S(1)}, u32[]{:S(2)}, u32[]{:S(2)}) collective-permute-start(bf16[960,256]{1,0:T(8,128)(2,1)S(1)} %join_slots.1.own_ref), channel_id=1, source_target_pairs={{0,8},{8,0},{16,24},{24,16},{32,40},{40,32},{48,56},{56,48},{64,72... | collective-permute-start | bytes 1474568 | tf_op jit(solution)/shard_map/ppermute | solution.py:350
  32.8 2.8 %collective-permute-start.11 = (bf16[384,256]{1,0:T(8,128)(2,1)S(1)}, bf16[384,256]{1,0:T(8,128)(2,1)S(1)}, u32[]{:S(2)}, u32[]{:S(2)}) collective-permute-start(bf16[384,256]{1,0:T(8,128)(2,1)S(1)} %get-tuple-element.47), channel_id=1, source_target_pairs={{0,8},{8,0},{16,24},{24,16},{32,40},{40,32},{48,56},{56,48},{64,72... | collective-permute-start | bytes 589832 | tf_op jit(solution)/shard_map/ppermute | solution.py:350
  33.7 3.5 %collective-permute-start.12 = (bf16[576,256]{1,0:T(8,128)(2,1)S(1)}, bf16[576,256]{1,0:T(8,128)(2,1)S(1)}, u32[]{:S(2)}, u32[]{:S(2)}) collective-permute-start(bf16[576,256]{1,0:T(8,128)(2,1)S(1)} %get-tuple-element.51), channel_id=1, source_target_pairs={{0,8},{8,0},{16,24},{24,16},{32,40},{40,32},{48,56},{56,48},{64,72... | collective-permute-start | bytes 884744 | tf_op jit(solution)/shard_map/ppermute | solution.py:350
  35.6 5.6 %collective-permute-start.13 = (bf16[192,256]{1,0:T(8,128)(2,1)S(1)}, bf16[192,256]{1,0:T(8,128)(2,1)S(1)}, u32[]{:S(2)}, u32[]{:S(2)}) collective-permute-start(bf16[192,256]{1,0:T(8,128)(2,1)S(1)} %get-tuple-element.53), channel_id=1, source_target_pairs={{0,16},{8,24},{16,0},{24,8},{32,48},{40,56},{48,32},{56,40},{64,80... | collective-permute-start | bytes 294920 | tf_op jit(solution)/shard_map/ppermute | solution.py:350
  37.2 6.1 %collective-permute-start.14 = (bf16[192,256]{1,0:T(8,128)(2,1)S(1)}, bf16[192,256]{1,0:T(8,128)(2,1)S(1)}, u32[]{:S(2)}, u32[]{:S(2)}) collective-permute-start(bf16[192,256]{1,0:T(8,128)(2,1)S(1)} %get-tuple-element.55), channel_id=1, source_target_pairs={{0,240},{8,248},{16,0},{24,8},{32,16},{40,24},{48,32},{56,40},{64,... | collective-permute-start | bytes 294920 | tf_op jit(solution)/shard_map/ppermute | solution.py:350
  41.2 8.1 %collective-permute-start.15 = (bf16[192,256]{1,0:T(8,128)(2,1)S(1)}, bf16[192,256]{1,0:T(8,128)(2,1)S(1)}, u32[]{:S(2)}, u32[]{:S(2)}) collective-permute-start(bf16[192,256]{1,0:T(8,128)(2,1)S(1)} %get-tuple-element.54.refs_0_), channel_id=1, source_target_pairs={{0,192},{8,200},{16,208},{24,216},{32,224},{40,232},{48,240},{56,2... | collective-permute-start | bytes 294920 | tf_op jit(solution)/shard_map/ppermute | solution.py:350
  41.3 8.1 %collective-permute-start.16 = (bf16[192,256]{1,0:T(8,128)(2,1)S(1)}, bf16[192,256]{1,0:T(8,128)(2,1)S(1)}, u32[]{:S(2)}, u32[]{:S(2)}) collective-permute-start(bf16[192,256]{1,0:T(8,128)(2,1)S(1)} %get-tuple-element.58), channel_id=1, source_target_pairs={{0,224},{8,232},{16,240},{24,248},{32,0},{40,8},{48,16},{56,24},{6... | collective-permute-start | bytes 294920 | tf_op jit(solution)/shard_map/ppermute | solution.py:350
